TPU v7x, 32 devices: a whole 2x2x4 slice. The times are simulated.
32 devices in a mesh: ctx: 4 (over x, core), fsdp: 8 (over z, y).
Axes of the slice: x: 2, y: 2, z: 4, core: 2. Of those that a mesh axis runs over, the one named last changes fastest.
Arguments:
- tokens: bfloat16 [8, 1024, 1024], P('fsdp', 'ctx'), may hold values from -6 to 6
- teacher: bfloat16 [8, 1024, 1024], P('fsdp', 'ctx'), may hold values from -6 to 6
- segment_ids: int32 [8, 1024], P('fsdp'), may hold values from 0 to 5, as said below
- valid_mask: int32 [8, 1024], P('fsdp', 'ctx'), may hold values from 0 to 1, as said below
- gain_in: bfloat16 [1024], P('fsdp'), may hold values from 0.5 to 1.5
- w_in: bfloat16 [1024, 3352], P('fsdp'), may hold values from -0.1875 to 0.1875
- conv_w: bfloat16 [4, 1792], P(None, 'fsdp'), may hold values from -3 to 3
- conv_b: bfloat16 [1792], P('fsdp'), may hold values from -3 to 3
- dt_bias: float32 [24], replicated, may hold values from -2 to 1
- a_log: float32 [24], replicated, may hold values from -10.4 to -3
- d_skip: float32 [24], replicated, may hold values from 0.5 to 1.5
- gain_m: bfloat16 [1536], P('fsdp'), may hold values from 0.5 to 1.5
- w_out: bfloat16 [1536, 1024], P('fsdp'), may hold values from -0.15625 to 0.15625
- w_qkv: bfloat16 [1024, 768], P('fsdp'), may hold values from -0.1875 to 0.1875
- w_o: bfloat16 [512, 1024], P('fsdp'), may hold values from -3.5 to 3.5
- gain_ffn: bfloat16 [1024], P('fsdp'), may hold values from 0.5 to 1.5
- w_gate: bfloat16 [1024, 2048], P('fsdp'), may hold values from -0.1875 to 0.1875
- w_up: bfloat16 [1024, 2048], P('fsdp'), may hold values from -0.1875 to 0.1875
- w_down: bfloat16 [2048, 1024], P('fsdp'), may hold values from -0.125 to 0.125
Outputs:
- loss: float32 [], replicated
- layer_out: float32 [8, 1024, 1024], P('fsdp', 'ctx')
- grad_tokens: float32 [8, 1024, 1024], P('fsdp', 'ctx')
- grad_gain_in: float32 [1024], P('fsdp')
- grad_w_in: float32 [1024, 3352], P('fsdp')
- grad_conv_w: float32 [4, 1792], P(None, 'fsdp')
- grad_conv_b: float32 [1792], P('fsdp')
- grad_dt_bias: float32 [24], replicated
- grad_a_log: float32 [24], replicated
- grad_d_skip: float32 [24], replicated
- grad_gain_m: float32 [1536], P('fsdp')
- grad_w_out: float32 [1536, 1024], P('fsdp')
- grad_w_qkv: float32 [1024, 768], P('fsdp')
- grad_w_o: float32 [512, 1024], P('fsdp')
- grad_gain_ffn: float32 [1024], P('fsdp')
- grad_w_gate: float32 [1024, 2048], P('fsdp')
- grad_w_up: float32 [1024, 2048], P('fsdp')
- grad_w_down: float32 [2048, 1024], P('fsdp')
Inputs may be any that keep to these rules, and one draw needn't show every extreme that they name: `segment_ids`: segment numbers start at 0 in each sequence and rise by one at each document's first token; every document but the last of a sequence has 200 to 2000 tokens, the last one at most 2000; in the first sequence every document but the last has exactly 200 tokens. `valid_mask`: the first token of every sequence is valid.
All inputs are finite; a program needn't handle non-finite values.
Results may differ from a plain program's by a relative error of at most 0.019.
Values may be sent and summed in bfloat16 or wider, within the bound.
No kernel may reach another device: no remote copies, remote signals or barrier semaphores. Data moves between devices by JAX's collectives and lax.ppermute only.
A program may use at most 192 MiB of HBM per device.

v0:
```python
import jax
import jax.numpy as jnp
from jax import lax
from jax.sharding import PartitionSpec as P

MH = 24
HP = 64
NS = 128
KW = 4
QH = 8
KVH = 2
HD = 64
SPAN = 128


EPSILON = 1e-05
ROPE_BASE = 100000000000.0
MASKED = -1e30


def from_behind(value, axis, by):
    count = lax.axis_size(axis)
    pairs = [(i, i + by) for i in range(count) if 0 <= i + by < count]
    return lax.ppermute(value, axis, pairs)


def carried_in(value, axis, join, neutral):
    place = lax.axis_index(axis)
    gathered = jax.tree.map(
        lambda a, kind: lax.all_gather(a.astype(kind), axis), value, (jnp.bfloat16, jnp.bfloat16)
    )
    state = jax.tree.map(lambda a, e: jnp.zeros_like(a) + jnp.asarray(e, a.dtype), value, neutral)

    def carried_one(turn, state):
        return join(
            state,
            jax.tree.map(
                lambda a, own: lax.dynamic_index_in_dim(a, turn, 0, False).astype(own.dtype),
                gathered,
                value,
            ),
        )

    return lax.fori_loop(0, place, carried_one, state)


def prefix(value, axis, join, neutral):
    count = lax.axis_size(axis)
    place = lax.axis_index(axis)
    ahead = count - 1 - place
    gathered = jax.tree.map(
        lambda a, kind: lax.all_gather(a.astype(kind), axis),
        value,
        jax.tree.map(lambda a: jnp.bfloat16 if a.dtype == jnp.float32 else a.dtype, value),
    )
    state = jax.tree.map(lambda a, e: jnp.zeros_like(a) + jnp.asarray(e, a.dtype), value, neutral)

    def prefix_one(turn, state):
        source = count - 1 - turn
        return join(
            state,
            jax.tree.map(
                lambda a, own: lax.dynamic_index_in_dim(a, source, 0, False).astype(own.dtype),
                gathered,
                value,
            ),
        )

    return lax.fori_loop(0, ahead, prefix_one, state)


def plain_dot(left, right):
    return jnp.dot(left, right, preferred_element_type=jnp.float32)


def dot_back(left, right):
    return lax.dot_general(
        left, right, (((1,), (1,)), ((), ())), preferred_element_type=jnp.float32
    )


def dot_over_rows(left, right):
    return lax.dot_general(
        left, right, (((0,), (0,)), ((), ())), preferred_element_type=jnp.float32
    )


def norm_rows(values, gain):
    return values * lax.rsqrt(jnp.mean(values * values, axis=-1, keepdims=True) + EPSILON) * gain


def rotary(values, positions):
    half = values.shape[-1] // 2
    freq = ROPE_BASE ** (-(jnp.arange(half, dtype=jnp.float32) * 2.0 / values.shape[-1]))
    angle = positions.astype(jnp.float32)[:, None] * freq[None, :]
    cosine = jnp.cos(angle)[:, None, :]
    sine = jnp.sin(angle)[:, None, :]
    first_half = values[..., :half]
    second_half = values[..., half:]
    return jnp.concatenate(
        [first_half * cosine - second_half * sine, second_half * cosine + first_half * sine],
        axis=-1,
    )


def conv_silu(extended, seg_ext, kernel, kernel_bias):
    width = kernel.shape[0]
    count_rows = extended.shape[0] - width + 1
    last_seg = seg_ext[width - 1 :]
    total = kernel_bias[None, :] + jnp.zeros((count_rows, kernel.shape[1]), jnp.float32)
    for tap in range(width):
        same = (seg_ext[tap : tap + count_rows] == last_seg).astype(jnp.float32)
        total = total + kernel[tap][None, :] * extended[tap : tap + count_rows] * same[:, None]
    return jax.nn.silu(total)


def state_space(x_in, b_in, c_in, step_size, log_decay, segment, seg_before):
    count_rows = x_in.shape[0]
    blocks = count_rows // SPAN

    def split(values):
        return values.reshape((blocks, SPAN) + values.shape[1:])

    inputs = (
        split(x_in),
        split(b_in),
        split(c_in),
        split(step_size),
        split(log_decay),
        split(segment),
    )
    lower = jnp.tril(jnp.ones((SPAN, SPAN), bool))

    def step(carry, block):
        state, decay, last_seg = carry
        x_blk, b_blk, c_blk, step_blk, decay_blk, seg_blk = block
        running = jnp.cumsum(decay_blk, axis=0)
        same = ((seg_blk[:, None] == seg_blk[None, :]) & lower)[:, :, None]
        gap = jnp.where(same, running[:, None, :] - running[None, :, :], 0.0)
        decay_matrix = jnp.where(same, jnp.exp(gap), 0.0)
        gram = dot_back(c_blk.astype(jnp.bfloat16), b_blk.astype(jnp.bfloat16))
        mixing = gram[:, :, None] * decay_matrix * step_blk[None, :, :]
        inside = jnp.einsum(
            "tsh,shp->thp",
            mixing,
            x_blk,
            precision=lax.Precision.HIGHEST,
            preferred_element_type=jnp.float32,
        )
        keep = (seg_blk == last_seg).astype(jnp.float32)
        carry_weight = jnp.exp(running) * keep[:, None]
        from_state = jnp.einsum(
            "tn,hpn->thp",
            c_blk,
            state,
            precision=lax.Precision.HIGHEST,
            preferred_element_type=jnp.float32,
        )
        end_seg = seg_blk[-1]
        tail = (seg_blk == end_seg).astype(jnp.float32)
        end_weight = jnp.exp(running[-1][None, :] - running) * tail[:, None] * step_blk
        local = jnp.einsum(
            "sh,shp,sn->hpn",
            end_weight,
            x_blk,
            b_blk,
            precision=lax.Precision.HIGHEST,
            preferred_element_type=jnp.float32,
        )
        link = jnp.exp(running[-1]) * (end_seg == last_seg).astype(jnp.float32)
        new_state = link[:, None, None] * state + local
        return ((new_state, decay * link, end_seg), inside + from_state * carry_weight[:, :, None])

    init = (jnp.zeros((MH, HP, NS), jnp.float32), jnp.ones((MH,), jnp.float32), seg_before)
    (state, decay, _), outputs = lax.scan(jax.checkpoint(step), init, inputs)
    return (outputs.reshape(x_in.shape), decay, state)


def chain_combine(earlier, later):
    return (earlier[0] * later[0], later[0][:, None, None] * earlier[1] + later[1])


def per_device(
    tokens,
    teacher,
    segment_ids,
    valid_mask,
    gain_in,
    w_in,
    conv_w,
    conv_b,
    dt_bias,
    a_log,
    d_skip,
    gain_m,
    w_out,
    w_qkv,
    w_o,
    gain_ffn,
    w_gate,
    w_up,
    w_down,
):
    rows = tokens.shape[1]
    length = segment_ids.shape[1]
    ssm_width = MH * HP
    conv_width = ssm_width + 2 * NS
    q_width = QH * HD
    kv_width = KVH * HD
    group = QH // KVH
    scale = HD ** (-0.5)
    ctx_index = lax.axis_index("ctx")
    row_start = ctx_index * rows
    seg_all = segment_ids[0]
    tok_seg = lax.dynamic_slice_in_dim(seg_all, row_start, rows)
    padded_seg = jnp.concatenate([jnp.full((KW - 1,), -1, jnp.int32), seg_all])
    seg_ext = lax.dynamic_slice_in_dim(padded_seg, row_start, rows + KW - 1)
    seg_prev = seg_ext[KW - 2]
    tok_pos = row_start + jnp.arange(rows, dtype=jnp.int32)
    gathered = (
        lax.all_gather(gain_in, "fsdp", axis=0, tiled=True),
        lax.all_gather(w_in, "fsdp", axis=0, tiled=True),
        lax.all_gather(conv_w, "fsdp", axis=1, tiled=True),
        lax.all_gather(conv_b, "fsdp", axis=0, tiled=True),
        lax.all_gather(gain_m, "fsdp", axis=0, tiled=True),
        lax.all_gather(w_out, "fsdp", axis=0, tiled=True),
        lax.all_gather(w_qkv, "fsdp", axis=0, tiled=True),
        lax.all_gather(w_o, "fsdp", axis=0, tiled=True),
        lax.all_gather(gain_ffn, "fsdp", axis=0, tiled=True),
        lax.all_gather(w_gate, "fsdp", axis=0, tiled=True),
        lax.all_gather(w_up, "fsdp", axis=0, tiled=True),
        lax.all_gather(w_down, "fsdp", axis=0, tiled=True),
    )
    (
        gain_input,
        weight_in,
        kernel,
        kernel_bias,
        gain_mamba,
        weight_mamba,
        weight_qkv,
        weight_attn,
        gain_second,
        weight_gate,
        weight_up,
        weight_down,
    ) = gathered
    resid = tokens[0].astype(jnp.float32)
    normed, norm1_back = jax.vjp(norm_rows, resid, gain_input.astype(jnp.float32))
    normed_low = normed.astype(jnp.bfloat16)
    projected = plain_dot(normed_low, weight_in)
    gate_ssm = projected[:, :ssm_width]
    conv_input = projected[:, ssm_width : ssm_width + conv_width]
    step_raw = projected[:, ssm_width + conv_width :]
    edge_rows = from_behind(conv_input[rows - KW + 1 :], "ctx", 1)

    def mamba_pre(edge, conv_in, step_in, taps, tap_bias, step_bias, decay_log):
        activated = conv_silu(jnp.concatenate([edge, conv_in], axis=0), seg_ext, taps, tap_bias)
        step_size = jax.nn.softplus(step_in + step_bias)
        return (activated, step_size, -step_size * jnp.exp(decay_log))

    (activated, step_size, log_decay), pre_back = jax.vjp(
        mamba_pre,
        edge_rows,
        conv_input,
        step_raw,
        kernel.astype(jnp.float32),
        kernel_bias.astype(jnp.float32),
        dt_bias,
        a_log,
    )
    x_ssm = activated[:, :ssm_width].astype(jnp.bfloat16).astype(jnp.float32).reshape(rows, MH, HP)
    b_ssm = activated[:, ssm_width : ssm_width + NS].astype(jnp.bfloat16).astype(jnp.float32)
    c_ssm = activated[:, ssm_width + NS :].astype(jnp.bfloat16).astype(jnp.float32)

    def local_scan(x_in, b_in, c_in, step_in, decay_in):
        return state_space(x_in, b_in, c_in, step_in, decay_in, tok_seg, seg_prev)

    (y_local, dev_decay, dev_state), local_back = jax.vjp(
        local_scan, x_ssm, b_ssm, c_ssm, step_size, log_decay
    )
    identity = (jnp.ones((MH,), jnp.float32), jnp.zeros((MH, HP, NS), jnp.float32))
    state_in = carried_in((dev_decay, dev_state), "ctx", chain_combine, identity)[1]

    def carried(c_in, decay_in, state):
        running = jnp.cumsum(decay_in, axis=0)
        keep = (tok_seg == seg_prev).astype(jnp.float32)
        weight = jnp.exp(running) * keep[:, None]
        return (
            jnp.einsum(
                "tn,hpn->thp",
                c_in,
                state,
                precision=lax.Precision.HIGHEST,
                preferred_element_type=jnp.float32,
            )
            * weight[:, :, None]
        )

    y_carry, carry_back = jax.vjp(carried, c_ssm, log_decay, state_in)
    ssm_out = y_local + y_carry + d_skip[None, :, None] * x_ssm

    def mamba_post(ssm_in, gate_in, gain):
        return norm_rows(ssm_in.reshape(rows, ssm_width) * jax.nn.silu(gate_in), gain)

    mamba_normed, post_back = jax.vjp(mamba_post, ssm_out, gate_ssm, gain_mamba.astype(jnp.float32))
    mamba_low = mamba_normed.astype(jnp.bfloat16)
    mamba_out = plain_dot(mamba_low, weight_mamba)
    qkv = plain_dot(normed_low, weight_qkv)

    def rotate_pair(q_raw, k_raw):
        return (rotary(q_raw, tok_pos), rotary(k_raw, tok_pos))

    (q_rot, k_rot), rotate_back = jax.vjp(
        rotate_pair,
        qkv[:, :q_width].reshape(rows, QH, HD),
        qkv[:, q_width : q_width + kv_width].reshape(rows, KVH, HD),
    )
    query = q_rot.astype(jnp.bfloat16).reshape(rows, KVH, group, HD)
    keys_own = k_rot.astype(jnp.bfloat16).reshape(rows, kv_width)
    values_own = qkv[:, q_width + kv_width :].astype(jnp.bfloat16)
    keys_all, values_all = (
        lax.all_gather(keys_own, "ctx", axis=0, tiled=True),
        lax.all_gather(values_own, "ctx", axis=0, tiled=True),
    )
    blocks = length // rows
    low_block = 0

    def block_scores(key_start):
        key_block = lax.dynamic_slice_in_dim(keys_all, key_start, rows).reshape(rows, KVH, HD)
        raw = (
            jnp.einsum("tkgd,skd->kgts", query, key_block, preferred_element_type=jnp.float32)
            * scale
        )
        key_seg = lax.dynamic_slice_in_dim(seg_all, key_start, rows)
        key_pos = key_start + jnp.arange(rows, dtype=jnp.int32)
        allowed = (tok_seg[:, None] == key_seg[None, :]) & (key_pos[None, :] <= tok_pos[:, None])
        return (jnp.where(allowed, raw, MASKED), key_block)

    def running_max(index, carry):
        top, total = carry
        scores, _ = block_scores(index * rows)
        new_top = jnp.maximum(top, jnp.max(scores, axis=-1))
        total = total * jnp.exp(top - new_top) + jnp.sum(
            jnp.exp(scores - new_top[..., None]), axis=-1
        )
        return (new_top, total)

    start_stats = (
        jnp.full((KVH, group, rows), MASKED, jnp.float32),
        jnp.zeros((KVH, group, rows), jnp.float32),
    )
    top, total = lax.fori_loop(low_block, blocks, running_max, start_stats)
    log_total = top + jnp.log(total)

    def weighted_values(index, accum):
        start = index * rows
        scores, _ = block_scores(start)
        probs = jnp.exp(scores - log_total[..., None]).astype(jnp.bfloat16)
        value_block = lax.dynamic_slice_in_dim(values_all, start, rows).reshape(rows, KVH, HD)
        return accum + jnp.einsum(
            "kgts,skd->tkgd", probs, value_block, preferred_element_type=jnp.float32
        )

    attended = lax.fori_loop(
        low_block, blocks, weighted_values, jnp.zeros((rows, KVH, group, HD), jnp.float32)
    )
    attended_low = attended.reshape(rows, q_width).astype(jnp.bfloat16)
    attn_out = plain_dot(attended_low, weight_attn)
    mixed = resid + mamba_out + attn_out
    normed2, norm2_back = jax.vjp(norm_rows, mixed, gain_second.astype(jnp.float32))
    normed2_low = normed2.astype(jnp.bfloat16)
    gate_val = plain_dot(normed2_low, weight_gate)
    up_val = plain_dot(normed2_low, weight_up)

    def swiglu(gate_in, up_in):
        return jax.nn.silu(gate_in) * up_in

    product, swiglu_back = jax.vjp(swiglu, gate_val, up_val)
    product_low = product.astype(jnp.bfloat16)
    layer_out = mixed + plain_dot(product_low, weight_down)
    target = teacher[0].astype(jnp.float32)
    valid = valid_mask[0].astype(jnp.float32)
    diff = layer_out - target
    squared_local = jnp.sum(valid[:, None] * diff * diff)
    count_local = jnp.sum(valid)
    squared_total, count_total = lax.psum((squared_local, count_local), ("ctx", "fsdp"))
    loss = squared_total / (2.0 * count_total)
    token_total = length * lax.axis_size("fsdp") * tokens.shape[0]
    grad_out = token_total * valid[:, None] * diff / count_total
    regathered = (
        lax.all_gather(gain_in, "fsdp", axis=0, tiled=True),
        lax.all_gather(w_in, "fsdp", axis=0, tiled=True),
        lax.all_gather(conv_w, "fsdp", axis=1, tiled=True),
        lax.all_gather(conv_b, "fsdp", axis=0, tiled=True),
        lax.all_gather(gain_m, "fsdp", axis=0, tiled=True),
        lax.all_gather(w_out, "fsdp", axis=0, tiled=True),
        lax.all_gather(w_qkv, "fsdp", axis=0, tiled=True),
        lax.all_gather(w_o, "fsdp", axis=0, tiled=True),
        lax.all_gather(gain_ffn, "fsdp", axis=0, tiled=True),
        lax.all_gather(w_gate, "fsdp", axis=0, tiled=True),
        lax.all_gather(w_up, "fsdp", axis=0, tiled=True),
        lax.all_gather(w_down, "fsdp", axis=0, tiled=True),
    )
    back_in = regathered[1]
    back_mamba = regathered[5]
    back_qkv = regathered[6]
    back_attn = regathered[7]
    back_gate = regathered[9]
    back_up = regathered[10]
    back_down = regathered[11]
    out_low = grad_out.astype(jnp.bfloat16)
    grad_down = dot_over_rows(product_low, out_low)
    grad_product = dot_back(out_low, back_down)
    grad_gate_val, grad_up_val = swiglu_back(grad_product)
    gate_low = grad_gate_val.astype(jnp.bfloat16)
    up_low = grad_up_val.astype(jnp.bfloat16)
    grad_gate_w = dot_over_rows(normed2_low, gate_low)
    grad_up_w = dot_over_rows(normed2_low, up_low)
    grad_normed2 = dot_back(gate_low, back_gate) + dot_back(up_low, back_up)
    grad_mixed_part, grad_gain_second = norm2_back(grad_normed2)
    grad_mixed = grad_out + grad_mixed_part
    mixed_low = grad_mixed.astype(jnp.bfloat16)
    grad_attn_w = dot_over_rows(attended_low, mixed_low)
    grad_mamba_w = dot_over_rows(mamba_low, mixed_low)
    grad_attended = (
        dot_back(mixed_low, back_attn).astype(jnp.bfloat16).reshape(rows, KVH, group, HD)
    )
    grad_mamba_normed = dot_back(mixed_low, back_mamba)
    delta = jnp.transpose(jnp.sum(grad_attended.astype(jnp.float32) * attended, axis=-1), (1, 2, 0))

    def attention_back(index, carry):
        grad_query, grad_pairs = carry
        start = index * rows
        scores, key_block = block_scores(start)
        value_block = lax.dynamic_slice_in_dim(values_all, start, rows).reshape(rows, KVH, HD)
        probs = jnp.exp(scores - log_total[..., None])
        grad_probs = jnp.einsum(
            "tkgd,skd->kgts", grad_attended, value_block, preferred_element_type=jnp.float32
        )
        grad_scores = (probs * (grad_probs - delta[..., None])).astype(jnp.bfloat16)
        grad_query = (
            grad_query
            + jnp.einsum(
                "kgts,skd->tkgd", grad_scores, key_block, preferred_element_type=jnp.float32
            )
            * scale
        )
        grad_keys = (
            jnp.einsum("kgts,tkgd->skd", grad_scores, query, preferred_element_type=jnp.float32)
            * scale
        )
        grad_values = jnp.einsum(
            "kgts,tkgd->skd",
            probs.astype(jnp.bfloat16),
            grad_attended,
            preferred_element_type=jnp.float32,
        )
        pair = jnp.stack(
            [grad_keys.reshape(rows, kv_width), grad_values.reshape(rows, kv_width)], axis=1
        )
        return (grad_query, lax.dynamic_update_slice_in_dim(grad_pairs, pair, start, 0))

    start_back = (
        jnp.zeros((rows, KVH, group, HD), jnp.float32),
        jnp.zeros((length, 2, kv_width), jnp.float32),
    )
    grad_query, grad_pairs = lax.fori_loop(low_block, blocks, attention_back, start_back)
    grad_pairs_own = lax.psum_scatter(
        grad_pairs.astype(jnp.bfloat16), "ctx", scatter_dimension=0, tiled=True
    ).astype(jnp.float32)
    grad_q_raw, grad_k_raw = rotate_back(
        (grad_query.reshape(rows, QH, HD), grad_pairs_own[:, 0].reshape(rows, KVH, HD))
    )
    grad_qkv = jnp.concatenate(
        [
            grad_q_raw.reshape(rows, q_width),
            grad_k_raw.reshape(rows, kv_width),
            grad_pairs_own[:, 1],
        ],
        axis=1,
    ).astype(jnp.bfloat16)
    grad_qkv_w = dot_over_rows(normed_low, grad_qkv)
    grad_ssm, grad_gate_ssm, grad_gain_mamba = post_back(grad_mamba_normed)
    grad_skip = jnp.sum(grad_ssm * x_ssm, axis=(0, 2))
    grad_c_carry, grad_decay_carry, state_grad_own = carry_back(grad_ssm)
    state_grad = prefix((dev_decay, state_grad_own), "ctx", chain_combine, identity)[1]
    grad_dev_decay = jnp.sum(state_grad * state_in, axis=(1, 2))
    grad_x, grad_b, grad_c, grad_step, grad_decay = local_back(
        (grad_ssm, grad_dev_decay, state_grad)
    )
    grad_x = grad_x + d_skip[None, :, None] * grad_ssm
    grad_c = grad_c + grad_c_carry
    grad_decay = grad_decay + grad_decay_carry
    grad_activated = jnp.concatenate([grad_x.reshape(rows, ssm_width), grad_b, grad_c], axis=1)
    (
        grad_edge,
        grad_conv_in,
        grad_step_raw,
        grad_kernel,
        grad_kernel_bias,
        grad_step_bias,
        grad_decay_log,
    ) = pre_back((grad_activated, grad_step, grad_decay))
    edge_back = from_behind(grad_edge, "ctx", -1)
    grad_conv_in = jnp.concatenate(
        [grad_conv_in[: rows - KW + 1], grad_conv_in[rows - KW + 1 :] + edge_back], axis=0
    )
    grad_projected = jnp.concatenate([grad_gate_ssm, grad_conv_in, grad_step_raw], axis=1).astype(
        jnp.bfloat16
    )
    grad_in_w = dot_over_rows(normed_low, grad_projected)
    grad_normed = dot_back(grad_projected, back_in) + dot_back(grad_qkv, back_qkv)
    grad_resid_part, grad_gain_input = norm1_back(grad_normed)
    grad_tokens = grad_mixed + grad_resid_part
    shards = (
        lax.psum_scatter(
            grad_gain_input.astype(jnp.bfloat16), "fsdp", scatter_dimension=0, tiled=True
        ).astype(jnp.float32),
        lax.psum_scatter(
            grad_in_w.astype(jnp.bfloat16), "fsdp", scatter_dimension=0, tiled=True
        ).astype(jnp.float32),
        lax.psum_scatter(
            grad_kernel.astype(jnp.bfloat16), "fsdp", scatter_dimension=1, tiled=True
        ).astype(jnp.float32),
        lax.psum_scatter(
            grad_kernel_bias.astype(jnp.bfloat16), "fsdp", scatter_dimension=0, tiled=True
        ).astype(jnp.float32),
        lax.psum_scatter(
            grad_gain_mamba.astype(jnp.bfloat16), "fsdp", scatter_dimension=0, tiled=True
        ).astype(jnp.float32),
        lax.psum_scatter(
            grad_mamba_w.astype(jnp.bfloat16), "fsdp", scatter_dimension=0, tiled=True
        ).astype(jnp.float32),
        lax.psum_scatter(
            grad_qkv_w.astype(jnp.bfloat16), "fsdp", scatter_dimension=0, tiled=True
        ).astype(jnp.float32),
        lax.psum_scatter(
            grad_attn_w.astype(jnp.bfloat16), "fsdp", scatter_dimension=0, tiled=True
        ).astype(jnp.float32),
        lax.psum_scatter(
            grad_gain_second.astype(jnp.bfloat16), "fsdp", scatter_dimension=0, tiled=True
        ).astype(jnp.float32),
        lax.psum_scatter(
            grad_gate_w.astype(jnp.bfloat16), "fsdp", scatter_dimension=0, tiled=True
        ).astype(jnp.float32),
        lax.psum_scatter(
            grad_up_w.astype(jnp.bfloat16), "fsdp", scatter_dimension=0, tiled=True
        ).astype(jnp.float32),
        lax.psum_scatter(
            grad_down.astype(jnp.bfloat16), "fsdp", scatter_dimension=0, tiled=True
        ).astype(jnp.float32),
    )
    shards = (
        lax.psum(shards[0].astype(jnp.bfloat16), "ctx").astype(jnp.float32),
        lax.psum(shards[1].astype(jnp.bfloat16), "ctx").astype(jnp.float32),
        lax.psum(shards[2].astype(jnp.bfloat16), "ctx").astype(jnp.float32),
        lax.psum(shards[3].astype(jnp.bfloat16), "ctx").astype(jnp.float32),
        lax.psum(shards[4].astype(jnp.bfloat16), "ctx").astype(jnp.float32),
        lax.psum(shards[5].astype(jnp.bfloat16), "ctx").astype(jnp.float32),
        lax.psum(shards[6].astype(jnp.bfloat16), "ctx").astype(jnp.float32),
        lax.psum(shards[7].astype(jnp.bfloat16), "ctx").astype(jnp.float32),
        lax.psum(shards[8].astype(jnp.bfloat16), "ctx").astype(jnp.float32),
        lax.psum(shards[9].astype(jnp.bfloat16), "ctx").astype(jnp.float32),
        lax.psum(shards[10].astype(jnp.bfloat16), "ctx").astype(jnp.float32),
        lax.psum(shards[11].astype(jnp.bfloat16), "ctx").astype(jnp.float32),
    )
    heads = lax.psum((grad_step_bias, grad_decay_log, grad_skip), ("ctx", "fsdp"))
    return (
        loss,
        layer_out[None],
        grad_tokens[None],
        shards[0],
        shards[1],
        shards[2],
        shards[3],
        heads[0],
        heads[1],
        heads[2],
        shards[4],
        shards[5],
        shards[6],
        shards[7],
        shards[8],
        shards[9],
        shards[10],
        shards[11],
    )


def solution(mesh):
    in_specs = (
        P("fsdp", "ctx", None),
        P("fsdp", "ctx", None),
        P("fsdp", None),
        P("fsdp", "ctx"),
        P("fsdp"),
        P("fsdp", None),
        P(None, "fsdp"),
        P("fsdp"),
        P(),
        P(),
        P(),
        P("fsdp"),
        P("fsdp", None),
        P("fsdp", None),
        P("fsdp", None),
        P("fsdp"),
        P("fsdp", None),
        P("fsdp", None),
        P("fsdp", None),
    )
    out_specs = (
        P(),
        P("fsdp", "ctx", None),
        P("fsdp", "ctx", None),
        P("fsdp"),
        P("fsdp", None),
        P(None, "fsdp"),
        P("fsdp"),
        P(),
        P(),
        P(),
        P("fsdp"),
        P("fsdp", None),
        P("fsdp", None),
        P("fsdp", None),
        P("fsdp"),
        P("fsdp", None),
        P("fsdp", None),
        P("fsdp", None),
    )
    return jax.shard_map(
        per_device, mesh=mesh, in_specs=in_specs, out_specs=out_specs, check_vma=False
    )
```

profile of v0, /device:TPU:0, one launch (start us, length us, event | category | flops | bytes accessed | tf_op | source)
XLA Modules:
  0.0 1521.0 jit_solution(11291394737319134312)
XLA Ops:
  12.0 22.5 %all-gather.3 = bf16[8,1,128]{2,1,0:T(2,128)(2,1)S(1)} all-gather(bf16[1,1,128]{2,1,0:T(2,128)(2,1)} %bitcast.652), channel_id=1, replica_groups=mesh['ctx'=4,'fsdp'=8] {'fsdp'}, dimensions={0}, use_global_device_ids=true | all-gather | bytes 2304 | tf_op jit(solution)/shard_map/all_gather | solution.py:221
  38.9 18.4 %all-reduce.24 = (bf16[1792]{0:T(1024)(128)(2,1)S(1)}, bf16[1536]{0:T(1024)(128)(2,1)}) all-reduce(bf16[1792]{0:T(1024)(128)(2,1)S(1)} %dynamic-update-slice, bf16[1536]{0:T(1024)(128)(2,1)S(1)} %dynamic-update-slice.2), channel_id=1, replica_groups=mesh['ctx'=4,'fsdp'=8] {'fsdp'}, use_global_device_ids=true, to_apply=%add.15 | all-reduce | flops 3328 | bytes 13312
  57.2 31.5 %all-gather.4 = bf16[8,224,4]{1,2,0:T(4,128)(2,1)S(1)} all-gather(bf16[1,224,4]{1,2,0:T(4,128)(2,1)} %bitcast.651), channel_id=1, replica_groups=mesh['ctx'=4,'fsdp'=8] {'fsdp'}, dimensions={0}, use_global_device_ids=true | all-gather | bytes 16128 | tf_op jit(solution)/shard_map/all_gather | solution.py:223
  90.9 29.7 %all-gather.16.cloned.1.call-done = bf16[1024,3352]{0,1:T(8,128)(2,1)} async-done(((bf16[128,3352]{0,1:T(8,128)(2,1)}), bf16[1024,3352]{0,1:T(8,128)(2,1)}) %all-gather.16.cloned.1.call-update) | async-done | bytes 6864912 | tf_op jit(solution)/shard_map/all_gather | solution.py:222
  120.5 5.2 fusion.197
  133.5 6.2 multiply_convert_fusion.2
  147.8 64.2 %while.127 = (s32[]{:T(128)}, f32[24,64,128]{2,1,0:T(8,128)S(1)}, f32[24]{0:T(128)S(1)}, s32[]{:T(128)}, f32[2,128,24,64]{1,0,3,2:T(2,128)}, /*index=5*/f32[2,24...) while((s32[]{:T(128)}, f32[24,64,128]{2,1,0:T(8,128)S(1)}, ...), condition=%wide.region_3.4_spmd.clone, body=%wide.region_1.3_spmd.clone.sunk | while | flops 914155072 | bytes 10471392 | solution.py:175
  150.5 4.2 fusion.371
  156.7 19.0 %dynamic_update_slice.115 = f32[2,128,24,64]{1,0,3,2:T(2,128)} dynamic-update-slice(f32[2,128,24,64]{1,0,3,2:T(2,128)} %get-tuple-element.2564, f32[1,128,24,64]{1,0,3,2:T(1,128)S(1)} %bitcast.593, s32[]{:T(128)} %get-tuple-element.2560, s32[]{:T(128)} %constant.345.clone.1..sunk.2, s32[]{:T(128)} %constant.345.clone.1..sunk.2, s32[]{:T(128)} %constant.345.clone.1..sunk.2) | dynamic-update-slice | bytes 1572868 | tf_op jit(solution)/shard_map/jvp()/while/body/jit(dynamic_update_index_in_dim)/dynamic_update_slice | solution.py:175
  182.6 4.2 fusion.371
  188.8 19.0 %dynamic_update_slice.115 = f32[2,128,24,64]{1,0,3,2:T(2,128)} dynamic-update-slice(f32[2,128,24,64]{1,0,3,2:T(2,128)} %get-tuple-element.2564, f32[1,128,24,64]{1,0,3,2:T(1,128)S(1)} %bitcast.593, s32[]{:T(128)} %get-tuple-element.2560, s32[]{:T(128)} %constant.345.clone.1..sunk.2, s32[]{:T(128)} %constant.345.clone.1..sunk.2, s32[]{:T(128)} %constant.345.clone.1..sunk.2) | dynamic-update-slice | bytes 1572868 | tf_op jit(solution)/shard_map/jvp()/while/body/jit(dynamic_update_index_in_dim)/dynamic_update_slice | solution.py:175
  220.8 18.2 %all-gather.5 = bf16[8,1,128]{2,1,0:T(2,128)(2,1)S(1)} all-gather(bf16[1,1,128]{2,1,0:T(2,128)(2,1)S(1)} %bitcast.653), channel_id=1, replica_groups=mesh['ctx'=4,'fsdp'=8] {'fsdp'}, dimensions={0}, use_global_device_ids=true | all-gather | bytes 2304 | tf_op jit(solution)/shard_map/all_gather | solution.py:229
  240.2 38.4 %psum.120 = f32[]{:T(128)} all-reduce(f32[]{:T(128)} %convert_reduce_fusion), channel_id=1, replica_groups=mesh['ctx'=4,'fsdp'=8] {'ctx','fsdp'}, use_global_device_ids=true, to_apply=%region_19.20 | all-reduce | flops 1 | bytes 8 | tf_op jit(solution)/shard_map/psum | solution.py:387
  283.5 7.0 all_gather.81
  290.6 12.9 while.128
  303.5 5.8 all_gather.80
  310.2 16.2 %while.129 = (s32[]{:T(128)}, f32[256,2,4,64]{0,3,2,1:T(8,128)}, bf16[1024,128]{0,1:T(8,128)(2,1)S(1)}, s32[256]{0:T(256)}, s32[1024]{0:T(1024)}, /*index=5*/bf1...) while((s32[]{:T(128)}, f32[256,2,4,64]{0,3,2,1:T(8,128)}, ...), condition=%wide.region_14.15_spmd.clone, body=%wide.region_13.14_spmd.clone.sunk | while | flops 136774144 | bytes 1851589 | solution.py:365
  315.1 2.7 fusion.380
  319.4 2.7 fusion.380
  323.7 2.7 fusion.380
  332.4 7.4 all-reduce.16
  339.9 3.3 reshape.595
  345.2 3.5 multiply_add_fusion.2
  348.8 3.0 copy.309
  354.8 4.1 convert_add_fusion.2
  363.0 48.7 %all-gather.24.cloned.1.call-done = bf16[1024,2048]{1,0:T(8,128)(2,1)} async-done(((bf16[128,2048]{1,0:T(8,128)(2,1)}), bf16[1024,2048]{1,0:T(8,128)(2,1)}) %all-gather.24.cloned.1.call-update) | async-done | bytes 4194320 | tf_op jit(solution)/shard_map/all_gather | solution.py:230
  411.7 4.9 fusion.210
  416.7 68.9 %all-gather.26.cloned.1.call-done = bf16[1024,2048]{1,0:T(8,128)(2,1)} async-done(((bf16[128,2048]{1,0:T(8,128)(2,1)}), bf16[1024,2048]{1,0:T(8,128)(2,1)}) %all-gather.26.cloned.1.call-update) | async-done | bytes 4194320 | tf_op jit(solution)/shard_map/all_gather | solution.py:231
  485.5 6.1 multiply_convert_fusion.1
  491.7 67.7 %all-gather.28.cloned.1.call-done = bf16[2048,1024]{1,0:T(8,128)(2,1)} async-done(((bf16[256,1024]{1,0:T(8,128)(2,1)}), bf16[2048,1024]{1,0:T(8,128)(2,1)}) %all-gather.28.cloned.1.call-update) | async-done | bytes 4194320 | tf_op jit(solution)/shard_map/all_gather | solution.py:232
  559.4 4.2 convolution_add_fusion.5
  564.3 4.7 multiply_convert_fusion
  574.4 2.8 fusion.204
  581.6 4.1 multiply_reduce_fusion.7
  585.8 3.3 multiply_reduce_fusion.8
  594.6 25.0 %while.130 = (s32[]{:T(128)}, f32[256,2,4,64]{0,3,2,1:T(8,128)S(1)}, bf16[1024,2,128]{0,2,1:T(8,128)(2,1)}, bf16[1024,128]{0,1:T(8,128)(2,1)}, s32[256]{0:T(256)...) while((s32[]{:T(128)}, f32[256,2,4,64]{0,3,2,1:T(8,128)S(1)}, ...), condition=%wide.region_41.42_spmd.clone, body=%wide.region_40.41_spmd.clone.sunk | while | flops 340132352 | bytes 13066521 | solution.py:468
  619.6 3.5 reshape.683
  623.2 3.3 copy.317
  632.0 3.8 while.125
  640.6 80.4 %while.126 = (s32[]{:T(128)}, f32[24,64,128]{2,1,0:T(8,128)S(1)}, f32[24]{0:T(128)}, f32[2,128,24,64]{1,3,2,0:T(8,128)}, f32[2,128,128]{2,1,0:T(8,128)}, /*index...) while((s32[]{:T(128)}, f32[24,64,128]{2,1,0:T(8,128)S(1)}, ...), condition=%wide.region_35.36_spmd.clone, body=%wide.region_25.35_spmd.clone.sunk | while | flops 2137938560 | bytes 31043496 | solution.py:175
  653.3 5.2 fusion.352
  672.0 4.1 fusion.356
  693.2 5.2 fusion.352
  711.9 4.1 fusion.356
  721.0 3.2 copy.344
  724.3 3.7 reshape.684
  740.3 4.9 convolution_convert_fusion.2
  745.2 10.1 copy.346
  761.0 2.9 convolution_convert_fusion.3
  765.2 5.2 convolution_convert_fusion.4
  771.8 3.3 convolution_convert_fusion.6
  776.4 3.4 convolution_convert_fusion.5
  783.8 98.8 %reduce-scatter.28.cloned.1.call-done = bf16[128,3352]{1,0:T(8,128)(2,1)} async-done(((bf16[1024,3352]{1,0:T(8,128)(2,1)}), bf16[128,3352]{1,0:T(8,128)(2,1)}) %reduce-scatter.28.cloned.1.call-update) | async-done | bytes 858128
  884.8 64.1 %reduce-scatter.20.cloned.1.call-done = bf16[64,1024]{1,0:T(8,128)(2,1)} async-done(((bf16[512,1024]{1,0:T(8,128)(2,1)}), bf16[64,1024]{1,0:T(8,128)(2,1)}) %reduce-scatter.20.cloned.1.call-update) | async-done | bytes 131088 | tf_op jit(solution)/shard_map/reduce_scatter | solution.py:538
  949.0 68.3 %reduce-scatter.18.cloned.1.call-done = bf16[128,768]{1,0:T(8,128)(2,1)} async-done(((bf16[1024,768]{1,0:T(8,128)(2,1)}), bf16[128,768]{1,0:T(8,128)(2,1)}) %reduce-scatter.18.cloned.1.call-update) | async-done | bytes 196624 | tf_op jit(solution)/shard_map/reduce_scatter | solution.py:535
  1017.3 76.6 %reduce-scatter.16.cloned.1.call-done = bf16[192,1024]{1,0:T(8,128)(2,1)} async-done(((bf16[1536,1024]{1,0:T(8,128)(2,1)}), bf16[192,1024]{1,0:T(8,128)(2,1)}) %reduce-scatter.16.cloned.1.call-update) | async-done | bytes 393232 | tf_op jit(solution)/shard_map/reduce_scatter | solution.py:532
  1093.9 90.6 %reduce-scatter.26.cloned.1.call-done = bf16[256,1024]{1,0:T(8,128)(2,1)} async-done(((bf16[2048,1024]{1,0:T(8,128)(2,1)}), bf16[256,1024]{1,0:T(8,128)(2,1)}) %reduce-scatter.26.cloned.1.call-update) | async-done | bytes 524304 | tf_op jit(solution)/shard_map/reduce_scatter | solution.py:550
  1184.6 91.7 %reduce-scatter.22.cloned.1.call-done = bf16[128,2048]{1,0:T(8,128)(2,1)} async-done(((bf16[1024,2048]{1,0:T(8,128)(2,1)}), bf16[128,2048]{1,0:T(8,128)(2,1)}) %reduce-scatter.22.cloned.1.call-update) | async-done | bytes 524304 | tf_op jit(solution)/shard_map/reduce_scatter | solution.py:544
  1276.3 91.3 %reduce-scatter.24.cloned.1.call-done = bf16[128,2048]{1,0:T(8,128)(2,1)} async-done(((bf16[1024,2048]{1,0:T(8,128)(2,1)}), bf16[128,2048]{1,0:T(8,128)(2,1)}) %reduce-scatter.24.cloned.1.call-update) | async-done | bytes 524304 | tf_op jit(solution)/shard_map/reduce_scatter | solution.py:547
  1369.4 40.8 %all-reduce.22 = (f32[]{:T(128)}, f32[24]{0:T(128)}, f32[24]{0:T(128)}, f32[24]{0:T(128)}) all-reduce(f32[]{:T(128)} %get-tuple-element.1972, f32[24]{0:T(128)S(1)} %reduce_sum.424, f32[24]{0:T(128)S(1)} %exponential_multiply_fusion.4, f32[24]{0:T(128)S(1)} %reduce_sum.428), channel_id=1, replica_groups=mesh['ctx'=4,'fsdp'=8] {'ctx','fsdp'}, use_global_device_ids=true, to_apply=%region_17.18 | all-reduce | flops 73 | bytes 584 | tf_op jit(solution)/shard_map/psum | solution.py:387
  1410.9 6.1 fusion.160
  1417.1 36.7 %all-reduce.23 = (bf16[1024]{0:T(1024)(128)(2,1)S(1)}, bf16[1792]{0:T(1024)(128)(2,1)S(1)}, bf16[1536]{0:T(1024)(128)(2,1)S(1)}, bf16[1024]{0:T(1024)(128)(2,1)S(1)}) all-reduce(bf16[1024]{0:T(1024)(128)(2,1)S(1)} %get-tuple-element.1748, ...), channel_id=6, replica_groups=mesh['ctx'=4,'fsdp'=8] {'fsdp'}, use_global_device_ids=true, to_apply=%region_45.46.clone | all-reduce | flops 5376 | bytes 21504
  1456.2 6.6 all-reduce.25
  1465.6 39.3 %all-reduce.29.cloned.1.call-done = (bf16[128,3352]{0,1:T(8,128)(2,1)}, bf16[192,1024]{1,0:T(8,128)(2,1)}, bf16[128,768]{1,0:T(8,128)(2,1)}, bf16[64,1024]{1,0:T...) async-done(((bf16[128,3352]{0,1:T(8,128)(2,1)}, bf16[192,1024]{1,0:T(8,128)(2,1)}, bf16[128,768]{1,0:T(8,128)(2,1)}, ...) | async-done | bytes 3151888 | tf_op jit(solution)/shard_map/psum | solution.py:556
  (826 shorter events, 243.4 us)
Async XLA Ops:
  7.2 113.3 %copy-start.23 = (bf16[1,256,1024]{2,1,0:T(8,128)(2,1)S(1)}, bf16[1,256,1024]{2,1,0:T(8,128)(2,1)}, u32[]{:S(2)}) copy-start(bf16[1,256,1024]{2,1,0:T(8,128)(2,1)} %param.33) | copy-start | bytes 1572868
  7.2 83.7 %copy-start.156 = (f32[24]{0:T(128)S(1)}, f32[24]{0:T(128)}, u32[]{:S(2)}) copy-start(f32[24]{0:T(128)} %param.42) | copy-start | bytes 292
  7.2 113.3 %all-gather.16.cloned.1.call-start = ((), (), s32[]{:S(2)}) async-start(), calls=%async_computation.9 | async-start | bytes 7723008 | tf_op jit(solution)/shard_map/all_gather | solution.py:222
  7.9 272.3 %all-gather.20.cloned.1.call-start = ((), (), s32[]{:S(2)}) async-start(), calls=%async_computation.11 | async-start | bytes 1769472 | tf_op jit(solution)/shard_map/all_gather | solution.py:227
  8.7 334.5 %all-gather.30.cloned.1.call-start = ((), (), s32[]{:S(2)}) async-start(), calls=%async_computation.23 | async-start | bytes 1966080 | tf_op jit(solution)/shard_map/all_gather | solution.py:30
  9.6 123.8 %copy-start.119 = (f32[256]{0:T(256)}, f32[256]{0:T(256)S(1)}, u32[]{:S(2)}) copy-start(f32[256]{0:T(256)S(1)} %get-tuple-element.1988) | copy-start | bytes 3076
  9.6 123.8 %copy-start.121 = (f32[256]{0:T(256)}, f32[256]{0:T(256)S(1)}, u32[]{:S(2)}) copy-start(f32[256]{0:T(256)S(1)} %get-tuple-element.1989) | copy-start | bytes 3076
  9.6 123.8 %copy-start.123 = (f32[256]{0:T(256)}, f32[256]{0:T(256)S(1)}, u32[]{:S(2)}) copy-start(f32[256]{0:T(256)S(1)} %get-tuple-element.1990) | copy-start | bytes 3076
  11.4 109.1 %copy-start.116 = (f32[256]{0:T(256)}, f32[256]{0:T(256)S(1)}, u32[]{:S(2)}) copy-start(f32[256]{0:T(256)S(1)} %fusion.184) | copy-start | bytes 3076
  34.5 86.0 %copy-start.94 = (f32[8,1,128]{2,1,0:T(1,128)}, f32[8,1,128]{2,1,0:T(1,128)S(1)}, u32[]{:S(2)}) copy-start(f32[8,1,128]{2,1,0:T(1,128)S(1)} %convert_element_type.483) | copy-start | bytes 12292
  88.9 44.5 %copy-start.104 = (f32[1792]{0:T(1024)}, f32[1792]{0:T(1024)S(1)}, u32[]{:S(2)}) copy-start(f32[1792]{0:T(1024)S(1)} %get-tuple-element.1750) | copy-start | bytes 21508
  88.9 44.5 %copy-start.106 = (f32[1792]{0:T(1024)}, f32[1792]{0:T(1024)S(1)}, u32[]{:S(2)}) copy-start(f32[1792]{0:T(1024)S(1)} %get-tuple-element.1751) | copy-start | bytes 21508
  88.9 44.5 %copy-start.108 = (f32[1792]{0:T(1024)}, f32[1792]{0:T(1024)S(1)}, u32[]{:S(2)}) copy-start(f32[1792]{0:T(1024)S(1)} %get-tuple-element.1752) | copy-start | bytes 21508
  88.9 44.5 %copy-start.110 = (f32[1792]{0:T(1024)}, f32[1792]{0:T(1024)S(1)}, u32[]{:S(2)}) copy-start(f32[1792]{0:T(1024)S(1)} %get-tuple-element.1753) | copy-start | bytes 21508
  90.9 38.6 %copy-start.146 = (f32[24]{0:T(128)}, f32[24]{0:T(128)S(1)}, u32[]{:S(2)}) copy-start(f32[24]{0:T(128)S(1)} %exp.145) | copy-start | bytes 292
  127.8 5.6 collective-permute-start
  133.4 6.2 copy-start.98
  147.9 6.9 copy-start.37
  147.9 6.9 copy-start.42
  180.0 6.9 copy-start.37
  180.0 6.9 copy-start.42
  213.4 66.9 %copy-start.24 = (bf16[1,256,1024]{2,1,0:T(8,128)(2,1)S(1)}, bf16[1,256,1024]{2,1,0:T(8,128)(2,1)}, u32[]{:S(2)}) copy-start(bf16[1,256,1024]{2,1,0:T(8,128)(2,1)} %param.33) | copy-start | bytes 1572868
  214.2 6.6 copy-start.141
  214.2 6.6 copy-start.151
  214.2 64.4 %copy-start.148 = (f32[24]{0:T(128)S(1)}, f32[24]{0:T(128)}, u32[]{:S(2)}) copy-start(f32[24]{0:T(128)} %param.43) | copy-start | bytes 292
  214.2 66.1 %copy-start.95 = (f32[8,1,128]{2,1,0:T(1,128)S(1)}, f32[8,1,128]{2,1,0:T(1,128)}, u32[]{:S(2)}) copy-start(f32[8,1,128]{2,1,0:T(1,128)} %copy-done.94) | copy-start | bytes 12292
  214.2 66.1 %copy-start.117 = (f32[256]{0:T(256)S(1)}, f32[256]{0:T(256)}, u32[]{:S(2)}) copy-start(f32[256]{0:T(256)} %copy-done.116) | copy-start | bytes 3076
  214.3 140.0 %all-gather.18.cloned.1.call-start = ((), (), s32[]{:S(2)}) async-start(), calls=%async_computation.10 | async-start | bytes 3538944 | tf_op jit(solution)/shard_map/all_gather | solution.py:226
  214.8 144.1 %all-gather.22.cloned.1.call-start = ((), (), s32[]{:S(2)}) async-start(), calls=%async_computation.12 | async-start | bytes 1179648 | tf_op jit(solution)/shard_map/all_gather | solution.py:228
  215.4 196.3 %all-gather.24.cloned.1.call-start = ((), (), s32[]{:S(2)}) async-start(), calls=%async_computation.13 | async-start | bytes 4718592 | tf_op jit(solution)/shard_map/all_gather | solution.py:230
  216.0 269.5 %all-gather.26.cloned.1.call-start = ((), (), s32[]{:S(2)}) async-start(), calls=%async_computation.14 | async-start | bytes 4718592 | tf_op jit(solution)/shard_map/all_gather | solution.py:231
  216.7 342.6 %all-gather.28.cloned.1.call-start = ((), (), s32[]{:S(2)}) async-start(), calls=%async_computation.15 | async-start | bytes 4718592 | tf_op jit(solution)/shard_map/all_gather | solution.py:232
  217.5 414.4 %all-gather.32.cloned.1.call-start = ((), (), s32[]{:S(2)}) async-start(), calls=%async_computation.24 | async-start | bytes 1966080 | tf_op jit(solution)/shard_map/all_gather | solution.py:52
  217.7 61.0 %copy-start.137 = (f32[1,256]{1,0:T(1,128)}, f32[1,256]{1,0:T(1,128)S(1)}, u32[]{:S(2)}) copy-start(f32[1,256]{1,0:T(1,128)S(1)} %convert_element_type.419) | copy-start | bytes 3076
  290.6 13.0 copy-start.92
  329.6 13.6 copy-start.83
  330.4 12.8 copy-start.133
  332.1 13.1 copy-start.81
  343.3 5.4 copy-start.158
  343.3 292.5 %copy-start = (f32[24,64,128]{2,1,0:T(8,128)}, f32[24,64,128]{2,1,0:T(8,128)S(1)}, u32[]{:S(2)}) copy-start(f32[24,64,128]{2,1,0:T(8,128)S(1)} %get-tuple-element.1199) | copy-start | bytes 2359300
  354.2 6.8 copy-start.135
  354.2 231.5 %copy-start.3 = (f32[256,1536]{1,0:T(8,128)}, f32[256,1536]{1,0:T(8,128)S(1)}, u32[]{:S(2)}) copy-start(f32[256,1536]{1,0:T(8,128)S(1)} %get-tuple-element.1934) | copy-start | bytes 4718596
  563.6 10.8 copy-start.57
  593.6 164.5 %reduce-scatter.14.cloned.1.call-start = ((), (), s32[]{:S(2)}) async-start(), calls=%async_computation.16 | async-start | bytes 655360 | tf_op jit(solution)/shard_map/reduce_scatter | solution.py:469
  626.5 5.5 copy-start.159
  631.9 250.8 %reduce-scatter.28.cloned.1.call-start = ((), (), s32[]{:S(2)}) async-start(), calls=%async_computation.25 | async-start | bytes 7962624
  644.8 8.2 copy-start.35
  660.9 5.7 copy-start.88
  684.7 8.2 copy-start.35
  700.8 5.7 copy-start.88
  736.8 3.2 collective-permute-start.1
  755.3 193.6 %reduce-scatter.20.cloned.1.call-start = ((), (), s32[]{:S(2)}) async-start(), calls=%async_computation.19 | async-start | bytes 1179648 | tf_op jit(solution)/shard_map/reduce_scatter | solution.py:538
  757.8 259.5 %reduce-scatter.18.cloned.1.call-start = ((), (), s32[]{:S(2)}) async-start(), calls=%async_computation.18 | async-start | bytes 1769472 | tf_op jit(solution)/shard_map/reduce_scatter | solution.py:535
  760.9 333.0 %reduce-scatter.16.cloned.1.call-start = ((), (), s32[]{:S(2)}) async-start(), calls=%async_computation.17 | async-start | bytes 3538944 | tf_op jit(solution)/shard_map/reduce_scatter | solution.py:532
  763.9 420.7 %reduce-scatter.26.cloned.1.call-start = ((), (), s32[]{:S(2)}) async-start(), calls=%async_computation.22 | async-start | bytes 4718592 | tf_op jit(solution)/shard_map/reduce_scatter | solution.py:550
  770.5 505.8 %reduce-scatter.22.cloned.1.call-start = ((), (), s32[]{:S(2)}) async-start(), calls=%async_computation.20 | async-start | bytes 4718592 | tf_op jit(solution)/shard_map/reduce_scatter | solution.py:544
  775.2 592.5 %reduce-scatter.24.cloned.1.call-start = ((), (), s32[]{:S(2)}) async-start(), calls=%async_computation.21 | async-start | bytes 4718592 | tf_op jit(solution)/shard_map/reduce_scatter | solution.py:547
  779.8 675.5 %reduce-scatter.30.cloned.1.call-start = ((), (), s32[]{:S(2)}) async-start(), calls=%async_computation.26 | async-start | bytes 516096
  781.0 723.9 %all-reduce.29.cloned.1.call-start = ((), (), s32[]{:S(2)}) async-start(), calls=%async_computation.27 | async-start | bytes 6303744 | tf_op jit(solution)/shard_map/psum | solution.py:556
  884.8 482.9 %copy-start.54 = (bf16[1024,768]{1,0:T(8,128)(2,1)S(1)}, bf16[1024,768]{1,0:T(8,128)(2,1)}, u32[]{:S(2)}) copy-start(bf16[1024,768]{1,0:T(8,128)(2,1)} %all-gather.20.cloned.1.call-done) | copy-start | bytes 4718596
  1410.8 6.2 copy-start.115
  1410.9 6.2 copy-start.140
  1410.9 43.2 %copy-start.130 = (f32[256]{0:T(256)S(1)}, f32[256]{0:T(256)}, u32[]{:S(2)}) copy-start(f32[256]{0:T(256)} %copy-done.129) | copy-start | bytes 3076
  1410.9 43.2 %copy-start.47 = (f32[256,1024]{1,0:T(8,128)S(1)}, f32[256,1024]{1,0:T(8,128)}, u32[]{:S(2)}) copy-start(f32[256,1024]{1,0:T(8,128)} %get-tuple-element.1932) | copy-start | bytes 3145732
  (161 other events, 401.1 us)
Sparse Core Ops, SparseCore 0:
  10.1 110.3 all-gather.15
  122.7 42.0 all-gather.19
  214.4 18.8 all-gather.29
  235.3 61.3 all-gather.17
  298.7 38.7 all-gather.21
  339.5 72.1 all-gather.23
  413.8 71.6 all-gather.25
  487.7 71.6 all-gather.27
  593.7 17.8 all-gather.31
  632.0 19.9 reduce-scatter.13
  755.4 127.1 reduce-scatter.27
  886.5 62.4 reduce-scatter.19
  953.3 63.9 reduce-scatter.17
  1020.7 73.1 reduce-scatter.15
  1097.4 87.1 reduce-scatter.25
  1188.5 87.7 reduce-scatter.21
  1279.8 87.8 reduce-scatter.23
  1371.2 61.6 reduce-scatter.29
  1435.7 69.0 all-reduce.28
where the time goes:
time: 1530 us; the launch traced here: 1520 us
  waiting for transfers between devices  842 us (55%)
  blocking collectives  233 us (15%)
  local copies, waits for them, and re-layouts  162 us (11%)
  matrix products  155 us (10%)
  other arithmetic  94.8 us (6%)
  between operations  23.1 us (2%)
    unnamed x21, waiting for transfers between devices  103 us
    reduce_scatter x1, waiting for transfers between devices, per_device(): lax.psum_scatter(grad_gate_w.astype(jnp.bfloat16), 'fsdp', scatter_dimens...  91.7 us
    reduce_scatter x1, waiting for transfers between devices, per_device(): lax.psum_scatter(grad_up_w.astype(jnp.bfloat16), 'fsdp', scatter_dimensio...  91.3 us
    reduce_scatter x1, waiting for transfers between devices, per_device(): lax.psum_scatter(grad_down.astype(jnp.bfloat16), 'fsdp', scatter_dimensio...  90.6 us
    psum x2, blocking collectives, per_device(): lax.psum((squared_local, count_local), ('ctx', 'fsdp'))  79.2 us
    reduce_scatter x1, waiting for transfers between devices, per_device(): lax.psum_scatter(grad_mamba_w.astype(jnp.bfloat16), 'fsdp', scatter_dimen...  76.6 us
    all_gather x1, waiting for transfers between devices, per_device(): lax.all_gather(w_up, 'fsdp', axis=0, tiled=True)  68.9 us
    reduce_scatter x1, waiting for transfers between devices, per_device(): lax.psum_scatter(grad_qkv_w.astype(jnp.bfloat16), 'fsdp', scatter_dimensi...  68.3 us
  transfers between devices with their start and end apart: 21, of which 13 were waited for; matrix products, arithmetic and copies ran while one was open for 23% of the time, Pallas kernels for 0%

commit v1 on v0

v1 whole, which is shorter than its diff:
```python
import functools

import jax
import jax.numpy as jnp
from jax import lax
from jax.experimental import pallas as pl
from jax.experimental.pallas import tpu as pltpu
from jax.sharding import PartitionSpec as P

MH = 24
HP = 64
NS = 128
KW = 4
QH = 8
KVH = 2
HD = 64
SPAN = 128
QBLK = 256

EPSILON = 1e-05
ROPE_BASE = 100000000000.0
MASKED = -1e30

F32 = jnp.float32
BF16 = jnp.bfloat16
HIGH = lax.Precision.HIGHEST


def nn(left, right, precision=None):
    return lax.dot_general(
        left, right, (((1,), (0,)), ((), ())), precision=precision, preferred_element_type=F32
    )


def nt(left, right):
    return lax.dot_general(left, right, (((1,), (1,)), ((), ())), preferred_element_type=F32)


def tn(left, right):
    return lax.dot_general(left, right, (((0,), (0,)), ((), ())), preferred_element_type=F32)


def decays(seg_c, seg_r, loga_c, loga_r, before, end):
    row = lax.broadcasted_iota(jnp.int32, (SPAN, SPAN), 0)
    col = lax.broadcasted_iota(jnp.int32, (SPAN, SPAN), 1)
    lower = row >= col
    same = (seg_c == seg_r) & lower
    run_c = nn(lower.astype(F32), loga_c, HIGH)
    run_r = nn(loga_r, (row <= col).astype(F32), HIGH)
    keep = (seg_c == before).astype(F32)
    tail = (seg_c == end).astype(F32)
    return lower, same, run_c, run_r, keep, tail


def ssm_fwd_kernel(
    heads, ends, skip, act, dt_c, loga_c, dt_r, loga_r, seg_c, seg_r, y_ref, st_ref, state
):
    step = pl.program_id(0)

    @pl.when(step == 0)
    def _():
        state[...] = jnp.zeros_like(state)

    before, end = ends[step], ends[step + 1]
    link = (before == end).astype(F32)
    _, same, run_c, run_r, keep, tail = decays(
        seg_c[...], seg_r[...], loga_c[...], loga_r[...], before, end
    )
    width = heads * HP
    b_in = act[:, width : width + NS]
    c_in = act[:, width + NS : width + 2 * NS]
    gram = nt(c_in, b_in)
    for h in range(heads):
        lanes = slice(h * HP, (h + 1) * HP)
        x_in = act[:, lanes]
        own_c = run_c[:, h : h + 1]
        last = own_c[SPAN - 1 :, :]
        decay = jnp.where(same, jnp.exp(own_c - run_r[h : h + 1, :]), 0.0)
        mixing = (gram * decay * dt_r[h : h + 1, :]).astype(BF16)
        prior = state[h]
        st_ref[0, h] = prior
        x_wide = x_in.astype(F32)
        y_out = nn(mixing, x_in) + nt(c_in, prior.astype(BF16)) * (jnp.exp(own_c) * keep)
        y_ref[:, lanes] = y_out + skip[h] * x_wide
        weight = jnp.exp(last - own_c) * tail * dt_c[:, h : h + 1]
        state[h] = (jnp.exp(last) * link) * prior + tn((x_wide * weight).astype(BF16), b_in)


def ssm_bwd_kernel(
    heads,
    ends,
    skip,
    act,
    dt_c,
    loga_c,
    dt_r,
    loga_r,
    seg_c,
    seg_r,
    st_ref,
    gy_ref,
    gact_ref,
    gcol_ref,
    grow_ref,
    gstate,
):
    step = pl.num_programs(0) - 1 - pl.program_id(0)

    @pl.when(pl.program_id(0) == 0)
    def _():
        gstate[...] = jnp.zeros_like(gstate)

    before, end = ends[step], ends[step + 1]
    link = (before == end).astype(F32)
    lower, same, run_c, run_r, keep, tail = decays(
        seg_c[...], seg_r[...], loga_c[...], loga_r[...], before, end
    )
    width = heads * HP
    b_in = act[:, width : width + NS]
    c_in = act[:, width + NS : width + 2 * NS]
    gram = nt(c_in, b_in)
    g_gram = jnp.zeros((SPAN, SPAN), F32)
    g_b = jnp.zeros((SPAN, NS), F32)
    g_c = jnp.zeros((SPAN, NS), F32)
    for h in range(heads):
        lanes = slice(h * HP, (h + 1) * HP)
        x_in = act[:, lanes]
        x_wide = x_in.astype(F32)
        gy = gy_ref[:, lanes]
        gy_low = gy.astype(BF16)
        own_c = run_c[:, h : h + 1]
        last = own_c[SPAN - 1 :, :]
        dt_row = dt_r[h : h + 1, :]
        decay = jnp.where(same, jnp.exp(own_c - run_r[h : h + 1, :]), 0.0)
        prior = st_ref[0, h]
        prior_low = prior.astype(BF16)
        after = gstate[h]
        after_low = after.astype(BF16)
        carry_w = jnp.exp(own_c) * keep
        tail_w = jnp.exp(last - own_c) * tail
        end_w = tail_w * dt_c[:, h : h + 1]
        mixing = (gram * decay * dt_row).astype(BF16)
        g_mix = nt(gy_low, x_in) * decay
        g_gram_h = g_mix * dt_row
        g_gram = g_gram + g_gram_h
        inner = g_gram_h * gram
        g_dt_row = jnp.sum(g_mix * gram, axis=0, keepdims=True)
        from_state = nt(b_in, after_low)
        g_x = tn(mixing, gy_low) + from_state * end_w
        gact_ref[:, lanes] = g_x + skip[h] * gy
        g_carry = jnp.sum(gy * nt(c_in, prior_low), axis=1, keepdims=True)
        g_tail = jnp.sum(x_wide * from_state, axis=1, keepdims=True)
        g_link = jnp.exp(last) * link
        total_last = jnp.sum(g_tail * end_w, axis=0, keepdims=True) + g_link * jnp.sum(
            jnp.sum(after * prior, axis=1, keepdims=True), axis=0, keepdims=True
        )
        g_run_c = jnp.sum(inner, axis=1, keepdims=True) + g_carry * carry_w - g_tail * end_w
        at_last = lax.broadcasted_iota(jnp.int32, (SPAN, 1), 0) == SPAN - 1
        gcol_ref[:, h : h + 1] = g_run_c + jnp.where(at_last, total_last, 0.0)
        gcol_ref[:, heads + h : heads + h + 1] = g_tail * tail_w
        grow_ref[h : h + 1, :] = jnp.sum(inner, axis=0, keepdims=True)
        grow_ref[heads + h : heads + h + 1, :] = g_dt_row
        weighted = (gy * carry_w).astype(BF16)
        g_c = g_c + nn(weighted, prior_low)
        g_b = g_b + nn((x_wide * end_w).astype(BF16), after_low)
        gstate[h] = g_link * after + tn(weighted, c_in)
    g_gram_low = g_gram.astype(BF16)
    gact_ref[:, width : width + NS] = g_b + tn(g_gram_low, c_in)
    gact_ref[:, width + NS :] = g_c + nn(g_gram_low, b_in)


def ssm_specs(heads, width, at):
    return [
        pl.BlockSpec(memory_space=pltpu.SMEM),
        pl.BlockSpec(memory_space=pltpu.SMEM),
        pl.BlockSpec((SPAN, width + 2 * NS), lambda i: (at(i), 0)),
        pl.BlockSpec((SPAN, heads), lambda i: (at(i), 0)),
        pl.BlockSpec((SPAN, heads), lambda i: (at(i), 0)),
        pl.BlockSpec((heads, SPAN), lambda i: (0, at(i))),
        pl.BlockSpec((heads, SPAN), lambda i: (0, at(i))),
        pl.BlockSpec((SPAN, 1), lambda i: (at(i), 0)),
        pl.BlockSpec((1, SPAN), lambda i: (0, at(i))),
    ]


def ssm_forward(heads, inputs):
    length = inputs[2].shape[0]
    steps = length // SPAN
    width = heads * HP
    return pl.pallas_call(
        functools.partial(ssm_fwd_kernel, heads),
        grid=(steps,),
        in_specs=ssm_specs(heads, width, lambda i: i),
        out_specs=[
            pl.BlockSpec((SPAN, width), lambda i: (i, 0)),
            pl.BlockSpec((1, heads, HP, NS), lambda i: (i, 0, 0, 0)),
        ],
        out_shape=[
            jax.ShapeDtypeStruct((length, width), F32),
            jax.ShapeDtypeStruct((steps, heads, HP, NS), F32),
        ],
        scratch_shapes=[pltpu.VMEM((heads, HP, NS), F32)],
        compiler_params=pltpu.CompilerParams(vmem_limit_bytes=32 * 1024 * 1024),
        cost_estimate=pl.CostEstimate(flops=10**9, bytes_accessed=10**7, transcendentals=10**6),
        name="ssm_forward",
    )(*inputs)


def ssm_backward(heads, inputs, states, gy):
    length = inputs[2].shape[0]
    steps = length // SPAN
    width = heads * HP

    def at(i):
        return steps - 1 - i

    return pl.pallas_call(
        functools.partial(ssm_bwd_kernel, heads),
        grid=(steps,),
        in_specs=ssm_specs(heads, width, at)
        + [
            pl.BlockSpec((1, heads, HP, NS), lambda i: (at(i), 0, 0, 0)),
            pl.BlockSpec((SPAN, width), lambda i: (at(i), 0)),
        ],
        out_specs=[
            pl.BlockSpec((SPAN, width + 2 * NS), lambda i: (at(i), 0)),
            pl.BlockSpec((SPAN, 2 * heads), lambda i: (at(i), 0)),
            pl.BlockSpec((2 * heads, SPAN), lambda i: (0, at(i))),
        ],
        out_shape=[
            jax.ShapeDtypeStruct((length, width + 2 * NS), F32),
            jax.ShapeDtypeStruct((length, 2 * heads), F32),
            jax.ShapeDtypeStruct((2 * heads, length), F32),
        ],
        scratch_shapes=[pltpu.VMEM((heads, HP, NS), F32)],
        compiler_params=pltpu.CompilerParams(vmem_limit_bytes=32 * 1024 * 1024),
        cost_estimate=pl.CostEstimate(flops=3 * 10**9, bytes_accessed=10**7, transcendentals=10**6),
        name="ssm_backward",
    )(*inputs, states, gy)


def allowed_keys(index, reach, seg_c, seg_r):
    row = lax.broadcasted_iota(jnp.int32, (QBLK, reach), 0) + index * QBLK
    col = lax.broadcasted_iota(jnp.int32, (QBLK, reach), 1)
    return (seg_c[...] == seg_r[:, :reach]) & (col <= row)


def attn_fwd_kernel(heads, blocks, q_ref, k_ref, v_ref, seg_c, seg_r, out_ref, lse_ref):
    for index in range(blocks):

        @pl.when(pl.program_id(0) == index)
        def _(index=index):
            reach = (index + 1) * QBLK
            allowed = allowed_keys(index, reach, seg_c, seg_r)
            keys = k_ref[:reach, :]
            values = v_ref[:reach, :]
            for h in range(heads):
                lanes = slice(h * HD, (h + 1) * HD)
                scores = nt(q_ref[:, lanes], keys) * (HD**-0.5)
                scores = jnp.where(allowed, scores, MASKED)
                top = jnp.max(scores, axis=1, keepdims=True)
                expo = jnp.exp(scores - top)
                total = jnp.sum(expo, axis=1, keepdims=True)
                probs = (expo * (1.0 / total)).astype(BF16)
                out_ref[:, lanes] = nn(probs, values).astype(BF16)
                lse_ref[:, h : h + 1] = top + jnp.log(total)


def attn_bwd_kernel(
    heads, blocks, q_ref, k_ref, v_ref, seg_c, seg_r, lse_ref, go_ref, gq_ref, gk_ref, gv_ref
):
    @pl.when(pl.program_id(0) == 0)
    def _():
        gk_ref[...] = jnp.zeros_like(gk_ref)
        gv_ref[...] = jnp.zeros_like(gv_ref)

    for index in range(blocks):

        @pl.when(pl.program_id(0) == index)
        def _(index=index):
            reach = (index + 1) * QBLK
            allowed = allowed_keys(index, reach, seg_c, seg_r)
            keys = k_ref[:reach, :]
            values = v_ref[:reach, :]
            for h in range(heads):
                lanes = slice(h * HD, (h + 1) * HD)
                query = q_ref[:, lanes]
                g_out = go_ref[:, lanes]
                scores = nt(query, keys) * (HD**-0.5)
                probs = jnp.where(allowed, jnp.exp(scores - lse_ref[:, h : h + 1]), 0.0)
                g_probs = nt(g_out, values)
                delta = jnp.sum(probs * g_probs, axis=1, keepdims=True)
                g_scores = (probs * (g_probs - delta)).astype(BF16)
                gq_ref[:, lanes] = nn(g_scores, keys) * (HD**-0.5)
                gk_ref[:reach, :] += tn(g_scores, query) * (HD**-0.5)
                gv_ref[:reach, :] += tn(probs.astype(BF16), g_out)


def attn_specs(heads, length):
    return [
        pl.BlockSpec((QBLK, heads * HD), lambda i: (i, 0)),
        pl.BlockSpec((length, HD), lambda i: (0, 0)),
        pl.BlockSpec((length, HD), lambda i: (0, 0)),
        pl.BlockSpec((QBLK, 1), lambda i: (i, 0)),
        pl.BlockSpec((1, length), lambda i: (0, 0)),
    ]


def attn_forward(heads, inputs):
    length = inputs[0].shape[0]
    blocks = length // QBLK
    return pl.pallas_call(
        functools.partial(attn_fwd_kernel, heads, blocks),
        grid=(blocks,),
        in_specs=attn_specs(heads, length),
        out_specs=[
            pl.BlockSpec((QBLK, heads * HD), lambda i: (i, 0)),
            pl.BlockSpec((QBLK, heads), lambda i: (i, 0)),
        ],
        out_shape=[
            jax.ShapeDtypeStruct((length, heads * HD), BF16),
            jax.ShapeDtypeStruct((length, heads), F32),
        ],
        compiler_params=pltpu.CompilerParams(vmem_limit_bytes=32 * 1024 * 1024),
        cost_estimate=pl.CostEstimate(flops=10**9, bytes_accessed=10**7, transcendentals=10**6),
        name="attn_forward",
    )(*inputs)


def attn_backward(heads, inputs, lse, g_out):
    length = inputs[0].shape[0]
    blocks = length // QBLK
    return pl.pallas_call(
        functools.partial(attn_bwd_kernel, heads, blocks),
        grid=(blocks,),
        in_specs=attn_specs(heads, length)
        + [
            pl.BlockSpec((QBLK, heads), lambda i: (i, 0)),
            pl.BlockSpec((QBLK, heads * HD), lambda i: (i, 0)),
        ],
        out_specs=[
            pl.BlockSpec((QBLK, heads * HD), lambda i: (i, 0)),
            pl.BlockSpec((length, HD), lambda i: (0, 0)),
            pl.BlockSpec((length, HD), lambda i: (0, 0)),
        ],
        out_shape=[
            jax.ShapeDtypeStruct((length, heads * HD), F32),
            jax.ShapeDtypeStruct((length, HD), F32),
            jax.ShapeDtypeStruct((length, HD), F32),
        ],
        compiler_params=pltpu.CompilerParams(vmem_limit_bytes=32 * 1024 * 1024),
        cost_estimate=pl.CostEstimate(flops=3 * 10**9, bytes_accessed=10**7, transcendentals=10**6),
        name="attn_backward",
    )(*inputs, lse, g_out)


class Net:
    def __init__(self):
        self.n = lax.axis_size("ctx")
        self.m = lax.axis_size("fsdp")
        self.c = lax.axis_index("ctx")
        self.f = lax.axis_index("fsdp")
        self.direct = self.n == 4 and self.m == 8
        self.x, self.core = self.c // 2, self.c % 2
        self.z, self.y = self.f // 2, self.f % 2

    def flip(self, value, axis, bit):
        size = lax.axis_size(axis)
        return lax.ppermute(value, axis, [(i, i ^ bit) for i in range(size)])

    def shift_z(self, value, by):
        return lax.ppermute(value, "fsdp", [(i, (i + 2 * by) % self.m) for i in range(self.m)])

    def spread(self, block, share_x=False):
        if not self.direct:
            if share_x:
                block = lax.all_gather(block, "ctx", axis=0, tiled=False)
                half = self.n // 2
                block = block.reshape((half, 2) + block.shape[1:])
                block = lax.dynamic_index_in_dim(block, self.core, 1, False)
                block = block.reshape((half * block.shape[1],) + block.shape[2:])
            return lax.all_gather(block, "fsdp", axis=0, tiled=False)
        parts, places = [], []
        for k in range(4):
            got = self.shift_z(block, k) if k else block
            z_from = (self.z - k) % 4
            for other in range(2):
                piece = self.flip(got, "fsdp", 1) if other else got
                place = 2 * z_from + (self.y ^ other)
                if share_x:
                    parts.append(piece)
                    places.append(2 * place + self.x)
                    parts.append(self.flip(piece, "ctx", 2))
                    places.append(2 * place + 1 - self.x)
                else:
                    parts.append(piece)
                    places.append(place)
        out = put(parts, places)
        if share_x:
            out = out.reshape((8, 2 * block.shape[0]) + block.shape[1:])
        return out

    def collect(self, sums, share_x=False, kind=BF16):
        if not self.direct:
            out = lax.psum_scatter(sums.astype(kind), "fsdp", scatter_dimension=0, tiled=False)
            if share_x:
                half = self.n // 2
                groups = [[i * 2 + k for i in range(half)] for k in range(2)]
                out = lax.psum_scatter(
                    out, "ctx", scatter_dimension=0, axis_index_groups=groups, tiled=True
                )
            return out
        low = sums.astype(kind)
        if share_x:
            low = low.reshape((8, 2, low.shape[1] // 2) + low.shape[2:])
            away = lax.dynamic_index_in_dim(low, 1 - self.x, 1, False)
            here = lax.dynamic_index_in_dim(low, self.x, 1, False)
            low = (here.astype(F32) + self.flip(away, "ctx", 2).astype(F32)).astype(kind)
        low = low.reshape((4, 2) + low.shape[1:])
        away = lax.dynamic_index_in_dim(low, 1 - self.y, 1, False)
        here = lax.dynamic_index_in_dim(low, self.y, 1, False)
        both = (here.astype(F32) + self.flip(away, "fsdp", 1).astype(F32)).astype(kind)
        total = lax.dynamic_index_in_dim(both, self.z, 0, False).astype(F32)
        for k in range(1, 4):
            block = lax.dynamic_index_in_dim(both, (self.z + k) % 4, 0, False)
            total = total + self.shift_z(block, k).astype(F32)
        return total.astype(kind)

    def total(self, value):
        if not self.direct:
            return lax.psum(value, ("ctx", "fsdp"))
        value = self.ctx_sum(value)
        value = value + self.flip(value, "fsdp", 1)
        return value + sum(self.shift_z(value, k) for k in range(1, 4))

    def ctx_all(self, value):
        if not self.direct:
            return lax.all_gather(value, "ctx", axis=0, tiled=False)
        mate = self.flip(value, "ctx", 1)
        across = self.flip(value, "ctx", 2)
        far = self.flip(across, "ctx", 1)
        return put([value, mate, across, far], [self.c, self.c ^ 1, self.c ^ 2, self.c ^ 3])

    def ctx_sum(self, value):
        if not self.direct:
            return lax.psum(value, "ctx")
        value = value + self.flip(value, "ctx", 1)
        return value + self.flip(value, "ctx", 2)

    def ctx_collect(self, parts):
        if not self.direct:
            low = lax.psum_scatter(parts.astype(BF16), "ctx", scatter_dimension=0, tiled=False)
            return low.astype(F32)
        pairs = parts.reshape((2, 2) + parts.shape[1:])
        pairs = lax.dynamic_index_in_dim(pairs, 1 - self.core, 1, False), (
            lax.dynamic_index_in_dim(pairs, self.core, 1, False)
        )

        def half(which):
            away = lax.dynamic_index_in_dim(pairs[0], which, 0, False).astype(BF16)
            here = lax.dynamic_index_in_dim(pairs[1], which, 0, False)
            return here.astype(F32) + self.flip(away, "ctx", 1).astype(F32)

        across = self.flip(half(1 - self.x).astype(BF16), "ctx", 2)
        return half(self.x) + across.astype(F32)

    def ctx_swap(self, parts):
        if not self.direct:
            return lax.all_to_all(parts, "ctx", 0, 0, tiled=True)
        got = [lax.dynamic_index_in_dim(parts, self.c, 0, False)]
        for bit in range(1, 4):
            block = lax.dynamic_index_in_dim(parts, self.c ^ bit, 0, False)
            got.append(self.flip(block, "ctx", bit))
        return put(got, [self.c ^ bit for bit in range(4)])


def put_kernel(count, places, *refs):
    parts, out = refs[:count], refs[count]
    for i in range(count):

        @pl.when(pl.program_id(0) == i)
        def _(i=i):
            out[0] = parts[i][...]


def put(parts, places):
    count = len(parts)
    shape = parts[0].shape
    zeros = (0,) * len(shape)
    places = jnp.stack([jnp.asarray(p, jnp.int32) for p in places])
    size = parts[0].size * parts[0].dtype.itemsize
    return pl.pallas_call(
        functools.partial(put_kernel, count),
        grid_spec=pltpu.PrefetchScalarGridSpec(
            num_scalar_prefetch=1,
            grid=(count,),
            in_specs=[pl.BlockSpec(shape, lambda i, at: zeros)] * count,
            out_specs=pl.BlockSpec((1,) + shape, lambda i, at: (at[i],) + zeros),
        ),
        out_shape=jax.ShapeDtypeStruct((count,) + shape, parts[0].dtype),
        compiler_params=pltpu.CompilerParams(vmem_limit_bytes=40 * 1024 * 1024),
        cost_estimate=pl.CostEstimate(
            flops=0, bytes_accessed=2 * count * size, transcendentals=0
        ),
        name="put",
    )(places, *parts)


def rms_scale(values):
    return lax.rsqrt(jnp.mean(values * values, axis=-1, keepdims=True) + EPSILON)


def rms_back(values, gain, scale, grad):
    scaled = grad * gain
    inner = jnp.mean(values * scaled, axis=-1, keepdims=True)
    return scale * scaled - values * (scale * scale * scale * inner), jnp.sum(
        grad * values * scale, axis=0
    )


def turn(values, cosine, sine):
    half = values.shape[-1] // 2
    first, second = values[..., :half], values[..., half:]
    return jnp.concatenate(
        [first * cosine - second * sine, second * cosine + first * sine], axis=-1
    )


def columns_of(w, start, size):
    return lax.dynamic_slice_in_dim(w, start, size, 1)


def per_device(
    tokens,
    teacher,
    segment_ids,
    valid_mask,
    gain_in,
    w_in,
    conv_w,
    conv_b,
    dt_bias,
    a_log,
    d_skip,
    gain_m,
    w_out,
    w_qkv,
    w_o,
    gain_ffn,
    w_gate,
    w_up,
    w_down,
):
    net = Net()
    n, m, c, f = net.n, net.m, net.c, net.f
    rows, dim = tokens.shape[1:]
    length = segment_ids.shape[1]
    shard = w_in.shape[0]
    wide = MH * HP
    conv_full = wide + 2 * NS
    heads = MH // n
    q_heads = QH // n
    width = heads * HP
    conv_width = width + 2 * NS
    q_width = q_heads * HD
    group = QH // KVH
    kv_at = (c * q_heads) // group
    ff = w_gate.shape[1]
    ff_shard = w_down.shape[0]
    ff_part = ff_shard // 2
    seg = segment_ids[0]
    seg_c, seg_r = seg[:, None], seg[None, :]
    ends = jnp.concatenate([jnp.full((1,), -1, jnp.int32), seg[SPAN - 1 :: SPAN]])

    def lay(values):
        values = values.reshape((-1, values.shape[-1]))
        room = -values.shape[1] % 128
        return jnp.pad(values, ((0, 0), (0, room))).reshape(-1, 128)

    def lay_all(pieces, dtype):
        laid = [lay(p) for p in pieces]
        used = sum(p.shape[0] for p in laid)
        return jnp.concatenate(laid + [jnp.zeros((-used % 16, 128), dtype)], axis=0)

    def unlay(small, start, lead, size):
        room = size + -size % 128
        count = lead * room // 128
        return small[..., start : start + count, :].reshape(small.shape[:-2] + (lead, room))[
            ..., :size
        ]

    shapes = [(1, shard), (1, shard), (1, w_out.shape[0]), (1, conv_b.shape[0])]
    shapes += [(KW, conv_b.shape[0]), (MH, shard)]
    starts = [0]
    for lead, size in shapes:
        starts.append(starts[-1] + lead * (size + -size % 128) // 128)
    small = net.spread(
        lay_all(
            [
                gain_in[None],
                gain_ffn[None],
                gain_m[None],
                conv_b[None],
                conv_w,
                w_in[:, wide + conv_full :].T,
            ],
            BF16,
        )
    )
    cuts = [
        jnp.transpose(unlay(small, start, *shape), (1, 0, 2)).reshape(shape[0], -1)
        for start, shape in zip(starts, shapes)
    ]
    gain_input = cuts[0][0].astype(F32)
    gain_second = cuts[1][0].astype(F32)
    gain_mamba = lax.dynamic_slice_in_dim(cuts[2][0], c * width, width).astype(F32)

    def conv_cut(values):
        own = lax.dynamic_slice_in_dim(values, c * width, width, values.ndim - 1)
        return jnp.concatenate([own, values[..., wide:]], axis=-1)

    bias = conv_cut(cuts[3][0].astype(F32))
    taps = conv_cut(cuts[4].astype(F32))
    w_step = lax.dynamic_slice_in_dim(cuts[5], c * heads, heads, 0)
    step_bias = lax.dynamic_slice_in_dim(dt_bias, c * heads, heads)
    decay_log = lax.dynamic_slice_in_dim(a_log, c * heads, heads)
    skip = lax.dynamic_slice_in_dim(d_skip, c * heads, heads)

    all_tokens = net.ctx_all(tokens[0]).reshape(length, dim)
    first = jnp.concatenate(
        [
            columns_of(w_in, c * width, width),
            columns_of(w_in, wide + c * width, width),
            w_in[:, 2 * wide : 2 * wide + 2 * NS],
            columns_of(w_qkv, c * q_width, q_width),
            columns_of(w_qkv, QH * HD + kv_at * HD, HD),
            columns_of(w_qkv, (QH + KVH) * HD + kv_at * HD, HD),
        ],
        axis=1,
    )
    w_first = net.spread(first).reshape(dim, first.shape[1])
    quarter = dim // n
    both_out = jnp.concatenate([w_out, w_o], axis=0)
    out_rows = both_out.shape[0]
    own_out = columns_of(both_out, c * quarter, quarter)
    per = m // n
    spread_out = net.spread(own_out)
    swapped = net.ctx_swap(spread_out.reshape((n, per) + own_out.shape))
    w_outs = jnp.transpose(swapped, (1, 2, 0, 3)).reshape(per, out_rows, dim)
    mamba_rows = w_out.shape[0]
    w_mamba = w_outs[:, :mamba_rows].reshape(per * mamba_rows, dim)
    w_attn = w_outs[:, mamba_rows:].reshape(per * (out_rows - mamba_rows), dim)

    def ff_cut(w):
        w = w.reshape(shard, m, 2, ff_part)
        return lax.dynamic_index_in_dim(w, net.core, 2, False).reshape(shard, m * ff_part)

    halves = n // 2
    gate_up = jnp.concatenate([ff_cut(w_gate), ff_cut(w_up)], axis=1)
    gu_rows = shard // halves
    gate_up = lax.dynamic_slice_in_dim(gate_up, net.x * gu_rows, gu_rows, 0)
    w_gu = net.spread(gate_up, share_x=True).reshape(dim, ff)
    down = lax.dynamic_slice_in_dim(w_down, net.core * ff_part, ff_part, 0)
    d_rows = ff_part // halves
    down = lax.dynamic_slice_in_dim(down, net.x * d_rows, d_rows, 0)
    w_dn = net.spread(down, share_x=True).reshape(m * ff_part, dim)

    valid = valid_mask[0].astype(F32)
    count = net.total(jnp.full((8, 128), jnp.sum(valid), F32))[0, 0]
    resid_all = all_tokens.astype(F32)
    normed = (resid_all * rms_scale(resid_all) * gain_input).astype(BF16)
    proj = nn(normed, w_first)
    gate_z = proj[:, :width]
    conv_in = proj[:, width : width + conv_width]
    qkv = proj[:, width + conv_width :]
    step_raw = nt(normed, w_step) + step_bias
    dt = jax.nn.softplus(step_raw)
    rate = jnp.exp(decay_log)
    loga = -dt * rate

    def same_back(by):
        ahead = jnp.concatenate([jnp.full((by,), -1, jnp.int32), seg[: length - by]])
        return (ahead == seg).astype(F32)[:, None]

    def behind(values, by):
        if by == 0:
            return values
        return jnp.concatenate(
            [jnp.zeros((by,) + values.shape[1:], values.dtype), values[: length - by]]
        )

    def before(values, by):
        if by == 0:
            return values
        return jnp.concatenate([values[by:], jnp.zeros((by,) + values.shape[1:], values.dtype)])

    pre = bias[None, :]
    for tap in range(KW):
        by = KW - 1 - tap
        term = taps[tap][None, :] * behind(conv_in, by)
        pre = pre + (term * same_back(by) if by else term)
    act = jax.nn.silu(pre).astype(BF16)
    ssm_in = (ends, skip, act, dt, loga, dt.T, loga.T, seg_c, seg_r)
    ssm_y, states = ssm_forward(heads, ssm_in)
    gated = ssm_y * jax.nn.silu(gate_z)
    square = net.ctx_sum(jnp.sum(gated * gated, axis=1))

    half = HD // 2
    freq = ROPE_BASE ** (-(jnp.arange(half, dtype=F32) * 2.0 / HD))
    angle = jnp.arange(length, dtype=jnp.int32).astype(F32)[:, None] * freq[None, :]
    cosine, sine = jnp.cos(angle), jnp.sin(angle)
    q_rot = turn(qkv[:, :q_width].reshape(length, q_heads, HD), cosine[:, None], sine[:, None])
    query = q_rot.astype(BF16).reshape(length, q_width)
    keys = turn(qkv[:, q_width : q_width + HD], cosine, sine).astype(BF16)
    values = qkv[:, q_width + HD : q_width + 2 * HD].astype(BF16)
    attn_in = (query, keys, values, seg_c, seg_r)
    attended, lse = attn_forward(q_heads, attn_in)
    scale_m = lax.rsqrt(square / wide + EPSILON)[:, None]
    ym = (gated * scale_m * gain_mamba).astype(BF16)
    outs = nn(ym, w_mamba) + nn(attended, w_attn)
    mixed = tokens[0].astype(F32) + net.ctx_collect(outs.reshape(n, rows, dim))

    scale2 = rms_scale(mixed)
    normed2 = (mixed * scale2 * gain_second).astype(BF16)
    mate = [(i, i ^ 1) for i in range(n)]
    both = jnp.concatenate([normed2, lax.ppermute(normed2, "ctx", mate)], axis=0)
    gu = nn(both, w_gu)
    gate_v, up_v = gu[:, : ff // 2], gu[:, ff // 2 :]
    sig = jax.nn.sigmoid(gate_v)
    product = (gate_v * sig * up_v).astype(BF16)
    down_out = nn(product, w_dn)
    from_mate = lax.ppermute(down_out[rows:].astype(BF16), "ctx", mate)
    layer_out = mixed + down_out[:rows] + from_mate.astype(F32)
    diff = layer_out - teacher[0].astype(F32)
    squared = jnp.sum(valid[:, None] * diff * diff)
    token_total = length * m * tokens.shape[0]
    grad_out = token_total * valid[:, None] * diff / count

    gb = grad_out.astype(BF16)
    gb_both = jnp.concatenate([gb, lax.ppermute(gb, "ctx", mate)], axis=0)
    g_prod = nt(gb_both, w_dn)
    g_gate = (g_prod * up_v * (sig * (1.0 + gate_v * (1.0 - sig)))).astype(BF16)
    g_up = (g_prod * gate_v * sig).astype(BF16)
    g_gu = jnp.concatenate([g_gate, g_up], axis=1)
    g_n2 = nt(g_gu, w_gu)
    from_mate = lax.ppermute(g_n2[rows:].astype(BF16), "ctx", mate)
    grad_n2 = g_n2[:rows] + from_mate.astype(F32)
    grad_down = net.collect(tn(product, gb_both).reshape(m, ff_part, dim), share_x=True)
    grad_gu = net.collect(tn(both, g_gu).reshape(m, shard, ff), share_x=True)
    part, grad_gain_second = rms_back(mixed, gain_second, scale2, grad_n2)
    grad_mixed = grad_out + part
    gm = net.ctx_all(grad_mixed.astype(BF16)).reshape(length, dim)

    g_ym = nt(gm, w_mamba)
    g_ob = nt(gm, w_attn).astype(BF16)
    sig_z = jax.nn.sigmoid(gate_z)
    scaled = g_ym * gain_mamba
    inner = net.ctx_sum(jnp.sum(gated * scaled, axis=1))[:, None] / wide
    grad_gain_mamba = jnp.sum(g_ym * gated * scale_m, axis=0)
    g_query, g_keys, g_values = attn_backward(q_heads, attn_in, lse, g_ob)
    g_qkv = jnp.concatenate(
        [
            turn(g_query.reshape(length, q_heads, HD), cosine[:, None], -sine[:, None]).reshape(
                length, q_width
            ),
            turn(g_keys, cosine, -sine),
            g_values,
        ],
        axis=1,
    ).astype(BF16)
    g_gated = scale_m * scaled - gated * (scale_m * scale_m * scale_m * inner)
    g_ssm = g_gated * gate_z * sig_z
    g_z = (g_gated * ssm_y * (sig_z * (1.0 + gate_z * (1.0 - sig_z)))).astype(BF16)
    x_wide = act[:, :width].astype(F32)
    grad_skip = jnp.sum((g_ssm * x_wide).reshape(length, heads, HP), axis=(0, 2))
    g_act, g_col, g_row = ssm_backward(heads, ssm_in, states, g_ssm)
    g_run = g_col[:, :heads] - g_row[:heads].T
    g_run = g_run.reshape(length // SPAN, SPAN, heads)
    g_loga = lax.cumsum(g_run, axis=1, reverse=True).reshape(length, heads)
    g_dt = g_col[:, heads:] + g_row[heads:].T - g_loga * rate
    grad_decay_log = jnp.sum(g_loga * loga, axis=0)
    g_step = g_dt * jax.nn.sigmoid(step_raw)
    grad_step_bias = jnp.sum(g_step, axis=0)
    sig_pre = jax.nn.sigmoid(pre)
    g_pre = g_act * (sig_pre * (1.0 + pre * (1.0 - sig_pre)))
    grad_bias = jnp.sum(g_pre, axis=0)
    grad_taps = []
    g_conv = jnp.zeros_like(g_pre)
    for tap in range(KW):
        by = KW - 1 - tap
        masked = g_pre * same_back(by) if by else g_pre
        grad_taps.append(jnp.sum(masked * behind(conv_in, by), axis=0))
        g_conv = g_conv + taps[tap][None, :] * before(masked, by)
    grad_taps = jnp.stack(grad_taps)
    g_first = jnp.concatenate([g_z, g_conv.astype(BF16), g_qkv], axis=1)
    g_step_low = g_step.astype(BF16)
    grad_first = net.collect(tn(normed, g_first).reshape(m, shard, first.shape[1]))
    g_normed = nt(g_first, w_first) + nn(g_step_low, w_step)
    grad_normed = net.ctx_collect(g_normed.reshape(n, rows, dim))
    resid = tokens[0].astype(F32)
    part, grad_gain_input = rms_back(resid, gain_input, rms_scale(resid), grad_normed)
    grad_tokens = grad_mixed + part
    grad_w_step = tn(g_step_low, normed)

    g_outs = jnp.concatenate(
        [
            tn(ym, gm).reshape(per, mamba_rows, dim),
            tn(attended, gm).reshape(per, out_rows - mamba_rows, dim),
        ],
        axis=1,
    ).astype(BF16)
    g_outs = jnp.transpose(g_outs.reshape(per, out_rows, n, quarter), (2, 0, 1, 3))
    grad_outs = net.collect(net.ctx_swap(g_outs).reshape(m, out_rows, quarter))

    def to_wide(values, at, size):
        out = jnp.zeros(values.shape[:-1] + (size,), F32)
        return lax.dynamic_update_slice_in_dim(out, values, at, values.ndim - 1)

    def conv_wide(values):
        return jnp.concatenate(
            [to_wide(values[..., :width], c * width, wide), values[..., width:]], axis=-1
        )

    def for_shards(values):
        values = values.reshape((-1, m, values.shape[-1] // m))
        return jnp.transpose(values, (1, 0, 2))

    small_grads = [
        grad_gain_input,
        grad_gain_second,
        to_wide(grad_gain_mamba, c * width, wide),
        conv_wide(grad_bias),
        conv_wide(grad_taps),
        lax.dynamic_update_slice_in_dim(
            jnp.zeros((MH, dim), F32), grad_w_step, c * heads, 0
        ),
    ]
    heads_grads = jnp.stack(
        [
            to_wide(grad_step_bias, c * heads, MH),
            to_wide(grad_decay_log, c * heads, MH),
            to_wide(grad_skip, c * heads, MH),
            jnp.full((MH,), squared),
        ]
    )
    laid = [jax.vmap(lay)(for_shards(g)) for g in small_grads]
    laid.append(jnp.broadcast_to(lay(heads_grads)[None], (m, 4, 128)))
    used = sum(p.shape[1] for p in laid)
    laid.append(jnp.zeros((m, -used % 16, 128), F32))
    totals = net.ctx_sum(net.collect(jnp.concatenate(laid, axis=1), kind=F32))
    own_small = [unlay(totals, start, *shape) for start, shape in zip(starts, shapes)]
    head_totals = totals[starts[-1] : starts[-1] + 4, :MH]
    loss = head_totals[3, 0] / (2.0 * count)

    got = net.ctx_all(grad_first).astype(F32)
    cuts = [0, width, 2 * width, 2 * width + 2 * NS]
    cuts += [cuts[-1] + q_width, cuts[-1] + q_width + HD, cuts[-1] + q_width + 2 * HD]

    def side(i):
        return [got[j][:, cuts[i] : cuts[i + 1]] for j in range(n)]

    shared = n // KVH
    out_w_in = jnp.concatenate(
        side(0) + side(1) + [sum(side(2)), own_small[5].T],
        axis=1,
    )
    out_w_qkv = jnp.concatenate(
        side(3)
        + [sum(side(i)[k * shared : (k + 1) * shared]) for i in (4, 5) for k in range(KVH)],
        axis=1,
    )
    got = net.ctx_all(grad_outs).astype(F32)
    out_outs = jnp.transpose(got, (1, 0, 2)).reshape(out_rows, dim)
    got = net.ctx_all(grad_gu).astype(F32)
    got = got.reshape(halves, 2, gu_rows, 2, m, ff_part)
    got = jnp.transpose(got, (3, 0, 2, 4, 1, 5)).reshape(2, shard, ff)
    out_down = net.ctx_all(grad_down).astype(F32).reshape(halves, 2, d_rows, dim)
    out_down = jnp.transpose(out_down, (1, 0, 2, 3)).reshape(ff_shard, dim)
    return (
        loss,
        layer_out[None],
        grad_tokens[None],
        own_small[0][0],
        out_w_in,
        own_small[4],
        own_small[3][0],
        head_totals[0],
        head_totals[1],
        head_totals[2],
        own_small[2][0],
        out_outs[:mamba_rows],
        out_w_qkv,
        out_outs[mamba_rows:],
        own_small[1][0],
        got[0],
        got[1],
        out_down,
    )


def solution(mesh):
    in_specs = (
        P("fsdp", "ctx", None),
        P("fsdp", "ctx", None),
        P("fsdp", None),
        P("fsdp", "ctx"),
        P("fsdp"),
        P("fsdp", None),
        P(None, "fsdp"),
        P("fsdp"),
        P(),
        P(),
        P(),
        P("fsdp"),
        P("fsdp", None),
        P("fsdp", None),
        P("fsdp", None),
        P("fsdp"),
        P("fsdp", None),
        P("fsdp", None),
        P("fsdp", None),
    )
    out_specs = (
        P(),
        P("fsdp", "ctx", None),
        P("fsdp", "ctx", None),
        P("fsdp"),
        P("fsdp", None),
        P(None, "fsdp"),
        P("fsdp"),
        P(),
        P(),
        P(),
        P("fsdp"),
        P("fsdp", None),
        P("fsdp", None),
        P("fsdp", None),
        P("fsdp"),
        P("fsdp", None),
        P("fsdp", None),
        P("fsdp", None),
    )
    return jax.shard_map(
        per_device, mesh=mesh, in_specs=in_specs, out_specs=out_specs, check_vma=False
    )
```

time: 1530 us -> 655 us (0.43)
  waiting for transfers between devices: 842 us -> 165 us
  blocking collectives: 233 us -> 0 us
  starting transfers between devices: 3.91 us -> 145 us
  matrix products: 155 us -> 47.5 us
  Pallas kernels: 0 us -> 71.7 us
  local copies, waits for them, and re-layouts: 162 us -> 137 us
  other arithmetic: 94.8 us -> 76.8 us
  between operations: 23.1 us -> 6.16 us
    reduce_scatter x7 -> x0, waiting for transfers between devices: 483 us -> none  [the longest x1 91.7 us: per_device(): lax.psum_scatter(grad_gate_w.astype(jnp.bfloat16), 'fsdp', scatter_dimens...]
    all_gather x9 -> x0, waiting for transfers between devices: 215 us -> none  [the longest x1 68.9 us: per_device(): lax.all_gather(w_up, 'fsdp', axis=0, tiled=True)]
    ppermute x2 -> x119, waiting for transfers between devices: 1.3 us -> 165 us  [the longest x82 97 us: flip(): return lax.ppermute(value, axis, [(i, i ^ bit) for i in range(size)])]
    ppermute x2 -> x119, starting transfers between devices: 2.98 us -> 145 us  [the longest x82 77 us: flip(): return lax.ppermute(value, axis, [(i, i ^ bit) for i in range(size)])]
    dot_general x80 -> x18, matrix products: 155 us -> 47.5 us  [the longest x6 19 us: tn(): lax.dot_general(left, right, (((0,), (0,)), ((), ())), preferred_element_...]
    unnamed x21 -> x0, waiting for transfers between devices: 103 us -> none
    psum x3 -> x0, blocking collectives: 85.8 us -> none  [the longest x2 79.2 us: per_device(): lax.psum((squared_local, count_local), ('ctx', 'fsdp'))]
    all_gather x5 -> x0, blocking collectives: 85 us -> none  [the longest x1 31.5 us: per_device(): lax.all_gather(conv_w, 'fsdp', axis=1, tiled=True)]
  transfers between devices with their start and end apart: 21 -> 119, of which waited for: 13 -> 38; matrix products, arithmetic and copies ran while one was open for 23% -> 25% of each run, Pallas kernels for 0% -> 9%
where the time goes in v1:
time: 655 us; the launch traced here: 650 us
  waiting for transfers between devices  165 us (25%)
  starting transfers between devices  145 us (22%)
  local copies, waits for them, and re-layouts  137 us (21%)
  other arithmetic  76.8 us (12%)
  Pallas kernels  71.7 us (11%)
  matrix products  47.5 us (7%)
    ppermute x82, waiting for transfers between devices, flip(): return lax.ppermute(value, axis, [(i, i ^ bit) for i in range(size)])  97 us
    ppermute x82, starting transfers between devices, flip(): return lax.ppermute(value, axis, [(i, i ^ bit) for i in range(size)])  77 us
    ppermute x33, starting transfers between devices, shift_z(): lax.ppermute(value, 'fsdp', [(i, (i + 2 * by) % self.m) for i in range(se...  67.8 us
    ppermute x33, waiting for transfers between devices, shift_z(): lax.ppermute(value, 'fsdp', [(i, (i + 2 * by) % self.m) for i in range(se...  66.1 us
    unnamed x399, local copies, waits for them, and re-layouts  47.5 us
    pallas_call x1, Pallas kernels, ssm_backward(): pl.pallas_call(functools.partial(ssm_bwd_kernel, heads), grid=(steps,), i...  28.9 us
    pallas_call x13, Pallas kernels, put(): pl.pallas_call(functools.partial(put_kernel, count), grid_spec=pltpu.Pref...  19 us
    dot_general x6, matrix products, tn(): lax.dot_general(left, right, (((0,), (0,)), ((), ())), preferred_element_...  19 us
  transfers between devices with their start and end apart: 119, of which 38 were waited for; matrix products, arithmetic and copies ran while one was open for 25% of the time, Pallas kernels for 9%

profile of v1, /device:TPU:0, one launch (start us, length us, event | category | flops | bytes accessed | tf_op | source)
XLA Modules:
  0.0 649.6 jit_solution(3838348199020167358)
XLA Ops:
  4.6 3.0 collective-permute-start
  9.2 2.6 collective-permute-start.3
  28.5 2.9 collective-permute-start.24
  35.7 2.5 collective-permute-done.22.refs_4_
  39.9 3.3 collective-permute-start.13
  48.4 2.5 collective-permute-done.25.refs_7_
  71.6 3.5 collective-permute-done.28.refs_3_
  87.8 3.6 collective-permute-done.16.refs_7_
  91.4 2.5 put.15
  93.9 2.5 put.14
  98.1 2.9 fusion.113
  110.4 4.7 fusion.36
  123.8 6.5 %multiply_convert_fusion.1 = (bf16[1024,640]{1,0:T(8,128)(2,1)S(1)}, f32[1024,640]{1,0:T(8,128)}) fusion(f32[1024,1280]{1,0:T(8,128)} %copy-done.81, f32[640]{0:T(1024)S(1)} %copy-done.151, f32[1024]{0:T(1024)S(1)} %copy-done.140, f32[1023,640]{1,0:T(8,128)} %slice.490, f32[640]{0:T(1024)S(1)} %copy-done.153, f32[1024]{0:T(1024)S(1)} %copy-done.142, ...), kind=kLoop, calls=%fused_computation.18 | loop fusion | flops 10485760 | bytes 14427648 | tf_op jit(solution)/shard_map/convert_element_type | solution.py:702
  130.4 12.2 %ssm_forward.1 = (f32[1024,384]{1,0:T(8,128)S(1)}, f32[8,6,64,128]{3,2,1,0:T(8,128)S(1)}) custom-call(s32[9]{0:T(128)S(1)} %pad_add_fusion.ends, f32[6]{0:T(128)S(1)} %dynamic_slice.216.skip, bf16[1024,640]{1,0:T(8,128)(2,1)S(1)} %get-tuple-element.165.act, f32[1024,6]{1,0:T(8,128)S(1)} %copy.231.dt_c, f32[1024,6]{1,0:T(8,128)S(1)} %copy.232.loga_c, ...), custom_call_target="tpu_custom_call" | custom-call | flops 1000000000 | bytes 10000000 | tf_op jit(solution)/shard_map/ssm_forward/pallas_call | solution.py:190
  142.6 3.1 multiply_reduce_fusion.8
  146.1 5.0 attn_forward.1
  162.9 3.1 dynamic-slice_reduce_fusion
  167.9 4.6 collective-permute-start.51
  172.5 2.8 collective-permute-start.55
  179.1 4.9 collective-permute-done.55.refs_8_
  184.5 2.7 collective-permute-start.36
  189.9 5.8 collective-permute-done.36.refs_4_
  197.2 8.4 %collective-permute-done.40.refs_8_ = bf16[64,2048]{1,0:T(8,128)(2,1)S(1)} collective-permute-done((bf16[64,2048]{1,0:T(8,128)(2,1)S(1)}, bf16[64,2048]{1,0:T(8,128)(2,1)S(1)}, u32[]{:S(2)}, u32[]{:S(2)}) %collective-permute-start.40) | collective-permute-done | bytes 262176 | tf_op jit(solution)/shard_map/ppermute | solution.py:372
  222.1 3.2 collective-permute-done.60.refs_13_
  265.4 3.9 put.18
  269.3 3.6 fusion.28
  279.3 6.6 %collective-permute-start.69 = (f32[8,128]{1,0:T(8,128)S(1)}, f32[8,128]{1,0:T(8,128)S(1)}, u32[]{:S(2)}, u32[]{:S(2)}) collective-permute-start(f32[8,128]{1,0:T(8,128)S(1)} %add.795), channel_id=1, source_target_pairs={{0,6},{1,7},{2,0},{3,1},{4,2},{5,3},{6,4},{7,5},{8,14},{9,15},{10,... | collective-permute-start | bytes 12296 | tf_op jit(solution)/shard_map/ppermute | solution.py:372
  287.2 4.1 collective-permute-done.67
  303.1 4.3 copy.265
  308.3 2.8 convolution_convert_fusion.2
  313.8 3.3 fusion.108
  320.1 3.6 convolution_convert_fusion
  323.9 24.1 %collective-permute-done.73.refs_2_ = bf16[256,1024]{1,0:T(8,128)(2,1)S(1)} collective-permute-done((bf16[256,1024]{1,0:T(8,128)(2,1)S(1)}, bf16[256,1024]{1,0:T(8,128)(2,1)S(1)}, u32[]{:S(2)}, u32[]{:S(2)}) %collective-permute-start.73) | collective-permute-done | bytes 524320 | tf_op jit(solution)/shard_map/ppermute | solution.py:369
  355.3 3.1 multiply_reduce_fusion.6
  359.8 6.6 %attn_backward.1 = (f32[1024,128]{1,0:T(8,128)S(1)}, f32[1024,64]{1,0:T(8,128)S(1)}, f32[1024,64]{1,0:T(8,128)S(1)}) custom-call(bf16[1024,128]{1,0:T(8,128)(2,1)S(1)} %copy-done.31, bf16[1024,64]{1,0:T(8,128)(2,1)S(1)} %pad_maximum_fusion.10.k_ref, bf16[1024,64]{1,0:T(8,128)(2,1)S(1)} %copy-done.29, s32[1024,1]{1,0:T(8,128)S(1)} %copy-done.13, ...), custom_call_target="tpu_custom_call" | custom-call | flops 3000000000 | bytes 10000000 | tf_op jit(solution)/shard_map/attn_backward/pallas_call | solution.py:333
  370.0 3.8 fusion.42
  381.7 2.5 copy.271
  384.2 3.3 convolution_convert_fusion.4
  391.2 2.9 collective-permute-start.115
  394.7 3.1 collective-permute-done.76
  397.9 4.6 multiply_reduce_fusion.5
  402.6 28.9 %ssm_backward.1 = (f32[1024,640]{1,0:T(8,128)S(1)}, f32[1024,12]{1,0:T(8,128)S(1)}, f32[12,1024]{1,0:T(8,128)S(1)}) custom-call(s32[9]{0:T(128)S(1)} %pad_add_fusion.ends, f32[6]{0:T(128)S(1)} %copy-done.76, bf16[1024,640]{1,0:T(8,128)(2,1)S(1)} %copy-done.6, f32[1024,6]{1,0:T(8,128)S(1)} %copy-done.16, f32[1024,6]{1,0:T(8,128)S(1)} %copy-done.18, ...), custom_call_target="tpu_custom_call" | custom-call | flops 3000000000 | bytes 10000000 | tf_op jit(solution)/shard_map/ssm_backward/pallas_call | solution.py:217
  437.3 2.9 fusion.112
  443.7 3.6 fusion.80
  448.3 3.1 multiply_reduce_fusion.4
  458.1 5.2 concatenate.143
  463.3 5.2 convolution_convert_fusion.1
  472.4 3.0 convolution_convert_fusion.3
  477.1 5.5 convolution_add_fusion.1
  488.4 11.9 %collective-permute-done.117.refs_2_ = bf16[64,1024]{1,0:T(8,128)(2,1)S(1)} collective-permute-done((bf16[64,1024]{1,0:T(8,128)(2,1)S(1)}, bf16[64,1024]{1,0:T(8,128)(2,1)S(1)}, u32[]{:S(2)}, u32[]{:S(2)}) %collective-permute-start.117) | collective-permute-done | bytes 131104 | tf_op jit(solution)/shard_map/ppermute | solution.py:369
  508.0 2.6 fusion
  512.1 5.8 collective-permute-done.96
  518.1 3.0 collective-permute-start.99
  526.5 5.1 collective-permute-done.98
  536.4 18.6 %collective-permute-done.80 = f32[4,48,128]{2,1,0:T(8,128)S(1)} collective-permute-done((f32[4,48,128]{2,1,0:T(8,128)S(1)}, f32[4,48,128]{2,1,0:T(8,128)S(1)}, u32[]{:S(2)}, u32[]{:S(2)}) %collective-permute-start.80) | collective-permute-done | bytes 98336 | tf_op jit(solution)/shard_map/ppermute | solution.py:369
  555.1 4.2 collective-permute-start.83
  560.2 2.8 fusion.15
  573.2 3.3 collective-permute-start.89
  577.8 6.4 collective-permute-done.104
  584.7 3.6 collective-permute-start.107
  588.4 12.4 %collective-permute-start.105 = (bf16[64,2048]{1,0:T(8,128)(2,1)S(1)}, bf16[64,2048]{1,0:T(8,128)(2,1)S(1)}, u32[]{:S(2)}, u32[]{:S(2)}) collective-permute-start(bf16[64,2048]{1,0:T(8,128)(2,1)S(1)} %get-tuple-element.193), channel_id=1, source_target_pairs={{0,2},{1,3},{2,4},{3,5},{4,6},{5,7},{6,0},{7,1},{8,10},{9,11},{10,... | collective-permute-start | bytes 786440 | tf_op jit(solution)/shard_map/ppermute | solution.py:372
  600.9 17.7 %collective-permute-done.88 = bf16[128,1280]{1,0:T(8,128)(2,1)S(1)} collective-permute-done((bf16[128,1280]{1,0:T(8,128)(2,1)S(1)}, bf16[128,1280]{1,0:T(8,128)(2,1)S(1)}, u32[]{:S(2)}, u32[]{:S(2)}) %collective-permute-start.88) | collective-permute-done | bytes 327712 | tf_op jit(solution)/shard_map/ppermute | solution.py:372
  620.1 8.2 %collective-permute-done.106 = bf16[64,2048]{1,0:T(8,128)(2,1)S(1)} collective-permute-done((bf16[64,2048]{1,0:T(8,128)(2,1)S(1)}, bf16[64,2048]{1,0:T(8,128)(2,1)S(1)}, u32[]{:S(2)}, u32[]{:S(2)}) %collective-permute-start.106) | collective-permute-done | bytes 262176 | tf_op jit(solution)/shard_map/ppermute | solution.py:372
  638.2 2.7 copy.283
  (846 shorter events, 292.8 us)
Async XLA Ops:
  4.6 22.8 %collective-permute-start = (bf16[48,128]{1,0:T(8,128)(2,1)S(1)}, bf16[48,128]{1,0:T(8,128)(2,1)S(1)}, u32[]{:S(2)}, u32[]{:S(2)}) collective-permute-start(bf16[48,128]{1,0:T(8,128)(2,1)S(1)} %concatenate.121.refs_0_), channel_id=1, source_target_pairs={{0,1},{1,0},{2,3},{3,2},{4,5},{5,4},{6,7},{7,6},{8,9},{9,8},{10,11... | collective-permute-start | bytes 36872 | tf_op jit(solution)/shard_map/ppermute | solution.py:369
  7.7 13.7 %collective-permute-start.1 = (bf16[48,128]{1,0:T(8,128)(2,1)S(1)}, bf16[48,128]{1,0:T(8,128)(2,1)S(1)}, u32[]{:S(2)}, u32[]{:S(2)}) collective-permute-start(bf16[48,128]{1,0:T(8,128)(2,1)S(1)} %concatenate.121.refs_0_), channel_id=1, source_target_pairs={{0,2},{1,3},{2,4},{3,5},{4,6},{5,7},{6,0},{7,1},{8,10},{9,11},{10,... | collective-permute-start | bytes 36872 | tf_op jit(solution)/shard_map/ppermute | solution.py:372
  9.2 13.7 %collective-permute-start.3 = (bf16[48,128]{1,0:T(8,128)(2,1)S(1)}, bf16[48,128]{1,0:T(8,128)(2,1)S(1)}, u32[]{:S(2)}, u32[]{:S(2)}) collective-permute-start(bf16[48,128]{1,0:T(8,128)(2,1)S(1)} %concatenate.121.refs_0_), channel_id=1, source_target_pairs={{0,4},{1,5},{2,6},{3,7},{4,0},{5,1},{6,2},{7,3},{8,12},{9,13},{10,... | collective-permute-start | bytes 36872 | tf_op jit(solution)/shard_map/ppermute | solution.py:372
  11.8 11.6 %collective-permute-start.5 = (bf16[48,128]{1,0:T(8,128)(2,1)S(1)}, bf16[48,128]{1,0:T(8,128)(2,1)S(1)}, u32[]{:S(2)}, u32[]{:S(2)}) collective-permute-start(bf16[48,128]{1,0:T(8,128)(2,1)S(1)} %concatenate.121.refs_0_), channel_id=1, source_target_pairs={{0,6},{1,7},{2,0},{3,1},{4,2},{5,3},{6,4},{7,5},{8,14},{9,15},{10,... | collective-permute-start | bytes 36872 | tf_op jit(solution)/shard_map/ppermute | solution.py:372
  14.1 25.4 %collective-permute-start.19 = (bf16[256,256]{1,0:T(8,128)(2,1)S(1)}, bf16[256,256]{1,0:T(8,128)(2,1)S(1)}, u32[]{:S(2)}, u32[]{:S(2)}) collective-permute-start(bf16[256,256]{1,0:T(8,128)(2,1)S(1)} %fusion.65.refs_0_), channel_id=1, source_target_pairs={{0,1},{1,0},{2,3},{3,2},{4,5},{5,4},{6,7},{7,6},{8,9},{9,8},{10,11... | collective-permute-start | bytes 393224 | tf_op jit(solution)/shard_map/ppermute | solution.py:369
  28.5 11.4 %collective-permute-start.24 = (bf16[256,256]{1,0:T(8,128)(2,1)S(1)}, bf16[256,256]{1,0:T(8,128)(2,1)S(1)}, u32[]{:S(2)}, u32[]{:S(2)}) collective-permute-start(bf16[256,256]{1,0:T(8,128)(2,1)S(1)} %fusion.65.refs_0_), channel_id=1, source_target_pairs={{0,6},{1,7},{2,0},{3,1},{4,2},{5,3},{6,4},{7,5},{8,14},{9,15},{10,... | collective-permute-start | bytes 393224 | tf_op jit(solution)/shard_map/ppermute | solution.py:372
  31.3 29.7 %collective-permute-start.10 = (bf16[128,1280]{1,0:T(8,128)(2,1)S(1)}, bf16[128,1280]{1,0:T(8,128)(2,1)S(1)}, u32[]{:S(2)}, u32[]{:S(2)}) collective-permute-start(bf16[128,1280]{1,0:T(8,128)(2,1)S(1)} %concatenate.124.refs_0_), channel_id=1, source_target_pairs={{0,1},{1,0},{2,3},{3,2},{4,5},{5,4},{6,7},{7,6},{8,9},{9,8},{10,11... | collective-permute-start | bytes 983048 | tf_op jit(solution)/shard_map/ppermute | solution.py:369
  39.4 21.6 %collective-permute-start.11 = (bf16[128,1280]{1,0:T(8,128)(2,1)S(1)}, bf16[128,1280]{1,0:T(8,128)(2,1)S(1)}, u32[]{:S(2)}, u32[]{:S(2)}) collective-permute-start(bf16[128,1280]{1,0:T(8,128)(2,1)S(1)} %concatenate.124.refs_0_), channel_id=1, source_target_pairs={{0,2},{1,3},{2,4},{3,5},{4,6},{5,7},{6,0},{7,1},{8,10},{9,11},{10,... | collective-permute-start | bytes 983048 | tf_op jit(solution)/shard_map/ppermute | solution.py:372
  39.9 23.0 %collective-permute-start.13 = (bf16[128,1280]{1,0:T(8,128)(2,1)S(1)}, bf16[128,1280]{1,0:T(8,128)(2,1)}, u32[]{:S(2)}, u32[]{:S(2)}) collective-permute-start(bf16[128,1280]{1,0:T(8,128)(2,1)S(1)} %concatenate.124.refs_0_), channel_id=1, source_target_pairs={{0,4},{1,5},{2,6},{3,7},{4,0},{5,1},{6,2},{7,3},{8,12},{9,13},{10,... | collective-permute-start | bytes 983048 | tf_op jit(solution)/shard_map/ppermute | solution.py:372
  43.8 22.0 %collective-permute-start.8 = (bf16[256,1024]{1,0:T(8,128)(2,1)S(1)}, bf16[256,1024]{1,0:T(8,128)(2,1)}, u32[]{:S(2)}, u32[]{:S(2)}) collective-permute-start(bf16[256,1024]{1,0:T(8,128)(2,1)S(1)} %bitcast.409), channel_id=1, source_target_pairs={{0,16},{8,24},{16,0},{24,8},{1,17},{9,25},{17,1},{25,9},{2,18},{10... | collective-permute-start | bytes 1572872 | tf_op jit(solution)/shard_map/ppermute | solution.py:369
  51.6 14.0 %collective-permute-start.15 = (bf16[128,1280]{1,0:T(8,128)(2,1)S(1)}, bf16[128,1280]{1,0:T(8,128)(2,1)}, u32[]{:S(2)}, u32[]{:S(2)}) collective-permute-start(bf16[128,1280]{1,0:T(8,128)(2,1)S(1)} %concatenate.124.refs_0_), channel_id=1, source_target_pairs={{0,6},{1,7},{2,0},{3,1},{4,2},{5,3},{6,4},{7,5},{8,14},{9,15},{10,... | collective-permute-start | bytes 983048 | tf_op jit(solution)/shard_map/ppermute | solution.py:372
  62.8 12.2 %collective-permute-start.28 = (bf16[2,256,256]{2,1,0:T(8,128)(2,1)}, bf16[2,256,256]{2,1,0:T(8,128)(2,1)S(1)}, u32[]{:S(2)}, u32[]{:S(2)}) collective-permute-start(bf16[2,256,256]{2,1,0:T(8,128)(2,1)} %get-tuple-element.200), channel_id=1, source_target_pairs={{0,24},{8,16},{16,8},{24,0},{1,25},{9,17},{17,9},{25,1},{2,26},{10... | collective-permute-start | bytes 786440 | tf_op jit(solution)/shard_map/ppermute | solution.py:369
  65.6 28.3 %collective-permute-start.7 = (bf16[256,1024]{1,0:T(8,128)(2,1)S(1)}, bf16[256,1024]{1,0:T(8,128)(2,1)}, u32[]{:S(2)}, u32[]{:S(2)}) collective-permute-start(bf16[256,1024]{1,0:T(8,128)(2,1)S(1)} %bitcast.410), channel_id=1, source_target_pairs={{0,8},{8,0},{16,24},{24,16},{1,9},{9,1},{17,25},{25,17},{2,10},{10... | collective-permute-start | bytes 1572872 | tf_op jit(solution)/shard_map/ppermute | solution.py:369
  65.8 28.2 %collective-permute-start.9 = (bf16[256,1024]{1,0:T(8,128)(2,1)}, bf16[256,1024]{1,0:T(8,128)(2,1)}, u32[]{:S(2)}, u32[]{:S(2)}) collective-permute-start(bf16[256,1024]{1,0:T(8,128)(2,1)} %collective-permute-done.8.refs_2_), channel_id=1, source_target_pairs={{0,8},{8,0},{16,24},{24,16},{1,9},{9,1},{17,25},{25,17},{2,10},{10... | collective-permute-start | bytes 1572872 | tf_op jit(solution)/shard_map/ppermute | solution.py:369
  67.4 20.4 %collective-permute-start.12 = (bf16[128,1280]{1,0:T(8,128)(2,1)S(1)}, bf16[128,1280]{1,0:T(8,128)(2,1)}, u32[]{:S(2)}, u32[]{:S(2)}) collective-permute-start(bf16[128,1280]{1,0:T(8,128)(2,1)S(1)} %collective-permute-done.11.refs_2_), channel_id=1, source_target_pairs={{0,1},{1,0},{2,3},{3,2},{4,5},{5,4},{6,7},{7,6},{8,9},{9,8},{10,11... | collective-permute-start | bytes 983048 | tf_op jit(solution)/shard_map/ppermute | solution.py:369
  71.1 16.7 %collective-permute-start.14 = (bf16[128,1280]{1,0:T(8,128)(2,1)}, bf16[128,1280]{1,0:T(8,128)(2,1)}, u32[]{:S(2)}, u32[]{:S(2)}) collective-permute-start(bf16[128,1280]{1,0:T(8,128)(2,1)} %collective-permute-done.13.refs_4_), channel_id=1, source_target_pairs={{0,1},{1,0},{2,3},{3,2},{4,5},{5,4},{6,7},{7,6},{8,9},{9,8},{10,11... | collective-permute-start | bytes 983048 | tf_op jit(solution)/shard_map/ppermute | solution.py:369
  75.8 15.6 %collective-permute-start.16 = (bf16[128,1280]{1,0:T(8,128)(2,1)}, bf16[128,1280]{1,0:T(8,128)(2,1)}, u32[]{:S(2)}, u32[]{:S(2)}) collective-permute-start(bf16[128,1280]{1,0:T(8,128)(2,1)} %collective-permute-done.15.refs_6_), channel_id=1, source_target_pairs={{0,1},{1,0},{2,3},{3,2},{4,5},{5,4},{6,7},{7,6},{8,9},{9,8},{10,11... | collective-permute-start | bytes 983048 | tf_op jit(solution)/shard_map/ppermute | solution.py:369
  157.4 17.9 %collective-permute-start.30 = (bf16[256,1024]{1,0:T(8,128)(2,1)}, bf16[256,1024]{1,0:T(8,128)(2,1)}, u32[]{:S(2)}, u32[]{:S(2)}) collective-permute-start(bf16[256,1024]{1,0:T(8,128)(2,1)} %get-tuple-element.175), channel_id=1, source_target_pairs={{0,8},{8,0},{16,24},{24,16},{1,9},{9,1},{17,25},{25,17},{2,10},{10... | collective-permute-start | bytes 1572872 | tf_op jit(solution)/shard_map/ppermute | solution.py:369
  159.4 13.1 %collective-permute-start.49 = (bf16[64,1024]{1,0:T(8,128)(2,1)S(1)}, bf16[64,1024]{1,0:T(8,128)(2,1)S(1)}, u32[]{:S(2)}, u32[]{:S(2)}) collective-permute-start(bf16[64,1024]{1,0:T(8,128)(2,1)S(1)} %constant_dynamic-slice_fusion.4.refs_0_), channel_id=1, source_target_pairs={{0,1},{1,0},{2,3},{3,2},{4,5},{5,4},{6,7},{7,6},{8,9},{9,8},{10,11... | collective-permute-start | bytes 393224 | tf_op jit(solution)/shard_map/ppermute | solution.py:369
  166.1 21.1 %collective-permute-start.33 = (bf16[64,2048]{1,0:T(8,128)(2,1)S(1)}, bf16[64,2048]{1,0:T(8,128)(2,1)S(1)}, u32[]{:S(2)}, u32[]{:S(2)}) collective-permute-start(bf16[64,2048]{1,0:T(8,128)(2,1)S(1)} %fusion.50.refs_0_), channel_id=1, source_target_pairs={{0,16},{8,24},{16,0},{24,8},{1,17},{9,25},{17,1},{25,9},{2,18},{10... | collective-permute-start | bytes 786440 | tf_op jit(solution)/shard_map/ppermute | solution.py:369
  167.4 21.5 %collective-permute-start.34 = (bf16[64,2048]{1,0:T(8,128)(2,1)S(1)}, bf16[64,2048]{1,0:T(8,128)(2,1)S(1)}, u32[]{:S(2)}, u32[]{:S(2)}) collective-permute-start(bf16[64,2048]{1,0:T(8,128)(2,1)S(1)} %fusion.50.refs_0_), channel_id=1, source_target_pairs={{0,1},{1,0},{2,3},{3,2},{4,5},{5,4},{6,7},{7,6},{8,9},{9,8},{10,11... | collective-permute-start | bytes 786440 | tf_op jit(solution)/shard_map/ppermute | solution.py:369
  172.5 11.5 %collective-permute-start.55 = (bf16[64,1024]{1,0:T(8,128)(2,1)S(1)}, bf16[64,1024]{1,0:T(8,128)(2,1)S(1)}, u32[]{:S(2)}, u32[]{:S(2)}) collective-permute-start(bf16[64,1024]{1,0:T(8,128)(2,1)S(1)} %constant_dynamic-slice_fusion.4.refs_0_), channel_id=1, source_target_pairs={{0,4},{1,5},{2,6},{3,7},{4,0},{5,1},{6,2},{7,3},{8,12},{9,13},{10,... | collective-permute-start | bytes 393224 | tf_op jit(solution)/shard_map/ppermute | solution.py:372
  179.1 34.5 %collective-permute-start.29 = (bf16[256,1024]{1,0:T(8,128)(2,1)}, bf16[256,1024]{1,0:T(8,128)(2,1)S(1)}, u32[]{:S(2)}, u32[]{:S(2)}) collective-permute-start(bf16[256,1024]{1,0:T(8,128)(2,1)} %get-tuple-element.174), channel_id=1, source_target_pairs={{0,8},{8,0},{16,24},{24,16},{1,9},{9,1},{17,25},{25,17},{2,10},{10... | collective-permute-start | bytes 1572872 | tf_op jit(solution)/shard_map/ppermute | solution.py:369
  184.0 29.7 %collective-permute-start.31 = (bf16[256,1024]{1,0:T(8,128)(2,1)S(1)}, bf16[256,1024]{1,0:T(8,128)(2,1)S(1)}, u32[]{:S(2)}, u32[]{:S(2)}) collective-permute-start(bf16[256,1024]{1,0:T(8,128)(2,1)S(1)} %fusion.21), channel_id=1, source_target_pairs={{0,16},{8,24},{16,0},{24,8},{1,17},{9,25},{17,1},{25,9},{2,18},{10... | collective-permute-start | bytes 1572872 | tf_op jit(solution)/shard_map/ppermute | solution.py:369
  187.3 18.3 %collective-permute-start.40 = (bf16[64,2048]{1,0:T(8,128)(2,1)S(1)}, bf16[64,2048]{1,0:T(8,128)(2,1)S(1)}, u32[]{:S(2)}, u32[]{:S(2)}) collective-permute-start(bf16[64,2048]{1,0:T(8,128)(2,1)S(1)} %fusion.50.refs_0_), channel_id=1, source_target_pairs={{0,4},{1,5},{2,6},{3,7},{4,0},{5,1},{6,2},{7,3},{8,12},{9,13},{10,... | collective-permute-start | bytes 786440 | tf_op jit(solution)/shard_map/ppermute | solution.py:372
  188.9 18.1 %collective-permute-start.44 = (bf16[64,2048]{1,0:T(8,128)(2,1)S(1)}, bf16[64,2048]{1,0:T(8,128)(2,1)S(1)}, u32[]{:S(2)}, u32[]{:S(2)}) collective-permute-start(bf16[64,2048]{1,0:T(8,128)(2,1)S(1)} %fusion.50.refs_0_), channel_id=1, source_target_pairs={{0,6},{1,7},{2,0},{3,1},{4,2},{5,3},{6,4},{7,5},{8,14},{9,15},{10,... | collective-permute-start | bytes 786440 | tf_op jit(solution)/shard_map/ppermute | solution.py:372
  195.7 12.8 %collective-permute-start.50 = (bf16[64,1024]{1,0:T(8,128)(2,1)S(1)}, bf16[64,1024]{1,0:T(8,128)(2,1)S(1)}, u32[]{:S(2)}, u32[]{:S(2)}) collective-permute-start(bf16[64,1024]{1,0:T(8,128)(2,1)S(1)} %collective-permute-done.49.refs_2_), channel_id=1, source_target_pairs={{0,16},{8,24},{16,0},{24,8},{1,17},{9,25},{17,1},{25,9},{2,18},{10... | collective-permute-start | bytes 393224 | tf_op jit(solution)/shard_map/ppermute | solution.py:369
  213.7 22.9 %collective-permute-start.35 = (bf16[64,2048]{1,0:T(8,128)(2,1)S(1)}, bf16[64,2048]{1,0:T(8,128)(2,1)S(1)}, u32[]{:S(2)}, u32[]{:S(2)}) collective-permute-start(bf16[64,2048]{1,0:T(8,128)(2,1)S(1)} %collective-permute-done.34.refs_2_), channel_id=1, source_target_pairs={{0,16},{8,24},{16,0},{24,8},{1,17},{9,25},{17,1},{25,9},{2,18},{10... | collective-permute-start | bytes 786440 | tf_op jit(solution)/shard_map/ppermute | solution.py:369
  220.2 13.9 %collective-permute-start.62 = (bf16[64,1024]{1,0:T(8,128)(2,1)S(1)}, bf16[64,1024]{1,0:T(8,128)(2,1)S(1)}, u32[]{:S(2)}, u32[]{:S(2)}) collective-permute-start(bf16[64,1024]{1,0:T(8,128)(2,1)S(1)} %collective-permute-done.61.refs_14_), channel_id=1, source_target_pairs={{0,16},{8,24},{16,0},{24,8},{1,17},{9,25},{17,1},{25,9},{2,18},{10... | collective-permute-start | bytes 393224 | tf_op jit(solution)/shard_map/ppermute | solution.py:369
  226.0 13.3 %collective-permute-start.37 = (bf16[64,2048]{1,0:T(8,128)(2,1)S(1)}, bf16[64,2048]{1,0:T(8,128)(2,1)S(1)}, u32[]{:S(2)}, u32[]{:S(2)}) collective-permute-start(bf16[64,2048]{1,0:T(8,128)(2,1)S(1)} %collective-permute-done.36.refs_4_), channel_id=1, source_target_pairs={{0,16},{8,24},{16,0},{24,8},{1,17},{9,25},{17,1},{25,9},{2,18},{10... | collective-permute-start | bytes 786440 | tf_op jit(solution)/shard_map/ppermute | solution.py:369
  239.3 30.0 %collective-permute-start.32 = (bf16[256,1024]{1,0:T(8,128)(2,1)}, bf16[256,1024]{1,0:T(8,128)(2,1)}, u32[]{:S(2)}, u32[]{:S(2)}) collective-permute-start(bf16[256,1024]{1,0:T(8,128)(2,1)} %multiply_convert_fusion.7), channel_id=1, source_target_pairs={{0,8},{8,0},{16,24},{24,16},{1,9},{9,1},{17,25},{25,17},{2,10},{10... | collective-permute-start | bytes 1572872 | tf_op jit(solution)/shard_map/ppermute | solution.py:726
  239.3 23.2 %collective-permute-start.45 = (bf16[64,2048]{1,0:T(8,128)(2,1)S(1)}, bf16[64,2048]{1,0:T(8,128)(2,1)}, u32[]{:S(2)}, u32[]{:S(2)}) collective-permute-start(bf16[64,2048]{1,0:T(8,128)(2,1)S(1)} %collective-permute-done.44.refs_12_), channel_id=1, source_target_pairs={{0,16},{8,24},{16,0},{24,8},{1,17},{9,25},{17,1},{25,9},{2,18},{10... | collective-permute-start | bytes 786440 | tf_op jit(solution)/shard_map/ppermute | solution.py:369
  243.5 20.7 %collective-permute-start.39 = (bf16[64,2048]{1,0:T(8,128)(2,1)}, bf16[64,2048]{1,0:T(8,128)(2,1)}, u32[]{:S(2)}, u32[]{:S(2)}) collective-permute-start(bf16[64,2048]{1,0:T(8,128)(2,1)} %collective-permute-done.38.refs_6_), channel_id=1, source_target_pairs={{0,16},{8,24},{16,0},{24,8},{1,17},{9,25},{17,1},{25,9},{2,18},{10... | collective-permute-start | bytes 786440 | tf_op jit(solution)/shard_map/ppermute | solution.py:369
  244.9 19.2 %collective-permute-start.43 = (bf16[64,2048]{1,0:T(8,128)(2,1)}, bf16[64,2048]{1,0:T(8,128)(2,1)}, u32[]{:S(2)}, u32[]{:S(2)}) collective-permute-start(bf16[64,2048]{1,0:T(8,128)(2,1)} %collective-permute-done.42.refs_10_), channel_id=1, source_target_pairs={{0,16},{8,24},{16,0},{24,8},{1,17},{9,25},{17,1},{25,9},{2,18},{10... | collective-permute-start | bytes 786440 | tf_op jit(solution)/shard_map/ppermute | solution.py:369
  246.9 18.5 %collective-permute-start.47 = (bf16[64,2048]{1,0:T(8,128)(2,1)}, bf16[64,2048]{1,0:T(8,128)(2,1)}, u32[]{:S(2)}, u32[]{:S(2)}) collective-permute-start(bf16[64,2048]{1,0:T(8,128)(2,1)} %collective-permute-done.46.refs_14_), channel_id=1, source_target_pairs={{0,16},{8,24},{16,0},{24,8},{1,17},{9,25},{17,1},{25,9},{2,18},{10... | collective-permute-start | bytes 786440 | tf_op jit(solution)/shard_map/ppermute | solution.py:369
  262.5 12.5 %collective-permute-start.65 = (f32[8,128]{1,0:T(8,128)S(1)}, f32[8,128]{1,0:T(8,128)S(1)}, u32[]{:S(2)}, u32[]{:S(2)}) collective-permute-start(f32[8,128]{1,0:T(8,128)S(1)} %broadcast_add_fusion), channel_id=1, source_target_pairs={{0,16},{8,24},{16,0},{24,8},{1,17},{9,25},{17,1},{25,9},{2,18},{10... | collective-permute-start | bytes 12296 | tf_op jit(solution)/shard_map/ppermute | solution.py:369
  274.9 16.9 %collective-permute-start.63 = (bf16[256,1024]{1,0:T(8,128)(2,1)S(1)}, bf16[256,1024]{1,0:T(8,128)(2,1)S(1)}, u32[]{:S(2)}, u32[]{:S(2)}) collective-permute-start(bf16[256,1024]{1,0:T(8,128)(2,1)S(1)} %slice.691), channel_id=1, source_target_pairs={{0,8},{8,0},{16,24},{24,16},{1,9},{9,1},{17,25},{25,17},{2,10},{10... | collective-permute-start | bytes 1572872 | tf_op jit(solution)/shard_map/ppermute | solution.py:732
  311.2 39.4 %collective-permute-start.111 = (bf16[8,64,1024]{2,1,0:T(8,128)(2,1)S(1)}, bf16[8,64,1024]{2,1,0:T(8,128)(2,1)S(1)}, u32[]{:S(2)}, u32[]{:S(2)}) collective-permute-start(bf16[8,64,1024]{2,1,0:T(8,128)(2,1)S(1)} %dynamic-slice_bitcast_fusion.2), channel_id=1, source_target_pairs={{0,16},{8,24},{16,0},{24,8},{1,17},{9,25},{17,1},{25,9},{2,18},{10... | collective-permute-start | bytes 3145736 | tf_op jit(solution)/shard_map/ppermute | solution.py:369
  317.1 30.9 %collective-permute-start.73 = (bf16[256,1024]{1,0:T(8,128)(2,1)S(1)}, bf16[256,1024]{1,0:T(8,128)(2,1)S(1)}, u32[]{:S(2)}, u32[]{:S(2)}) collective-permute-start(bf16[256,1024]{1,0:T(8,128)(2,1)S(1)} %get-tuple-element.159.refs_0_), channel_id=1, source_target_pairs={{0,16},{8,24},{16,0},{24,8},{1,17},{9,25},{17,1},{25,9},{2,18},{10... | collective-permute-start | bytes 1572872 | tf_op jit(solution)/shard_map/ppermute | solution.py:369
  323.8 30.6 %collective-permute-start.72 = (bf16[256,1024]{1,0:T(8,128)(2,1)S(1)}, bf16[256,1024]{1,0:T(8,128)(2,1)S(1)}, u32[]{:S(2)}, u32[]{:S(2)}) collective-permute-start(bf16[256,1024]{1,0:T(8,128)(2,1)S(1)} %get-tuple-element.159.refs_0_), channel_id=1, source_target_pairs={{0,8},{8,0},{16,24},{24,16},{1,9},{9,1},{17,25},{25,17},{2,10},{10... | collective-permute-start | bytes 1572872 | tf_op jit(solution)/shard_map/ppermute | solution.py:369
  349.4 157.9 %collective-permute-start.103 = (bf16[8,64,2048]{2,1,0:T(8,128)(2,1)}, bf16[8,64,2048]{2,1,0:T(8,128)(2,1)}, u32[]{:S(2)}, u32[]{:S(2)}) collective-permute-start(bf16[8,64,2048]{2,1,0:T(8,128)(2,1)} %dynamic-slice_bitcast_fusion), channel_id=1, source_target_pairs={{0,16},{8,24},{16,0},{24,8},{1,17},{9,25},{17,1},{25,9},{2,18},{10... | collective-permute-start | bytes 6291464 | tf_op jit(solution)/shard_map/ppermute | solution.py:369
  352.9 34.6 %collective-permute-start.112 = (bf16[4,64,1024]{2,1,0:T(8,128)(2,1)}, bf16[4,64,1024]{2,1,0:T(8,128)(2,1)}, u32[]{:S(2)}, u32[]{:S(2)}) collective-permute-start(bf16[4,64,1024]{2,1,0:T(8,128)(2,1)} %dynamic-slice_bitcast_fusion.4), channel_id=1, source_target_pairs={{0,1},{1,0},{2,3},{3,2},{4,5},{5,4},{6,7},{7,6},{8,9},{9,8},{10,11... | collective-permute-start | bytes 1572872 | tf_op jit(solution)/shard_map/ppermute | solution.py:369
  359.2 29.8 %collective-permute-start.75 = (f32[1024]{0:T(1024)}, f32[1024]{0:T(1024)}, u32[]{:S(2)}, u32[]{:S(2)}) collective-permute-start(f32[1024]{0:T(1024)} %get-tuple-element.131), channel_id=1, source_target_pairs={{0,8},{8,0},{16,24},{24,16},{1,9},{9,1},{17,25},{25,17},{2,10},{10... | collective-permute-start | bytes 12296 | tf_op jit(solution)/shard_map/ppermute | solution.py:369
  391.2 91.5 %collective-permute-start.115 = (bf16[64,1024]{1,0:T(8,128)(2,1)}, bf16[64,1024]{1,0:T(8,128)(2,1)}, u32[]{:S(2)}, u32[]{:S(2)}) collective-permute-start(bf16[64,1024]{1,0:T(8,128)(2,1)} %get-tuple-element.213), channel_id=1, source_target_pairs={{0,6},{1,7},{2,0},{3,1},{4,2},{5,3},{6,4},{7,5},{8,14},{9,15},{10,... | collective-permute-start | bytes 393224 | tf_op jit(solution)/shard_map/ppermute | solution.py:372
  394.1 90.1 %collective-permute-start.114 = (bf16[64,1024]{1,0:T(8,128)(2,1)}, bf16[64,1024]{1,0:T(8,128)(2,1)}, u32[]{:S(2)}, u32[]{:S(2)}) collective-permute-start(bf16[64,1024]{1,0:T(8,128)(2,1)} %get-tuple-element.214), channel_id=1, source_target_pairs={{0,4},{1,5},{2,6},{3,7},{4,0},{5,1},{6,2},{7,3},{8,12},{9,13},{10,... | collective-permute-start | bytes 393224 | tf_op jit(solution)/shard_map/ppermute | solution.py:372
  394.1 90.8 %collective-permute-start.113 = (bf16[64,1024]{1,0:T(8,128)(2,1)}, bf16[64,1024]{1,0:T(8,128)(2,1)}, u32[]{:S(2)}, u32[]{:S(2)}) collective-permute-start(bf16[64,1024]{1,0:T(8,128)(2,1)} %get-tuple-element.212), channel_id=1, source_target_pairs={{0,2},{1,3},{2,4},{3,5},{4,6},{5,7},{6,0},{7,1},{8,10},{9,11},{10,... | collective-permute-start | bytes 393224 | tf_op jit(solution)/shard_map/ppermute | solution.py:372
  476.3 24.1 %collective-permute-start.93 = (bf16[2,256,256]{2,1,0:T(8,128)(2,1)}, bf16[2,256,256]{2,1,0:T(8,128)(2,1)}, u32[]{:S(2)}, u32[]{:S(2)}) collective-permute-start(bf16[2,256,256]{2,1,0:T(8,128)(2,1)} %get-tuple-element.198), channel_id=1, source_target_pairs={{0,8},{8,0},{16,24},{24,16},{1,9},{9,1},{17,25},{25,17},{2,10},{10... | collective-permute-start | bytes 786440 | tf_op jit(solution)/shard_map/ppermute | solution.py:369
  482.7 18.8 %collective-permute-start.94 = (bf16[2,256,256]{2,1,0:T(8,128)(2,1)}, bf16[2,256,256]{2,1,0:T(8,128)(2,1)S(1)}, u32[]{:S(2)}, u32[]{:S(2)}) collective-permute-start(bf16[2,256,256]{2,1,0:T(8,128)(2,1)} %get-tuple-element.199), channel_id=1, source_target_pairs={{0,16},{8,24},{16,0},{24,8},{1,17},{9,25},{17,1},{25,9},{2,18},{10... | collective-permute-start | bytes 786440 | tf_op jit(solution)/shard_map/ppermute | solution.py:369
  484.2 17.5 %collective-permute-start.95 = (bf16[2,256,256]{2,1,0:T(8,128)(2,1)}, bf16[2,256,256]{2,1,0:T(8,128)(2,1)S(1)}, u32[]{:S(2)}, u32[]{:S(2)}) collective-permute-start(bf16[2,256,256]{2,1,0:T(8,128)(2,1)} %get-tuple-element.196), channel_id=1, source_target_pairs={{0,24},{8,16},{16,8},{24,0},{1,25},{9,17},{17,9},{25,1},{2,26},{10... | collective-permute-start | bytes 786440 | tf_op jit(solution)/shard_map/ppermute | solution.py:369
  486.0 14.3 %collective-permute-start.117 = (bf16[64,1024]{1,0:T(8,128)(2,1)S(1)}, bf16[64,1024]{1,0:T(8,128)(2,1)S(1)}, u32[]{:S(2)}, u32[]{:S(2)}) collective-permute-start(bf16[64,1024]{1,0:T(8,128)(2,1)S(1)} %fusion.61.refs_0_), channel_id=1, source_target_pairs={{0,16},{8,24},{16,0},{24,8},{1,17},{9,25},{17,1},{25,9},{2,18},{10... | collective-permute-start | bytes 393224 | tf_op jit(solution)/shard_map/ppermute | solution.py:369
  501.7 31.3 %collective-permute-start.77 = (bf16[256,1024]{1,0:T(8,128)(2,1)}, bf16[256,1024]{1,0:T(8,128)(2,1)S(1)}, u32[]{:S(2)}, u32[]{:S(2)}) collective-permute-start(bf16[256,1024]{1,0:T(8,128)(2,1)} %get-tuple-element.172), channel_id=1, source_target_pairs={{0,8},{8,0},{16,24},{24,16},{1,9},{9,1},{17,25},{25,17},{2,10},{10... | collective-permute-start | bytes 1572872 | tf_op jit(solution)/shard_map/ppermute | solution.py:369
  503.9 14.0 %collective-permute-start.96 = (bf16[4,256,256]{2,1,0:T(8,128)(2,1)S(1)}, bf16[4,256,256]{2,1,0:T(8,128)(2,1)S(1)}, u32[]{:S(2)}, u32[]{:S(2)}) collective-permute-start(bf16[4,256,256]{2,1,0:T(8,128)(2,1)S(1)} %dynamic-slice_bitcast_fusion.5), channel_id=1, source_target_pairs={{0,1},{1,0},{2,3},{3,2},{4,5},{5,4},{6,7},{7,6},{8,9},{9,8},{10,11... | collective-permute-start | bytes 1572872 | tf_op jit(solution)/shard_map/ppermute | solution.py:369
  510.8 22.1 %collective-permute-start.79 = (bf16[256,1024]{1,0:T(8,128)(2,1)S(1)}, bf16[256,1024]{1,0:T(8,128)(2,1)S(1)}, u32[]{:S(2)}, u32[]{:S(2)}) collective-permute-start(bf16[256,1024]{1,0:T(8,128)(2,1)S(1)} %fusion.19), channel_id=1, source_target_pairs={{0,16},{8,24},{16,0},{24,8},{1,17},{9,25},{17,1},{25,9},{2,18},{10... | collective-permute-start | bytes 1572872 | tf_op jit(solution)/shard_map/ppermute | solution.py:369
  525.0 46.4 %collective-permute-start.86 = (bf16[4,128,1280]{2,1,0:T(8,128)(2,1)}, bf16[4,128,1280]{2,1,0:T(8,128)(2,1)}, u32[]{:S(2)}, u32[]{:S(2)}) collective-permute-start(bf16[4,128,1280]{2,1,0:T(8,128)(2,1)} %dynamic-slice_bitcast_fusion.1), channel_id=1, source_target_pairs={{0,1},{1,0},{2,3},{3,2},{4,5},{5,4},{6,7},{7,6},{8,9},{9,8},{10,11... | collective-permute-start | bytes 3932168 | tf_op jit(solution)/shard_map/ppermute | solution.py:369
  531.7 31.4 %collective-permute-start.101 = (bf16[256,256]{1,0:T(8,128)(2,1)S(1)}, bf16[256,256]{1,0:T(8,128)(2,1)S(1)}, u32[]{:S(2)}, u32[]{:S(2)}) collective-permute-start(bf16[256,256]{1,0:T(8,128)(2,1)S(1)} %fusion.64.refs_0_), channel_id=1, source_target_pairs={{0,16},{8,24},{16,0},{24,8},{1,17},{9,25},{17,1},{25,9},{2,18},{10... | collective-permute-start | bytes 393224 | tf_op jit(solution)/shard_map/ppermute | solution.py:369
  534.8 20.2 %collective-permute-start.80 = (f32[4,48,128]{2,1,0:T(8,128)S(1)}, f32[4,48,128]{2,1,0:T(8,128)S(1)}, u32[]{:S(2)}, u32[]{:S(2)}) collective-permute-start(f32[4,48,128]{2,1,0:T(8,128)S(1)} %dynamic-slice_bitcast_fusion.22), channel_id=1, source_target_pairs={{0,1},{1,0},{2,3},{3,2},{4,5},{5,4},{6,7},{7,6},{8,9},{9,8},{10,11... | collective-permute-start | bytes 294920 | tf_op jit(solution)/shard_map/ppermute | solution.py:369
  563.1 21.2 %collective-permute-start.104 = (bf16[4,64,2048]{2,1,0:T(8,128)(2,1)}, bf16[4,64,2048]{2,1,0:T(8,128)(2,1)S(1)}, u32[]{:S(2)}, u32[]{:S(2)}) collective-permute-start(bf16[4,64,2048]{2,1,0:T(8,128)(2,1)} %dynamic-slice_bitcast_fusion.3), channel_id=1, source_target_pairs={{0,1},{1,0},{2,3},{3,2},{4,5},{5,4},{6,7},{7,6},{8,9},{9,8},{10,11... | collective-permute-start | bytes 3145736 | tf_op jit(solution)/shard_map/ppermute | solution.py:369
  573.2 15.2 %collective-permute-start.89 = (bf16[128,1280]{1,0:T(8,128)(2,1)S(1)}, bf16[128,1280]{1,0:T(8,128)(2,1)S(1)}, u32[]{:S(2)}, u32[]{:S(2)}) collective-permute-start(bf16[128,1280]{1,0:T(8,128)(2,1)S(1)} %get-tuple-element.191), channel_id=1, source_target_pairs={{0,6},{1,7},{2,0},{3,1},{4,2},{5,3},{6,4},{7,5},{8,14},{9,15},{10,... | collective-permute-start | bytes 983048 | tf_op jit(solution)/shard_map/ppermute | solution.py:372
  576.5 42.0 %collective-permute-start.88 = (bf16[128,1280]{1,0:T(8,128)(2,1)S(1)}, bf16[128,1280]{1,0:T(8,128)(2,1)S(1)}, u32[]{:S(2)}, u32[]{:S(2)}) collective-permute-start(bf16[128,1280]{1,0:T(8,128)(2,1)S(1)} %get-tuple-element.192), channel_id=1, source_target_pairs={{0,4},{1,5},{2,6},{3,7},{4,0},{5,1},{6,2},{7,3},{8,12},{9,13},{10,... | collective-permute-start | bytes 983048 | tf_op jit(solution)/shard_map/ppermute | solution.py:372
  577.7 40.9 %collective-permute-start.87 = (bf16[128,1280]{1,0:T(8,128)(2,1)S(1)}, bf16[128,1280]{1,0:T(8,128)(2,1)S(1)}, u32[]{:S(2)}, u32[]{:S(2)}) collective-permute-start(bf16[128,1280]{1,0:T(8,128)(2,1)S(1)} %get-tuple-element.190), channel_id=1, source_target_pairs={{0,2},{1,3},{2,4},{3,5},{4,6},{5,7},{6,0},{7,1},{8,10},{9,11},{10,... | collective-permute-start | bytes 983048 | tf_op jit(solution)/shard_map/ppermute | solution.py:372
  584.7 35.4 %collective-permute-start.107 = (bf16[64,2048]{1,0:T(8,128)(2,1)S(1)}, bf16[64,2048]{1,0:T(8,128)(2,1)S(1)}, u32[]{:S(2)}, u32[]{:S(2)}) collective-permute-start(bf16[64,2048]{1,0:T(8,128)(2,1)S(1)} %get-tuple-element.194), channel_id=1, source_target_pairs={{0,6},{1,7},{2,0},{3,1},{4,2},{5,3},{6,4},{7,5},{8,14},{9,15},{10,... | collective-permute-start | bytes 786440 | tf_op jit(solution)/shard_map/ppermute | solution.py:372
  588.3 40.0 %collective-permute-start.106 = (bf16[64,2048]{1,0:T(8,128)(2,1)S(1)}, bf16[64,2048]{1,0:T(8,128)(2,1)S(1)}, u32[]{:S(2)}, u32[]{:S(2)}) collective-permute-start(bf16[64,2048]{1,0:T(8,128)(2,1)S(1)} %get-tuple-element.195), channel_id=1, source_target_pairs={{0,4},{1,5},{2,6},{3,7},{4,0},{5,1},{6,2},{7,3},{8,12},{9,13},{10,... | collective-permute-start | bytes 786440 | tf_op jit(solution)/shard_map/ppermute | solution.py:372
  588.4 39.9 %collective-permute-start.105 = (bf16[64,2048]{1,0:T(8,128)(2,1)S(1)}, bf16[64,2048]{1,0:T(8,128)(2,1)S(1)}, u32[]{:S(2)}, u32[]{:S(2)}) collective-permute-start(bf16[64,2048]{1,0:T(8,128)(2,1)S(1)} %get-tuple-element.193), channel_id=1, source_target_pairs={{0,2},{1,3},{2,4},{3,5},{4,6},{5,7},{6,0},{7,1},{8,10},{9,11},{10,... | collective-permute-start | bytes 786440 | tf_op jit(solution)/shard_map/ppermute | solution.py:372
  618.8 16.6 %collective-permute-start.90 = (bf16[128,1280]{1,0:T(8,128)(2,1)S(1)}, bf16[128,1280]{1,0:T(8,128)(2,1)S(1)}, u32[]{:S(2)}, u32[]{:S(2)}) collective-permute-start(bf16[128,1280]{1,0:T(8,128)(2,1)S(1)} %fusion.31.refs_0_), channel_id=1, source_target_pairs={{0,8},{8,0},{16,24},{24,16},{1,9},{9,1},{17,25},{25,17},{2,10},{10... | collective-permute-start | bytes 983048 | tf_op jit(solution)/shard_map/ppermute | solution.py:369
  (245 other events, 2039.7 us)

commit v2 on v1

v2 whole, which is shorter than its diff:
```python
import functools

import jax
import jax.numpy as jnp
import numpy as np
from jax import lax
from jax.experimental import pallas as pl
from jax.experimental.pallas import tpu as pltpu
from jax.sharding import PartitionSpec as P

MH = 24
HP = 64
NS = 128
KW = 4
QH = 8
KVH = 2
HD = 64
SPAN = 128
QBLK = 256

EPSILON = 1e-05
ROPE_BASE = 100000000000.0
MASKED = -1e30

F32 = jnp.float32
BF16 = jnp.bfloat16
HIGH = lax.Precision.HIGHEST


def nn(left, right, precision=None):
    return lax.dot_general(
        left, right, (((1,), (0,)), ((), ())), precision=precision, preferred_element_type=F32
    )


def nt(left, right):
    return lax.dot_general(left, right, (((1,), (1,)), ((), ())), preferred_element_type=F32)


def tn(left, right):
    return lax.dot_general(left, right, (((0,), (0,)), ((), ())), preferred_element_type=F32)


def swap_halves(values):
    lane = lax.broadcasted_iota(jnp.int32, values.shape, 1) % HD
    size = values.shape[1]
    return jnp.where(
        lane < HD // 2,
        pltpu.roll(values, size - HD // 2, 1),
        pltpu.roll(values, HD // 2, 1),
    )


def conv_kernel(
    tok, gain, weight, taps, bias, same, params, normed_ref, cin_ref, pre_ref, act_ref, step_ref,
    row_ref, halo,
):
    conv = taps.shape[1]
    block = tok.shape[0]

    @pl.when(pl.program_id(0) == 0)
    def _():
        halo[...] = jnp.zeros_like(halo)

    values = tok[...].astype(F32)
    scale = lax.rsqrt(jnp.mean(values * values, axis=-1, keepdims=True) + EPSILON)
    normed = (values * scale * gain[...]).astype(BF16)
    normed_ref[...] = normed
    cin = nn(normed, weight[:, :conv])
    cin_ref[...] = cin.astype(BF16)
    halo[8 : 8 + block, :] = cin
    pre = bias[...] + taps[KW - 1 : KW, :] * cin
    for by in range(1, KW):
        tap = taps[KW - 1 - by : KW - by, :]
        pre = pre + tap * halo[8 - by : 8 - by + block, :] * same[:, by : by + 1]
    halo[0:8, :] = halo[block : block + 8, :]
    pre_ref[...] = pre.astype(BF16)
    act_ref[...] = (pre * jax.nn.sigmoid(pre)).astype(BF16)
    raw = nn(normed, weight[:, conv:]) + params[0:1, :]
    dt = jnp.maximum(raw, 0.0) + jnp.log1p(jnp.exp(-jnp.abs(raw)))
    loga = -dt * params[1:2, :]
    step_ref[:, :128] = dt
    step_ref[:, 128:] = loga
    row_ref[0:8, :] = jnp.transpose(dt)[0:8, :]
    row_ref[8:16, :] = jnp.transpose(loga)[0:8, :]


def by_rows(size):
    return pl.BlockSpec((QBLK, size), lambda i: (i, 0))


def whole(a):
    return pl.BlockSpec(a.shape, lambda i: (0, 0))


def project_conv(tokens, gain, weight, taps, bias, same, params):
    length, dim = tokens.shape
    conv = taps.shape[1]
    sizes = [(dim, BF16), (conv, BF16), (conv, BF16), (conv, BF16), (256, F32)]
    return pl.pallas_call(
        conv_kernel,
        grid=(length // QBLK,),
        in_specs=[
            by_rows(dim),
            whole(gain),
            whole(weight),
            whole(taps),
            whole(bias),
            by_rows(same.shape[1]),
            whole(params),
        ],
        out_specs=[by_rows(size) for size, _ in sizes]
        + [pl.BlockSpec((16, QBLK), lambda i: (0, i))],
        out_shape=[jax.ShapeDtypeStruct((length, size), kind) for size, kind in sizes]
        + [jax.ShapeDtypeStruct((16, length), F32)],
        scratch_shapes=[pltpu.VMEM((QBLK + 8, conv), F32)],
        compiler_params=pltpu.CompilerParams(vmem_limit_bytes=40 * 1024 * 1024),
        cost_estimate=pl.CostEstimate(
            flops=2 * length * dim * weight.shape[1], bytes_accessed=10**7, transcendentals=10**6
        ),
        name="project_conv",
    )(tokens, gain, weight, taps, bias, same, params)


def gate_kernel(normed_ref, weight, y_ref, cosine, sine, z_ref, qkv_ref, sq_ref):
    width = y_ref.shape[1]
    normed = normed_ref[...]
    gate = nn(normed, weight[:, :width])
    z_ref[...] = gate
    qkv = nn(normed, weight[:, width:])
    qkv_ref[...] = (qkv * cosine[...] + swap_halves(qkv) * sine[...]).astype(BF16)
    gated = y_ref[...] * (gate * jax.nn.sigmoid(gate))
    sq_ref[...] = lax.dot_general(
        jnp.ones((8, width), F32),
        gated * gated,
        (((1,), (1,)), ((), ())),
        precision=HIGH,
        preferred_element_type=F32,
    )


def project_gate(normed, weight, y, cosine, sine):
    length, dim = normed.shape
    width = y.shape[1]
    slab = cosine.shape[1]
    return pl.pallas_call(
        gate_kernel,
        grid=(length // QBLK,),
        in_specs=[by_rows(dim), whole(weight), by_rows(width), by_rows(slab), by_rows(slab)],
        out_specs=[
            by_rows(width),
            by_rows(slab),
            pl.BlockSpec((8, QBLK), lambda i: (0, i)),
        ],
        out_shape=[
            jax.ShapeDtypeStruct((length, width), F32),
            jax.ShapeDtypeStruct((length, slab), BF16),
            jax.ShapeDtypeStruct((8, length), F32),
        ],
        compiler_params=pltpu.CompilerParams(vmem_limit_bytes=40 * 1024 * 1024),
        cost_estimate=pl.CostEstimate(
            flops=2 * length * dim * weight.shape[1], bytes_accessed=10**7, transcendentals=10**6
        ),
        name="project_gate",
    )(normed, weight, y, cosine, sine)


def decays(seg_c, seg_r, loga_c, loga_r, before, end):
    row = lax.broadcasted_iota(jnp.int32, (SPAN, SPAN), 0)
    col = lax.broadcasted_iota(jnp.int32, (SPAN, SPAN), 1)
    lower = row >= col
    same = (seg_c == seg_r) & lower
    run_c = nn(lower.astype(F32), loga_c, HIGH)
    run_r = nn(loga_r, (row <= col).astype(F32), HIGH)
    keep = (seg_c == before).astype(F32)
    tail = (seg_c == end).astype(F32)
    return row, col, same, run_c, run_r, keep, tail


def ssm_fwd_kernel(
    heads, ends, skip, act, steps, rows, seg_c, seg_r, y_ref, st_ref, state
):
    step = pl.program_id(0)

    @pl.when(step == 0)
    def _():
        state[...] = jnp.zeros_like(state)

    before, end = ends[step], ends[step + 1]
    link = (before == end).astype(F32)
    _, _, same, run_c, run_r, keep, tail = decays(
        seg_c[...], seg_r[...], steps[:, 128:], rows[8:16, :], before, end
    )
    width = heads * HP
    b_in = act[:, width : width + NS]
    c_in = act[:, width + NS : width + 2 * NS]
    gram = nt(c_in, b_in)
    for h in range(heads):
        lanes = slice(h * HP, (h + 1) * HP)
        x_in = act[:, lanes]
        own_c = run_c[:, h : h + 1]
        last = own_c[SPAN - 1 :, :]
        decay = jnp.where(same, jnp.exp(own_c - run_r[h : h + 1, :]), 0.0)
        mixing = (gram * decay * rows[h : h + 1, :]).astype(BF16)
        prior = state[h]
        st_ref[0, h] = prior
        x_wide = x_in.astype(F32)
        y_out = nn(mixing, x_in) + nt(c_in, prior.astype(BF16)) * (jnp.exp(own_c) * keep)
        y_ref[:, lanes] = y_out + skip[h] * x_wide
        weight = jnp.exp(last - own_c) * tail * steps[:, h : h + 1]
        state[h] = (jnp.exp(last) * link) * prior + tn((x_wide * weight).astype(BF16), b_in)


def ssm_bwd_kernel(
    heads,
    ends,
    skip,
    act,
    steps,
    rows,
    seg_c,
    seg_r,
    st_ref,
    z_ref,
    gym_ref,
    y_ref,
    stat_ref,
    gain_ref,
    pre_ref,
    cin_ref,
    up_ref,
    taps,
    params,
    first_ref,
    gconv_ref,
    gwide_ref,
    gstep_ref,
    gstate,
    gbuf,
    gcol,
    grow,
):
    step = pl.num_programs(0) - 1 - pl.program_id(0)
    width = heads * HP
    conv = width + 2 * NS

    @pl.when(pl.program_id(0) == 0)
    def _():
        gstate[...] = jnp.zeros_like(gstate)
        gbuf[...] = jnp.zeros_like(gbuf)
        gcol[...] = jnp.zeros_like(gcol)
        grow[...] = jnp.zeros_like(grow)
        gconv_ref[...] = jnp.zeros_like(gconv_ref)
        gwide_ref[...] = jnp.zeros_like(gwide_ref)
        gstep_ref[...] = jnp.zeros_like(gstep_ref)

    before, end = ends[step], ends[step + 1]
    link = (before == end).astype(F32)
    row, col, same, run_c, run_r, keep, tail = decays(
        seg_c[...], seg_r[...], steps[:, 128:], rows[8:16, :], before, end
    )
    gate = z_ref[...]
    sig = jax.nn.sigmoid(gate)
    silu = gate * sig
    y_all = y_ref[...]
    gated = y_all * silu
    scale = stat_ref[:, 0:1]
    g_ym = gym_ref[...]
    g_gated = scale * (g_ym * gain_ref[...]) - gated * stat_ref[:, 1:2]
    g_all = g_gated * silu
    gwide_ref[0:1, :] += jnp.sum(g_all * act[:, :width].astype(F32), axis=0, keepdims=True)

    b_in = act[:, width : width + NS]
    c_in = act[:, width + NS : width + 2 * NS]
    gram = nt(c_in, b_in)
    g_gram = jnp.zeros((SPAN, SPAN), F32)
    g_b = jnp.zeros((SPAN, NS), F32)
    g_c = jnp.zeros((SPAN, NS), F32)
    at_last = lax.broadcasted_iota(jnp.int32, (SPAN, 1), 0) == SPAN - 1
    for h in range(heads):
        lanes = slice(h * HP, (h + 1) * HP)
        x_in = act[:, lanes]
        x_wide = x_in.astype(F32)
        gy = g_all[:, lanes]
        gy_low = gy.astype(BF16)
        own_c = run_c[:, h : h + 1]
        last = own_c[SPAN - 1 :, :]
        dt_row = rows[h : h + 1, :]
        decay = jnp.where(same, jnp.exp(own_c - run_r[h : h + 1, :]), 0.0)
        prior = st_ref[0, h]
        prior_low = prior.astype(BF16)
        after = gstate[h]
        after_low = after.astype(BF16)
        carry_w = jnp.exp(own_c) * keep
        tail_w = jnp.exp(last - own_c) * tail
        end_w = tail_w * steps[:, h : h + 1]
        mixing = (gram * decay * dt_row).astype(BF16)
        g_mix = nt(gy_low, x_in) * decay
        g_gram_h = g_mix * dt_row
        g_gram = g_gram + g_gram_h
        inner = g_gram_h * gram
        from_state = nt(b_in, after_low)
        gbuf[0:SPAN, lanes] = tn(mixing, gy_low) + from_state * end_w + skip[h] * gy
        g_carry = jnp.sum(gy * nt(c_in, prior_low), axis=1, keepdims=True)
        g_tail = jnp.sum(x_wide * from_state, axis=1, keepdims=True)
        g_link = jnp.exp(last) * link
        total_last = jnp.sum(g_tail * end_w, axis=0, keepdims=True) + g_link * jnp.sum(
            jnp.sum(after * prior, axis=1, keepdims=True), axis=0, keepdims=True
        )
        g_run_c = jnp.sum(inner, axis=1, keepdims=True) + g_carry * carry_w - g_tail * end_w
        gcol[:, h : h + 1] = g_run_c + jnp.where(at_last, total_last, 0.0)
        gcol[:, 128 + h : 128 + h + 1] = g_tail * tail_w
        grow[h : h + 1, :] = jnp.sum(inner, axis=0, keepdims=True)
        grow[128 + h : 128 + h + 1, :] = jnp.sum(g_mix * gram, axis=0, keepdims=True)
        weighted = (gy * carry_w).astype(BF16)
        g_c = g_c + nn(weighted, prior_low)
        g_b = g_b + nn((x_wide * end_w).astype(BF16), after_low)
        gstate[h] = g_link * after + tn(weighted, c_in)
    g_gram_low = g_gram.astype(BF16)
    gbuf[0:SPAN, width : width + NS] = g_b + tn(g_gram_low, c_in)
    gbuf[0:SPAN, width + NS :] = g_c + nn(g_gram_low, b_in)

    pre = pre_ref[...].astype(F32)
    sig = jax.nn.sigmoid(pre)
    g_pre = gbuf[0:SPAN, :] * (sig + pre * sig * (1.0 - sig))
    gbuf[0:SPAN, :] = g_pre
    cin = cin_ref[...].astype(F32)
    g_conv = taps[KW - 1 : KW, :] * g_pre
    gconv_ref[KW - 1 : KW, :] += jnp.sum(g_pre * cin, axis=0, keepdims=True)
    gconv_ref[KW : KW + 1, :] += jnp.sum(g_pre, axis=0, keepdims=True)
    for by in range(1, KW):
        ahead = gbuf[by : by + SPAN, :] * up_ref[:, by : by + 1]
        tap = KW - 1 - by
        g_conv = g_conv + taps[tap : tap + 1, :] * ahead
        gconv_ref[tap : tap + 1, :] += jnp.sum(ahead * cin, axis=0, keepdims=True)
    gbuf[SPAN : SPAN + 8, :] = gbuf[0:8, :]
    first_ref[:, :conv] = g_conv.astype(BF16)

    later = (col >= row).astype(F32)
    eye = (col == row).astype(F32)

    def across(left, right):
        return lax.dot_general(
            left, right, (((1,), (1,)), ((), ())), precision=HIGH, preferred_element_type=F32
        )

    g_loga = nn(later, gcol[:, :128], HIGH) - across(later, grow[:128, :])
    g_dt = gcol[:, 128:] + across(eye, grow[128:, :]) - g_loga * params[1:2, :]
    g_step = g_dt * (1.0 - jnp.exp(-steps[:, :128]))
    first_ref[:, conv:] = g_step.astype(BF16)
    gstep_ref[0:1, :] += jnp.sum(g_step, axis=0, keepdims=True)
    gstep_ref[1:2, :] += jnp.sum(g_loga * steps[:, 128:], axis=0, keepdims=True)


def ssm_specs(heads, at):
    width = heads * HP
    return [
        pl.BlockSpec(memory_space=pltpu.SMEM),
        pl.BlockSpec(memory_space=pltpu.SMEM),
        pl.BlockSpec((SPAN, width + 2 * NS), lambda i: (at(i), 0)),
        pl.BlockSpec((SPAN, 256), lambda i: (at(i), 0)),
        pl.BlockSpec((16, SPAN), lambda i: (0, at(i))),
        pl.BlockSpec((SPAN, 1), lambda i: (at(i), 0)),
        pl.BlockSpec((1, SPAN), lambda i: (0, at(i))),
    ]


def ssm_forward(heads, inputs):
    length = inputs[2].shape[0]
    steps = length // SPAN
    width = heads * HP
    return pl.pallas_call(
        functools.partial(ssm_fwd_kernel, heads),
        grid=(steps,),
        in_specs=ssm_specs(heads, lambda i: i),
        out_specs=[
            pl.BlockSpec((SPAN, width), lambda i: (i, 0)),
            pl.BlockSpec((1, heads, HP, NS), lambda i: (i, 0, 0, 0)),
        ],
        out_shape=[
            jax.ShapeDtypeStruct((length, width), F32),
            jax.ShapeDtypeStruct((steps, heads, HP, NS), F32),
        ],
        scratch_shapes=[pltpu.VMEM((heads, HP, NS), F32)],
        compiler_params=pltpu.CompilerParams(vmem_limit_bytes=32 * 1024 * 1024),
        cost_estimate=pl.CostEstimate(
            flops=10**9, bytes_accessed=4 * 10**7, transcendentals=10**6
        ),
        name="ssm_forward",
    )(*inputs)


def ssm_backward(heads, inputs, states, gate_z, g_ym, ssm_y, stats, gain, pre, cin, up, taps, params):
    length = inputs[2].shape[0]
    steps = length // SPAN
    width = heads * HP
    conv = width + 2 * NS
    total = conv + 128

    def at(i):
        return steps - 1 - i

    def part(size):
        return pl.BlockSpec((SPAN, size), lambda i: (at(i), 0))

    def fixed(shape):
        return pl.BlockSpec(shape, lambda i: (0, 0))

    return pl.pallas_call(
        functools.partial(ssm_bwd_kernel, heads),
        grid=(steps,),
        in_specs=ssm_specs(heads, at)
        + [
            pl.BlockSpec((1, heads, HP, NS), lambda i: (at(i), 0, 0, 0)),
            part(width),
            part(width),
            part(width),
            part(stats.shape[1]),
            fixed(gain.shape),
            part(conv),
            part(conv),
            part(up.shape[1]),
            fixed(taps.shape),
            fixed(params.shape),
        ],
        out_specs=[part(total), fixed((8, conv)), fixed((8, width)), fixed((8, 128))],
        out_shape=[
            jax.ShapeDtypeStruct((length, total), BF16),
            jax.ShapeDtypeStruct((8, conv), F32),
            jax.ShapeDtypeStruct((8, width), F32),
            jax.ShapeDtypeStruct((8, 128), F32),
        ],
        scratch_shapes=[
            pltpu.VMEM((heads, HP, NS), F32),
            pltpu.VMEM((SPAN + 8, conv), F32),
            pltpu.VMEM((SPAN, 256), F32),
            pltpu.VMEM((256, SPAN), F32),
        ],
        compiler_params=pltpu.CompilerParams(vmem_limit_bytes=56 * 1024 * 1024),
        cost_estimate=pl.CostEstimate(
            flops=3 * 10**9, bytes_accessed=10**8, transcendentals=10**6
        ),
        name="ssm_backward",
    )(*inputs, states, gate_z, g_ym, ssm_y, stats, gain, pre, cin, up, taps, params)


def allowed_keys(index, reach, seg_c, seg_r):
    row = lax.broadcasted_iota(jnp.int32, (QBLK, reach), 0) + index * QBLK
    col = lax.broadcasted_iota(jnp.int32, (QBLK, reach), 1)
    return (seg_c[...] == seg_r[:, :reach]) & (col <= row)


def attn_fwd_kernel(heads, blocks, qkv_ref, seg_c, seg_r, out_ref, lse_ref):
    wide = heads * HD
    for index in range(blocks):

        @pl.when(pl.program_id(0) == index)
        def _(index=index):
            reach = (index + 1) * QBLK
            allowed = allowed_keys(index, reach, seg_c, seg_r)
            own = slice(index * QBLK, reach)
            keys = qkv_ref[:reach, wide : wide + HD]
            values = qkv_ref[:reach, wide + HD : wide + 2 * HD]
            for h in range(heads):
                lanes = slice(h * HD, (h + 1) * HD)
                scores = nt(qkv_ref[own, lanes], keys) * (HD**-0.5)
                scores = jnp.where(allowed, scores, MASKED)
                top = jnp.max(scores, axis=1, keepdims=True)
                expo = jnp.exp(scores - top)
                total = jnp.sum(expo, axis=1, keepdims=True)
                probs = (expo * (1.0 / total)).astype(BF16)
                out_ref[:, lanes] = nn(probs, values).astype(BF16)
                lse_ref[:, h : h + 1] = top + jnp.log(total)


def attn_bwd_kernel(
    heads, blocks, qkv_ref, seg_c, seg_r, lse_ref, go_ref, cosine, sine, out_ref, grads
):
    wide = heads * HD

    @pl.when(pl.program_id(0) == 0)
    def _():
        grads[...] = jnp.zeros_like(grads)

    for index in range(blocks):

        @pl.when(pl.program_id(0) == index)
        def _(index=index):
            reach = (index + 1) * QBLK
            allowed = allowed_keys(index, reach, seg_c, seg_r)
            own = slice(index * QBLK, reach)
            keys = qkv_ref[:reach, wide : wide + HD]
            values = qkv_ref[:reach, wide + HD : wide + 2 * HD]
            for h in range(heads):
                lanes = slice(h * HD, (h + 1) * HD)
                query = qkv_ref[own, lanes]
                g_out = go_ref[:, lanes]
                scores = nt(query, keys) * (HD**-0.5)
                probs = jnp.where(allowed, jnp.exp(scores - lse_ref[:, h : h + 1]), 0.0)
                g_probs = nt(g_out, values)
                delta = jnp.sum(probs * g_probs, axis=1, keepdims=True)
                g_scores = (probs * (g_probs - delta)).astype(BF16)
                grads[own, lanes] = nn(g_scores, keys) * (HD**-0.5)
                grads[:reach, wide : wide + HD] += tn(g_scores, query) * (HD**-0.5)
                grads[:reach, wide + HD : wide + 2 * HD] += tn(probs.astype(BF16), g_out)
            if index == blocks - 1:
                for b in range(blocks):
                    part = slice(b * QBLK, (b + 1) * QBLK)
                    slab = grads[part, :]
                    out_ref[part, :] = (
                        slab * cosine[part, :] - swap_halves(slab) * sine[part, :]
                    ).astype(BF16)


def attn_specs(length, slab):
    return [
        pl.BlockSpec((length, slab), lambda i: (0, 0)),
        pl.BlockSpec((QBLK, 1), lambda i: (i, 0)),
        pl.BlockSpec((1, length), lambda i: (0, 0)),
    ]


def attn_forward(heads, inputs):
    length, slab = inputs[0].shape
    blocks = length // QBLK
    return pl.pallas_call(
        functools.partial(attn_fwd_kernel, heads, blocks),
        grid=(blocks,),
        in_specs=attn_specs(length, slab),
        out_specs=[
            pl.BlockSpec((QBLK, heads * HD), lambda i: (i, 0)),
            pl.BlockSpec((QBLK, heads), lambda i: (i, 0)),
        ],
        out_shape=[
            jax.ShapeDtypeStruct((length, heads * HD), BF16),
            jax.ShapeDtypeStruct((length, heads), F32),
        ],
        compiler_params=pltpu.CompilerParams(vmem_limit_bytes=32 * 1024 * 1024),
        cost_estimate=pl.CostEstimate(
            flops=10**9, bytes_accessed=2 * 10**7, transcendentals=10**6
        ),
        name="attn_forward",
    )(*inputs)


def attn_backward(heads, inputs, lse, g_out, cosine, sine):
    length, slab = inputs[0].shape
    blocks = length // QBLK
    full = pl.BlockSpec((length, slab), lambda i: (0, 0))
    return pl.pallas_call(
        functools.partial(attn_bwd_kernel, heads, blocks),
        grid=(blocks,),
        in_specs=attn_specs(length, slab)
        + [
            pl.BlockSpec((QBLK, heads), lambda i: (i, 0)),
            pl.BlockSpec((QBLK, heads * HD), lambda i: (i, 0)),
            full,
            full,
        ],
        out_specs=full,
        out_shape=jax.ShapeDtypeStruct((length, slab), BF16),
        scratch_shapes=[pltpu.VMEM((length, slab), F32)],
        compiler_params=pltpu.CompilerParams(vmem_limit_bytes=40 * 1024 * 1024),
        cost_estimate=pl.CostEstimate(
            flops=3 * 10**9, bytes_accessed=3 * 10**7, transcendentals=10**6
        ),
        name="attn_backward",
    )(*inputs, lse, g_out, cosine, sine)


def tie(value, *after):
    return lax.optimization_barrier((value,) + after)[0]


def stage(compute, inputs, sends):
    inputs, operands = lax.optimization_barrier((inputs, [operand for _, operand in sends]))
    got = [send(operand) for (send, _), operand in zip(sends, operands)]
    return lax.optimization_barrier((compute(*inputs), got))


class Net:
    def __init__(self):
        self.n = lax.axis_size("ctx")
        self.m = lax.axis_size("fsdp")
        self.c = lax.axis_index("ctx")
        self.f = lax.axis_index("fsdp")
        self.direct = self.n == 4 and self.m == 8
        self.x, self.core = self.c // 2, self.c % 2
        self.z, self.y = self.f // 2, self.f % 2
        self.by_core = [[i * 2 + k for i in range(self.n // 2)] for k in range(2)]

    def flip(self, value, axis, bit):
        size = lax.axis_size(axis)
        return lax.ppermute(value, axis, [(i, i ^ bit) for i in range(size)])

    def shift_z(self, value, by):
        return lax.ppermute(value, "fsdp", [(i, (i + 2 * by) % self.m) for i in range(self.m)])

    def cross(self, value):
        pairs = [
            (c * 8 + z * 2 + y, z * 8 + c * 2 + y)
            for c in range(4)
            for z in range(4)
            for y in range(2)
        ]
        return lax.ppermute(value, ("ctx", "fsdp"), pairs)

    def along_z(self, block):
        return [block] + [self.shift_z(block, k) for k in range(1, 4)]

    def along_y(self, pieces):
        return [self.flip(piece, "fsdp", 1) for piece in pieces]

    def in_order(self, own, mate, columns=None):
        places = [2 * ((self.z - k) % 4) + (self.y ^ o) for o in range(2) for k in range(4)]
        return put(own + mate, places, columns)

    def flip_y(self, value):
        return self.flip(value, "fsdp", 1)

    def flip_x(self, value):
        return self.flip(value, "ctx", 2)

    def flip_core(self, value):
        return self.flip(value, "ctx", 1)

    def halves_y(self, sums):
        low = sums.astype(BF16)
        low = low.reshape((4, 2) + low.shape[1:])
        away = lax.dynamic_index_in_dim(low, 1 - self.y, 1, False)
        return lax.dynamic_index_in_dim(low, self.y, 1, False), away

    def shifts_z(self, both):
        sent = [lax.dynamic_index_in_dim(both, (self.z + k) % 4, 0, False) for k in range(4)]
        return [sent[0]] + [self.shift_z(sent[k], k) for k in range(1, 4)]

    def collect(self, sums):
        return lax.psum_scatter(sums.astype(BF16), "fsdp", scatter_dimension=0, tiled=False)

    def ctx_all(self, value):
        if not self.direct:
            return lax.all_gather(value, "ctx", axis=0, tiled=False)
        pair = jnp.stack([value, self.flip(value, "ctx", 2)])
        mates = self.flip(pair, "ctx", 1)
        return put([pair, mates], [self.c, self.c ^ 2, self.c ^ 1, self.c ^ 3])

    def ctx_sum(self, value):
        if not self.direct:
            return lax.psum(value, "ctx")
        value = value + self.flip(value, "ctx", 1)
        return value + self.flip(value, "ctx", 2)

    def ctx_collect(self, parts):
        if not self.direct:
            low = lax.psum_scatter(parts.astype(BF16), "ctx", scatter_dimension=0, tiled=False)
            return low.astype(F32)
        pairs = parts.reshape((2, 2) + parts.shape[1:])
        away = lax.dynamic_index_in_dim(pairs, 1 - self.core, 1, False).astype(BF16)
        here = lax.dynamic_index_in_dim(pairs, self.core, 1, False)
        got = self.flip(away, "ctx", 1)

        def half(which):
            return lax.dynamic_index_in_dim(here, which, 0, False).astype(
                F32
            ) + lax.dynamic_index_in_dim(got, which, 0, False).astype(F32)

        across = self.flip(half(1 - self.x).astype(BF16), "ctx", 2)
        return half(self.x) + across.astype(F32)

    def over_cores(self, value):
        if not self.direct:
            value = lax.psum(value, "ctx", axis_index_groups=self.by_core)
            return lax.all_gather(value, "ctx", axis=0)[:2].astype(F32)
        value = (value.astype(F32) + self.flip(value, "ctx", 2).astype(F32)).astype(BF16)
        mate = self.flip(value, "ctx", 1)
        pair = jnp.stack([value, mate]).astype(F32)
        return jnp.where(self.core == 0, pair, pair[::-1])

    def rows_out(self, shard):
        per = self.m // self.n
        got = lax.all_gather(shard, "fsdp", axis=0, tiled=False)
        return lax.dynamic_slice_in_dim(got, self.c * per, per, 0)

    def rows_back(self, sums):
        wide = jnp.zeros((self.m,) + sums.shape[1:], BF16)
        wide = lax.dynamic_update_slice_in_dim(
            wide, sums.astype(BF16), self.c * (self.m // self.n), 0
        )
        out = lax.psum_scatter(wide, "fsdp", scatter_dimension=0, tiled=False)
        return lax.psum(out, "ctx")


def put_kernel(counts, cuts, places, *refs):
    parts, outs = refs[: len(counts)], refs[len(counts) :]
    start = 0
    for part, count in zip(parts, counts):

        @pl.when((pl.program_id(0) >= start) & (pl.program_id(0) < start + count))
        def _(part=part):
            for out, low, high in zip(outs, cuts[:-1], cuts[1:]):
                out[...] = part[..., low:high]

        start += count


def put(parts, places, columns=None):
    counts = [part.shape[0] for part in parts]
    total = sum(counts)
    shape = parts[0].shape[1:]
    zeros = (0,) * len(shape)
    sizes = columns or [shape[-1]]
    cuts = [0]
    for size in sizes:
        cuts.append(cuts[-1] + size)
    places = jnp.stack([jnp.asarray(p, jnp.int32) for p in places])
    size = parts[0][0].size * parts[0].dtype.itemsize
    specs = []
    for p in range(len(parts)):
        start = sum(counts[:p])

        def at(i, at, start=start, last=counts[p] - 1):
            return (jnp.clip(i - start, 0, last),) + zeros

        specs.append(pl.BlockSpec((1,) + shape, at))
    out = pl.pallas_call(
        functools.partial(put_kernel, counts, cuts),
        grid_spec=pltpu.PrefetchScalarGridSpec(
            num_scalar_prefetch=1,
            grid=(total,),
            in_specs=specs,
            out_specs=[
                pl.BlockSpec((1,) + shape[:-1] + (w,), lambda i, at: (at[i],) + zeros)
                for w in sizes
            ],
        ),
        out_shape=[
            jax.ShapeDtypeStruct((total,) + shape[:-1] + (w,), parts[0].dtype) for w in sizes
        ],
        compiler_params=pltpu.CompilerParams(vmem_limit_bytes=40 * 1024 * 1024),
        cost_estimate=pl.CostEstimate(
            flops=0, bytes_accessed=2 * total * size, transcendentals=0
        ),
        name="put",
    )(places, *parts)
    return out if columns else out[0]


def rms_scale(values):
    return lax.rsqrt(jnp.mean(values * values, axis=-1, keepdims=True) + EPSILON)


def rms_back(values, gain, scale, grad):
    scaled = grad * gain
    inner = jnp.mean(values * scaled, axis=-1, keepdims=True)
    return scale * scaled - values * (scale * scale * scale * inner)


def columns_of(w, start, size):
    return lax.dynamic_slice_in_dim(w, start, size, 1)


def rotary_tables(length, q_heads, slab):
    half = HD // 2
    freq = (ROPE_BASE ** (-(np.arange(half) * 2.0 / HD))).astype(np.float32)
    angle = np.arange(length, dtype=np.float32)[:, None] * freq[None, :]
    one = np.concatenate([np.cos(angle), np.cos(angle)], axis=1)
    two = np.concatenate([-np.sin(angle), np.sin(angle)], axis=1)
    room = slab - (q_heads + 1) * HD
    cosine = np.concatenate([one] * (q_heads + 1) + [np.ones((length, room))], axis=1)
    sine = np.concatenate([two] * (q_heads + 1) + [np.zeros((length, room))], axis=1)
    return jnp.asarray(cosine, F32), jnp.asarray(sine, F32)


def per_device(
    tokens,
    teacher,
    segment_ids,
    valid_mask,
    gain_in,
    w_in,
    conv_w,
    conv_b,
    dt_bias,
    a_log,
    d_skip,
    gain_m,
    w_out,
    w_qkv,
    w_o,
    gain_ffn,
    w_gate,
    w_up,
    w_down,
):
    net = Net()
    n, m, c, f = net.n, net.m, net.c, net.f
    rows, dim = tokens.shape[1:]
    length = segment_ids.shape[1]
    shard = w_in.shape[0]
    wide = MH * HP
    conv_full = wide + 2 * NS
    heads = MH // n
    q_heads = QH // n
    width = heads * HP
    conv_width = width + 2 * NS
    q_width = q_heads * HD
    slab = q_width + 2 * HD
    slab += -slab % 128
    group = QH // KVH
    kv_at = (c * q_heads) // group
    ff = w_gate.shape[1]
    ff_shard = w_down.shape[0]
    per = m // n
    seg = segment_ids[0]
    seg_c, seg_r = seg[:, None], seg[None, :]
    ends = jnp.concatenate([jnp.full((1,), -1, jnp.int32), seg[SPAN - 1 :: SPAN]])
    valid = valid_mask[0].astype(F32)

    def lay(values):
        values = values.reshape((-1, values.shape[-1]))
        room = -values.shape[1] % 128
        return jnp.pad(values, ((0, 0), (0, room))).reshape(-1, 128)

    def unlay(small, start, lead, size):
        room = size + -size % 128
        count = lead * room // 128
        return small[..., start : start + count, :].reshape(small.shape[:-2] + (lead, room))[
            ..., :size
        ]

    shapes = [(1, shard), (1, shard), (1, w_out.shape[0]), (1, conv_b.shape[0])]
    shapes += [(KW, conv_b.shape[0])]
    starts = [0]
    for lead, size in shapes:
        starts.append(starts[-1] + lead * (size + -size % 128) // 128)
    laid = [lay(p) for p in (gain_in[None], gain_ffn[None], gain_m[None], conv_b[None], conv_w)]
    laid.append(jnp.full((1, 128), jnp.sum(valid), F32).astype(BF16))
    laid.append(jnp.zeros((-(starts[-1] + 1) % 16, 128), BF16))
    at_small = 64
    packed = jnp.concatenate(laid, axis=0)
    first = jnp.concatenate(
        [
            columns_of(w_in, wide + c * width, width),
            w_in[:, 2 * wide : 2 * wide + 2 * NS],
            columns_of(w_in, wide + conv_full + c * heads, heads),
            jnp.zeros((shard, at_small - heads), BF16),
            packed.T if net.direct else jnp.zeros((shard, packed.shape[0]), BF16),
            jnp.zeros((shard, 128 - at_small - packed.shape[0]), BF16),
        ],
        axis=1,
    )
    second = jnp.concatenate(
        [
            columns_of(w_in, c * width, width),
            columns_of(w_qkv, c * q_width, q_width),
            columns_of(w_qkv, QH * HD + kv_at * HD, HD),
            columns_of(w_qkv, (QH + KVH) * HD + kv_at * HD, HD),
            jnp.zeros((shard, slab - q_width - 2 * HD), BF16),
        ],
        axis=1,
    )
    both_out = jnp.concatenate([w_out, w_o], axis=0)
    out_rows, mamba_rows = both_out.shape[0], w_out.shape[0]
    ff_half = ff_shard // 2
    size = m * ff_half

    def ff_cut(w):
        w = w.reshape(shard, m, 2, ff_half)
        return lax.dynamic_index_in_dim(w, net.core, 2, False).reshape(shard, size)

    w_ff = jnp.concatenate(
        [
            ff_cut(w_gate).reshape(-1, dim),
            ff_cut(w_up).reshape(-1, dim),
            lax.dynamic_slice_in_dim(w_down, net.core * ff_half, ff_half, 0),
        ],
        axis=0,
    )
    w_ff = lax.all_gather(w_ff, "fsdp", axis=0, tiled=False)
    if net.direct:
        both_cols = jnp.concatenate([first, second], axis=1)
        pair = jnp.stack([tokens[0], net.flip_x(tokens[0])])
        near = net.along_z(both_cols)
        far = net.along_y([tie(near[0], pair)] + near[1:])
        w_first, w_second = net.in_order(
            [p[None] for p in near],
            [p[None] for p in far],
            [first.shape[1], second.shape[1]],
        )
        at = conv_width + at_small
        small = jnp.swapaxes(w_first[:, :, at : at + packed.shape[0]], 1, 2)
        all_tokens = put([pair, net.flip_core(pair)], [c, c ^ 2, c ^ 1, c ^ 3])
        crossed = net.cross(tie(both_out, *near[1:]))
    else:
        small = lax.all_gather(packed, "fsdp", axis=0, tiled=False)
        w_first = lax.all_gather(first, "fsdp", axis=0, tiled=False)
        w_second = lax.all_gather(second, "fsdp", axis=0, tiled=False)
        w_outs = net.rows_out(both_out)
        all_tokens = net.ctx_all(tokens[0])
    all_tokens = all_tokens.reshape(length, dim)
    w_first = w_first.reshape(dim, first.shape[1])
    cuts = [
        jnp.transpose(unlay(small, start, *shape), (1, 0, 2)).reshape(shape[0], -1)
        for start, shape in zip(starts, shapes)
    ]
    gain_input = cuts[0].astype(F32)
    gain_second = cuts[1].astype(F32)
    gain_mamba = lax.dynamic_slice_in_dim(cuts[2], c * width, width, 1).astype(F32)
    count_ctx = jnp.sum(small[:, starts[-1], 0].astype(F32))

    def conv_cut(values):
        own = lax.dynamic_slice_in_dim(values, c * width, width, 1)
        return jnp.concatenate([own, values[:, wide:]], axis=1).astype(F32)

    bias, taps = conv_cut(cuts[3]), conv_cut(cuts[4])
    rate = jnp.exp(a_log)
    params = jnp.stack(
        [lax.dynamic_slice_in_dim(v, c * heads, heads) for v in (dt_bias, rate)]
    )
    params = jnp.pad(params, ((0, 6), (0, 128 - heads)))
    skip = lax.dynamic_slice_in_dim(d_skip, c * heads, heads)

    def shifted(by):
        return jnp.concatenate([jnp.full((by,), -1, jnp.int32), seg[: length - by]]) == seg

    same = jnp.stack([shifted(by) for by in range(KW)], axis=1).astype(F32)
    up = jnp.stack(
        [
            jnp.concatenate([seg[by:], jnp.full((by,), -1, jnp.int32)]) == seg
            for by in range(KW)
        ],
        axis=1,
    ).astype(F32)
    cosine, sine = rotary_tables(length, q_heads, slab)
    conv_args = (all_tokens, gain_input, w_first, taps, bias, same, params)

    def square_rows(square):
        return jnp.concatenate([square[0].reshape(-1, 128), jnp.full((8, 128), count_ctx)])

    def ssm(act, steps, step_rows):
        return ssm_forward(heads, (ends, skip, act, steps, step_rows, seg_c, seg_r))

    def attend(qkv):
        return attn_forward(q_heads, (qkv, seg_c, seg_r))

    w_second = w_second.reshape(dim, second.shape[1])
    if net.direct:
        normed, cin, pre, act, steps, step_rows = project_conv(*conv_args)
        ssm_y, states = ssm(act, steps, step_rows)
        gate_z, qkv, square = project_gate(normed, w_second, ssm_y, cosine, sine)
        mated = net.flip_y(tie(crossed, ssm_y))
        (attended, lse), (square,) = stage(
            attend, (qkv,), [(net.ctx_sum, square_rows(square))]
        )
        w_outs = jnp.where(
            net.y == 0, jnp.stack([crossed, mated]), jnp.stack([mated, crossed])
        )
    else:
        normed, cin, pre, act, steps, step_rows = project_conv(*conv_args)
        ssm_y, states = ssm(act, steps, step_rows)
        gate_z, qkv, square = project_gate(normed, w_second, ssm_y, cosine, sine)
        square = net.ctx_sum(square_rows(square))
        attended, lse = attend(qkv)
    w_mamba = w_outs[:, :mamba_rows].reshape(per * mamba_rows, dim)
    w_attn = w_outs[:, mamba_rows:].reshape(per * (out_rows - mamba_rows), dim)
    ssm_in = (ends, skip, act, steps, step_rows, seg_c, seg_r)
    count = square[-1, 0]
    scale_m = lax.rsqrt(square[:-8].reshape(length, 1) / wide + EPSILON)
    gated = ssm_y * (gate_z * jax.nn.sigmoid(gate_z))
    ym = (gated * scale_m * gain_mamba).astype(BF16)
    outs = nn(ym, w_mamba) + nn(attended, w_attn)
    mixed = tokens[0].astype(F32) + net.ctx_collect(outs.reshape(n, rows, dim))

    ff_rows = shard * size // dim
    w_g = w_ff[:, :ff_rows].reshape(dim, size)
    w_u = w_ff[:, ff_rows : 2 * ff_rows].reshape(dim, size)
    w_d = w_ff[:, 2 * ff_rows :].reshape(size, dim)
    scale2 = rms_scale(mixed)
    normed2 = (mixed * scale2 * gain_second).astype(BF16)
    mate = [(i, i ^ 1) for i in range(n)]
    both = jnp.concatenate([normed2, lax.ppermute(normed2, "ctx", mate)], axis=0)
    gate_v, up_v = nn(both, w_g), nn(both, w_u)
    sig = jax.nn.sigmoid(gate_v)
    product = (gate_v * sig * up_v).astype(BF16)
    down_out = nn(product, w_d)
    from_mate = lax.ppermute(down_out[rows:].astype(BF16), "ctx", mate)
    layer_out = mixed + down_out[:rows] + from_mate.astype(F32)
    diff = layer_out - teacher[0].astype(F32)
    squared = jnp.sum(valid[:, None] * diff * diff)
    token_total = length * m * tokens.shape[0]
    grad_out = token_total * valid[:, None] * diff / count

    gb = grad_out.astype(BF16)
    gb_both = jnp.concatenate([gb, lax.ppermute(gb, "ctx", mate)], axis=0)
    g_prod = nt(gb_both, w_d)
    g_gate = (g_prod * up_v * (sig * (1.0 + gate_v * (1.0 - sig)))).astype(BF16)
    g_up = (g_prod * gate_v * sig).astype(BF16)
    g_n2 = nt(g_gate, w_g) + nt(g_up, w_u)
    from_mate = lax.ppermute(g_n2[rows:].astype(BF16), "ctx", mate)
    grad_n2 = g_n2[:rows] + from_mate.astype(F32)
    part = rms_back(mixed, gain_second, scale2, grad_n2)
    grad_mixed = grad_out + part

    def ff_weights(both, g_gate, g_up, product, gb_both):
        return jnp.concatenate(
            [
                tn(both, g_gate).reshape(m, ff_rows, dim),
                tn(both, g_up).reshape(m, ff_rows, dim),
                tn(product, gb_both).reshape(m, ff_half, dim),
            ],
            axis=1,
        ).astype(BF16)

    ff_args = (both, g_gate, g_up, product, gb_both)
    gm = grad_mixed.astype(BF16)
    if net.direct:
        g_ff, (across,) = stage(ff_weights, ff_args, [(net.flip_x, gm)])
        pair = jnp.stack([gm, across])
        gm = put([pair, net.flip_core(pair)], [c, c ^ 2, c ^ 1, c ^ 3])
    else:
        gm = net.ctx_all(gm)
        g_ff = ff_weights(*ff_args)
    gm = gm.reshape(length, dim)
    g_ff = lax.psum_scatter(g_ff, "fsdp", scatter_dimension=0, tiled=False)

    g_ym = nt(gm, w_mamba)
    inner = jnp.sum(gated * (g_ym * gain_mamba), axis=1).reshape(-1, 128)

    def outs_back(gm):
        g_ob = nt(gm, w_attn).astype(BF16)
        g_outs = jnp.concatenate(
            [
                tn(ym, gm).reshape(per, mamba_rows, dim),
                tn(attended, gm).reshape(per, out_rows - mamba_rows, dim),
            ],
            axis=1,
        )
        return g_ob, g_outs.astype(BF16)

    def attend_back(qkv, g_ob):
        return attn_backward(q_heads, (qkv, seg_c, seg_r), lse, g_ob, cosine, sine)

    def plus(here, got):
        return (here.astype(F32) + got.astype(F32)).astype(BF16)

    if net.direct:
        (g_ob, g_outs), (got,) = stage(outs_back, (gm,), [(net.flip_core, inner)])
        inner = inner + got
        here = lax.dynamic_index_in_dim(g_outs, net.y, 0, False)
        away = lax.dynamic_index_in_dim(g_outs, 1 - net.y, 0, False)
        g_qkv, (got_x, got) = stage(
            attend_back, (qkv, g_ob), [(net.flip_x, inner), (net.flip_y, away)]
        )
        inner = inner + got_x
        out_both = plus(here, got).reshape(4, out_rows // 4, dim)
    else:
        g_ob, g_outs = outs_back(gm)
        inner = net.ctx_sum(inner)
        g_qkv = attend_back(qkv, g_ob)
    inner = inner.reshape(length, 1) / wide
    stats = jnp.concatenate([scale_m, scale_m * scale_m * scale_m * inner], axis=1)
    g_gated = stats[:, :1] * (g_ym * gain_mamba) - gated * stats[:, 1:]
    sig_z = jax.nn.sigmoid(gate_z)
    g_z = (g_gated * ssm_y * (sig_z + gate_z * sig_z * (1.0 - sig_z))).astype(BF16)
    early = jnp.concatenate([g_z, g_qkv], axis=1)
    grad_early = tn(normed, early).reshape(m, shard, width + slab)

    def ssm_back(states):
        return ssm_backward(
            heads,
            ssm_in,
            states,
            gate_z,
            g_ym,
            ssm_y,
            stats,
            gain_mamba,
            pre,
            cin,
            up,
            taps,
            params,
        )

    if net.direct:
        here, away = net.halves_y(grad_early)
        (g_late, g_conv, g_wide, g_steps), (got, out_parts) = stage(
            ssm_back, (states,), [(net.flip_y, away), (net.shifts_z, out_both)]
        )
        grad_early = plus(here, got)
        out_quarter = sum(p.astype(F32) for p in out_parts).astype(BF16)
    else:
        g_late, g_conv, g_wide, g_steps = ssm_back(states)

    def to_wide(values, at, size):
        out = jnp.zeros(values.shape[:-1] + (size,), F32)
        return lax.dynamic_update_slice_in_dim(out, values, at, values.ndim - 1)

    def for_shards(values):
        values = jnp.concatenate(
            [to_wide(values[:, :width], c * width, wide), values[:, width:]], axis=1
        )
        values = values.reshape((-1, m, values.shape[-1] // m))
        return jnp.transpose(values, (1, 0, 2))

    conv_rows = (conv_b.shape[0] + 127) // 128
    heads_grads = jnp.stack(
        [
            to_wide(g_steps[0, :heads], c * heads, MH),
            to_wide(g_steps[1, :heads], c * heads, MH),
            to_wide(jnp.sum(g_wide[0].reshape(heads, HP), axis=1), c * heads, MH),
            jnp.full((MH,), squared),
        ]
    )
    laid = [jax.vmap(lay)(for_shards(g_conv[: KW + 1]))]
    laid.append(jnp.broadcast_to(lay(heads_grads)[None], (m, 4, 128)))
    laid = jnp.concatenate(laid, axis=1)
    room = -laid.shape[1] % 16
    laid = jnp.pad(laid, ((0, 0), (0, room), (0, conv_width)))
    late_size = conv_width + 128
    grad_late = jnp.concatenate(
        [tn(normed, g_late).reshape(m, shard, late_size).astype(BF16), laid.astype(BF16)], axis=1
    )
    resid = tokens[0].astype(F32)

    def normed_back(early, g_late):
        return (nt(early, w_second) + nt(g_late, w_first)).reshape(n, rows, dim)

    def tokens_back(grad_normed):
        return grad_mixed + rms_back(resid, gain_input, rms_scale(resid), grad_normed)

    if net.direct:
        here, away = net.halves_y(grad_late)
        g_normed, (got, early_parts, out_quarter) = stage(
            normed_back,
            (early, g_late),
            [(net.flip_y, away), (net.shifts_z, grad_early), (net.cross, out_quarter)],
        )
        grad_early = sum(p.astype(F32) for p in early_parts).astype(BF16)
        _, (late_parts, grad_normed) = stage(
            tuple,
            (),
            [(net.shifts_z, plus(here, got)), (net.ctx_collect, g_normed)],
        )
        grad_late = sum(p.astype(F32) for p in late_parts).astype(BF16)
        joined = jnp.concatenate([grad_early, out_quarter.reshape(shard, -1)], axis=1)
        joined = jnp.pad(joined, ((0, grad_late.shape[0] - shard), (0, 0)))
        joined = jnp.concatenate([grad_late, joined], axis=1)
        grad_tokens, (got, got_ff) = stage(
            tokens_back, (grad_normed,), [(net.ctx_all, joined), (net.over_cores, g_ff)]
        )
        got_late = got[:, :, :late_size]
        got = got[:, :shard, late_size:].astype(F32)
        got_early = got[:, :, : width + slab]
        out_outs = got[:, :, width + slab :].reshape(out_rows, dim)
    else:
        grad_tokens = tokens_back(net.ctx_collect(normed_back(early, g_late)))
        got_early = net.ctx_all(net.collect(grad_early)).astype(F32)
        got_late = net.ctx_all(net.collect(grad_late))
        out_outs = net.rows_back(g_outs).astype(F32)
        got_ff = net.over_cores(g_ff)
    got_late = got_late.astype(F32)
    totals = jnp.sum(got_late[:, shard:, :128], axis=0)
    got_late = got_late[:, :shard]
    grad_conv = unlay(totals, 0, KW + 1, conv_b.shape[0])
    head_totals = totals[(KW + 1) * conv_rows : (KW + 1) * conv_rows + 4, :MH]
    loss = head_totals[3, 0] / (2.0 * count)

    def side(got, start, size):
        return [got[j][:, start : start + size] for j in range(n)]

    shared = n // KVH
    out_w_in = jnp.concatenate(
        side(got_early, 0, width)
        + side(got_late, 0, width)
        + [sum(side(got_late, width, 2 * NS))]
        + side(got_late, conv_width, heads),
        axis=1,
    )
    out_w_qkv = jnp.concatenate(
        side(got_early, width, q_width)
        + [
            sum(side(got_early, width + q_width + i * HD, HD)[k * shared : (k + 1) * shared])
            for i in range(2)
            for k in range(KVH)
        ],
        axis=1,
    )

    def ff_wide(values):
        values = values.reshape(2, shard, m, ff_half)
        return jnp.transpose(values, (1, 2, 0, 3)).reshape(shard, ff)

    out_gate = ff_wide(got_ff[:, :ff_rows])
    out_up = ff_wide(got_ff[:, ff_rows : 2 * ff_rows])
    out_mamba = out_outs[:mamba_rows]

    def along(*pairs):
        return sum(jnp.sum(w.astype(F32) * g, axis=1) for w, g in pairs)

    return (
        loss,
        layer_out[None],
        grad_tokens[None],
        along((w_in, out_w_in), (w_qkv, out_w_qkv)) / gain_in.astype(F32),
        out_w_in,
        grad_conv[:KW],
        grad_conv[KW],
        head_totals[0],
        head_totals[1],
        head_totals[2],
        along((w_out, out_mamba)) / gain_m.astype(F32),
        out_mamba,
        out_w_qkv,
        out_outs[mamba_rows:],
        along((w_gate, out_gate), (w_up, out_up)) / gain_ffn.astype(F32),
        out_gate,
        out_up,
        got_ff[:, 2 * ff_rows :].reshape(ff_shard, dim),
    )


def solution(mesh):
    in_specs = (
        P("fsdp", "ctx", None),
        P("fsdp", "ctx", None),
        P("fsdp", None),
        P("fsdp", "ctx"),
        P("fsdp"),
        P("fsdp", None),
        P(None, "fsdp"),
        P("fsdp"),
        P(),
        P(),
        P(),
        P("fsdp"),
        P("fsdp", None),
        P("fsdp", None),
        P("fsdp", None),
        P("fsdp"),
        P("fsdp", None),
        P("fsdp", None),
        P("fsdp", None),
    )
    out_specs = (
        P(),
        P("fsdp", "ctx", None),
        P("fsdp", "ctx", None),
        P("fsdp"),
        P("fsdp", None),
        P(None, "fsdp"),
        P("fsdp"),
        P(),
        P(),
        P(),
        P("fsdp"),
        P("fsdp", None),
        P("fsdp", None),
        P("fsdp", None),
        P("fsdp"),
        P("fsdp", None),
        P("fsdp", None),
        P("fsdp", None),
    )
    return jax.shard_map(
        per_device, mesh=mesh, in_specs=in_specs, out_specs=out_specs, check_vma=False
    )
```

time: 655 us -> 493 us (0.75)
  the two profiles are of different devices: /device:TPU:0 before, /device:TPU:13 now
where the time goes in v2:
time: 493 us; the launch traced here: 486 us
  waiting for transfers between devices  169 us (34%)
  Pallas kernels  80.2 us (16%)
  local copies, waits for them, and re-layouts  75 us (15%)
  starting transfers between devices  57.4 us (12%)
  other arithmetic  51.9 us (11%)
  matrix products  33.3 us (7%)
  between operations  19.1 us (4%)
    ppermute x12, waiting for transfers between devices, shift_z(): lax.ppermute(value, 'fsdp', [(i, (i + 2 * by) % self.m) for i in range(se...  89.5 us
    ppermute x24, waiting for transfers between devices, flip(): return lax.ppermute(value, axis, [(i, i ^ bit) for i in range(size)])  76.4 us
    pallas_call x1, Pallas kernels, ssm_backward(): pl.pallas_call(functools.partial(ssm_bwd_kernel, heads), grid=(steps,), i...  38.7 us
    ppermute x24, starting transfers between devices, flip(): return lax.ppermute(value, axis, [(i, i ^ bit) for i in range(size)])  34.6 us
    unnamed x195, local copies, waits for them, and re-layouts  23.6 us
    ppermute x12, starting transfers between devices, shift_z(): lax.ppermute(value, 'fsdp', [(i, (i + 2 * by) % self.m) for i in range(se...  14.6 us
    dot_general x7, matrix products, nt(): lax.dot_general(left, right, (((1,), (1,)), ((), ())), preferred_element_...  12.1 us
    pallas_call x1, Pallas kernels, ssm_forward(): pl.pallas_call(functools.partial(ssm_fwd_kernel, heads), grid=(steps,), i...  12.1 us
  transfers between devices with their start and end apart: 44, of which 21 were waited for; matrix products, arithmetic and copies ran while one was open for 16% of the time, Pallas kernels for 16%

profile of v2, /device:TPU:13, one launch (start us, length us, event | category | flops | bytes accessed | tf_op | source)
XLA Modules:
  0.0 486.0 jit_solution(13665680214432600292)
XLA Ops:
  10.1 3.1 dynamic-slice_reduce_fusion
  23.6 4.3 collective-permute-done.2
  28.3 42.0 %collective-permute-done.3 = bf16[128,1408]{1,0:T(8,128)(2,1)} collective-permute-done((bf16[128,1408]{1,0:T(8,128)(2,1)S(1)}, bf16[128,1408]{1,0:T(8,128)(2,1)}, u32[]{:S(2)}, u32[]{:S(2)}) %collective-permute-start.3) | collective-permute-done | bytes 360480 | tf_op jit(solution)/shard_map/ppermute | solution.py:597
  70.6 7.0 %collective-permute-done.4 = bf16[128,1408]{1,0:T(8,128)(2,1)} collective-permute-done((bf16[128,1408]{1,0:T(8,128)(2,1)S(1)}, bf16[128,1408]{1,0:T(8,128)(2,1)}, u32[]{:S(2)}, u32[]{:S(2)}) %collective-permute-start.4) | collective-permute-done | bytes 360480 | tf_op jit(solution)/shard_map/ppermute | solution.py:597
  81.0 1.9 pad_maximum_fusion.10
  82.9 5.5 %collective-permute-start.11 = (bf16[256,1024]{1,0:T(8,128)(2,1)}, bf16[256,1024]{1,0:T(8,128)(2,1)}, u32[]{:S(2)}, u32[]{:S(2)}) collective-permute-start(bf16[256,1024]{1,0:T(8,128)(2,1)} %pad_maximum_fusion.10), channel_id=1, source_target_pairs={{0,0},{1,1},{2,8},{3,9},{4,16},{5,17},{6,24},{7,25},{8,2},{9,3},{1... | collective-permute-start | bytes 1572872 | tf_op jit(solution)/shard_map/ppermute | solution.py:606
  89.2 2.9 collective-permute-done.8
  92.0 15.4 %collective-permute-done.5 = bf16[128,1408]{1,0:T(8,128)(2,1)} collective-permute-done((bf16[128,1408]{1,0:T(8,128)(2,1)S(1)}, bf16[128,1408]{1,0:T(8,128)(2,1)}, u32[]{:S(2)}, u32[]{:S(2)}) %collective-permute-start.5) | collective-permute-done | bytes 360480 | tf_op jit(solution)/shard_map/ppermute | solution.py:594
  109.4 2.6 put.5
  118.2 5.3 %project_conv.1 = (bf16[1024,1024]{1,0:T(8,128)(2,1)S(1)}, bf16[1024,640]{1,0:T(8,128)(2,1)S(1)}, bf16[1024,640]{1,0:T(8,128)(2,1)S(1)}, bf16[1024,640]{1,0:T(8,...) custom-call(bf16[1024,1024]{1,0:T(8,128)(2,1)S(1)} %bitcast.285, f32[1,1024]{1,0:T(1,128)S(1)} %bitcast.294, ...), custom_call_target="tpu_custom_call" | custom-call | flops 1610612736 | bytes 10000000 | tf_op jit(solution)/shard_map/project_conv/pallas_call | solution.py:100
  124.7 12.1 %ssm_forward.1 = (f32[1024,384]{1,0:T(8,128)S(1)}, f32[8,6,64,128]{3,2,1,0:T(8,128)S(1)}) custom-call(s32[9]{0:T(128)S(1)} %pad_add_fusion.ends, f32[6]{0:T(128)S(1)} %dynamic_slice.140.skip, bf16[1024,640]{1,0:T(8,128)(2,1)S(1)} %get-tuple-element.104.act, f32[1024,256]{1,0:T(8,128)S(1)} %get-tuple-element.105.steps, ...), custom_call_target="tpu_custom_call" | custom-call | flops 1000000000 | bytes 40000000 | tf_op jit(solution)/shard_map/ssm_forward/pallas_call | solution.py:372
  140.0 4.1 project_gate.1
  144.8 2.9 collective-permute-start.9
  149.8 5.6 %attn_forward.1 = (bf16[1024,128]{1,0:T(8,128)(2,1)S(1)}, f32[1024,2]{1,0:T(8,128)S(1)}) custom-call(bf16[1024,256]{1,0:T(8,128)(2,1)S(1)} %get-tuple-element.134.qkv_ref, s32[1024,1]{1,0:T(8,128)S(1)} %copy-done.11, s32[1,1024]{1,0:T(1,128)S(1)} %copy-done.25), custom_call_target="tpu_custom_call" | custom-call | flops 1000000000 | bytes 20000000 | tf_op jit(solution)/shard_map/attn_forward/pallas_call | solution.py:526
  158.6 2.8 convolution_add_fusion
  161.4 2.7 fusion.11
  164.7 2.6 collective-permute-done.13
  167.4 2.3 fusion.18
  169.8 13.3 %collective-permute-done.14 = bf16[256,1024]{1,0:T(8,128)(2,1)} collective-permute-done((bf16[256,1024]{1,0:T(8,128)(2,1)}, bf16[256,1024]{1,0:T(8,128)(2,1)}, u32[]{:S(2)}, u32[]{:S(2)}) %collective-permute-start.14) | collective-permute-done | bytes 524320 | tf_op jit(solution)/shard_map/ppermute | solution.py:594
  183.1 2.0 multiply_reduce_fusion.5
  188.3 3.9 fusion.41
  192.2 2.5 fusion.34
  194.7 2.6 multiply_convert_fusion.2
  202.8 1.8 collective-permute-done.17
  204.5 1.8 multiply_convert_fusion
  211.3 2.2 fusion.38
  217.7 6.6 %pad_maximum_fusion = bf16[8,384,1024]{2,1,0:T(8,128)(2,1)} fusion(bf16[8,128,1024]{2,1,0:T(8,128)(2,1)S(1)} %bitcast.323, bf16[8,128,1024]{2,1,0:T(8,128)(2,1)S(1)} %bitcast.321, bf16[8,128,1024]{2,1,0:T(8,128)(2,1)S(1)} %bitcast.322), kind=kLoop, calls=%fused_computation | loop fusion | flops 18874368 | bytes 12582912 | tf_op jit(solution)/shard_map/concatenate | solution.py:1005
  224.3 5.4 %collective-permute-done.19 = bf16[256,1024]{1,0:T(8,128)(2,1)} collective-permute-done((bf16[256,1024]{1,0:T(8,128)(2,1)}, bf16[256,1024]{1,0:T(8,128)(2,1)}, u32[]{:S(2)}, u32[]{:S(2)}) %collective-permute-start.19) | collective-permute-done | bytes 524320 | tf_op jit(solution)/shard_map/ppermute | solution.py:594
  229.7 2.3 pad_maximum_fusion.6.refs_0_
  233.2 2.6 collective-permute-done.20.refs_1_
  235.7 3.1 put.6
  238.9 2.6 multiply_reduce_fusion.1
  246.9 1.7 collective-permute-start.23
  256.2 7.2 %attn_backward.1 = bf16[1024,256]{1,0:T(8,128)(2,1)S(1)} custom-call(bf16[1024,256]{1,0:T(8,128)(2,1)S(1)} %copy-done.40, s32[1024,1]{1,0:T(8,128)S(1)} %copy-done.12, s32[1,1024]{1,0:T(1,128)S(1)} %copy-done.25, f32[1024,2]{1,0:T(8,128)S(1)} %copy-done.42, bf16[1024,128]{1,0:T(8,128)(2,1)S(1)} %copy-done.30, f32[1024,256]{1,0:T(8,128)S(1)} %copy-done.18, ...), custom_call_target="tpu_custom_call" | custom-call | flops 3000000000 | bytes 30000000 | tf_op jit(solution)/shard_map/attn_backward/pallas_call | solution.py:550
  263.4 2.9 collective-permute-done.23
  267.9 1.9 convolution_convert_fusion.4
  276.4 1.9 collective-permute-start.26
  279.7 38.7 %ssm_backward.1 = (bf16[1024,768]{1,0:T(8,128)(2,1)}, f32[8,640]{1,0:T(8,128)}, f32[8,384]{1,0:T(8,128)}, f32[8,128]{1,0:T(8,128)}) custom-call(s32[9]{0:T(128)} %copy-done.37, f32[6]{0:T(128)} %copy-done.38, bf16[1024,640]{1,0:T(8,128)(2,1)} %copy-done.16, f32[1024,256]{1,0:T(8,128)} %copy-done.21, f32[16,1024]{1,0:T(8,128)} %copy-done.31, ...), custom_call_target="tpu_custom_call" | custom-call | flops 3000000000 | bytes 100000000 | tf_op jit(solution)/shard_map/ssm_backward/pallas_call | solution.py:409
  321.5 3.3 convolution_convert_fusion.3
  329.8 2.2 collective-permute-start.30
  332.8 1.8 fusion.49
  334.7 1.9 convolution_add_fusion.1
  336.6 6.2 %collective-permute-done.30 = bf16[128,640]{1,0:T(8,128)(2,1)S(1)} collective-permute-done((bf16[128,640]{1,0:T(8,128)(2,1)S(1)}, bf16[128,640]{1,0:T(8,128)(2,1)S(1)}, u32[]{:S(2)}, u32[]{:S(2)}) %collective-permute-start.30) | collective-permute-done | bytes 163872 | tf_op jit(solution)/shard_map/ppermute | solution.py:597
  342.7 20.7 %collective-permute-done.31 = bf16[128,640]{1,0:T(8,128)(2,1)S(1)} collective-permute-done((bf16[128,640]{1,0:T(8,128)(2,1)S(1)}, bf16[128,640]{1,0:T(8,128)(2,1)S(1)}, u32[]{:S(2)}, u32[]{:S(2)}) %collective-permute-start.31) | collective-permute-done | bytes 163872 | tf_op jit(solution)/shard_map/ppermute | solution.py:597
  363.8 1.9 collective-permute-start.36
  365.7 2.3 collective-permute-done.36
  368.2 9.7 %collective-permute-start.37 = (bf16[256,1024]{1,0:T(8,128)(2,1)S(1)}, bf16[256,1024]{1,0:T(8,128)(2,1)}, u32[]{:S(2)}, u32[]{:S(2)}) collective-permute-start(bf16[256,1024]{1,0:T(8,128)(2,1)S(1)} %fusion.15), channel_id=1, source_target_pairs={{0,16},{8,24},{16,0},{24,8},{1,17},{9,25},{17,1},{25,9},{2,18},{10... | collective-permute-start | bytes 1572872 | tf_op jit(solution)/shard_map/ppermute | solution.py:594
  378.7 3.6 collective-permute-start.34
  382.7 7.2 %collective-permute-done.37 = bf16[256,1024]{1,0:T(8,128)(2,1)} collective-permute-done((bf16[256,1024]{1,0:T(8,128)(2,1)S(1)}, bf16[256,1024]{1,0:T(8,128)(2,1)}, u32[]{:S(2)}, u32[]{:S(2)}) %collective-permute-start.37) | collective-permute-done | bytes 524320 | tf_op jit(solution)/shard_map/ppermute | solution.py:594
  389.9 1.6 fusion.16
  391.6 6.1 %collective-permute-done.34 = bf16[144,768]{1,0:T(8,128)(2,1)} collective-permute-done((bf16[144,768]{1,0:T(8,128)(2,1)}, bf16[144,768]{1,0:T(8,128)(2,1)}, u32[]{:S(2)}, u32[]{:S(2)}) %collective-permute-start.34) | collective-permute-done | bytes 221216 | tf_op jit(solution)/shard_map/ppermute | solution.py:597
  397.7 3.2 collective-permute-done.35
  405.4 15.5 %collective-permute-done.40 = bf16[384,1024]{1,0:T(8,128)(2,1)} collective-permute-done((bf16[384,1024]{1,0:T(8,128)(2,1)}, bf16[384,1024]{1,0:T(8,128)(2,1)}, u32[]{:S(2)}, u32[]{:S(2)}) %collective-permute-start.40) | collective-permute-done | bytes 786464 | tf_op jit(solution)/shard_map/ppermute | solution.py:594
  422.3 4.4 collective-permute-start.41
  426.7 6.0 %collective-permute-done.38 = bf16[144,1920]{1,0:T(8,128)(2,1)} collective-permute-done((bf16[144,1920]{1,0:T(8,128)(2,1)}, bf16[144,1920]{1,0:T(8,128)(2,1)}, u32[]{:S(2)}, u32[]{:S(2)}) %collective-permute-start.38) | collective-permute-done | bytes 552992 | tf_op jit(solution)/shard_map/ppermute | solution.py:594
  434.1 2.4 collective-permute-start.39
  438.0 2.1 reverse_select_fusion
  453.0 1.7 copy.151
  456.9 2.1 slice.491
  458.9 1.7 slice.492
  462.0 2.3 slice.419
  466.9 1.7 slice.421
  468.7 1.5 fusion.42
  472.3 1.6 copy.162
  (450 shorter events, 120.3 us)
Async XLA Ops:
  7.2 181.1 %all-gather.3.cloned.1.call-start = ((), (), s32[]{:S(2)}) async-start(), calls=%async_computation.2 | async-start | bytes 7077888 | tf_op jit(solution)/shard_map/all_gather | solution.py:879
  14.4 388.6 %reduce-scatter.2.cloned.1.call-start = ((), (), s32[]{:S(2)}) async-start(), calls=%async_computation.1 | async-start | bytes 7077888 | tf_op jit(solution)/shard_map/reduce_scatter | solution.py:1024
  15.4 62.4 %copy-start.52 = (bf16[128,3352]{1,0:T(8,128)(2,1)}, bf16[128,3352]{1,0:T(8,128)(2,1)S(1)}, u32[]{:S(2)}) copy-start(bf16[128,3352]{1,0:T(8,128)(2,1)S(1)} %copy.124) | copy-start | bytes 2574340
  17.4 63.0 %copy-start.92 = (f32[24]{0:T(128)S(1)}, f32[24]{0:T(128)}, u32[]{:S(2)}) copy-start(f32[24]{0:T(128)} %param.30) | copy-start | bytes 292
  17.6 63.0 %copy-start.93 = (f32[24]{0:T(128)S(1)}, f32[24]{0:T(128)}, u32[]{:S(2)}) copy-start(f32[24]{0:T(128)} %param.31) | copy-start | bytes 292
  17.6 63.2 %copy-start.88 = (f32[24]{0:T(128)S(1)}, f32[24]{0:T(128)}, u32[]{:S(2)}) copy-start(f32[24]{0:T(128)} %param.29) | copy-start | bytes 292
  17.8 10.1 %collective-permute-start.2 = (bf16[128,1408]{1,0:T(8,128)(2,1)S(1)}, bf16[128,1408]{1,0:T(8,128)(2,1)S(1)}, u32[]{:S(2)}, u32[]{:S(2)}) collective-permute-start(bf16[128,1408]{1,0:T(8,128)(2,1)S(1)} %concatenate.113), channel_id=1, source_target_pairs={{0,2},{1,3},{2,4},{3,5},{4,6},{5,7},{6,0},{7,1},{8,10},{9,11},{10,... | collective-permute-start | bytes 1081352 | tf_op jit(solution)/shard_map/ppermute | solution.py:597
  19.2 51.2 %collective-permute-start.3 = (bf16[128,1408]{1,0:T(8,128)(2,1)S(1)}, bf16[128,1408]{1,0:T(8,128)(2,1)}, u32[]{:S(2)}, u32[]{:S(2)}) collective-permute-start(bf16[128,1408]{1,0:T(8,128)(2,1)S(1)} %concatenate.113), channel_id=1, source_target_pairs={{0,4},{1,5},{2,6},{3,7},{4,0},{5,1},{6,2},{7,3},{8,12},{9,13},{10,... | collective-permute-start | bytes 1081352 | tf_op jit(solution)/shard_map/ppermute | solution.py:597
  20.2 57.4 %collective-permute-start.4 = (bf16[128,1408]{1,0:T(8,128)(2,1)S(1)}, bf16[128,1408]{1,0:T(8,128)(2,1)}, u32[]{:S(2)}, u32[]{:S(2)}) collective-permute-start(bf16[128,1408]{1,0:T(8,128)(2,1)S(1)} %concatenate.113), channel_id=1, source_target_pairs={{0,6},{1,7},{2,0},{3,1},{4,2},{5,3},{6,4},{7,5},{8,14},{9,15},{10,... | collective-permute-start | bytes 1081352 | tf_op jit(solution)/shard_map/ppermute | solution.py:597
  21.6 56.2 %collective-permute-start = (bf16[256,1024]{1,0:T(8,128)(2,1)S(1)}, bf16[256,1024]{1,0:T(8,128)(2,1)S(1)}, u32[]{:S(2)}, u32[]{:S(2)}) collective-permute-start(bf16[256,1024]{1,0:T(8,128)(2,1)S(1)} %bitcast.301), channel_id=1, source_target_pairs={{0,16},{8,24},{16,0},{24,8},{1,17},{9,25},{17,1},{25,9},{2,18},{10... | collective-permute-start | bytes 1572872 | tf_op jit(solution)/shard_map/ppermute | solution.py:594
  23.5 101.2 %copy-start.37 = (s32[9]{0:T(128)}, s32[9]{0:T(128)S(1)}, u32[]{:S(2)}) copy-start(s32[9]{0:T(128)S(1)} %pad_add_fusion.ends) | copy-start | bytes 112
  27.9 55.0 %copy-start.26 = (bf16[128,1408]{1,0:T(8,128)(2,1)}, bf16[128,1408]{1,0:T(8,128)(2,1)S(1)}, u32[]{:S(2)}) copy-start(bf16[128,1408]{1,0:T(8,128)(2,1)S(1)} %collective-permute-done.2) | copy-start | bytes 1081348
  27.9 60.5 %collective-permute-start.6 = (bf16[128,1408]{1,0:T(8,128)(2,1)S(1)}, bf16[128,1408]{1,0:T(8,128)(2,1)S(1)}, u32[]{:S(2)}, u32[]{:S(2)}) collective-permute-start(bf16[128,1408]{1,0:T(8,128)(2,1)S(1)} %collective-permute-done.2), channel_id=1, source_target_pairs={{0,1},{1,0},{2,3},{3,2},{4,5},{5,4},{6,7},{7,6},{8,9},{9,8},{10,11... | collective-permute-start | bytes 1081352 | tf_op jit(solution)/shard_map/ppermute | solution.py:594
  70.3 18.8 %collective-permute-start.7 = (bf16[128,1408]{1,0:T(8,128)(2,1)}, bf16[128,1408]{1,0:T(8,128)(2,1)}, u32[]{:S(2)}, u32[]{:S(2)}) collective-permute-start(bf16[128,1408]{1,0:T(8,128)(2,1)} %collective-permute-done.3), channel_id=1, source_target_pairs={{0,1},{1,0},{2,3},{3,2},{4,5},{5,4},{6,7},{7,6},{8,9},{9,8},{10,11... | collective-permute-start | bytes 1081352 | tf_op jit(solution)/shard_map/ppermute | solution.py:594
  77.6 14.4 %collective-permute-start.8 = (bf16[128,1408]{1,0:T(8,128)(2,1)}, bf16[128,1408]{1,0:T(8,128)(2,1)}, u32[]{:S(2)}, u32[]{:S(2)}) collective-permute-start(bf16[128,1408]{1,0:T(8,128)(2,1)} %collective-permute-done.4), channel_id=1, source_target_pairs={{0,1},{1,0},{2,3},{3,2},{4,5},{5,4},{6,7},{7,6},{8,9},{9,8},{10,11... | collective-permute-start | bytes 1081352 | tf_op jit(solution)/shard_map/ppermute | solution.py:594
  78.0 29.5 %collective-permute-start.5 = (bf16[128,1408]{1,0:T(8,128)(2,1)S(1)}, bf16[128,1408]{1,0:T(8,128)(2,1)}, u32[]{:S(2)}, u32[]{:S(2)}) collective-permute-start(bf16[128,1408]{1,0:T(8,128)(2,1)S(1)} %concatenate.113), channel_id=1, source_target_pairs={{0,1},{1,0},{2,3},{3,2},{4,5},{5,4},{6,7},{7,6},{8,9},{9,8},{10,11... | collective-permute-start | bytes 1081352 | tf_op jit(solution)/shard_map/ppermute | solution.py:594
  80.7 44.0 %copy-start.10 = (s32[1024,1]{1,0:T(8,128)}, s32[1024,1]{1,0:T(8,128)S(1)}, u32[]{:S(2)}) copy-start(s32[1024,1]{1,0:T(8,128)S(1)} %copy.133.seg_c) | copy-start | bytes 12292
  80.8 43.9 %copy-start.38 = (f32[6]{0:T(128)}, f32[6]{0:T(128)S(1)}, u32[]{:S(2)}) copy-start(f32[6]{0:T(128)S(1)} %dynamic_slice.140.skip) | copy-start | bytes 76
  80.9 36.5 %copy-start.36 = (f32[8,128]{1,0:T(8,128)}, f32[8,128]{1,0:T(8,128)S(1)}, u32[]{:S(2)}) copy-start(f32[8,128]{1,0:T(8,128)S(1)} %select_maximum_fusion.params) | copy-start | bytes 12292
  82.9 57.0 %collective-permute-start.11 = (bf16[256,1024]{1,0:T(8,128)(2,1)}, bf16[256,1024]{1,0:T(8,128)(2,1)}, u32[]{:S(2)}, u32[]{:S(2)}) collective-permute-start(bf16[256,1024]{1,0:T(8,128)(2,1)} %pad_maximum_fusion.10), channel_id=1, source_target_pairs={{0,0},{1,1},{2,8},{3,9},{4,16},{5,17},{6,24},{7,25},{8,2},{9,3},{1... | collective-permute-start | bytes 1572872 | tf_op jit(solution)/shard_map/ppermute | solution.py:606
  89.2 27.5 %collective-permute-start.1 = (bf16[2,256,1024]{2,1,0:T(8,128)(2,1)S(1)}, bf16[2,256,1024]{2,1,0:T(8,128)(2,1)S(1)}, u32[]{:S(2)}, u32[]{:S(2)}) collective-permute-start(bf16[2,256,1024]{2,1,0:T(8,128)(2,1)S(1)} %pad_maximum_fusion.3.refs_0_), channel_id=1, source_target_pairs={{0,8},{8,0},{16,24},{24,16},{1,9},{9,1},{17,25},{25,17},{2,10},{10... | collective-permute-start | bytes 3145736 | tf_op jit(solution)/shard_map/ppermute | solution.py:594
  124.6 19.4 %copy-start.7 = (bf16[1024,1024]{1,0:T(8,128)(2,1)}, bf16[1024,1024]{1,0:T(8,128)(2,1)S(1)}, u32[]{:S(2)}) copy-start(bf16[1024,1024]{1,0:T(8,128)(2,1)S(1)} %get-tuple-element.108.normed_ref) | copy-start | bytes 6291460
  124.6 19.5 %copy-start.31 = (f32[16,1024]{1,0:T(8,128)}, f32[16,1024]{1,0:T(8,128)S(1)}, u32[]{:S(2)}) copy-start(f32[16,1024]{1,0:T(8,128)S(1)} %get-tuple-element.106.rows) | copy-start | bytes 196612
  124.6 15.3 %copy-start.17 = (f32[1024,256]{1,0:T(8,128)S(1)}, f32[1024,256]{1,0:T(8,128)}, u32[]{:S(2)}) copy-start(f32[1024,256]{1,0:T(8,128)} %constant.365.clone.cosine) | copy-start | bytes 3145732
  139.9 126.4 %copy-start.2 = (f32[1024,384]{1,0:T(8,128)}, f32[1024,384]{1,0:T(8,128)S(1)}, u32[]{:S(2)}) copy-start(f32[1024,384]{1,0:T(8,128)S(1)} %get-tuple-element.107.y_ref) | copy-start | bytes 4718596
  139.9 15.6 %collective-permute-start.12 = (bf16[256,1024]{1,0:T(8,128)(2,1)}, bf16[256,1024]{1,0:T(8,128)(2,1)S(1)}, u32[]{:S(2)}, u32[]{:S(2)}) collective-permute-start(bf16[256,1024]{1,0:T(8,128)(2,1)} %collective-permute-done.11), channel_id=1, source_target_pairs={{0,1},{1,0},{2,3},{3,2},{4,5},{5,4},{6,7},{7,6},{8,9},{9,8},{10,11... | collective-permute-start | bytes 1572872 | tf_op jit(solution)/shard_map/ppermute | solution.py:594
  144.1 122.2 %copy-start.3 = (f32[1024,384]{1,0:T(8,128)}, f32[1024,384]{1,0:T(8,128)S(1)}, u32[]{:S(2)}) copy-start(f32[1024,384]{1,0:T(8,128)S(1)} %get-tuple-element.110.z_ref) | copy-start | bytes 4718596
  144.8 3.7 collective-permute-start.9
  148.5 7.0 %collective-permute-start.10 = (f32[16,128]{1,0:T(8,128)S(1)}, f32[16,128]{1,0:T(8,128)S(1)}, u32[]{:S(2)}, u32[]{:S(2)}) collective-permute-start(f32[16,128]{1,0:T(8,128)S(1)} %add.443), channel_id=1, source_target_pairs={{0,16},{8,24},{16,0},{24,8},{1,17},{9,25},{17,1},{25,9},{2,18},{10... | collective-permute-start | bytes 24584 | tf_op jit(solution)/shard_map/ppermute | solution.py:594
  164.1 3.3 collective-permute-start.13
  169.7 13.5 %collective-permute-start.14 = (bf16[256,1024]{1,0:T(8,128)(2,1)}, bf16[256,1024]{1,0:T(8,128)(2,1)}, u32[]{:S(2)}, u32[]{:S(2)}) collective-permute-start(bf16[256,1024]{1,0:T(8,128)(2,1)} %fusion.18), channel_id=1, source_target_pairs={{0,16},{8,24},{16,0},{24,8},{1,17},{9,25},{17,1},{25,9},{2,18},{10... | collective-permute-start | bytes 1572872 | tf_op jit(solution)/shard_map/ppermute | solution.py:594
  187.1 5.1 %collective-permute-start.15 = (bf16[256,1024]{1,0:T(8,128)(2,1)}, bf16[256,1024]{1,0:T(8,128)(2,1)}, u32[]{:S(2)}, u32[]{:S(2)}) collective-permute-start(bf16[256,1024]{1,0:T(8,128)(2,1)} %multiply_convert_fusion.5), channel_id=1, source_target_pairs={{0,8},{8,0},{16,24},{24,16},{1,9},{9,1},{17,25},{25,17},{2,10},{10... | collective-permute-start | bytes 1572872 | tf_op jit(solution)/shard_map/ppermute | solution.py:981
  198.6 2.0 collective-permute-start.16
  202.6 2.0 collective-permute-start.17
  209.0 2.0 collective-permute-start.18
  216.1 13.5 %collective-permute-start.19 = (bf16[256,1024]{1,0:T(8,128)(2,1)}, bf16[256,1024]{1,0:T(8,128)(2,1)}, u32[]{:S(2)}, u32[]{:S(2)}) collective-permute-start(bf16[256,1024]{1,0:T(8,128)(2,1)} %get-tuple-element.127), channel_id=1, source_target_pairs={{0,16},{8,24},{16,0},{24,8},{1,17},{9,25},{17,1},{25,9},{2,18},{10... | collective-permute-start | bytes 1572872 | tf_op jit(solution)/shard_map/ppermute | solution.py:594
  231.9 3.8 collective-permute-start.20
  241.5 3.6 collective-permute-start.21
  246.9 19.4 %collective-permute-start.23 = (bf16[256,1024]{1,0:T(8,128)(2,1)}, bf16[256,1024]{1,0:T(8,128)(2,1)}, u32[]{:S(2)}, u32[]{:S(2)}) collective-permute-start(bf16[256,1024]{1,0:T(8,128)(2,1)} %dynamic-slice_bitcast_fusion.2), channel_id=1, source_target_pairs={{0,1},{1,0},{2,3},{3,2},{4,5},{5,4},{6,7},{7,6},{8,9},{9,8},{10,11... | collective-permute-start | bytes 1572872 | tf_op jit(solution)/shard_map/ppermute | solution.py:594
  250.4 13.0 %collective-permute-start.22 = (f32[8,128]{1,0:T(8,128)S(1)}, f32[8,128]{1,0:T(8,128)S(1)}, u32[]{:S(2)}, u32[]{:S(2)}) collective-permute-start(f32[8,128]{1,0:T(8,128)S(1)} %bitcast_add_fusion), channel_id=1, source_target_pairs={{0,16},{8,24},{16,0},{24,8},{1,17},{9,25},{17,1},{25,9},{2,18},{10... | collective-permute-start | bytes 12296 | tf_op jit(solution)/shard_map/ppermute | solution.py:594
  272.1 46.5 %collective-permute-start.24 = (bf16[4,128,640]{2,1,0:T(8,128)(2,1)}, bf16[4,128,640]{2,1,0:T(8,128)(2,1)}, u32[]{:S(2)}, u32[]{:S(2)}) collective-permute-start(bf16[4,128,640]{2,1,0:T(8,128)(2,1)} %dynamic-slice_bitcast_fusion.1), channel_id=1, source_target_pairs={{0,1},{1,0},{2,3},{3,2},{4,5},{5,4},{6,7},{7,6},{8,9},{9,8},{10,11... | collective-permute-start | bytes 1966088 | tf_op jit(solution)/shard_map/ppermute | solution.py:594
  275.0 43.6 %collective-permute-start.25 = (bf16[64,1024]{1,0:T(8,128)(2,1)S(1)}, bf16[64,1024]{1,0:T(8,128)(2,1)}, u32[]{:S(2)}, u32[]{:S(2)}) collective-permute-start(bf16[64,1024]{1,0:T(8,128)(2,1)S(1)} %get-tuple-element.304), channel_id=1, source_target_pairs={{0,2},{1,3},{2,4},{3,5},{4,6},{5,7},{6,0},{7,1},{8,10},{9,11},{10,... | collective-permute-start | bytes 393224 | tf_op jit(solution)/shard_map/ppermute | solution.py:597
  276.4 42.2 %collective-permute-start.26 = (bf16[64,1024]{1,0:T(8,128)(2,1)S(1)}, bf16[64,1024]{1,0:T(8,128)(2,1)}, u32[]{:S(2)}, u32[]{:S(2)}) collective-permute-start(bf16[64,1024]{1,0:T(8,128)(2,1)S(1)} %get-tuple-element.303), channel_id=1, source_target_pairs={{0,4},{1,5},{2,6},{3,7},{4,0},{5,1},{6,2},{7,3},{8,12},{9,13},{10,... | collective-permute-start | bytes 393224 | tf_op jit(solution)/shard_map/ppermute | solution.py:597
  278.3 40.4 %collective-permute-start.27 = (bf16[64,1024]{1,0:T(8,128)(2,1)S(1)}, bf16[64,1024]{1,0:T(8,128)(2,1)}, u32[]{:S(2)}, u32[]{:S(2)}) collective-permute-start(bf16[64,1024]{1,0:T(8,128)(2,1)S(1)} %get-tuple-element.302), channel_id=1, source_target_pairs={{0,6},{1,7},{2,0},{3,1},{4,2},{5,3},{6,4},{7,5},{8,14},{9,15},{10,... | collective-permute-start | bytes 393224 | tf_op jit(solution)/shard_map/ppermute | solution.py:597
  279.7 38.7 %copy-start.23 = (bf16[1024,256]{1,0:T(8,128)(2,1)S(1)}, bf16[1024,256]{1,0:T(8,128)(2,1)}, u32[]{:S(2)}) copy-start(bf16[1024,256]{1,0:T(8,128)(2,1)} %copy-done.22) | copy-start | bytes 1572868
  279.7 38.7 %copy-start.61 = (bf16[1024,384]{1,0:T(8,128)(2,1)S(1)}, bf16[1024,384]{1,0:T(8,128)(2,1)}, u32[]{:S(2)}) copy-start(bf16[1024,384]{1,0:T(8,128)(2,1)} %copy-done.60) | copy-start | bytes 2359300
  328.2 35.2 %collective-permute-start.28 = (bf16[4,144,768]{2,1,0:T(8,128)(2,1)S(1)}, bf16[4,144,768]{2,1,0:T(8,128)(2,1)S(1)}, u32[]{:S(2)}, u32[]{:S(2)}) collective-permute-start(bf16[4,144,768]{2,1,0:T(8,128)(2,1)S(1)} %dynamic-slice_bitcast_fusion), channel_id=1, source_target_pairs={{0,1},{1,0},{2,3},{3,2},{4,5},{5,4},{6,7},{7,6},{8,9},{9,8},{10,11... | collective-permute-start | bytes 2654216 | tf_op jit(solution)/shard_map/ppermute | solution.py:594
  329.7 6.8 %collective-permute-start.29 = (bf16[128,640]{1,0:T(8,128)(2,1)S(1)}, bf16[128,640]{1,0:T(8,128)(2,1)S(1)}, u32[]{:S(2)}, u32[]{:S(2)}) collective-permute-start(bf16[128,640]{1,0:T(8,128)(2,1)S(1)} %get-tuple-element.300), channel_id=1, source_target_pairs={{0,2},{1,3},{2,4},{3,5},{4,6},{5,7},{6,0},{7,1},{8,10},{9,11},{10,... | collective-permute-start | bytes 491528 | tf_op jit(solution)/shard_map/ppermute | solution.py:597
  329.8 12.9 %collective-permute-start.30 = (bf16[128,640]{1,0:T(8,128)(2,1)S(1)}, bf16[128,640]{1,0:T(8,128)(2,1)S(1)}, u32[]{:S(2)}, u32[]{:S(2)}) collective-permute-start(bf16[128,640]{1,0:T(8,128)(2,1)S(1)} %get-tuple-element.299), channel_id=1, source_target_pairs={{0,4},{1,5},{2,6},{3,7},{4,0},{5,1},{6,2},{7,3},{8,12},{9,13},{10,... | collective-permute-start | bytes 491528 | tf_op jit(solution)/shard_map/ppermute | solution.py:597
  332.0 31.4 %collective-permute-start.31 = (bf16[128,640]{1,0:T(8,128)(2,1)S(1)}, bf16[128,640]{1,0:T(8,128)(2,1)S(1)}, u32[]{:S(2)}, u32[]{:S(2)}) collective-permute-start(bf16[128,640]{1,0:T(8,128)(2,1)S(1)} %get-tuple-element.298), channel_id=1, source_target_pairs={{0,6},{1,7},{2,0},{3,1},{4,2},{5,3},{6,4},{7,5},{8,14},{9,15},{10,... | collective-permute-start | bytes 491528 | tf_op jit(solution)/shard_map/ppermute | solution.py:597
  332.0 4.5 collective-permute-start.32
  336.5 31.5 %copy-start.43 = (f32[1024,1024]{1,0:T(8,128)}, f32[1024,1024]{1,0:T(8,128)S(1)}, u32[]{:S(2)}) copy-start(f32[1024,1024]{1,0:T(8,128)S(1)} %convolution_add_fusion.1) | copy-start | bytes 12582916
  363.8 4.2 collective-permute-start.36
  368.2 21.8 %collective-permute-start.37 = (bf16[256,1024]{1,0:T(8,128)(2,1)S(1)}, bf16[256,1024]{1,0:T(8,128)(2,1)}, u32[]{:S(2)}, u32[]{:S(2)}) collective-permute-start(bf16[256,1024]{1,0:T(8,128)(2,1)S(1)} %fusion.15), channel_id=1, source_target_pairs={{0,16},{8,24},{16,0},{24,8},{1,17},{9,25},{17,1},{25,9},{2,18},{10... | collective-permute-start | bytes 1572872 | tf_op jit(solution)/shard_map/ppermute | solution.py:594
  378.7 12.9 %collective-permute-start.33 = (bf16[144,768]{1,0:T(8,128)(2,1)}, bf16[144,768]{1,0:T(8,128)(2,1)}, u32[]{:S(2)}, u32[]{:S(2)}) collective-permute-start(bf16[144,768]{1,0:T(8,128)(2,1)} %get-tuple-element.290), channel_id=1, source_target_pairs={{0,2},{1,3},{2,4},{3,5},{4,6},{5,7},{6,0},{7,1},{8,10},{9,11},{10,... | collective-permute-start | bytes 663560 | tf_op jit(solution)/shard_map/ppermute | solution.py:597
  378.7 19.0 %collective-permute-start.34 = (bf16[144,768]{1,0:T(8,128)(2,1)}, bf16[144,768]{1,0:T(8,128)(2,1)}, u32[]{:S(2)}, u32[]{:S(2)}) collective-permute-start(bf16[144,768]{1,0:T(8,128)(2,1)} %get-tuple-element.289), channel_id=1, source_target_pairs={{0,4},{1,5},{2,6},{3,7},{4,0},{5,1},{6,2},{7,3},{8,12},{9,13},{10,... | collective-permute-start | bytes 663560 | tf_op jit(solution)/shard_map/ppermute | solution.py:597
  382.2 18.6 %collective-permute-start.35 = (bf16[144,768]{1,0:T(8,128)(2,1)}, bf16[144,768]{1,0:T(8,128)(2,1)}, u32[]{:S(2)}, u32[]{:S(2)}) collective-permute-start(bf16[144,768]{1,0:T(8,128)(2,1)} %get-tuple-element.288), channel_id=1, source_target_pairs={{0,6},{1,7},{2,0},{3,1},{4,2},{5,3},{6,4},{7,5},{8,14},{9,15},{10,... | collective-permute-start | bytes 663560 | tf_op jit(solution)/shard_map/ppermute | solution.py:597
  382.7 22.4 %copy-start.50 = (bf16[1,256,1024]{2,1,0:T(8,128)(2,1)S(1)}, bf16[1,256,1024]{2,1,0:T(8,128)(2,1)}, u32[]{:S(2)}) copy-start(bf16[1,256,1024]{2,1,0:T(8,128)(2,1)} %param.21) | copy-start | bytes 1572868
  403.0 17.9 %collective-permute-start.40 = (bf16[384,1024]{1,0:T(8,128)(2,1)}, bf16[384,1024]{1,0:T(8,128)(2,1)}, u32[]{:S(2)}, u32[]{:S(2)}) collective-permute-start(bf16[384,1024]{1,0:T(8,128)(2,1)} %bitcast.337), channel_id=1, source_target_pairs={{0,16},{8,24},{16,0},{24,8},{1,17},{9,25},{17,1},{25,9},{2,18},{10... | collective-permute-start | bytes 2359304 | tf_op jit(solution)/shard_map/ppermute | solution.py:594
  403.0 29.7 %collective-permute-start.38 = (bf16[144,1920]{1,0:T(8,128)(2,1)}, bf16[144,1920]{1,0:T(8,128)(2,1)}, u32[]{:S(2)}, u32[]{:S(2)}) collective-permute-start(bf16[144,1920]{1,0:T(8,128)(2,1)} %pad_maximum_fusion.9), channel_id=1, source_target_pairs={{0,16},{8,24},{16,0},{24,8},{1,17},{9,25},{17,1},{25,9},{2,18},{10... | collective-permute-start | bytes 1658888 | tf_op jit(solution)/shard_map/ppermute | solution.py:594
  405.1 15.8 %copy-start.72 = (bf16[1,384,1024]{2,1,0:T(8,128)(2,1)S(1)}, bf16[1,384,1024]{2,1,0:T(8,128)(2,1)}, u32[]{:S(2)}) copy-start(bf16[1,384,1024]{2,1,0:T(8,128)(2,1)} %reduce-scatter.2.cloned.1.call-done) | copy-start | bytes 2359300
  405.4 31.1 %copy-start.59 = (f32[256,1024]{1,0:T(8,128)S(1)}, f32[256,1024]{1,0:T(8,128)}, u32[]{:S(2)}) copy-start(f32[256,1024]{1,0:T(8,128)} %get-tuple-element.267) | copy-start | bytes 3145732
  422.3 15.4 %collective-permute-start.41 = (bf16[384,1024]{1,0:T(8,128)(2,1)S(1)}, bf16[384,1024]{1,0:T(8,128)(2,1)S(1)}, u32[]{:S(2)}, u32[]{:S(2)}) collective-permute-start(bf16[384,1024]{1,0:T(8,128)(2,1)S(1)} %add_convert_fusion), channel_id=1, source_target_pairs={{0,8},{8,0},{16,24},{24,16},{1,9},{9,1},{17,25},{25,17},{2,10},{10... | collective-permute-start | bytes 2359304 | tf_op jit(solution)/shard_map/ppermute | solution.py:594
  434.1 6.0 %collective-permute-start.39 = (bf16[2,144,1920]{2,1,0:T(8,128)(2,1)S(1)}, bf16[2,144,1920]{2,1,0:T(8,128)(2,1)S(1)}, u32[]{:S(2)}, u32[]{:S(2)}) collective-permute-start(bf16[2,144,1920]{2,1,0:T(8,128)(2,1)S(1)} %pad_maximum_fusion.2.refs_0_), channel_id=1, source_target_pairs={{0,8},{8,0},{16,24},{24,16},{1,9},{9,1},{17,25},{25,17},{2,10},{10... | collective-permute-start | bytes 3317768 | tf_op jit(solution)/shard_map/ppermute | solution.py:594
  (74 other events, 316.4 us)
Sparse Core Ops, SparseCore 0:
  14.5 139.3 all-gather.2
  233.3 146.6 reduce-scatter.1

commit v3 on v2

--- a/solution.py
+++ b/solution.py
@@ -177,8 +177,30 @@
     return row, col, same, run_c, run_r, keep, tail
 
 
+def head_groups(heads):
+    return [tuple(range(g, min(g + 2, heads))) for g in range(0, heads, 2)]
+
+
+def by_lane(columns, group, size):
+    first = columns[:, group[0] : group[0] + 1]
+    if len(group) == 1:
+        return first
+    lane = lax.broadcasted_iota(jnp.int32, (columns.shape[0], size), 1)
+    return jnp.where(lane < HP, first, columns[:, group[1] : group[1] + 1])
+
+
+def stacked(values, group):
+    if len(group) == 1:
+        return values
+    lane = lax.broadcasted_iota(jnp.int32, values.shape, 1)
+    zero = jnp.zeros_like(values)
+    return jnp.concatenate(
+        [jnp.where(lane < HP, values, zero), jnp.where(lane < HP, zero, values)], axis=0
+    )
+
+
 def ssm_fwd_kernel(
-    heads, ends, skip, act, steps, rows, seg_c, seg_r, y_ref, st_ref, state
+    heads, ends, skip, act, steps, rows, seg_c, seg_r, y_ref, st_ref, state, weighted
 ):
     step = pl.program_id(0)
 
@@ -195,20 +217,33 @@
     b_in = act[:, width : width + NS]
     c_in = act[:, width + NS : width + 2 * NS]
     gram = nt(c_in, b_in)
+    last = run_c[SPAN - 1 :, :]
+    carry_w = jnp.exp(run_c) * keep
+    end_w = jnp.exp(last - run_c) * tail * steps[:, :128]
+    prior = state[...]
+    st_ref[0] = prior
+    from_state = nt(c_in, prior.astype(BF16))
+    for group in head_groups(heads):
+        size = len(group) * HP
+        lanes = slice(group[0] * HP, group[0] * HP + size)
+        x_in = act[:, lanes]
+        x_wide = x_in.astype(F32)
+        mixing = []
+        for h in group:
+            decay = jnp.where(same, jnp.exp(run_c[:, h : h + 1] - run_r[h : h + 1, :]), 0.0)
+            mixing.append((gram * decay * rows[h : h + 1, :]).astype(BF16))
+        y_in = nn(jnp.concatenate(mixing, axis=1), stacked(x_in, group))
+        skips = [skip[h] for h in group]
+        lane = lax.broadcasted_iota(jnp.int32, (1, size), 1)
+        skip_w = jnp.where(lane < HP, skips[0], skips[-1])
+        y_ref[:, lanes] = (
+            y_in + from_state[:, lanes] * by_lane(carry_w, group, size) + skip_w * x_wide
+        )
+        weighted[:, lanes] = (x_wide * by_lane(end_w, group, size)).astype(BF16)
+    local = tn(weighted[...], b_in)
     for h in range(heads):
-        lanes = slice(h * HP, (h + 1) * HP)
-        x_in = act[:, lanes]
-        own_c = run_c[:, h : h + 1]
-        last = own_c[SPAN - 1 :, :]
-        decay = jnp.where(same, jnp.exp(own_c - run_r[h : h + 1, :]), 0.0)
-        mixing = (gram * decay * rows[h : h + 1, :]).astype(BF16)
-        prior = state[h]
-        st_ref[0, h] = prior
-        x_wide = x_in.astype(F32)
-        y_out = nn(mixing, x_in) + nt(c_in, prior.astype(BF16)) * (jnp.exp(own_c) * keep)
-        y_ref[:, lanes] = y_out + skip[h] * x_wide
-        weight = jnp.exp(last - own_c) * tail * steps[:, h : h + 1]
-        state[h] = (jnp.exp(last) * link) * prior + tn((x_wide * weight).astype(BF16), b_in)
+        part = slice(h * HP, (h + 1) * HP)
+        state[part, :] = (jnp.exp(last[:, h : h + 1]) * link) * prior[part, :] + local[part, :]
 
 
 def ssm_bwd_kernel(
@@ -237,8 +272,9 @@
     gstep_ref,
     gstate,
     gbuf,
-    gcol,
     grow,
+    carried,
+    ended,
 ):
     step = pl.num_programs(0) - 1 - pl.program_id(0)
     width = heads * HP
@@ -248,7 +284,6 @@
     def _():
         gstate[...] = jnp.zeros_like(gstate)
         gbuf[...] = jnp.zeros_like(gbuf)
-        gcol[...] = jnp.zeros_like(gcol)
         grow[...] = jnp.zeros_like(grow)
         gconv_ref[...] = jnp.zeros_like(gconv_ref)
         gwide_ref[...] = jnp.zeros_like(gwide_ref)
@@ -260,65 +295,87 @@
         seg_c[...], seg_r[...], steps[:, 128:], rows[8:16, :], before, end
     )
     gate = z_ref[...]
-    sig = jax.nn.sigmoid(gate)
-    silu = gate * sig
-    y_all = y_ref[...]
-    gated = y_all * silu
-    scale = stat_ref[:, 0:1]
-    g_ym = gym_ref[...]
-    g_gated = scale * (g_ym * gain_ref[...]) - gated * stat_ref[:, 1:2]
+    silu = gate * jax.nn.sigmoid(gate)
+    gated = y_ref[...] * silu
+    g_gated = stat_ref[:, 0:1] * (gym_ref[...] * gain_ref[...]) - gated * stat_ref[:, 1:2]
     g_all = g_gated * silu
-    gwide_ref[0:1, :] += jnp.sum(g_all * act[:, :width].astype(F32), axis=0, keepdims=True)
+    x_all = act[:, :width].astype(F32)
+    gwide_ref[0:1, :] += jnp.sum(g_all * x_all, axis=0, keepdims=True)
 
     b_in = act[:, width : width + NS]
     c_in = act[:, width + NS : width + 2 * NS]
     gram = nt(c_in, b_in)
+    last = run_c[SPAN - 1 :, :]
+    carry_w = jnp.exp(run_c) * keep
+    tail_w = jnp.exp(last - run_c) * tail
+    end_w = tail_w * steps[:, :128]
+    prior = st_ref[0]
+    prior_low = prior.astype(BF16)
+    after = gstate[...]
+    after_low = after.astype(BF16)
+    from_prior = nt(c_in, prior_low)
+    from_after = nt(b_in, after_low)
     g_gram = jnp.zeros((SPAN, SPAN), F32)
-    g_b = jnp.zeros((SPAN, NS), F32)
-    g_c = jnp.zeros((SPAN, NS), F32)
-    at_last = lax.broadcasted_iota(jnp.int32, (SPAN, 1), 0) == SPAN - 1
+    row_sums = jnp.zeros((SPAN, SPAN), F32)
+    for group in head_groups(heads):
+        size = len(group) * HP
+        lanes = slice(group[0] * HP, group[0] * HP + size)
+        gy = g_all[:, lanes]
+        gy_parts = stacked(gy.astype(BF16), group)
+        g_mixes = nt(gy_parts, act[:, lanes])
+        mixing = []
+        for i, h in enumerate(group):
+            dt_row = rows[h : h + 1, :]
+            decay = jnp.where(same, jnp.exp(run_c[:, h : h + 1] - run_r[h : h + 1, :]), 0.0)
+            mixing.append((gram * decay * dt_row).astype(BF16))
+            g_mix = g_mixes[i * SPAN : (i + 1) * SPAN, :] * decay
+            g_gram_h = g_mix * dt_row
+            g_gram = g_gram + g_gram_h
+            sums = jnp.sum(g_gram_h * gram, axis=1, keepdims=True)
+            row_sums = jnp.where(col == h, sums, row_sums)
+            by_key = jnp.sum(g_mix * gram, axis=0, keepdims=True)
+            grow[h : h + 1, :] = by_key * dt_row
+            grow[128 + h : 128 + h + 1, :] = by_key
+        skips = [skip[h] for h in group]
+        lane = lax.broadcasted_iota(jnp.int32, (1, size), 1)
+        skip_w = jnp.where(lane < HP, skips[0], skips[-1])
+        end_l = by_lane(end_w, group, size)
+        gbuf[0:SPAN, lanes] = (
+            tn(jnp.concatenate(mixing, axis=0), gy_parts)
+            + from_after[:, lanes] * end_l
+            + skip_w * gy
+        )
+        carried[:, lanes] = (gy * by_lane(carry_w, group, size)).astype(BF16)
+        ended[:, lanes] = (x_all[:, lanes] * end_l).astype(BF16)
+    of_head = (
+        lax.broadcasted_iota(jnp.int32, (width, 128), 0) // HP
+        == lax.broadcasted_iota(jnp.int32, (width, 128), 1)
+    ).astype(BF16)
+
+    def head_sums(values):
+        high = values.astype(BF16)
+        return nn(high, of_head) + nn((values - high.astype(F32)).astype(BF16), of_head)
+
+    g_carry = head_sums(g_all * from_prior)
+    g_tail = head_sums(x_all * from_after)
+    state_sums = jnp.sum(after * prior, axis=1, keepdims=True)
+    of_head_t = (
+        lax.broadcasted_iota(jnp.int32, (width, 128), 0) // HP
+        == lax.broadcasted_iota(jnp.int32, (width, 128), 1)
+    )
+    state_sums = jnp.sum(jnp.where(of_head_t, state_sums, 0.0), axis=0, keepdims=True)
+    g_end = g_tail * end_w
+    g_link = jnp.exp(last) * link
+    total_last = jnp.sum(g_end, axis=0, keepdims=True) + g_link * state_sums
+    g_run = row_sums + g_carry * carry_w - g_end + jnp.where(row == SPAN - 1, total_last, 0.0)
+    weighted = carried[...]
+    g_gram_low = g_gram.astype(BF16)
+    gbuf[0:SPAN, width : width + NS] = nn(ended[...], after_low) + tn(g_gram_low, c_in)
+    gbuf[0:SPAN, width + NS :] = nn(weighted, prior_low) + nn(g_gram_low, b_in)
+    to_state = tn(weighted, c_in)
     for h in range(heads):
-        lanes = slice(h * HP, (h + 1) * HP)
-        x_in = act[:, lanes]
-        x_wide = x_in.astype(F32)
-        gy = g_all[:, lanes]
-        gy_low = gy.astype(BF16)
-        own_c = run_c[:, h : h + 1]
-        last = own_c[SPAN - 1 :, :]
-        dt_row = rows[h : h + 1, :]
-        decay = jnp.where(same, jnp.exp(own_c - run_r[h : h + 1, :]), 0.0)
-        prior = st_ref[0, h]
-        prior_low = prior.astype(BF16)
-        after = gstate[h]
-        after_low = after.astype(BF16)
-        carry_w = jnp.exp(own_c) * keep
-        tail_w = jnp.exp(last - own_c) * tail
-        end_w = tail_w * steps[:, h : h + 1]
-        mixing = (gram * decay * dt_row).astype(BF16)
-        g_mix = nt(gy_low, x_in) * decay
-        g_gram_h = g_mix * dt_row
-        g_gram = g_gram + g_gram_h
-        inner = g_gram_h * gram
-        from_state = nt(b_in, after_low)
-        gbuf[0:SPAN, lanes] = tn(mixing, gy_low) + from_state * end_w + skip[h] * gy
-        g_carry = jnp.sum(gy * nt(c_in, prior_low), axis=1, keepdims=True)
-        g_tail = jnp.sum(x_wide * from_state, axis=1, keepdims=True)
-        g_link = jnp.exp(last) * link
-        total_last = jnp.sum(g_tail * end_w, axis=0, keepdims=True) + g_link * jnp.sum(
-            jnp.sum(after * prior, axis=1, keepdims=True), axis=0, keepdims=True
-        )
-        g_run_c = jnp.sum(inner, axis=1, keepdims=True) + g_carry * carry_w - g_tail * end_w
-        gcol[:, h : h + 1] = g_run_c + jnp.where(at_last, total_last, 0.0)
-        gcol[:, 128 + h : 128 + h + 1] = g_tail * tail_w
-        grow[h : h + 1, :] = jnp.sum(inner, axis=0, keepdims=True)
-        grow[128 + h : 128 + h + 1, :] = jnp.sum(g_mix * gram, axis=0, keepdims=True)
-        weighted = (gy * carry_w).astype(BF16)
-        g_c = g_c + nn(weighted, prior_low)
-        g_b = g_b + nn((x_wide * end_w).astype(BF16), after_low)
-        gstate[h] = g_link * after + tn(weighted, c_in)
-    g_gram_low = g_gram.astype(BF16)
-    gbuf[0:SPAN, width : width + NS] = g_b + tn(g_gram_low, c_in)
-    gbuf[0:SPAN, width + NS :] = g_c + nn(g_gram_low, b_in)
+        part = slice(h * HP, (h + 1) * HP)
+        gstate[part, :] = g_link[:, h : h + 1] * after[part, :] + to_state[part, :]
 
     pre = pre_ref[...].astype(F32)
     sig = jax.nn.sigmoid(pre)
@@ -344,8 +401,8 @@
             left, right, (((1,), (1,)), ((), ())), precision=HIGH, preferred_element_type=F32
         )
 
-    g_loga = nn(later, gcol[:, :128], HIGH) - across(later, grow[:128, :])
-    g_dt = gcol[:, 128:] + across(eye, grow[128:, :]) - g_loga * params[1:2, :]
+    g_loga = nn(later, g_run, HIGH) - across(later, grow[:128, :])
+    g_dt = g_tail * tail_w + across(eye, grow[128:, :]) - g_loga * params[1:2, :]
     g_step = g_dt * (1.0 - jnp.exp(-steps[:, :128]))
     first_ref[:, conv:] = g_step.astype(BF16)
     gstep_ref[0:1, :] += jnp.sum(g_step, axis=0, keepdims=True)
@@ -375,13 +432,13 @@
         in_specs=ssm_specs(heads, lambda i: i),
         out_specs=[
             pl.BlockSpec((SPAN, width), lambda i: (i, 0)),
-            pl.BlockSpec((1, heads, HP, NS), lambda i: (i, 0, 0, 0)),
+            pl.BlockSpec((1, width, NS), lambda i: (i, 0, 0)),
         ],
         out_shape=[
             jax.ShapeDtypeStruct((length, width), F32),
-            jax.ShapeDtypeStruct((steps, heads, HP, NS), F32),
-        ],
-        scratch_shapes=[pltpu.VMEM((heads, HP, NS), F32)],
+            jax.ShapeDtypeStruct((steps, width, NS), F32),
+        ],
+        scratch_shapes=[pltpu.VMEM((width, NS), F32), pltpu.VMEM((SPAN, width), BF16)],
         compiler_params=pltpu.CompilerParams(vmem_limit_bytes=32 * 1024 * 1024),
         cost_estimate=pl.CostEstimate(
             flops=10**9, bytes_accessed=4 * 10**7, transcendentals=10**6
@@ -411,7 +468,7 @@
         grid=(steps,),
         in_specs=ssm_specs(heads, at)
         + [
-            pl.BlockSpec((1, heads, HP, NS), lambda i: (at(i), 0, 0, 0)),
+            pl.BlockSpec((1, width, NS), lambda i: (at(i), 0, 0)),
             part(width),
             part(width),
             part(width),
@@ -431,14 +488,15 @@
             jax.ShapeDtypeStruct((8, 128), F32),
         ],
         scratch_shapes=[
-            pltpu.VMEM((heads, HP, NS), F32),
+            pltpu.VMEM((width, NS), F32),
             pltpu.VMEM((SPAN + 8, conv), F32),
-            pltpu.VMEM((SPAN, 256), F32),
             pltpu.VMEM((256, SPAN), F32),
+            pltpu.VMEM((SPAN, width), BF16),
+            pltpu.VMEM((SPAN, width), BF16),
         ],
         compiler_params=pltpu.CompilerParams(vmem_limit_bytes=56 * 1024 * 1024),
         cost_estimate=pl.CostEstimate(
-            flops=3 * 10**9, bytes_accessed=10**8, transcendentals=10**6
+            flops=10**7, bytes_accessed=10**6, transcendentals=10**4
         ),
         name="ssm_backward",
     )(*inputs, states, gate_z, g_ym, ssm_y, stats, gain, pre, cin, up, taps, params)
@@ -560,12 +618,185 @@
         out_specs=full,
         out_shape=jax.ShapeDtypeStruct((length, slab), BF16),
         scratch_shapes=[pltpu.VMEM((length, slab), F32)],
-        compiler_params=pltpu.CompilerParams(vmem_limit_bytes=40 * 1024 * 1024),
+        compiler_params=pltpu.CompilerParams(vmem_limit_bytes=56 * 1024 * 1024),
         cost_estimate=pl.CostEstimate(
-            flops=3 * 10**9, bytes_accessed=3 * 10**7, transcendentals=10**6
+            flops=10**7, bytes_accessed=10**6, transcendentals=10**4
         ),
         name="attn_backward",
     )(*inputs, lse, g_out, cosine, sine)
+
+
+def ff_kernel(both, product, g_gate, g_up, gb, out):
+    rows = both.shape[1]
+    out[0, :rows] = tn(both[...], g_gate[...]).astype(BF16)
+    out[0, rows : 2 * rows] = tn(both[...], g_up[...]).astype(BF16)
+    out[0, 2 * rows :] = tn(product[...], gb[...]).astype(BF16)
+
+
+def ff_gradients(m, both, product, g_gate, g_up, gb):
+    tokens, dim = both.shape
+    rows, down = dim // m, product.shape[1] // m
+    full = pl.BlockSpec((tokens, dim), lambda i: (0, 0))
+    return pl.pallas_call(
+        ff_kernel,
+        grid=(m,),
+        in_specs=[
+            pl.BlockSpec((tokens, rows), lambda i: (0, i)),
+            pl.BlockSpec((tokens, down), lambda i: (0, i)),
+            full,
+            full,
+            full,
+        ],
+        out_specs=pl.BlockSpec((1, 2 * rows + down, dim), lambda i: (i, 0, 0)),
+        out_shape=jax.ShapeDtypeStruct((m, 2 * rows + down, dim), BF16),
+        compiler_params=pltpu.CompilerParams(vmem_limit_bytes=40 * 1024 * 1024),
+        cost_estimate=pl.CostEstimate(
+            flops=6 * tokens * dim * dim, bytes_accessed=10**7, transcendentals=0
+        ),
+        name="ff_gradients",
+    )(both, product, g_gate, g_up, gb)
+
+
+def row_totals(values):
+    ones = jnp.ones((8, values.shape[1]), F32)
+    return lax.dot_general(
+        ones, values, (((1,), (1,)), ((), ())), precision=HIGH, preferred_element_type=F32
+    )
+
+
+def finish_ff_kernel(core, own, mate, w_gate, w_up, gain, gate_ref, up_ref, down_ref, gain_ref):
+    rows = w_gate.shape[0]
+    tiles = own.shape[1] // 128
+    total = jnp.zeros((rows, 128), F32)
+    for half in range(2):
+        mine = core[0] == half
+
+        def pick(low, high, lanes, mine=mine):
+            return jnp.where(mine, own[low:high, lanes], mate[low:high, lanes]).astype(F32)
+
+        for f in range(tiles):
+            lanes = slice(f * 128, (f + 1) * 128)
+            to = slice((2 * f + half) * 128, (2 * f + half + 1) * 128)
+            gate_ref[:, to] = pick(0, rows, lanes)
+            up_ref[:, to] = pick(rows, 2 * rows, lanes)
+        down = down_ref.shape[0] // 2
+        down_ref[half * down : (half + 1) * down, :] = pick(2 * rows, 2 * rows + down, slice(None))
+    for t in range(2 * tiles):
+        lanes = slice(t * 128, (t + 1) * 128)
+        total = total + gate_ref[:, lanes] * w_gate[:, lanes].astype(F32)
+        total = total + up_ref[:, lanes] * w_up[:, lanes].astype(F32)
+    gain_ref[...] = row_totals(total) / gain[...]
+
+
+def finish_ff(core, own, mate, w_gate, w_up, gain):
+    shard, ff = w_gate.shape
+    down = own.shape[0] - 2 * shard
+    vmem = pl.BlockSpec(memory_space=pltpu.VMEM)
+    out = pl.pallas_call(
+        finish_ff_kernel,
+        in_specs=[pl.BlockSpec(memory_space=pltpu.SMEM)] + [vmem] * 5,
+        out_specs=[vmem] * 4,
+        out_shape=[
+            jax.ShapeDtypeStruct((shard, ff), F32),
+            jax.ShapeDtypeStruct((shard, ff), F32),
+            jax.ShapeDtypeStruct((2 * down, own.shape[1]), F32),
+            jax.ShapeDtypeStruct((8, shard), F32),
+        ],
+        compiler_params=pltpu.CompilerParams(vmem_limit_bytes=40 * 1024 * 1024),
+        name="finish_ff",
+    )(core.astype(jnp.int32)[None], own, mate, w_gate, w_up, gain.astype(F32)[None])
+    return out[0], out[1], out[2], out[3][0]
+
+
+def finish_kernel(
+    got,
+    w_in,
+    w_qkv,
+    w_out,
+    gain_in,
+    gain_m,
+    in_ref,
+    qkv_ref,
+    out_ref,
+    o_ref,
+    gain_in_ref,
+    gain_m_ref,
+    small_ref,
+    steps,
+):
+    count = got.shape[0]
+    shard = w_qkv.shape[0]
+    heads = MH // count
+    width = heads * HP
+    conv = width + 2 * NS
+    late = conv + 128
+    q_width = QH * HD // count
+    wide = count * width
+    steps[...] = jnp.zeros_like(steps)
+    shared = jnp.zeros((shard, 2 * NS), F32)
+    gain = jnp.zeros((1, shard), F32)
+    small = jnp.zeros((shard, 128), F32)
+    pairs = []
+
+    def lay(at, values, gain):
+        flat = jnp.transpose(values)
+        rows = slice(at, at + flat.shape[0])
+        in_ref[rows, :] = flat
+        return gain + jnp.sum(flat * w_in[rows, :].astype(F32), axis=0, keepdims=True)
+
+    for j in range(count):
+
+        def part(low, high, j=j):
+            return got[j, :shard, low:high].astype(F32)
+
+        gain = lay(j * width, part(late, late + width), gain)
+        gain = lay(wide + j * width, part(0, width), gain)
+        shared = shared + part(width, conv)
+        steps[:, j * heads : (j + 1) * heads] = part(conv, conv + heads)
+        at = late + width
+        qkv_ref[:, j * q_width : (j + 1) * q_width] = part(at, at + q_width)
+        pairs.append(part(at + q_width, at + q_width + 128))
+        at = at + q_width + 128
+        rows = got[j, : shard // 2, at:], got[j, shard // 2 :, at:]
+        rows = jnp.concatenate(rows, axis=1).astype(F32)
+        low = j * (shard // 2)
+        if low < out_ref.shape[0]:
+            out_ref[low : low + shard // 2, :] = rows
+        else:
+            low -= out_ref.shape[0]
+            o_ref[low : low + shard // 2, :] = rows
+        small = small + part(conv, late)
+    gain = lay(2 * wide, shared, gain)
+    at = 2 * wide + 2 * NS
+    flat = jnp.transpose(steps[...])[: in_ref.shape[0] - at, :]
+    in_ref[at:, :] = flat
+    gain = gain + jnp.sum(flat * w_in[at:, :].astype(F32), axis=0, keepdims=True)
+    one, two = pairs[0] + pairs[1], pairs[2] + pairs[3]
+    low = lax.broadcasted_iota(jnp.int32, one.shape, 1) < HD
+    at = QH * HD
+    qkv_ref[:, at : at + 128] = jnp.where(low, one, pltpu.roll(two, HD, 1))
+    qkv_ref[:, at + 128 :] = jnp.where(low, pltpu.roll(one, HD, 1), two)
+    gain = row_totals(qkv_ref[...] * w_qkv[...].astype(F32)) + gain
+    gain_in_ref[...] = gain / gain_in[...]
+    gain_m_ref[...] = row_totals(out_ref[...] * w_out[...].astype(F32)) / gain_m[...]
+    small_ref[...] = jnp.transpose(small)
+
+
+def finish(got, w_in, w_qkv, w_out, w_o, gain_in, gain_m):
+    shard = w_qkv.shape[0]
+    vmem = pl.BlockSpec(memory_space=pltpu.VMEM)
+    shapes = [w_in.shape[::-1], w_qkv.shape, w_out.shape, w_o.shape]
+    shapes += [(8, shard), (8, w_out.shape[0]), (128, shard)]
+    out = pl.pallas_call(
+        finish_kernel,
+        in_specs=[vmem] * 6,
+        out_specs=[vmem] * 7,
+        out_shape=[jax.ShapeDtypeStruct(shape, F32) for shape in shapes],
+        scratch_shapes=[pltpu.VMEM((shard, 128), F32)],
+        compiler_params=pltpu.CompilerParams(vmem_limit_bytes=40 * 1024 * 1024),
+        name="finish",
+    )(got, w_in.T, w_qkv, w_out, gain_in.astype(F32)[None], gain_m.astype(F32)[None])
+    return out[0].T, out[1], out[2], out[3], out[4][0], out[5][0], out[6]
 
 
 def tie(value, *after):
@@ -668,13 +899,8 @@
         return half(self.x) + across.astype(F32)
 
     def over_cores(self, value):
-        if not self.direct:
-            value = lax.psum(value, "ctx", axis_index_groups=self.by_core)
-            return lax.all_gather(value, "ctx", axis=0)[:2].astype(F32)
-        value = (value.astype(F32) + self.flip(value, "ctx", 2).astype(F32)).astype(BF16)
-        mate = self.flip(value, "ctx", 1)
-        pair = jnp.stack([value, mate]).astype(F32)
-        return jnp.where(self.core == 0, pair, pair[::-1])
+        value = lax.psum(value, "ctx", axis_index_groups=self.by_core)
+        return lax.all_gather(value, "ctx", axis=0)[:2].astype(F32)
 
     def rows_out(self, shard):
         per = self.m // self.n
@@ -868,15 +1094,24 @@
         w = w.reshape(shard, m, 2, ff_half)
         return lax.dynamic_index_in_dim(w, net.core, 2, False).reshape(shard, size)
 
+    places_x = n // 2
+
+    def quarter_x(w):
+        size = w.shape[0] // places_x
+        return lax.dynamic_slice_in_dim(w, net.x * size, size, 0)
+
     w_ff = jnp.concatenate(
         [
-            ff_cut(w_gate).reshape(-1, dim),
-            ff_cut(w_up).reshape(-1, dim),
-            lax.dynamic_slice_in_dim(w_down, net.core * ff_half, ff_half, 0),
+            quarter_x(ff_cut(w_gate).reshape(-1, dim)),
+            quarter_x(ff_cut(w_up).reshape(-1, dim)),
+            quarter_x(lax.dynamic_slice_in_dim(w_down, net.core * ff_half, ff_half, 0)),
         ],
         axis=0,
     )
-    w_ff = lax.all_gather(w_ff, "fsdp", axis=0, tiled=False)
+    groups = [[d * m + i for d in net.by_core[k] for i in range(m)] for k in range(2)]
+    w_ff = lax.all_gather(
+        w_ff, ("ctx", "fsdp"), axis=0, tiled=False, axis_index_groups=groups
+    ).reshape((places_x, m) + w_ff.shape)
     if net.direct:
         both_cols = jnp.concatenate([first, second], axis=1)
         pair = jnp.stack([tokens[0], net.flip_x(tokens[0])])
@@ -972,9 +1207,14 @@
     mixed = tokens[0].astype(F32) + net.ctx_collect(outs.reshape(n, rows, dim))
 
     ff_rows = shard * size // dim
-    w_g = w_ff[:, :ff_rows].reshape(dim, size)
-    w_u = w_ff[:, ff_rows : 2 * ff_rows].reshape(dim, size)
-    w_d = w_ff[:, 2 * ff_rows :].reshape(size, dim)
+    part_rows = ff_rows // places_x
+
+    def ff_part(low, high, columns):
+        return jnp.swapaxes(w_ff[:, :, low:high], 0, 1).reshape(-1, columns)
+
+    w_g = ff_part(0, part_rows, size)
+    w_u = ff_part(part_rows, 2 * part_rows, size)
+    w_d = ff_part(2 * part_rows, w_ff.shape[2], dim)
     scale2 = rms_scale(mixed)
     normed2 = (mixed * scale2 * gain_second).astype(BF16)
     mate = [(i, i ^ 1) for i in range(n)]
@@ -995,14 +1235,10 @@
     g_prod = nt(gb_both, w_d)
     g_gate = (g_prod * up_v * (sig * (1.0 + gate_v * (1.0 - sig)))).astype(BF16)
     g_up = (g_prod * gate_v * sig).astype(BF16)
-    g_n2 = nt(g_gate, w_g) + nt(g_up, w_u)
-    from_mate = lax.ppermute(g_n2[rows:].astype(BF16), "ctx", mate)
-    grad_n2 = g_n2[:rows] + from_mate.astype(F32)
-    part = rms_back(mixed, gain_second, scale2, grad_n2)
-    grad_mixed = grad_out + part
-
-    def ff_weights(both, g_gate, g_up, product, gb_both):
-        return jnp.concatenate(
+    if net.direct:
+        g_ff = ff_gradients(m, both, product, g_gate, g_up, gb_both)
+    else:
+        g_ff = jnp.concatenate(
             [
                 tn(both, g_gate).reshape(m, ff_rows, dim),
                 tn(both, g_up).reshape(m, ff_rows, dim),
@@ -1010,16 +1246,13 @@
             ],
             axis=1,
         ).astype(BF16)
-
-    ff_args = (both, g_gate, g_up, product, gb_both)
-    gm = grad_mixed.astype(BF16)
-    if net.direct:
-        g_ff, (across,) = stage(ff_weights, ff_args, [(net.flip_x, gm)])
-        pair = jnp.stack([gm, across])
-        gm = put([pair, net.flip_core(pair)], [c, c ^ 2, c ^ 1, c ^ 3])
-    else:
-        gm = net.ctx_all(gm)
-        g_ff = ff_weights(*ff_args)
+    g_n2 = nt(tie(g_gate, g_ff), w_g) + nt(g_up, w_u)
+    from_mate = lax.ppermute(g_n2[rows:].astype(BF16), "ctx", mate)
+    grad_n2 = g_n2[:rows] + from_mate.astype(F32)
+    part = rms_back(mixed, gain_second, scale2, grad_n2)
+    grad_mixed = grad_out + part
+
+    gm = net.ctx_all(grad_mixed.astype(BF16))
     gm = gm.reshape(length, dim)
     g_ff = lax.psum_scatter(g_ff, "fsdp", scatter_dimension=0, tiled=False)
 
@@ -1048,9 +1281,8 @@
         inner = inner + got
         here = lax.dynamic_index_in_dim(g_outs, net.y, 0, False)
         away = lax.dynamic_index_in_dim(g_outs, 1 - net.y, 0, False)
-        g_qkv, (got_x, got) = stage(
-            attend_back, (qkv, g_ob), [(net.flip_x, inner), (net.flip_y, away)]
-        )
+        got = net.flip_y(away)
+        g_qkv, (got_x,) = stage(attend_back, (qkv, g_ob), [(net.flip_x, inner)])
         inner = inner + got_x
         out_both = plus(here, got).reshape(4, out_rows // 4, dim)
     else:
@@ -1115,12 +1347,15 @@
     laid = [jax.vmap(lay)(for_shards(g_conv[: KW + 1]))]
     laid.append(jnp.broadcast_to(lay(heads_grads)[None], (m, 4, 128)))
     laid = jnp.concatenate(laid, axis=1)
-    room = -laid.shape[1] % 16
-    laid = jnp.pad(laid, ((0, 0), (0, room), (0, conv_width)))
     late_size = conv_width + 128
-    grad_late = jnp.concatenate(
-        [tn(normed, g_late).reshape(m, shard, late_size).astype(BF16), laid.astype(BF16)], axis=1
-    )
+    grad_late = tn(normed, g_late).reshape(m, shard, late_size)
+    if net.direct:
+        laid = jnp.swapaxes(laid, 1, 2)
+        ends_at = conv_width + at_small
+        grad_late = jnp.concatenate(
+            [grad_late[..., :ends_at], laid, grad_late[..., ends_at + laid.shape[2] :]], axis=2
+        )
+    grad_late = grad_late.astype(BF16)
     resid = tokens[0].astype(F32)
 
     def normed_back(early, g_late):
@@ -1130,93 +1365,108 @@
         return grad_mixed + rms_back(resid, gain_input, rms_scale(resid), grad_normed)
 
     if net.direct:
+        g_normed = normed_back(early, g_late)
         here, away = net.halves_y(grad_late)
-        g_normed, (got, early_parts, out_quarter) = stage(
-            normed_back,
-            (early, g_late),
-            [(net.flip_y, away), (net.shifts_z, grad_early), (net.cross, out_quarter)],
-        )
-        grad_early = sum(p.astype(F32) for p in early_parts).astype(BF16)
-        _, (late_parts, grad_normed) = stage(
+        _, (grad_normed, got, early_parts) = stage(
             tuple,
             (),
-            [(net.shifts_z, plus(here, got)), (net.ctx_collect, g_normed)],
-        )
+            [
+                (net.ctx_collect, g_normed),
+                (net.flip_y, away),
+                (net.shifts_z, grad_early),
+            ],
+        )
+        grad_early = sum(p.astype(F32) for p in early_parts).astype(BF16)
+        grad_tokens, (late_parts, out_quarter, got_ff) = stage(
+            tokens_back,
+            (grad_normed,),
+            [
+                (net.shifts_z, plus(here, got)),
+                (net.cross, out_quarter),
+                (net.flip_x, g_ff),
+            ],
+        )
+        g_ff = plus(g_ff, got_ff)
         grad_late = sum(p.astype(F32) for p in late_parts).astype(BF16)
-        joined = jnp.concatenate([grad_early, out_quarter.reshape(shard, -1)], axis=1)
-        joined = jnp.pad(joined, ((0, grad_late.shape[0] - shard), (0, 0)))
+        joined = jnp.concatenate([out_quarter[:, : dim // 2], out_quarter[:, dim // 2 :]], axis=0)
+        joined = jnp.concatenate([grad_early, joined], axis=1)
         joined = jnp.concatenate([grad_late, joined], axis=1)
-        grad_tokens, (got, got_ff) = stage(
-            tokens_back, (grad_normed,), [(net.ctx_all, joined), (net.over_cores, g_ff)]
-        )
-        got_late = got[:, :, :late_size]
-        got = got[:, :shard, late_size:].astype(F32)
-        got_early = got[:, :, : width + slab]
-        out_outs = got[:, :, width + slab :].reshape(out_rows, dim)
+        got, got_ff = net.ctx_all(joined), net.flip_core(g_ff)
+        out_w_in, out_w_qkv, out_mamba, out_attn, out_gain_in, out_gain_m, totals = finish(
+            got, w_in, w_qkv, w_out, w_o, gain_in, gain_m
+        )
+        totals = totals[at_small : at_small + laid.shape[2]]
+        out_gate, out_up, out_down, out_gain_ffn = finish_ff(
+            net.core, g_ff, got_ff, w_gate, w_up, gain_ffn
+        )
     else:
         grad_tokens = tokens_back(net.ctx_collect(normed_back(early, g_late)))
         got_early = net.ctx_all(net.collect(grad_early)).astype(F32)
         got_late = net.ctx_all(net.collect(grad_late))
         out_outs = net.rows_back(g_outs).astype(F32)
         got_ff = net.over_cores(g_ff)
-    got_late = got_late.astype(F32)
-    totals = jnp.sum(got_late[:, shard:, :128], axis=0)
-    got_late = got_late[:, :shard]
+        got_late = got_late.astype(F32)
+        totals = lax.psum_scatter(laid, "fsdp", scatter_dimension=0, tiled=False)
+        totals = lax.psum(totals, "ctx")
+        def side(got, start, size):
+            return [got[j][:, start : start + size] for j in range(n)]
+
+        shared = n // KVH
+        out_w_in = jnp.concatenate(
+            side(got_early, 0, width)
+            + side(got_late, 0, width)
+            + [sum(side(got_late, width, 2 * NS))]
+            + side(got_late, conv_width, heads),
+            axis=1,
+        )
+        out_w_qkv = jnp.concatenate(
+            side(got_early, width, q_width)
+            + [
+                sum(side(got_early, width + q_width + i * HD, HD)[k * shared : (k + 1) * shared])
+                for i in range(2)
+                for k in range(KVH)
+            ],
+            axis=1,
+        )
+
+        def ff_wide(values):
+            values = values.reshape(2, shard, m, ff_half)
+            return jnp.transpose(values, (1, 2, 0, 3)).reshape(shard, ff)
+
+        out_gate = ff_wide(got_ff[:, :ff_rows])
+        out_up = ff_wide(got_ff[:, ff_rows : 2 * ff_rows])
+        out_mamba = out_outs[:mamba_rows]
+
+        def along(*pairs):
+            return sum(jnp.sum(w.astype(F32) * g, axis=1) for w, g in pairs)
+
+        out_attn = out_outs[mamba_rows:]
+        out_down = got_ff[:, 2 * ff_rows :].reshape(ff_shard, dim)
+        out_gain_in = along((w_in, out_w_in), (w_qkv, out_w_qkv)) / gain_in.astype(F32)
+        out_gain_m = along((w_out, out_mamba)) / gain_m.astype(F32)
+        out_gain_ffn = along((w_gate, out_gate), (w_up, out_up)) / gain_ffn.astype(F32)
     grad_conv = unlay(totals, 0, KW + 1, conv_b.shape[0])
     head_totals = totals[(KW + 1) * conv_rows : (KW + 1) * conv_rows + 4, :MH]
     loss = head_totals[3, 0] / (2.0 * count)
-
-    def side(got, start, size):
-        return [got[j][:, start : start + size] for j in range(n)]
-
-    shared = n // KVH
-    out_w_in = jnp.concatenate(
-        side(got_early, 0, width)
-        + side(got_late, 0, width)
-        + [sum(side(got_late, width, 2 * NS))]
-        + side(got_late, conv_width, heads),
-        axis=1,
-    )
-    out_w_qkv = jnp.concatenate(
-        side(got_early, width, q_width)
-        + [
-            sum(side(got_early, width + q_width + i * HD, HD)[k * shared : (k + 1) * shared])
-            for i in range(2)
-            for k in range(KVH)
-        ],
-        axis=1,
-    )
-
-    def ff_wide(values):
-        values = values.reshape(2, shard, m, ff_half)
-        return jnp.transpose(values, (1, 2, 0, 3)).reshape(shard, ff)
-
-    out_gate = ff_wide(got_ff[:, :ff_rows])
-    out_up = ff_wide(got_ff[:, ff_rows : 2 * ff_rows])
-    out_mamba = out_outs[:mamba_rows]
-
-    def along(*pairs):
-        return sum(jnp.sum(w.astype(F32) * g, axis=1) for w, g in pairs)
-
     return (
         loss,
         layer_out[None],
         grad_tokens[None],
-        along((w_in, out_w_in), (w_qkv, out_w_qkv)) / gain_in.astype(F32),
+        out_gain_in,
         out_w_in,
         grad_conv[:KW],
         grad_conv[KW],
         head_totals[0],
         head_totals[1],
         head_totals[2],
-        along((w_out, out_mamba)) / gain_m.astype(F32),
+        out_gain_m,
         out_mamba,
         out_w_qkv,
-        out_outs[mamba_rows:],
-        along((w_gate, out_gate), (w_up, out_up)) / gain_ffn.astype(F32),
+        out_attn,
+        out_gain_ffn,
         out_gate,
         out_up,
-        got_ff[:, 2 * ff_rows :].reshape(ff_shard, dim),
+        out_down,
     )
 
 

time: 493 us -> 421 us (0.85)
  the two profiles are of different devices: /device:TPU:13 before, /device:TPU:0 now
where the time goes in v3:
time: 421 us; the launch traced here: 413 us
  waiting for transfers between devices  130 us (31%)
  Pallas kernels  74.4 us (18%)
  local copies, waits for them, and re-layouts  63.3 us (15%)
  starting transfers between devices  63.1 us (15%)
  other arithmetic  34.4 us (8%)
  matrix products  29.3 us (7%)
  between operations  18.8 us (4%)
    ppermute x24, waiting for transfers between devices, flip(): return lax.ppermute(value, axis, [(i, i ^ bit) for i in range(size)])  68.9 us
    ppermute x12, waiting for transfers between devices, shift_z(): lax.ppermute(value, 'fsdp', [(i, (i + 2 * by) % self.m) for i in range(se...  46 us
    ppermute x24, starting transfers between devices, flip(): return lax.ppermute(value, axis, [(i, i ^ bit) for i in range(size)])  34.8 us
    unnamed x200, local copies, waits for them, and re-layouts  26.8 us
    ppermute x12, starting transfers between devices, shift_z(): lax.ppermute(value, 'fsdp', [(i, (i + 2 * by) % self.m) for i in range(se...  19.6 us
    pallas_call x1, Pallas kernels, ssm_backward(): pl.pallas_call(functools.partial(ssm_bwd_kernel, heads), grid=(steps,), i...  19.4 us
    dot_general x7, matrix products, nt(): lax.dot_general(left, right, (((1,), (1,)), ((), ())), preferred_element_...  14.1 us
    reduce_scatter x1, waiting for transfers between devices, per_device(): g_ff = lax.psum_scatter(g_ff, 'fsdp', scatter_dimension=0, tiled=False)  11.8 us
  transfers between devices with their start and end apart: 44, of which 21 were waited for; matrix products, arithmetic and copies ran while one was open for 18% of the time, Pallas kernels for 15%

profile of v3, /device:TPU:0, one launch (start us, length us, event | category | flops | bytes accessed | tf_op | source)
XLA Modules:
  0.0 413.3 jit_solution(672759909515615200)
XLA Ops:
  10.2 3.1 dynamic-slice_reduce_fusion
  17.1 3.1 collective-permute-start.2
  20.2 2.6 collective-permute-start.3
  26.3 6.0 %collective-permute-done.2 = bf16[128,1408]{1,0:T(8,128)(2,1)S(1)} collective-permute-done((bf16[128,1408]{1,0:T(8,128)(2,1)S(1)}, bf16[128,1408]{1,0:T(8,128)(2,1)S(1)}, u32[]{:S(2)}, u32[]{:S(2)}) %collective-permute-start.2) | collective-permute-done | bytes 360480 | tf_op jit(solution)/shard_map/ppermute | solution.py:828
  32.3 2.1 collective-permute-start.6
  34.3 19.7 %collective-permute-done.3 = bf16[128,1408]{1,0:T(8,128)(2,1)S(1)} collective-permute-done((bf16[128,1408]{1,0:T(8,128)(2,1)S(1)}, bf16[128,1408]{1,0:T(8,128)(2,1)S(1)}, u32[]{:S(2)}, u32[]{:S(2)}) %collective-permute-start.3) | collective-permute-done | bytes 360480 | tf_op jit(solution)/shard_map/ppermute | solution.py:828
  58.2 1.8 collective-permute-start.5
  62.5 1.8 pad_maximum_fusion.10
  64.2 5.5 %collective-permute-start.11 = (bf16[256,1024]{1,0:T(8,128)(2,1)}, bf16[256,1024]{1,0:T(8,128)(2,1)}, u32[]{:S(2)}, u32[]{:S(2)}) collective-permute-start(bf16[256,1024]{1,0:T(8,128)(2,1)} %pad_maximum_fusion.10), channel_id=1, source_target_pairs={{0,0},{1,1},{2,8},{3,9},{4,16},{5,17},{6,24},{7,25},{8,2},{9,3},{1... | collective-permute-start | bytes 1572872 | tf_op jit(solution)/shard_map/ppermute | solution.py:837
  70.5 3.8 collective-permute-start.1
  74.3 4.5 %collective-permute-done.8 = bf16[128,1408]{1,0:T(8,128)(2,1)} collective-permute-done((bf16[128,1408]{1,0:T(8,128)(2,1)S(1)}, bf16[128,1408]{1,0:T(8,128)(2,1)}, u32[]{:S(2)}, u32[]{:S(2)}) %collective-permute-start.8) | collective-permute-done | bytes 360480 | tf_op jit(solution)/shard_map/ppermute | solution.py:825
  78.8 6.7 %collective-permute-done.5 = bf16[128,1408]{1,0:T(8,128)(2,1)} collective-permute-done((bf16[128,1408]{1,0:T(8,128)(2,1)S(1)}, bf16[128,1408]{1,0:T(8,128)(2,1)}, u32[]{:S(2)}, u32[]{:S(2)}) %collective-permute-start.5) | collective-permute-done | bytes 360480 | tf_op jit(solution)/shard_map/ppermute | solution.py:825
  89.4 2.4 put.5
  95.4 2.8 put.4
  98.3 5.2 %project_conv.1 = (bf16[1024,1024]{1,0:T(8,128)(2,1)S(1)}, bf16[1024,640]{1,0:T(8,128)(2,1)S(1)}, bf16[1024,640]{1,0:T(8,128)(2,1)S(1)}, bf16[1024,640]{1,0:T(8,...) custom-call(bf16[1024,1024]{1,0:T(8,128)(2,1)S(1)} %bitcast.260, f32[1,1024]{1,0:T(1,128)S(1)} %bitcast.272, ...), custom_call_target="tpu_custom_call" | custom-call | flops 1610612736 | bytes 10000000 | tf_op jit(solution)/shard_map/project_conv/pallas_call | solution.py:100
  104.6 7.4 %ssm_forward.1 = (f32[1024,384]{1,0:T(8,128)S(1)}, f32[8,384,128]{2,1,0:T(8,128)S(1)}) custom-call(s32[9]{0:T(128)S(1)} %pad_add_fusion.1.ends, f32[6]{0:T(128)S(1)} %dynamic_slice.150.skip, bf16[1024,640]{1,0:T(8,128)(2,1)S(1)} %get-tuple-element.101.act, f32[1024,256]{1,0:T(8,128)S(1)} %get-tuple-element.102.steps, ...), custom_call_target="tpu_custom_call" | custom-call | flops 1000000000 | bytes 40000000 | tf_op jit(solution)/shard_map/ssm_forward/pallas_call | solution.py:429
  115.3 1.7 collective-permute-start.12
  117.0 4.1 project_gate.1
  124.5 5.7 %attn_forward.1 = (bf16[1024,128]{1,0:T(8,128)(2,1)S(1)}, f32[1024,2]{1,0:T(8,128)S(1)}) custom-call(bf16[1024,256]{1,0:T(8,128)(2,1)S(1)} %get-tuple-element.123.qkv_ref, s32[1024,1]{1,0:T(8,128)S(1)} %copy-done.6, s32[1,1024]{1,0:T(1,128)S(1)} %copy-done.26), custom_call_target="tpu_custom_call" | custom-call | flops 1000000000 | bytes 20000000 | tf_op jit(solution)/shard_map/attn_forward/pallas_call | solution.py:584
  130.2 10.4 %collective-permute-done.12 = bf16[256,1024]{1,0:T(8,128)(2,1)S(1)} collective-permute-done((bf16[256,1024]{1,0:T(8,128)(2,1)}, bf16[256,1024]{1,0:T(8,128)(2,1)S(1)}, u32[]{:S(2)}, u32[]{:S(2)}) %collective-permute-start.12) | collective-permute-done | bytes 524320 | tf_op jit(solution)/shard_map/ppermute | solution.py:825
  144.4 1.9 copy-done.51
  147.4 3.0 collective-permute-done.13
  150.4 2.3 fusion.16
  154.2 12.8 %collective-permute-done.14 = bf16[256,1024]{1,0:T(8,128)(2,1)} collective-permute-done((bf16[256,1024]{1,0:T(8,128)(2,1)}, bf16[256,1024]{1,0:T(8,128)(2,1)}, u32[]{:S(2)}, u32[]{:S(2)}) %collective-permute-start.14) | collective-permute-done | bytes 524320 | tf_op jit(solution)/shard_map/ppermute | solution.py:825
  167.0 2.0 multiply_reduce_fusion.2
  171.0 4.1 slice_bitcast_fusion.1
  176.7 2.5 fusion.32
  179.2 2.6 multiply_convert_fusion.2
  189.2 1.8 multiply_convert_fusion
  191.0 5.9 %ff_gradients.1 = bf16[8,384,1024]{2,1,0:T(8,128)(2,1)S(1)} custom-call(bf16[512,1024]{1,0:T(8,128)(2,1)S(1)} %pad_maximum_fusion.3.both, bf16[512,1024]{1,0:T(8,128)(2,1)S(1)} %get-tuple-element.244.product, bf16[512,1024]{1,0:T(8,128)(2,1)S(1)} %get-tuple-element.118.g_gate, bf16[512,1024]{1,0:T(8,128)(2,1)S(1)} %get-tuple-element.197.g_up, ...), custom_call_target="tpu_custom_call" | custom-call | flops 3221225472 | bytes 10000000 | tf_op jit(solution)/shard_map/ff_gradients/pallas_call | solution.py:640
  197.0 2.6 copy-done.3
  201.5 3.3 fusion.45
  208.8 1.8 collective-permute-done.18
  210.7 2.0 multiply_reduce_fusion.1
  212.7 3.4 fusion.36
  217.6 12.7 %collective-permute-done.19 = bf16[256,1024]{1,0:T(8,128)(2,1)S(1)} collective-permute-done((bf16[256,1024]{1,0:T(8,128)(2,1)S(1)}, bf16[256,1024]{1,0:T(8,128)(2,1)S(1)}, u32[]{:S(2)}, u32[]{:S(2)}) %collective-permute-start.19) | collective-permute-done | bytes 524320 | tf_op jit(solution)/shard_map/ppermute | solution.py:825
  231.4 3.0 collective-permute-done.20.refs_1_
  234.4 3.1 put.6
  237.5 2.6 multiply_reduce_fusion
  246.4 10.0 %attn_backward.1 = bf16[1024,256]{1,0:T(8,128)(2,1)} custom-call(bf16[1024,256]{1,0:T(8,128)(2,1)} %copy-done.23, s32[1024,1]{1,0:T(8,128)} %copy.187.seg_c, s32[1,1024]{1,0:T(1,128)} %seg_r.7, f32[1024,2]{1,0:T(8,128)} %copy-done.24, bf16[1024,128]{1,0:T(8,128)(2,1)} %convolution_convert_fusion.4.go_ref, f32[1024,256]{1,0:T(8,128)} %constant.374.clone.cosine, ...), custom_call_target="tpu_custom_call" | custom-call | flops 10000000 | bytes 1000000 | tf_op jit(solution)/shard_map/attn_backward/pallas_call | solution.py:608
  256.4 2.4 multiply_convert_fusion.3
  258.9 1.9 convolution_convert_fusion.1
  268.8 2.3 collective-permute-start.26
  273.1 19.4 %ssm_backward.1 = (bf16[1024,768]{1,0:T(8,128)(2,1)}, f32[8,640]{1,0:T(8,128)}, f32[8,384]{1,0:T(8,128)}, f32[8,128]{1,0:T(8,128)}) custom-call(s32[9]{0:T(128)} %copy-done.43, f32[6]{0:T(128)} %copy-done.44, bf16[1024,640]{1,0:T(8,128)(2,1)} %copy-done.21, f32[1024,256]{1,0:T(8,128)} %copy-done.22, f32[16,1024]{1,0:T(8,128)} %copy-done.37, ...), custom_call_target="tpu_custom_call" | custom-call | flops 10000000 | bytes 1000000 | tf_op jit(solution)/shard_map/ssm_backward/pallas_call | solution.py:466
  293.5 3.3 convolution_convert_fusion
  299.6 1.9 copy.220
  304.1 1.8 fusion.46
  305.9 1.8 convolution_add_fusion.1
  308.1 2.6 collective-permute-done.28
  314.1 2.7 collective-permute-start.33
  317.5 7.4 %collective-permute-done.29 = bf16[256,1024]{1,0:T(8,128)(2,1)S(1)} collective-permute-done((bf16[256,1024]{1,0:T(8,128)(2,1)S(1)}, bf16[256,1024]{1,0:T(8,128)(2,1)S(1)}, u32[]{:S(2)}, u32[]{:S(2)}) %collective-permute-start.29) | collective-permute-done | bytes 524320 | tf_op jit(solution)/shard_map/ppermute | solution.py:825
  325.3 10.6 %collective-permute-done.32 = bf16[128,640]{1,0:T(8,128)(2,1)S(1)} collective-permute-done((bf16[128,640]{1,0:T(8,128)(2,1)S(1)}, bf16[128,640]{1,0:T(8,128)(2,1)S(1)}, u32[]{:S(2)}, u32[]{:S(2)}) %collective-permute-start.32) | collective-permute-done | bytes 163872 | tf_op jit(solution)/shard_map/ppermute | solution.py:828
  337.8 11.8 %reduce-scatter.2.cloned.1.call-done = bf16[1,384,1024]{2,1,0:T(8,128)(2,1)} async-done(((bf16[8,384,1024]{2,1,0:T(8,128)(2,1)}), bf16[1,384,1024]{2,1,0:T(8,128)(2,1)}) %reduce-scatter.2.cloned.1.call-update) | async-done | bytes 786448 | tf_op jit(solution)/shard_map/reduce_scatter | solution.py:1257
  351.1 1.9 constant_dynamic-slice_fusion
  353.0 1.7 copy.209
  355.6 2.0 collective-permute-start.35
  358.4 1.8 collective-permute-start.36
  360.2 1.8 collective-permute-start.37
  364.7 8.5 %collective-permute-done.35 = bf16[128,768]{1,0:T(8,128)(2,1)} collective-permute-done((bf16[128,768]{1,0:T(8,128)(2,1)}, bf16[128,768]{1,0:T(8,128)(2,1)}, u32[]{:S(2)}, u32[]{:S(2)}) %collective-permute-start.35) | collective-permute-done | bytes 196640 | tf_op jit(solution)/shard_map/ppermute | solution.py:828
  374.6 9.8 %collective-permute-start.39 = (bf16[128,1920]{1,0:T(8,128)(2,1)S(1)}, bf16[128,1920]{1,0:T(8,128)(2,1)S(1)}, u32[]{:S(2)}, u32[]{:S(2)}) collective-permute-start(bf16[128,1920]{1,0:T(8,128)(2,1)S(1)} %get-tuple-element.214), channel_id=1, source_target_pairs={{0,16},{8,24},{16,0},{24,8},{1,17},{9,25},{17,1},{25,9},{2,18},{10... | collective-permute-start | bytes 1474568 | tf_op jit(solution)/shard_map/ppermute | solution.py:825
  385.9 5.3 %collective-permute-done.39 = bf16[128,1920]{1,0:T(8,128)(2,1)S(1)} collective-permute-done((bf16[128,1920]{1,0:T(8,128)(2,1)S(1)}, bf16[128,1920]{1,0:T(8,128)(2,1)S(1)}, u32[]{:S(2)}, u32[]{:S(2)}) %collective-permute-start.39) | collective-permute-done | bytes 491552 | tf_op jit(solution)/shard_map/ppermute | solution.py:825
  392.1 3.2 finish_ff.1
  395.9 2.8 put.7.got
  398.7 2.4 finish.1
  (427 shorter events, 99.5 us)
Async XLA Ops:
  7.2 163.8 %all-gather.3.cloned.1.call-start = ((), (), s32[]{:S(2)}) async-start(), calls=%async_computation.2 | async-start | bytes 6684672 | tf_op jit(solution)/shard_map/all_gather | solution.py:1112
  14.4 335.2 %reduce-scatter.2.cloned.1.call-start = ((), (), s32[]{:S(2)}) async-start(), calls=%async_computation.1 | async-start | bytes 7077888 | tf_op jit(solution)/shard_map/reduce_scatter | solution.py:1257
  16.7 44.4 %copy-start.93 = (f32[24]{0:T(128)S(1)}, f32[24]{0:T(128)}, u32[]{:S(2)}) copy-start(f32[24]{0:T(128)} %param.30) | copy-start | bytes 292
  16.9 45.3 %copy-start.94 = (f32[24]{0:T(128)S(1)}, f32[24]{0:T(128)}, u32[]{:S(2)}) copy-start(f32[24]{0:T(128)} %param.31) | copy-start | bytes 292
  16.9 45.5 %copy-start.88 = (f32[24]{0:T(128)S(1)}, f32[24]{0:T(128)}, u32[]{:S(2)}) copy-start(f32[24]{0:T(128)} %param.29) | copy-start | bytes 292
  16.9 45.5 %copy-start.15 = (bf16[192,1024]{1,0:T(8,128)(2,1)S(1)}, bf16[192,1024]{1,0:T(8,128)(2,1)}, u32[]{:S(2)}) copy-start(bf16[192,1024]{1,0:T(8,128)(2,1)} %w_out.1) | copy-start | bytes 1179652
  17.1 15.2 %collective-permute-start.2 = (bf16[128,1408]{1,0:T(8,128)(2,1)S(1)}, bf16[128,1408]{1,0:T(8,128)(2,1)S(1)}, u32[]{:S(2)}, u32[]{:S(2)}) collective-permute-start(bf16[128,1408]{1,0:T(8,128)(2,1)S(1)} %concatenate.111), channel_id=1, source_target_pairs={{0,2},{1,3},{2,4},{3,5},{4,6},{5,7},{6,0},{7,1},{8,10},{9,11},{10,... | collective-permute-start | bytes 1081352 | tf_op jit(solution)/shard_map/ppermute | solution.py:828
  20.2 33.9 %collective-permute-start.3 = (bf16[128,1408]{1,0:T(8,128)(2,1)S(1)}, bf16[128,1408]{1,0:T(8,128)(2,1)S(1)}, u32[]{:S(2)}, u32[]{:S(2)}) collective-permute-start(bf16[128,1408]{1,0:T(8,128)(2,1)S(1)} %concatenate.111), channel_id=1, source_target_pairs={{0,4},{1,5},{2,6},{3,7},{4,0},{5,1},{6,2},{7,3},{8,12},{9,13},{10,... | collective-permute-start | bytes 1081352 | tf_op jit(solution)/shard_map/ppermute | solution.py:828
  22.7 33.0 %collective-permute-start.4 = (bf16[128,1408]{1,0:T(8,128)(2,1)S(1)}, bf16[128,1408]{1,0:T(8,128)(2,1)S(1)}, u32[]{:S(2)}, u32[]{:S(2)}) collective-permute-start(bf16[128,1408]{1,0:T(8,128)(2,1)S(1)} %concatenate.111), channel_id=1, source_target_pairs={{0,6},{1,7},{2,0},{3,1},{4,2},{5,3},{6,4},{7,5},{8,14},{9,15},{10,... | collective-permute-start | bytes 1081352 | tf_op jit(solution)/shard_map/ppermute | solution.py:828
  24.1 32.0 %collective-permute-start = (bf16[256,1024]{1,0:T(8,128)(2,1)}, bf16[256,1024]{1,0:T(8,128)(2,1)S(1)}, u32[]{:S(2)}, u32[]{:S(2)}) collective-permute-start(bf16[256,1024]{1,0:T(8,128)(2,1)} %bitcast.282), channel_id=1, source_target_pairs={{0,16},{8,24},{16,0},{24,8},{1,17},{9,25},{17,1},{25,9},{2,18},{10... | collective-permute-start | bytes 1572872 | tf_op jit(solution)/shard_map/ppermute | solution.py:825
  26.2 78.4 %copy-start.43 = (s32[9]{0:T(128)}, s32[9]{0:T(128)S(1)}, u32[]{:S(2)}) copy-start(s32[9]{0:T(128)S(1)} %pad_add_fusion.1.ends) | copy-start | bytes 112
  32.3 31.9 %copy-start.29 = (bf16[128,1408]{1,0:T(8,128)(2,1)}, bf16[128,1408]{1,0:T(8,128)(2,1)S(1)}, u32[]{:S(2)}) copy-start(bf16[128,1408]{1,0:T(8,128)(2,1)S(1)} %collective-permute-done.2) | copy-start | bytes 1081348
  32.3 37.5 %collective-permute-start.6 = (bf16[128,1408]{1,0:T(8,128)(2,1)S(1)}, bf16[128,1408]{1,0:T(8,128)(2,1)S(1)}, u32[]{:S(2)}, u32[]{:S(2)}) collective-permute-start(bf16[128,1408]{1,0:T(8,128)(2,1)S(1)} %collective-permute-done.2), channel_id=1, source_target_pairs={{0,1},{1,0},{2,3},{3,2},{4,5},{5,4},{6,7},{7,6},{8,9},{9,8},{10,11... | collective-permute-start | bytes 1081352 | tf_op jit(solution)/shard_map/ppermute | solution.py:825
  54.1 20.3 %collective-permute-start.7 = (bf16[128,1408]{1,0:T(8,128)(2,1)S(1)}, bf16[128,1408]{1,0:T(8,128)(2,1)}, u32[]{:S(2)}, u32[]{:S(2)}) collective-permute-start(bf16[128,1408]{1,0:T(8,128)(2,1)S(1)} %collective-permute-done.3), channel_id=1, source_target_pairs={{0,1},{1,0},{2,3},{3,2},{4,5},{5,4},{6,7},{7,6},{8,9},{9,8},{10,11... | collective-permute-start | bytes 1081352 | tf_op jit(solution)/shard_map/ppermute | solution.py:825
  55.8 23.0 %collective-permute-start.8 = (bf16[128,1408]{1,0:T(8,128)(2,1)S(1)}, bf16[128,1408]{1,0:T(8,128)(2,1)}, u32[]{:S(2)}, u32[]{:S(2)}) collective-permute-start(bf16[128,1408]{1,0:T(8,128)(2,1)S(1)} %collective-permute-done.4), channel_id=1, source_target_pairs={{0,1},{1,0},{2,3},{3,2},{4,5},{5,4},{6,7},{7,6},{8,9},{9,8},{10,11... | collective-permute-start | bytes 1081352 | tf_op jit(solution)/shard_map/ppermute | solution.py:825
  58.2 27.3 %collective-permute-start.5 = (bf16[128,1408]{1,0:T(8,128)(2,1)S(1)}, bf16[128,1408]{1,0:T(8,128)(2,1)}, u32[]{:S(2)}, u32[]{:S(2)}) collective-permute-start(bf16[128,1408]{1,0:T(8,128)(2,1)S(1)} %concatenate.111), channel_id=1, source_target_pairs={{0,1},{1,0},{2,3},{3,2},{4,5},{5,4},{6,7},{7,6},{8,9},{9,8},{10,11... | collective-permute-start | bytes 1081352 | tf_op jit(solution)/shard_map/ppermute | solution.py:825
  62.3 42.3 %copy-start.44 = (f32[6]{0:T(128)}, f32[6]{0:T(128)S(1)}, u32[]{:S(2)}) copy-start(f32[6]{0:T(128)S(1)} %dynamic_slice.150.skip) | copy-start | bytes 76
  62.5 35.8 %copy-start.42 = (f32[8,128]{1,0:T(8,128)}, f32[8,128]{1,0:T(8,128)S(1)}, u32[]{:S(2)}) copy-start(f32[8,128]{1,0:T(8,128)S(1)} %select_maximum_fusion.params) | copy-start | bytes 12292
  64.2 51.0 %collective-permute-start.11 = (bf16[256,1024]{1,0:T(8,128)(2,1)}, bf16[256,1024]{1,0:T(8,128)(2,1)}, u32[]{:S(2)}, u32[]{:S(2)}) collective-permute-start(bf16[256,1024]{1,0:T(8,128)(2,1)} %pad_maximum_fusion.10), channel_id=1, source_target_pairs={{0,0},{1,1},{2,8},{3,9},{4,16},{5,17},{6,24},{7,25},{8,2},{9,3},{1... | collective-permute-start | bytes 1572872 | tf_op jit(solution)/shard_map/ppermute | solution.py:837
  70.5 24.9 %collective-permute-start.1 = (bf16[2,256,1024]{2,1,0:T(8,128)(2,1)S(1)}, bf16[2,256,1024]{2,1,0:T(8,128)(2,1)}, u32[]{:S(2)}, u32[]{:S(2)}) collective-permute-start(bf16[2,256,1024]{2,1,0:T(8,128)(2,1)S(1)} %pad_maximum_fusion.2.refs_0_), channel_id=1, source_target_pairs={{0,8},{8,0},{16,24},{24,16},{1,9},{9,1},{17,25},{25,17},{2,10},{10... | collective-permute-start | bytes 3145736 | tf_op jit(solution)/shard_map/ppermute | solution.py:825
  104.6 16.5 %copy-start.9 = (bf16[1024,1024]{1,0:T(8,128)(2,1)}, bf16[1024,1024]{1,0:T(8,128)(2,1)S(1)}, u32[]{:S(2)}) copy-start(bf16[1024,1024]{1,0:T(8,128)(2,1)S(1)} %get-tuple-element.105.normed_ref) | copy-start | bytes 6291460
  104.6 16.5 %copy-start.19 = (bf16[1024,640]{1,0:T(8,128)(2,1)}, bf16[1024,640]{1,0:T(8,128)(2,1)S(1)}, u32[]{:S(2)}) copy-start(bf16[1024,640]{1,0:T(8,128)(2,1)S(1)} %get-tuple-element.133.cin_ref) | copy-start | bytes 3932164
  104.6 16.5 %copy-start.37 = (f32[16,1024]{1,0:T(8,128)}, f32[16,1024]{1,0:T(8,128)S(1)}, u32[]{:S(2)}) copy-start(f32[16,1024]{1,0:T(8,128)S(1)} %get-tuple-element.103.rows) | copy-start | bytes 196612
  115.3 141.1 %copy-start.2 = (f32[1024,384]{1,0:T(8,128)}, f32[1024,384]{1,0:T(8,128)S(1)}, u32[]{:S(2)}) copy-start(f32[1024,384]{1,0:T(8,128)S(1)} %get-tuple-element.104.y_ref) | copy-start | bytes 4718596
  115.3 25.4 %collective-permute-start.12 = (bf16[256,1024]{1,0:T(8,128)(2,1)}, bf16[256,1024]{1,0:T(8,128)(2,1)S(1)}, u32[]{:S(2)}, u32[]{:S(2)}) collective-permute-start(bf16[256,1024]{1,0:T(8,128)(2,1)} %collective-permute-done.11), channel_id=1, source_target_pairs={{0,1},{1,0},{2,3},{3,2},{4,5},{5,4},{6,7},{7,6},{8,9},{9,8},{10,11... | collective-permute-start | bytes 1572872 | tf_op jit(solution)/shard_map/ppermute | solution.py:825
  121.1 21.0 %copy-start.23 = (bf16[1024,256]{1,0:T(8,128)(2,1)}, bf16[1024,256]{1,0:T(8,128)(2,1)S(1)}, u32[]{:S(2)}) copy-start(bf16[1024,256]{1,0:T(8,128)(2,1)S(1)} %get-tuple-element.123.qkv_ref) | copy-start | bytes 1572868
  121.1 21.1 %copy-start.4 = (f32[1024,384]{1,0:T(8,128)}, f32[1024,384]{1,0:T(8,128)S(1)}, u32[]{:S(2)}) copy-start(f32[1024,384]{1,0:T(8,128)S(1)} %get-tuple-element.107.z_ref) | copy-start | bytes 4718596
  121.8 1.2 collective-permute-start.9
  123.1 7.2 %collective-permute-start.10 = (f32[16,128]{1,0:T(8,128)S(1)}, f32[16,128]{1,0:T(8,128)S(1)}, u32[]{:S(2)}, u32[]{:S(2)}) collective-permute-start(f32[16,128]{1,0:T(8,128)S(1)} %add.419), channel_id=1, source_target_pairs={{0,16},{8,24},{16,0},{24,8},{1,17},{9,25},{17,1},{25,9},{2,18},{10... | collective-permute-start | bytes 24584 | tf_op jit(solution)/shard_map/ppermute | solution.py:825
  147.4 3.0 collective-permute-start.13
  152.7 14.3 %collective-permute-start.14 = (bf16[256,1024]{1,0:T(8,128)(2,1)}, bf16[256,1024]{1,0:T(8,128)(2,1)}, u32[]{:S(2)}, u32[]{:S(2)}) collective-permute-start(bf16[256,1024]{1,0:T(8,128)(2,1)} %fusion.16), channel_id=1, source_target_pairs={{0,16},{8,24},{16,0},{24,8},{1,17},{9,25},{17,1},{25,9},{2,18},{10... | collective-permute-start | bytes 1572872 | tf_op jit(solution)/shard_map/ppermute | solution.py:825
  171.0 4.9 %collective-permute-start.15 = (bf16[256,1024]{1,0:T(8,128)(2,1)}, bf16[256,1024]{1,0:T(8,128)(2,1)}, u32[]{:S(2)}, u32[]{:S(2)}) collective-permute-start(bf16[256,1024]{1,0:T(8,128)(2,1)} %multiply_convert_fusion.5), channel_id=1, source_target_pairs={{0,8},{8,0},{16,24},{24,16},{1,9},{9,1},{17,25},{25,17},{2,10},{10... | collective-permute-start | bytes 1572872 | tf_op jit(solution)/shard_map/ppermute | solution.py:1221
  183.1 2.1 collective-permute-start.16
  187.2 2.0 collective-permute-start.17
  208.4 2.3 collective-permute-start.18
  216.1 14.2 %collective-permute-start.19 = (bf16[256,1024]{1,0:T(8,128)(2,1)S(1)}, bf16[256,1024]{1,0:T(8,128)(2,1)S(1)}, u32[]{:S(2)}, u32[]{:S(2)}) collective-permute-start(bf16[256,1024]{1,0:T(8,128)(2,1)S(1)} %get-tuple-element.188), channel_id=1, source_target_pairs={{0,16},{8,24},{16,0},{24,8},{1,17},{9,25},{17,1},{25,9},{2,18},{10... | collective-permute-start | bytes 1572872 | tf_op jit(solution)/shard_map/ppermute | solution.py:825
  231.4 3.0 collective-permute-start.20
  240.1 3.3 collective-permute-start.21
  243.4 13.0 %collective-permute-start.22 = (f32[8,128]{1,0:T(8,128)S(1)}, f32[8,128]{1,0:T(8,128)S(1)}, u32[]{:S(2)}, u32[]{:S(2)}) collective-permute-start(f32[8,128]{1,0:T(8,128)S(1)} %bitcast_add_fusion), channel_id=1, source_target_pairs={{0,16},{8,24},{16,0},{24,8},{1,17},{9,25},{17,1},{25,9},{2,18},{10... | collective-permute-start | bytes 12296 | tf_op jit(solution)/shard_map/ppermute | solution.py:825
  245.8 16.2 %collective-permute-start.23 = (bf16[256,1024]{1,0:T(8,128)(2,1)}, bf16[256,1024]{1,0:T(8,128)(2,1)}, u32[]{:S(2)}, u32[]{:S(2)}) collective-permute-start(bf16[256,1024]{1,0:T(8,128)(2,1)} %dynamic-slice_bitcast_fusion.2), channel_id=1, source_target_pairs={{0,1},{1,0},{2,3},{3,2},{4,5},{5,4},{6,7},{7,6},{8,9},{9,8},{10,11... | collective-permute-start | bytes 1572872 | tf_op jit(solution)/shard_map/ppermute | solution.py:825
  263.2 29.4 %collective-permute-start.24 = (bf16[4,128,640]{2,1,0:T(8,128)(2,1)}, bf16[4,128,640]{2,1,0:T(8,128)(2,1)S(1)}, u32[]{:S(2)}, u32[]{:S(2)}) collective-permute-start(bf16[4,128,640]{2,1,0:T(8,128)(2,1)} %dynamic-slice_bitcast_fusion.1), channel_id=1, source_target_pairs={{0,1},{1,0},{2,3},{3,2},{4,5},{5,4},{6,7},{7,6},{8,9},{9,8},{10,11... | collective-permute-start | bytes 1966088 | tf_op jit(solution)/shard_map/ppermute | solution.py:825
  267.3 25.3 %collective-permute-start.25 = (bf16[64,1024]{1,0:T(8,128)(2,1)S(1)}, bf16[64,1024]{1,0:T(8,128)(2,1)S(1)}, u32[]{:S(2)}, u32[]{:S(2)}) collective-permute-start(bf16[64,1024]{1,0:T(8,128)(2,1)S(1)} %get-tuple-element.211), channel_id=1, source_target_pairs={{0,2},{1,3},{2,4},{3,5},{4,6},{5,7},{6,0},{7,1},{8,10},{9,11},{10,... | collective-permute-start | bytes 393224 | tf_op jit(solution)/shard_map/ppermute | solution.py:828
  268.8 23.7 %collective-permute-start.26 = (bf16[64,1024]{1,0:T(8,128)(2,1)S(1)}, bf16[64,1024]{1,0:T(8,128)(2,1)S(1)}, u32[]{:S(2)}, u32[]{:S(2)}) collective-permute-start(bf16[64,1024]{1,0:T(8,128)(2,1)S(1)} %get-tuple-element.210), channel_id=1, source_target_pairs={{0,4},{1,5},{2,6},{3,7},{4,0},{5,1},{6,2},{7,3},{8,12},{9,13},{10,... | collective-permute-start | bytes 393224 | tf_op jit(solution)/shard_map/ppermute | solution.py:828
  271.1 21.4 %collective-permute-start.27 = (bf16[64,1024]{1,0:T(8,128)(2,1)S(1)}, bf16[64,1024]{1,0:T(8,128)(2,1)S(1)}, u32[]{:S(2)}, u32[]{:S(2)}) collective-permute-start(bf16[64,1024]{1,0:T(8,128)(2,1)S(1)} %get-tuple-element.209), channel_id=1, source_target_pairs={{0,6},{1,7},{2,0},{3,1},{4,2},{5,3},{6,4},{7,5},{8,14},{9,15},{10,... | collective-permute-start | bytes 393224 | tf_op jit(solution)/shard_map/ppermute | solution.py:828
  273.1 20.4 %copy-start.11 = (bf16[1024,1024]{1,0:T(8,128)(2,1)S(1)}, bf16[1024,1024]{1,0:T(8,128)(2,1)}, u32[]{:S(2)}) copy-start(bf16[1024,1024]{1,0:T(8,128)(2,1)} %copy-done.9) | copy-start | bytes 6291460
  308.0 2.7 collective-permute-start.28
  310.9 14.0 %collective-permute-start.29 = (bf16[256,1024]{1,0:T(8,128)(2,1)S(1)}, bf16[256,1024]{1,0:T(8,128)(2,1)S(1)}, u32[]{:S(2)}, u32[]{:S(2)}) collective-permute-start(bf16[256,1024]{1,0:T(8,128)(2,1)S(1)} %fusion.13), channel_id=1, source_target_pairs={{0,16},{8,24},{16,0},{24,8},{1,17},{9,25},{17,1},{25,9},{2,18},{10... | collective-permute-start | bytes 1572872 | tf_op jit(solution)/shard_map/ppermute | solution.py:825
  311.9 24.0 %collective-permute-start.30 = (bf16[4,128,768]{1,2,0:T(8,128)(2,1)S(1)}, bf16[4,128,768]{1,2,0:T(8,128)(2,1)S(1)}, u32[]{:S(2)}, u32[]{:S(2)}) collective-permute-start(bf16[4,128,768]{1,2,0:T(8,128)(2,1)S(1)} %dynamic-slice_bitcast_fusion), channel_id=1, source_target_pairs={{0,1},{1,0},{2,3},{3,2},{4,5},{5,4},{6,7},{7,6},{8,9},{9,8},{10,11... | collective-permute-start | bytes 2359304 | tf_op jit(solution)/shard_map/ppermute | solution.py:825
  312.9 12.4 %collective-permute-start.31 = (bf16[128,640]{1,0:T(8,128)(2,1)S(1)}, bf16[128,640]{1,0:T(8,128)(2,1)S(1)}, u32[]{:S(2)}, u32[]{:S(2)}) collective-permute-start(bf16[128,640]{1,0:T(8,128)(2,1)S(1)} %get-tuple-element.207), channel_id=1, source_target_pairs={{0,2},{1,3},{2,4},{3,5},{4,6},{5,7},{6,0},{7,1},{8,10},{9,11},{10,... | collective-permute-start | bytes 491528 | tf_op jit(solution)/shard_map/ppermute | solution.py:828
  313.6 22.3 %collective-permute-start.32 = (bf16[128,640]{1,0:T(8,128)(2,1)S(1)}, bf16[128,640]{1,0:T(8,128)(2,1)S(1)}, u32[]{:S(2)}, u32[]{:S(2)}) collective-permute-start(bf16[128,640]{1,0:T(8,128)(2,1)S(1)} %get-tuple-element.206), channel_id=1, source_target_pairs={{0,4},{1,5},{2,6},{3,7},{4,0},{5,1},{6,2},{7,3},{8,12},{9,13},{10,... | collective-permute-start | bytes 491528 | tf_op jit(solution)/shard_map/ppermute | solution.py:828
  314.1 21.9 %collective-permute-start.33 = (bf16[128,640]{1,0:T(8,128)(2,1)S(1)}, bf16[128,640]{1,0:T(8,128)(2,1)S(1)}, u32[]{:S(2)}, u32[]{:S(2)}) collective-permute-start(bf16[128,640]{1,0:T(8,128)(2,1)S(1)} %get-tuple-element.205), channel_id=1, source_target_pairs={{0,6},{1,7},{2,0},{3,1},{4,2},{5,3},{6,4},{7,5},{8,14},{9,15},{10,... | collective-permute-start | bytes 491528 | tf_op jit(solution)/shard_map/ppermute | solution.py:828
  336.7 25.3 %copy-start.54 = (bf16[1,256,1024]{2,1,0:T(8,128)(2,1)S(1)}, bf16[1,256,1024]{2,1,0:T(8,128)(2,1)}, u32[]{:S(2)}) copy-start(bf16[1,256,1024]{2,1,0:T(8,128)(2,1)} %param.21) | copy-start | bytes 1572868
  349.6 12.7 %copy-start.57 = (f32[256,1024]{1,0:T(8,128)S(1)}, f32[256,1024]{1,0:T(8,128)}, u32[]{:S(2)}) copy-start(f32[256,1024]{1,0:T(8,128)} %get-tuple-element.189) | copy-start | bytes 3145732
  349.6 23.6 %collective-permute-start.38 = (bf16[384,1024]{1,0:T(8,128)(2,1)}, bf16[384,1024]{1,0:T(8,128)(2,1)}, u32[]{:S(2)}, u32[]{:S(2)}) collective-permute-start(bf16[384,1024]{1,0:T(8,128)(2,1)} %bitcast.305), channel_id=1, source_target_pairs={{0,16},{8,24},{16,0},{24,8},{1,17},{9,25},{17,1},{25,9},{2,18},{10... | collective-permute-start | bytes 2359304 | tf_op jit(solution)/shard_map/ppermute | solution.py:825
  354.8 10.0 %collective-permute-start.34 = (bf16[128,768]{1,0:T(8,128)(2,1)}, bf16[128,768]{1,0:T(8,128)(2,1)}, u32[]{:S(2)}, u32[]{:S(2)}) collective-permute-start(bf16[128,768]{1,0:T(8,128)(2,1)} %bitcast.315), channel_id=1, source_target_pairs={{0,2},{1,3},{2,4},{3,5},{4,6},{5,7},{6,0},{7,1},{8,10},{9,11},{10,... | collective-permute-start | bytes 589832 | tf_op jit(solution)/shard_map/ppermute | solution.py:828
  355.6 17.6 %collective-permute-start.35 = (bf16[128,768]{1,0:T(8,128)(2,1)}, bf16[128,768]{1,0:T(8,128)(2,1)}, u32[]{:S(2)}, u32[]{:S(2)}) collective-permute-start(bf16[128,768]{1,0:T(8,128)(2,1)} %bitcast.316), channel_id=1, source_target_pairs={{0,4},{1,5},{2,6},{3,7},{4,0},{5,1},{6,2},{7,3},{8,12},{9,13},{10,... | collective-permute-start | bytes 589832 | tf_op jit(solution)/shard_map/ppermute | solution.py:828
  358.4 14.8 %collective-permute-start.36 = (bf16[128,768]{1,0:T(8,128)(2,1)}, bf16[128,768]{1,0:T(8,128)(2,1)}, u32[]{:S(2)}, u32[]{:S(2)}) collective-permute-start(bf16[128,768]{1,0:T(8,128)(2,1)} %bitcast.108), channel_id=1, source_target_pairs={{0,6},{1,7},{2,0},{3,1},{4,2},{5,3},{6,4},{7,5},{8,14},{9,15},{10,... | collective-permute-start | bytes 589832 | tf_op jit(solution)/shard_map/ppermute | solution.py:828
  360.2 3.5 collective-permute-start.37
  363.6 20.8 %copy-start.73 = (bf16[1,384,1024]{2,1,0:T(8,128)(2,1)S(1)}, bf16[1,384,1024]{2,1,0:T(8,128)(2,1)}, u32[]{:S(2)}) copy-start(bf16[1,384,1024]{2,1,0:T(8,128)(2,1)} %reduce-scatter.2.cloned.1.call-done) | copy-start | bytes 2359300
  374.6 17.6 %copy-start.12 = (bf16[128,2048]{1,0:T(8,128)(2,1)S(1)}, bf16[128,2048]{1,0:T(8,128)(2,1)}, u32[]{:S(2)}) copy-start(bf16[128,2048]{1,0:T(8,128)(2,1)} %w_up.1) | copy-start | bytes 1572868
  374.6 17.6 %copy-start.13 = (bf16[128,2048]{1,0:T(8,128)(2,1)S(1)}, bf16[128,2048]{1,0:T(8,128)(2,1)}, u32[]{:S(2)}) copy-start(bf16[128,2048]{1,0:T(8,128)(2,1)} %w_gate.1) | copy-start | bytes 1572868
  374.6 16.7 %collective-permute-start.39 = (bf16[128,1920]{1,0:T(8,128)(2,1)S(1)}, bf16[128,1920]{1,0:T(8,128)(2,1)S(1)}, u32[]{:S(2)}, u32[]{:S(2)}) collective-permute-start(bf16[128,1920]{1,0:T(8,128)(2,1)S(1)} %get-tuple-element.214), channel_id=1, source_target_pairs={{0,16},{8,24},{16,0},{24,8},{1,17},{9,25},{17,1},{25,9},{2,18},{10... | collective-permute-start | bytes 1474568 | tf_op jit(solution)/shard_map/ppermute | solution.py:825
  385.9 6.2 %collective-permute-start.41 = (bf16[384,1024]{1,0:T(8,128)(2,1)S(1)}, bf16[384,1024]{1,0:T(8,128)(2,1)}, u32[]{:S(2)}, u32[]{:S(2)}) collective-permute-start(bf16[384,1024]{1,0:T(8,128)(2,1)S(1)} %add_convert_fusion.own), channel_id=1, source_target_pairs={{0,8},{8,0},{16,24},{24,16},{1,9},{9,1},{17,25},{25,17},{2,10},{10... | collective-permute-start | bytes 2359304 | tf_op jit(solution)/shard_map/ppermute | solution.py:825
  391.3 4.5 %collective-permute-start.40 = (bf16[2,128,1920]{2,1,0:T(8,128)(2,1)S(1)}, bf16[2,128,1920]{2,1,0:T(8,128)(2,1)}, u32[]{:S(2)}, u32[]{:S(2)}) collective-permute-start(bf16[2,128,1920]{2,1,0:T(8,128)(2,1)S(1)} %pad_maximum_fusion.7.refs_0_), channel_id=1, source_target_pairs={{0,8},{8,0},{16,24},{24,16},{1,9},{9,1},{17,25},{25,17},{2,10},{10... | collective-permute-start | bytes 2949128 | tf_op jit(solution)/shard_map/ppermute | solution.py:825
  (77 other events, 288.4 us)
Sparse Core Ops, SparseCore 0:
  14.5 139.5 all-gather.2
  208.9 140.6 reduce-scatter.1

commit v4 on v3

--- a/solution.py
+++ b/solution.py
@@ -709,7 +709,9 @@
 
 
 def finish_kernel(
-    got,
+    place,
+    own,
+    mates,
     w_in,
     w_qkv,
     w_out,
@@ -724,7 +726,7 @@
     small_ref,
     steps,
 ):
-    count = got.shape[0]
+    count = 2 * own.shape[0]
     shard = w_qkv.shape[0]
     heads = MH // count
     width = heads * HP
@@ -746,8 +748,14 @@
 
     for j in range(count):
 
-        def part(low, high, j=j):
-            return got[j, :shard, low:high].astype(F32)
+        at_x = (place[0] + j // 2) % 2
+        mine = place[1] == j % 2
+
+        def pick(rows, lanes, at_x=at_x, mine=mine):
+            return jnp.where(mine, own[at_x, rows, lanes], mates[at_x, rows, lanes]).astype(F32)
+
+        def part(low, high, pick=pick):
+            return pick(slice(None), slice(low, high))
 
         gain = lay(j * width, part(late, late + width), gain)
         gain = lay(wide + j * width, part(0, width), gain)
@@ -757,8 +765,9 @@
         qkv_ref[:, j * q_width : (j + 1) * q_width] = part(at, at + q_width)
         pairs.append(part(at + q_width, at + q_width + 128))
         at = at + q_width + 128
-        rows = got[j, : shard // 2, at:], got[j, shard // 2 :, at:]
-        rows = jnp.concatenate(rows, axis=1).astype(F32)
+        lanes = slice(at, own.shape[2])
+        rows = pick(slice(0, shard // 2), lanes), pick(slice(shard // 2, shard), lanes)
+        rows = jnp.concatenate(rows, axis=1)
         low = j * (shard // 2)
         if low < out_ref.shape[0]:
             out_ref[low : low + shard // 2, :] = rows
@@ -782,20 +791,20 @@
     small_ref[...] = jnp.transpose(small)
 
 
-def finish(got, w_in, w_qkv, w_out, w_o, gain_in, gain_m):
+def finish(place, own, mates, w_in, w_qkv, w_out, w_o, gain_in, gain_m):
     shard = w_qkv.shape[0]
     vmem = pl.BlockSpec(memory_space=pltpu.VMEM)
     shapes = [w_in.shape[::-1], w_qkv.shape, w_out.shape, w_o.shape]
     shapes += [(8, shard), (8, w_out.shape[0]), (128, shard)]
     out = pl.pallas_call(
         finish_kernel,
-        in_specs=[vmem] * 6,
+        in_specs=[pl.BlockSpec(memory_space=pltpu.SMEM)] + [vmem] * 7,
         out_specs=[vmem] * 7,
         out_shape=[jax.ShapeDtypeStruct(shape, F32) for shape in shapes],
         scratch_shapes=[pltpu.VMEM((shard, 128), F32)],
         compiler_params=pltpu.CompilerParams(vmem_limit_bytes=40 * 1024 * 1024),
         name="finish",
-    )(got, w_in.T, w_qkv, w_out, gain_in.astype(F32)[None], gain_m.astype(F32)[None])
+    )(place, own, mates, w_in.T, w_qkv, w_out, gain_in.astype(F32)[None], gain_m.astype(F32)[None])
     return out[0].T, out[1], out[2], out[3], out[4][0], out[5][0], out[6]
 
 
@@ -803,10 +812,11 @@
     return lax.optimization_barrier((value,) + after)[0]
 
 
-def stage(compute, inputs, sends):
+def stage(compute, inputs, sends, late=()):
     inputs, operands = lax.optimization_barrier((inputs, [operand for _, operand in sends]))
     got = [send(operand) for (send, _), operand in zip(sends, operands)]
-    return lax.optimization_barrier((compute(*inputs), got))
+    out, got, late = lax.optimization_barrier((compute(*inputs), got, late))
+    return (out, got, late) if late else (out, got)
 
 
 class Net:
@@ -862,8 +872,13 @@
         return lax.dynamic_index_in_dim(low, self.y, 1, False), away
 
     def shifts_z(self, both):
-        sent = [lax.dynamic_index_in_dim(both, (self.z + k) % 4, 0, False) for k in range(4)]
-        return [sent[0]] + [self.shift_z(sent[k], k) for k in range(1, 4)]
+        return self.send_z(self.blocks_z(both))
+
+    def blocks_z(self, both):
+        return [lax.dynamic_index_in_dim(both, (self.z + k) % 4, 0, False) for k in range(4)]
+
+    def send_z(self, blocks):
+        return [blocks[0]] + [self.shift_z(blocks[k], k) for k in range(1, 4)]
 
     def collect(self, sums):
         return lax.psum_scatter(sums.astype(BF16), "fsdp", scatter_dimension=0, tiled=False)
@@ -885,6 +900,10 @@
         if not self.direct:
             low = lax.psum_scatter(parts.astype(BF16), "ctx", scatter_dimension=0, tiled=False)
             return low.astype(F32)
+        own, away = self.ctx_halves(parts)
+        return own + self.flip(away, "ctx", 2).astype(F32)
+
+    def ctx_halves(self, parts):
         pairs = parts.reshape((2, 2) + parts.shape[1:])
         away = lax.dynamic_index_in_dim(pairs, 1 - self.core, 1, False).astype(BF16)
         here = lax.dynamic_index_in_dim(pairs, self.core, 1, False)
@@ -895,8 +914,7 @@
                 F32
             ) + lax.dynamic_index_in_dim(got, which, 0, False).astype(F32)
 
-        across = self.flip(half(1 - self.x).astype(BF16), "ctx", 2)
-        return half(self.x) + across.astype(F32)
+        return half(self.x), half(1 - self.x).astype(BF16)
 
     def over_cores(self, value):
         value = lax.psum(value, "ctx", axis_index_groups=self.by_core)
@@ -1117,14 +1135,14 @@
         pair = jnp.stack([tokens[0], net.flip_x(tokens[0])])
         near = net.along_z(both_cols)
         far = net.along_y([tie(near[0], pair)] + near[1:])
+        all_tokens = put([pair, net.flip_core(pair)], [c, c ^ 2, c ^ 1, c ^ 3])
         w_first, w_second = net.in_order(
-            [p[None] for p in near],
+            [tie(near[0], all_tokens)[None]] + [p[None] for p in near[1:]],
             [p[None] for p in far],
             [first.shape[1], second.shape[1]],
         )
         at = conv_width + at_small
         small = jnp.swapaxes(w_first[:, :, at : at + packed.shape[0]], 1, 2)
-        all_tokens = put([pair, net.flip_core(pair)], [c, c ^ 2, c ^ 1, c ^ 3])
         crossed = net.cross(tie(both_out, *near[1:]))
     else:
         small = lax.all_gather(packed, "fsdp", axis=0, tiled=False)
@@ -1204,17 +1222,30 @@
     gated = ssm_y * (gate_z * jax.nn.sigmoid(gate_z))
     ym = (gated * scale_m * gain_mamba).astype(BF16)
     outs = nn(ym, w_mamba) + nn(attended, w_attn)
-    mixed = tokens[0].astype(F32) + net.ctx_collect(outs.reshape(n, rows, dim))
-
     ff_rows = shard * size // dim
     part_rows = ff_rows // places_x
 
-    def ff_part(low, high, columns):
-        return jnp.swapaxes(w_ff[:, :, low:high], 0, 1).reshape(-1, columns)
-
-    w_g = ff_part(0, part_rows, size)
-    w_u = ff_part(part_rows, 2 * part_rows, size)
-    w_d = ff_part(2 * part_rows, w_ff.shape[2], dim)
+    def plus(here, got):
+        return (here.astype(F32) + got.astype(F32)).astype(BF16)
+
+    def ff_weights(w_ff):
+        def part(low, high, columns):
+            return jnp.swapaxes(w_ff[:, :, low:high], 0, 1).reshape(-1, columns)
+
+        return (
+            part(0, part_rows, size),
+            part(part_rows, 2 * part_rows, size),
+            part(2 * part_rows, w_ff.shape[2], dim),
+        )
+
+    if net.direct:
+        own, away = net.ctx_halves(outs.reshape(n, rows, dim))
+        (w_g, w_u, w_d), (across,) = stage(ff_weights, (w_ff,), [(net.flip_x, away)])
+        mixed = tokens[0].astype(F32) + own + across.astype(F32)
+    else:
+        w_g, w_u, w_d = ff_weights(w_ff)
+        mixed = tokens[0].astype(F32) + net.ctx_collect(outs.reshape(n, rows, dim))
+
     scale2 = rms_scale(mixed)
     normed2 = (mixed * scale2 * gain_second).astype(BF16)
     mate = [(i, i ^ 1) for i in range(n)]
@@ -1377,28 +1408,34 @@
             ],
         )
         grad_early = sum(p.astype(F32) for p in early_parts).astype(BF16)
-        grad_tokens, (late_parts, out_quarter, got_ff) = stage(
+        blocks = net.blocks_z(plus(here, got))
+        g_ff = tie(g_ff, grad_early, *blocks)
+        got_ff = net.flip_x(g_ff)
+        grad_tokens, (late_parts, out_quarter), (got_ff,) = stage(
             tokens_back,
             (grad_normed,),
-            [
-                (net.shifts_z, plus(here, got)),
-                (net.cross, out_quarter),
-                (net.flip_x, g_ff),
-            ],
+            [(net.send_z, blocks), (net.cross, out_quarter)],
+            (got_ff,),
         )
         g_ff = plus(g_ff, got_ff)
         grad_late = sum(p.astype(F32) for p in late_parts).astype(BF16)
         joined = jnp.concatenate([out_quarter[:, : dim // 2], out_quarter[:, dim // 2 :]], axis=0)
         joined = jnp.concatenate([grad_early, joined], axis=1)
         joined = jnp.concatenate([grad_late, joined], axis=1)
-        got, got_ff = net.ctx_all(joined), net.flip_core(g_ff)
+        def finish_halves(g_ff, got_ff):
+            return finish_ff(net.core, g_ff, got_ff, w_gate, w_up, gain_ffn)
+
+        ff_out, (across,) = stage(
+            finish_halves, (g_ff, net.flip_core(g_ff)), [(net.flip_x, joined)]
+        )
+        out_gate, out_up, out_down, out_gain_ffn = ff_out
+        joined = jnp.stack([joined, across])
+        mates = net.flip_core(joined)
+        place = jnp.stack([net.x, net.core]).astype(jnp.int32)
         out_w_in, out_w_qkv, out_mamba, out_attn, out_gain_in, out_gain_m, totals = finish(
-            got, w_in, w_qkv, w_out, w_o, gain_in, gain_m
+            place, joined, mates, w_in, w_qkv, w_out, w_o, gain_in, gain_m
         )
         totals = totals[at_small : at_small + laid.shape[2]]
-        out_gate, out_up, out_down, out_gain_ffn = finish_ff(
-            net.core, g_ff, got_ff, w_gate, w_up, gain_ffn
-        )
     else:
         grad_tokens = tokens_back(net.ctx_collect(normed_back(early, g_late)))
         got_early = net.ctx_all(net.collect(grad_early)).astype(F32)

time: 421 us -> 414 us (0.983)
    ppermute x24, waiting for transfers between devices: 68.9 us -> 83.9 us  [flip(): return lax.ppermute(value, axis, [(i, i ^ bit) for i in range(size)])]
    ppermute x12, waiting for transfers between devices: 46 us -> 35.2 us  [shift_z(): lax.ppermute(value, 'fsdp', [(i, (i + 2 * by) % self.m) for i in range(se...]
    ppermute x24, starting transfers between devices: 34.8 us -> 29.7 us  [flip(): return lax.ppermute(value, axis, [(i, i ^ bit) for i in range(size)])]
    slice x6, local copies, waits for them, and re-layouts: 0.74 us -> 5.26 us  [unlay(): small[..., start:start + count, :].reshape(small.shape[:-2] + (lead, room))]
    pallas_call x4 -> x3, Pallas kernels: 11.1 us -> 6.65 us  [put(): pl.pallas_call(functools.partial(put_kernel, counts, cuts), grid_spec=plt...]
  transfers between devices with their start and end apart: 44 -> 44, of which waited for: 21 -> 26; matrix products, arithmetic and copies ran while one was open for 18% -> 18% of each run, Pallas kernels for 15% -> 15%
where the time goes in v4:
time: 414 us; the launch traced here: 407 us
  waiting for transfers between devices  134 us (32%)
  Pallas kernels  70.2 us (17%)
  local copies, waits for them, and re-layouts  64.9 us (16%)
  starting transfers between devices  59.7 us (14%)
  other arithmetic  30.9 us (7%)
  matrix products  28.7 us (7%)
  between operations  19 us (5%)
    ppermute x24, waiting for transfers between devices, flip(): return lax.ppermute(value, axis, [(i, i ^ bit) for i in range(size)])  83.9 us
    ppermute x12, waiting for transfers between devices, shift_z(): lax.ppermute(value, 'fsdp', [(i, (i + 2 * by) % self.m) for i in range(se...  35.2 us
    ppermute x24, starting transfers between devices, flip(): return lax.ppermute(value, axis, [(i, i ^ bit) for i in range(size)])  29.7 us
    unnamed x200, local copies, waits for them, and re-layouts  26.4 us
    ppermute x12, starting transfers between devices, shift_z(): lax.ppermute(value, 'fsdp', [(i, (i + 2 * by) % self.m) for i in range(se...  22.8 us
    pallas_call x1, Pallas kernels, ssm_backward(): pl.pallas_call(functools.partial(ssm_bwd_kernel, heads), grid=(steps,), i...  19.4 us
    dot_general x7, matrix products, nt(): lax.dot_general(left, right, (((1,), (1,)), ((), ())), preferred_element_...  15.9 us
    pallas_call x1, Pallas kernels, attn_backward(): pl.pallas_call(functools.partial(attn_bwd_kernel, heads, blocks), grid=(b...  9.9 us
  transfers between devices with their start and end apart: 44, of which 26 were waited for; matrix products, arithmetic and copies ran while one was open for 18% of the time, Pallas kernels for 15%

profile of v4, /device:TPU:0, one launch (start us, length us, event | category | flops | bytes accessed | tf_op | source)
XLA Modules:
  0.0 407.4 jit_solution(14272763339107299886)
XLA Ops:
  16.1 3.1 collective-permute-start.2
  19.2 2.6 collective-permute-start.3
  24.9 13.9 %collective-permute-done = bf16[256,1024]{1,0:T(8,128)(2,1)S(1)} collective-permute-done((bf16[256,1024]{1,0:T(8,128)(2,1)S(1)}, bf16[256,1024]{1,0:T(8,128)(2,1)S(1)}, u32[]{:S(2)}, u32[]{:S(2)}) %collective-permute-start) | collective-permute-done | bytes 524320 | tf_op jit(solution)/shard_map/ppermute | solution.py:835
  41.1 12.3 %collective-permute-done.3 = bf16[128,1408]{1,0:T(8,128)(2,1)} collective-permute-done((bf16[128,1408]{1,0:T(8,128)(2,1)S(1)}, bf16[128,1408]{1,0:T(8,128)(2,1)}, u32[]{:S(2)}, u32[]{:S(2)}) %collective-permute-start.3) | collective-permute-done | bytes 360480 | tf_op jit(solution)/shard_map/ppermute | solution.py:838
  60.3 5.6 %collective-permute-start.11 = (bf16[256,1024]{1,0:T(8,128)(2,1)}, bf16[256,1024]{1,0:T(8,128)(2,1)}, u32[]{:S(2)}, u32[]{:S(2)}) collective-permute-start(bf16[256,1024]{1,0:T(8,128)(2,1)} %pad_maximum_fusion.10), channel_id=1, source_target_pairs={{0,0},{1,1},{2,8},{3,9},{4,16},{5,17},{6,24},{7,25},{8,2},{9,3},{1... | collective-permute-start | bytes 1572872 | tf_op jit(solution)/shard_map/ppermute | solution.py:847
  68.0 10.4 %collective-permute-done.8 = bf16[128,1408]{1,0:T(8,128)(2,1)} collective-permute-done((bf16[128,1408]{1,0:T(8,128)(2,1)}, bf16[128,1408]{1,0:T(8,128)(2,1)}, u32[]{:S(2)}, u32[]{:S(2)}) %collective-permute-start.8) | collective-permute-done | bytes 360480 | tf_op jit(solution)/shard_map/ppermute | solution.py:835
  78.4 6.5 %collective-permute-done.5 = bf16[128,1408]{1,0:T(8,128)(2,1)} collective-permute-done((bf16[128,1408]{1,0:T(8,128)(2,1)S(1)}, bf16[128,1408]{1,0:T(8,128)(2,1)}, u32[]{:S(2)}, u32[]{:S(2)}) %collective-permute-start.5) | collective-permute-done | bytes 360480 | tf_op jit(solution)/shard_map/ppermute | solution.py:835
  85.8 2.8 put.4
  92.8 2.0 fusion.40
  99.1 5.2 %project_conv.1 = (bf16[1024,1024]{1,0:T(8,128)(2,1)S(1)}, bf16[1024,640]{1,0:T(8,128)(2,1)S(1)}, bf16[1024,640]{1,0:T(8,128)(2,1)S(1)}, bf16[1024,640]{1,0:T(8,...) custom-call(bf16[1024,1024]{1,0:T(8,128)(2,1)S(1)} %bitcast.260, f32[1,1024]{1,0:T(1,128)S(1)} %bitcast.269, ...), custom_call_target="tpu_custom_call" | custom-call | flops 1610612736 | bytes 10000000 | tf_op jit(solution)/shard_map/project_conv/pallas_call | solution.py:100
  105.5 7.4 %ssm_forward.1 = (f32[1024,384]{1,0:T(8,128)S(1)}, f32[8,384,128]{2,1,0:T(8,128)S(1)}) custom-call(s32[9]{0:T(128)S(1)} %pad_add_fusion.1.ends, f32[6]{0:T(128)S(1)} %dynamic_slice.150.skip, bf16[1024,640]{1,0:T(8,128)(2,1)S(1)} %get-tuple-element.120.act, f32[1024,256]{1,0:T(8,128)S(1)} %get-tuple-element.121.steps, ...), custom_call_target="tpu_custom_call" | custom-call | flops 1000000000 | bytes 40000000 | tf_op jit(solution)/shard_map/ssm_forward/pallas_call | solution.py:429
  116.2 1.7 collective-permute-start.12
  122.2 4.0 project_gate.1
  131.1 5.9 %attn_forward.1 = (bf16[1024,128]{1,0:T(8,128)(2,1)S(1)}, f32[1024,2]{1,0:T(8,128)S(1)}) custom-call(bf16[1024,256]{1,0:T(8,128)(2,1)S(1)} %get-tuple-element.148.qkv_ref, s32[1024,1]{1,0:T(8,128)S(1)} %copy-done.7, s32[1,1024]{1,0:T(1,128)S(1)} %copy-done.31), custom_call_target="tpu_custom_call" | custom-call | flops 1000000000 | bytes 20000000 | tf_op jit(solution)/shard_map/attn_forward/pallas_call | solution.py:584
  137.1 2.1 collective-permute-done.12
  139.1 1.8 maximum_select_fusion
  143.3 1.9 copy-done.47
  146.3 3.0 collective-permute-done.13
  149.3 2.3 fusion.17
  153.1 4.1 %slice_bitcast_fusion = (bf16[8,2,64,1024]{3,2,0,1:T(8,128)(2,1)S(1)}, bf16[8,2,64,1024]{3,2,0,1:T(8,128)(2,1)S(1)}, bf16[8,2,64,1024]{3,2,0,1:T(8,128)(2,1)S(1)}) fusion(bf16[2,8,192,1024]{3,2,1,0:T(8,128)(2,1)} %bitcast.280), kind=kLoop, calls=%fused_computation.7 | loop fusion | bytes 12582912 | tf_op jit(solution)/shard_map/transpose | solution.py:1233
  157.9 8.0 %collective-permute-done.14 = bf16[256,1024]{1,0:T(8,128)(2,1)} collective-permute-done((bf16[256,1024]{1,0:T(8,128)(2,1)}, bf16[256,1024]{1,0:T(8,128)(2,1)}, u32[]{:S(2)}, u32[]{:S(2)}) %collective-permute-start.14) | collective-permute-done | bytes 524320 | tf_op jit(solution)/shard_map/ppermute | solution.py:835
  165.9 1.9 multiply_reduce_fusion.2
  168.1 1.9 collective-permute-done.15
  178.2 1.7 collective-permute-done.17
  179.9 1.8 multiply_convert_fusion.1
  181.7 2.6 fusion.46
  184.4 5.7 %ff_gradients.1 = bf16[8,384,1024]{2,1,0:T(8,128)(2,1)S(1)} custom-call(bf16[512,1024]{1,0:T(8,128)(2,1)S(1)} %pad_maximum_fusion.3.both, bf16[512,1024]{1,0:T(8,128)(2,1)S(1)} %get-tuple-element.280.product, bf16[512,1024]{1,0:T(8,128)(2,1)S(1)} %get-tuple-element.143.g_gate, bf16[512,1024]{1,0:T(8,128)(2,1)S(1)} %get-tuple-element.234.g_up, ...), custom_call_target="tpu_custom_call" | custom-call | flops 3221225472 | bytes 10000000 | tf_op jit(solution)/shard_map/ff_gradients/pallas_call | solution.py:640
  190.1 2.6 copy-done.3
  192.7 3.8 convolution_add_fusion.2
  199.0 2.1 collective-permute-done.18
  201.0 2.0 multiply_reduce_fusion.1
  203.0 3.4 fusion.36
  207.9 12.5 %collective-permute-done.19 = bf16[256,1024]{1,0:T(8,128)(2,1)S(1)} collective-permute-done((bf16[256,1024]{1,0:T(8,128)(2,1)S(1)}, bf16[256,1024]{1,0:T(8,128)(2,1)S(1)}, u32[]{:S(2)}, u32[]{:S(2)}) %collective-permute-start.19) | collective-permute-done | bytes 524320 | tf_op jit(solution)/shard_map/ppermute | solution.py:835
  221.5 3.0 collective-permute-done.20.refs_1_
  224.5 3.1 put.5
  227.6 2.5 multiply_reduce_fusion
  236.5 9.9 %attn_backward.1 = bf16[1024,256]{1,0:T(8,128)(2,1)} custom-call(bf16[1024,256]{1,0:T(8,128)(2,1)} %copy-done.28, s32[1024,1]{1,0:T(8,128)} %copy.187.seg_c, s32[1,1024]{1,0:T(1,128)} %seg_r.7, f32[1024,2]{1,0:T(8,128)} %copy-done.29, bf16[1024,128]{1,0:T(8,128)(2,1)} %convolution_convert_fusion.4.go_ref, f32[1024,256]{1,0:T(8,128)} %constant.374.clone.cosine, ...), custom_call_target="tpu_custom_call" | custom-call | flops 10000000 | bytes 1000000 | tf_op jit(solution)/shard_map/attn_backward/pallas_call | solution.py:608
  246.4 2.4 multiply_convert_fusion.3
  248.9 1.9 convolution_convert_fusion.1
  251.7 2.1 collective-permute-done.23
  259.7 4.0 collective-permute-start.26
  264.8 19.4 %ssm_backward.1 = (bf16[1024,768]{1,0:T(8,128)(2,1)}, f32[8,640]{1,0:T(8,128)}, f32[8,384]{1,0:T(8,128)}, f32[8,128]{1,0:T(8,128)}) custom-call(s32[9]{0:T(128)} %copy-done.42, f32[6]{0:T(128)} %copy-done.43, bf16[1024,640]{1,0:T(8,128)(2,1)} %copy-done.26, f32[1024,256]{1,0:T(8,128)} %copy-done.27, f32[16,1024]{1,0:T(8,128)} %copy-done.36, ...), custom_call_target="tpu_custom_call" | custom-call | flops 10000000 | bytes 1000000 | tf_op jit(solution)/shard_map/ssm_backward/pallas_call | solution.py:466
  285.1 3.3 convolution_convert_fusion
  291.2 1.9 copy.220
  295.7 1.8 fusion.47
  297.5 1.9 convolution_add_fusion.1
  299.6 2.6 collective-permute-done.28
  302.4 1.8 collective-permute-start.29
  305.5 2.0 collective-permute-start.31
  307.7 2.4 collective-permute-start.33
  310.0 6.5 %collective-permute-done.29 = bf16[256,1024]{1,0:T(8,128)(2,1)S(1)} collective-permute-done((bf16[256,1024]{1,0:T(8,128)(2,1)S(1)}, bf16[256,1024]{1,0:T(8,128)(2,1)S(1)}, u32[]{:S(2)}, u32[]{:S(2)}) %collective-permute-start.29) | collective-permute-done | bytes 524320 | tf_op jit(solution)/shard_map/ppermute | solution.py:835
  317.9 11.3 %collective-permute-done.32 = bf16[128,640]{1,0:T(8,128)(2,1)S(1)} collective-permute-done((bf16[128,640]{1,0:T(8,128)(2,1)S(1)}, bf16[128,640]{1,0:T(8,128)(2,1)S(1)}, u32[]{:S(2)}, u32[]{:S(2)}) %collective-permute-start.32) | collective-permute-done | bytes 163872 | tf_op jit(solution)/shard_map/ppermute | solution.py:838
  333.3 1.8 add_convert_fusion.2
  335.1 7.9 %reduce-scatter.2.cloned.1.call-done = bf16[1,384,1024]{2,1,0:T(8,128)(2,1)} async-done(((bf16[8,384,1024]{2,1,0:T(8,128)(2,1)}), bf16[1,384,1024]{2,1,0:T(8,128)(2,1)}) %reduce-scatter.2.cloned.1.call-update) | async-done | bytes 786448 | tf_op jit(solution)/shard_map/reduce_scatter | solution.py:1288
  345.7 3.3 collective-permute-start.34
  349.5 1.9 collective-permute-start.36
  353.9 1.8 collective-permute-done.34
  355.7 8.5 %collective-permute-done.35 = bf16[128,768]{1,0:T(8,128)(2,1)S(1)} collective-permute-done((bf16[128,768]{1,0:T(8,128)(2,1)}, bf16[128,768]{1,0:T(8,128)(2,1)S(1)}, u32[]{:S(2)}, u32[]{:S(2)}) %collective-permute-start.35) | collective-permute-done | bytes 196640 | tf_op jit(solution)/shard_map/ppermute | solution.py:838
  364.8 2.0 collective-permute-done.39.mate
  366.8 9.8 %collective-permute-start.40 = (bf16[128,1920]{1,0:T(8,128)(2,1)S(1)}, bf16[128,1920]{1,0:T(8,128)(2,1)S(1)}, u32[]{:S(2)}, u32[]{:S(2)}) collective-permute-start(bf16[128,1920]{1,0:T(8,128)(2,1)S(1)} %get-tuple-element.202), channel_id=1, source_target_pairs={{0,16},{8,24},{16,0},{24,8},{1,17},{9,25},{17,1},{25,9},{2,18},{10... | collective-permute-start | bytes 1474568 | tf_op jit(solution)/shard_map/ppermute | solution.py:835
  376.7 2.1 finish_ff.1
  379.3 8.9 %collective-permute-done.40 = bf16[128,1920]{1,0:T(8,128)(2,1)S(1)} collective-permute-done((bf16[128,1920]{1,0:T(8,128)(2,1)S(1)}, bf16[128,1920]{1,0:T(8,128)(2,1)S(1)}, u32[]{:S(2)}, u32[]{:S(2)}) %collective-permute-start.40) | collective-permute-done | bytes 491552 | tf_op jit(solution)/shard_map/ppermute | solution.py:835
  389.1 1.9 collective-permute-done.41.mates
  391.0 4.0 finish.1
  (427 shorter events, 102.1 us)
Async XLA Ops:
  7.2 144.4 %all-gather.3.cloned.1.call-start = ((), (), s32[]{:S(2)}) async-start(), calls=%async_computation.2 | async-start | bytes 6684672 | tf_op jit(solution)/shard_map/all_gather | solution.py:1130
  13.4 329.6 %reduce-scatter.2.cloned.1.call-start = ((), (), s32[]{:S(2)}) async-start(), calls=%async_computation.1 | async-start | bytes 7077888 | tf_op jit(solution)/shard_map/reduce_scatter | solution.py:1288
  15.7 42.4 %copy-start.92 = (f32[24]{0:T(128)S(1)}, f32[24]{0:T(128)}, u32[]{:S(2)}) copy-start(f32[24]{0:T(128)} %param.30) | copy-start | bytes 292
  15.9 43.2 %copy-start.93 = (f32[24]{0:T(128)S(1)}, f32[24]{0:T(128)}, u32[]{:S(2)}) copy-start(f32[24]{0:T(128)} %param.31) | copy-start | bytes 292
  15.9 43.4 %copy-start.87 = (f32[24]{0:T(128)S(1)}, f32[24]{0:T(128)}, u32[]{:S(2)}) copy-start(f32[24]{0:T(128)} %param.29) | copy-start | bytes 292
  15.9 43.4 %copy-start.20 = (bf16[192,1024]{1,0:T(8,128)(2,1)S(1)}, bf16[192,1024]{1,0:T(8,128)(2,1)}, u32[]{:S(2)}) copy-start(bf16[192,1024]{1,0:T(8,128)(2,1)} %w_out.1) | copy-start | bytes 1179652
  16.0 43.4 %copy-start.83 = (bf16[64,1024]{1,0:T(8,128)(2,1)S(1)}, bf16[64,1024]{1,0:T(8,128)(2,1)}, u32[]{:S(2)}) copy-start(bf16[64,1024]{1,0:T(8,128)(2,1)} %param.35) | copy-start | bytes 393220
  16.1 23.3 %collective-permute-start.2 = (bf16[128,1408]{1,0:T(8,128)(2,1)S(1)}, bf16[128,1408]{1,0:T(8,128)(2,1)S(1)}, u32[]{:S(2)}, u32[]{:S(2)}) collective-permute-start(bf16[128,1408]{1,0:T(8,128)(2,1)S(1)} %concatenate.111), channel_id=1, source_target_pairs={{0,2},{1,3},{2,4},{3,5},{4,6},{5,7},{6,0},{7,1},{8,10},{9,11},{10,... | collective-permute-start | bytes 1081352 | tf_op jit(solution)/shard_map/ppermute | solution.py:838
  19.2 34.2 %collective-permute-start.3 = (bf16[128,1408]{1,0:T(8,128)(2,1)S(1)}, bf16[128,1408]{1,0:T(8,128)(2,1)}, u32[]{:S(2)}, u32[]{:S(2)}) collective-permute-start(bf16[128,1408]{1,0:T(8,128)(2,1)S(1)} %concatenate.111), channel_id=1, source_target_pairs={{0,4},{1,5},{2,6},{3,7},{4,0},{5,1},{6,2},{7,3},{8,12},{9,13},{10,... | collective-permute-start | bytes 1081352 | tf_op jit(solution)/shard_map/ppermute | solution.py:838
  21.8 33.1 %collective-permute-start.4 = (bf16[128,1408]{1,0:T(8,128)(2,1)S(1)}, bf16[128,1408]{1,0:T(8,128)(2,1)}, u32[]{:S(2)}, u32[]{:S(2)}) collective-permute-start(bf16[128,1408]{1,0:T(8,128)(2,1)S(1)} %concatenate.111), channel_id=1, source_target_pairs={{0,6},{1,7},{2,0},{3,1},{4,2},{5,3},{6,4},{7,5},{8,14},{9,15},{10,... | collective-permute-start | bytes 1081352 | tf_op jit(solution)/shard_map/ppermute | solution.py:838
  23.1 15.6 %collective-permute-start = (bf16[256,1024]{1,0:T(8,128)(2,1)S(1)}, bf16[256,1024]{1,0:T(8,128)(2,1)S(1)}, u32[]{:S(2)}, u32[]{:S(2)}) collective-permute-start(bf16[256,1024]{1,0:T(8,128)(2,1)S(1)} %bitcast.279), channel_id=1, source_target_pairs={{0,16},{8,24},{16,0},{24,8},{1,17},{9,25},{17,1},{25,9},{2,18},{10... | collective-permute-start | bytes 1572872 | tf_op jit(solution)/shard_map/ppermute | solution.py:835
  38.9 21.4 %collective-permute-start.1 = (bf16[2,256,1024]{2,1,0:T(8,128)(2,1)S(1)}, bf16[2,256,1024]{2,1,0:T(8,128)(2,1)S(1)}, u32[]{:S(2)}, u32[]{:S(2)}) collective-permute-start(bf16[2,256,1024]{2,1,0:T(8,128)(2,1)S(1)} %pad_maximum_fusion.2.refs_0_), channel_id=1, source_target_pairs={{0,8},{8,0},{16,24},{24,16},{1,9},{9,1},{17,25},{25,17},{2,10},{10... | collective-permute-start | bytes 3145736 | tf_op jit(solution)/shard_map/ppermute | solution.py:835
  39.4 66.1 %copy-start.42 = (s32[9]{0:T(128)}, s32[9]{0:T(128)S(1)}, u32[]{:S(2)}) copy-start(s32[9]{0:T(128)S(1)} %pad_add_fusion.1.ends) | copy-start | bytes 112
  39.5 27.2 %copy-start.34 = (bf16[128,1408]{1,0:T(8,128)(2,1)}, bf16[128,1408]{1,0:T(8,128)(2,1)S(1)}, u32[]{:S(2)}) copy-start(bf16[128,1408]{1,0:T(8,128)(2,1)S(1)} %collective-permute-done.2) | copy-start | bytes 1081348
  39.5 28.5 %collective-permute-start.6 = (bf16[128,1408]{1,0:T(8,128)(2,1)S(1)}, bf16[128,1408]{1,0:T(8,128)(2,1)}, u32[]{:S(2)}, u32[]{:S(2)}) collective-permute-start(bf16[128,1408]{1,0:T(8,128)(2,1)S(1)} %collective-permute-done.2), channel_id=1, source_target_pairs={{0,1},{1,0},{2,3},{3,2},{4,5},{5,4},{6,7},{7,6},{8,9},{9,8},{10,11... | collective-permute-start | bytes 1081352 | tf_op jit(solution)/shard_map/ppermute | solution.py:835
  53.4 14.6 %collective-permute-start.7 = (bf16[128,1408]{1,0:T(8,128)(2,1)}, bf16[128,1408]{1,0:T(8,128)(2,1)}, u32[]{:S(2)}, u32[]{:S(2)}) collective-permute-start(bf16[128,1408]{1,0:T(8,128)(2,1)} %collective-permute-done.3), channel_id=1, source_target_pairs={{0,1},{1,0},{2,3},{3,2},{4,5},{5,4},{6,7},{7,6},{8,9},{9,8},{10,11... | collective-permute-start | bytes 1081352 | tf_op jit(solution)/shard_map/ppermute | solution.py:835
  54.9 23.4 %collective-permute-start.8 = (bf16[128,1408]{1,0:T(8,128)(2,1)}, bf16[128,1408]{1,0:T(8,128)(2,1)}, u32[]{:S(2)}, u32[]{:S(2)}) collective-permute-start(bf16[128,1408]{1,0:T(8,128)(2,1)} %collective-permute-done.4), channel_id=1, source_target_pairs={{0,1},{1,0},{2,3},{3,2},{4,5},{5,4},{6,7},{7,6},{8,9},{9,8},{10,11... | collective-permute-start | bytes 1081352 | tf_op jit(solution)/shard_map/ppermute | solution.py:835
  55.4 29.4 %collective-permute-start.5 = (bf16[128,1408]{1,0:T(8,128)(2,1)S(1)}, bf16[128,1408]{1,0:T(8,128)(2,1)}, u32[]{:S(2)}, u32[]{:S(2)}) collective-permute-start(bf16[128,1408]{1,0:T(8,128)(2,1)S(1)} %concatenate.111), channel_id=1, source_target_pairs={{0,1},{1,0},{2,3},{3,2},{4,5},{5,4},{6,7},{7,6},{8,9},{9,8},{10,11... | collective-permute-start | bytes 1081352 | tf_op jit(solution)/shard_map/ppermute | solution.py:835
  59.2 46.2 %copy-start.43 = (f32[6]{0:T(128)}, f32[6]{0:T(128)S(1)}, u32[]{:S(2)}) copy-start(f32[6]{0:T(128)S(1)} %dynamic_slice.150.skip) | copy-start | bytes 76
  59.4 38.1 %copy-start.41 = (f32[8,128]{1,0:T(8,128)}, f32[8,128]{1,0:T(8,128)S(1)}, u32[]{:S(2)}) copy-start(f32[8,128]{1,0:T(8,128)S(1)} %select_maximum_fusion.params) | copy-start | bytes 12292
  60.3 55.9 %collective-permute-start.11 = (bf16[256,1024]{1,0:T(8,128)(2,1)}, bf16[256,1024]{1,0:T(8,128)(2,1)}, u32[]{:S(2)}, u32[]{:S(2)}) collective-permute-start(bf16[256,1024]{1,0:T(8,128)(2,1)} %pad_maximum_fusion.10), channel_id=1, source_target_pairs={{0,0},{1,1},{2,8},{3,9},{4,16},{5,17},{6,24},{7,25},{8,2},{9,3},{1... | collective-permute-start | bytes 1572872 | tf_op jit(solution)/shard_map/ppermute | solution.py:847
  105.4 20.8 %copy-start.36 = (f32[16,1024]{1,0:T(8,128)}, f32[16,1024]{1,0:T(8,128)S(1)}, u32[]{:S(2)}) copy-start(f32[16,1024]{1,0:T(8,128)S(1)} %get-tuple-element.122.rows) | copy-start | bytes 196612
  116.2 130.2 %copy-start.2 = (f32[1024,384]{1,0:T(8,128)}, f32[1024,384]{1,0:T(8,128)S(1)}, u32[]{:S(2)}) copy-start(f32[1024,384]{1,0:T(8,128)S(1)} %get-tuple-element.123.y_ref) | copy-start | bytes 4718596
  116.2 23.0 %collective-permute-start.12 = (bf16[256,1024]{1,0:T(8,128)(2,1)}, bf16[256,1024]{1,0:T(8,128)(2,1)}, u32[]{:S(2)}, u32[]{:S(2)}) collective-permute-start(bf16[256,1024]{1,0:T(8,128)(2,1)} %collective-permute-done.11), channel_id=1, source_target_pairs={{0,1},{1,0},{2,3},{3,2},{4,5},{5,4},{6,7},{7,6},{8,9},{9,8},{10,11... | collective-permute-start | bytes 1572872 | tf_op jit(solution)/shard_map/ppermute | solution.py:835
  126.2 14.7 %copy-start.28 = (bf16[1024,256]{1,0:T(8,128)(2,1)}, bf16[1024,256]{1,0:T(8,128)(2,1)S(1)}, u32[]{:S(2)}) copy-start(bf16[1024,256]{1,0:T(8,128)(2,1)S(1)} %get-tuple-element.148.qkv_ref) | copy-start | bytes 1572868
  126.2 14.8 %copy-start.4 = (f32[1024,384]{1,0:T(8,128)}, f32[1024,384]{1,0:T(8,128)S(1)}, u32[]{:S(2)}) copy-start(f32[1024,384]{1,0:T(8,128)S(1)} %get-tuple-element.126.z_ref) | copy-start | bytes 4718596
  128.4 1.2 collective-permute-start.9
  129.6 7.4 %collective-permute-start.10 = (f32[16,128]{1,0:T(8,128)S(1)}, f32[16,128]{1,0:T(8,128)S(1)}, u32[]{:S(2)}, u32[]{:S(2)}) collective-permute-start(f32[16,128]{1,0:T(8,128)S(1)} %add.420), channel_id=1, source_target_pairs={{0,16},{8,24},{16,0},{24,8},{1,17},{9,25},{17,1},{25,9},{2,18},{10... | collective-permute-start | bytes 24584 | tf_op jit(solution)/shard_map/ppermute | solution.py:835
  146.3 3.0 collective-permute-start.13
  151.6 14.3 %collective-permute-start.14 = (bf16[256,1024]{1,0:T(8,128)(2,1)}, bf16[256,1024]{1,0:T(8,128)(2,1)}, u32[]{:S(2)}, u32[]{:S(2)}) collective-permute-start(bf16[256,1024]{1,0:T(8,128)(2,1)} %fusion.17), channel_id=1, source_target_pairs={{0,16},{8,24},{16,0},{24,8},{1,17},{9,25},{17,1},{25,9},{2,18},{10... | collective-permute-start | bytes 1572872 | tf_op jit(solution)/shard_map/ppermute | solution.py:835
  168.0 2.0 collective-permute-start.15
  174.0 2.0 collective-permute-start.16
  177.9 2.0 collective-permute-start.17
  198.8 2.3 collective-permute-start.18
  206.5 14.0 %collective-permute-start.19 = (bf16[256,1024]{1,0:T(8,128)(2,1)S(1)}, bf16[256,1024]{1,0:T(8,128)(2,1)S(1)}, u32[]{:S(2)}, u32[]{:S(2)}) collective-permute-start(bf16[256,1024]{1,0:T(8,128)(2,1)S(1)} %get-tuple-element.224), channel_id=1, source_target_pairs={{0,16},{8,24},{16,0},{24,8},{1,17},{9,25},{17,1},{25,9},{2,18},{10... | collective-permute-start | bytes 1572872 | tf_op jit(solution)/shard_map/ppermute | solution.py:835
  221.5 3.0 collective-permute-start.20
  230.2 3.3 collective-permute-start.21
  233.5 12.9 %collective-permute-start.22 = (f32[8,128]{1,0:T(8,128)S(1)}, f32[8,128]{1,0:T(8,128)S(1)}, u32[]{:S(2)}, u32[]{:S(2)}) collective-permute-start(f32[8,128]{1,0:T(8,128)S(1)} %bitcast_add_fusion), channel_id=1, source_target_pairs={{0,16},{8,24},{16,0},{24,8},{1,17},{9,25},{17,1},{25,9},{2,18},{10... | collective-permute-start | bytes 12296 | tf_op jit(solution)/shard_map/ppermute | solution.py:835
  235.9 17.9 %collective-permute-start.23 = (bf16[256,1024]{1,0:T(8,128)(2,1)}, bf16[256,1024]{1,0:T(8,128)(2,1)}, u32[]{:S(2)}, u32[]{:S(2)}) collective-permute-start(bf16[256,1024]{1,0:T(8,128)(2,1)} %dynamic-slice_bitcast_fusion.2), channel_id=1, source_target_pairs={{0,1},{1,0},{2,3},{3,2},{4,5},{5,4},{6,7},{7,6},{8,9},{9,8},{10,11... | collective-permute-start | bytes 1572872 | tf_op jit(solution)/shard_map/ppermute | solution.py:835
  255.1 29.1 %collective-permute-start.24 = (bf16[4,128,640]{2,1,0:T(8,128)(2,1)}, bf16[4,128,640]{2,1,0:T(8,128)(2,1)S(1)}, u32[]{:S(2)}, u32[]{:S(2)}) collective-permute-start(bf16[4,128,640]{2,1,0:T(8,128)(2,1)} %dynamic-slice_bitcast_fusion.1), channel_id=1, source_target_pairs={{0,1},{1,0},{2,3},{3,2},{4,5},{5,4},{6,7},{7,6},{8,9},{9,8},{10,11... | collective-permute-start | bytes 1966088 | tf_op jit(solution)/shard_map/ppermute | solution.py:835
  258.1 26.0 %collective-permute-start.25 = (bf16[64,1024]{1,0:T(8,128)(2,1)S(1)}, bf16[64,1024]{1,0:T(8,128)(2,1)S(1)}, u32[]{:S(2)}, u32[]{:S(2)}) collective-permute-start(bf16[64,1024]{1,0:T(8,128)(2,1)S(1)} %get-tuple-element.247), channel_id=1, source_target_pairs={{0,2},{1,3},{2,4},{3,5},{4,6},{5,7},{6,0},{7,1},{8,10},{9,11},{10,... | collective-permute-start | bytes 393224 | tf_op jit(solution)/shard_map/ppermute | solution.py:838
  259.7 24.5 %collective-permute-start.26 = (bf16[64,1024]{1,0:T(8,128)(2,1)S(1)}, bf16[64,1024]{1,0:T(8,128)(2,1)S(1)}, u32[]{:S(2)}, u32[]{:S(2)}) collective-permute-start(bf16[64,1024]{1,0:T(8,128)(2,1)S(1)} %get-tuple-element.246), channel_id=1, source_target_pairs={{0,4},{1,5},{2,6},{3,7},{4,0},{5,1},{6,2},{7,3},{8,12},{9,13},{10,... | collective-permute-start | bytes 393224 | tf_op jit(solution)/shard_map/ppermute | solution.py:838
  263.7 20.5 %collective-permute-start.27 = (bf16[64,1024]{1,0:T(8,128)(2,1)S(1)}, bf16[64,1024]{1,0:T(8,128)(2,1)S(1)}, u32[]{:S(2)}, u32[]{:S(2)}) collective-permute-start(bf16[64,1024]{1,0:T(8,128)(2,1)S(1)} %get-tuple-element.245), channel_id=1, source_target_pairs={{0,6},{1,7},{2,0},{3,1},{4,2},{5,3},{6,4},{7,5},{8,14},{9,15},{10,... | collective-permute-start | bytes 393224 | tf_op jit(solution)/shard_map/ppermute | solution.py:838
  264.8 20.4 %copy-start.13 = (bf16[1024,1024]{1,0:T(8,128)(2,1)S(1)}, bf16[1024,1024]{1,0:T(8,128)(2,1)}, u32[]{:S(2)}) copy-start(bf16[1024,1024]{1,0:T(8,128)(2,1)} %copy-done.10) | copy-start | bytes 6291460
  299.6 2.7 collective-permute-start.28
  302.4 14.0 %collective-permute-start.29 = (bf16[256,1024]{1,0:T(8,128)(2,1)S(1)}, bf16[256,1024]{1,0:T(8,128)(2,1)S(1)}, u32[]{:S(2)}, u32[]{:S(2)}) collective-permute-start(bf16[256,1024]{1,0:T(8,128)(2,1)S(1)} %fusion.14), channel_id=1, source_target_pairs={{0,16},{8,24},{16,0},{24,8},{1,17},{9,25},{17,1},{25,9},{2,18},{10... | collective-permute-start | bytes 1572872 | tf_op jit(solution)/shard_map/ppermute | solution.py:835
  304.3 25.1 %collective-permute-start.30 = (bf16[4,128,768]{1,2,0:T(8,128)(2,1)S(1)}, bf16[4,128,768]{1,2,0:T(8,128)(2,1)S(1)}, u32[]{:S(2)}, u32[]{:S(2)}) collective-permute-start(bf16[4,128,768]{1,2,0:T(8,128)(2,1)S(1)} %dynamic-slice_bitcast_fusion), channel_id=1, source_target_pairs={{0,1},{1,0},{2,3},{3,2},{4,5},{5,4},{6,7},{7,6},{8,9},{9,8},{10,11... | collective-permute-start | bytes 2359304 | tf_op jit(solution)/shard_map/ppermute | solution.py:835
  305.5 12.3 %collective-permute-start.31 = (bf16[128,640]{1,0:T(8,128)(2,1)S(1)}, bf16[128,640]{1,0:T(8,128)(2,1)S(1)}, u32[]{:S(2)}, u32[]{:S(2)}) collective-permute-start(bf16[128,640]{1,0:T(8,128)(2,1)S(1)} %get-tuple-element.243), channel_id=1, source_target_pairs={{0,2},{1,3},{2,4},{3,5},{4,6},{5,7},{6,0},{7,1},{8,10},{9,11},{10,... | collective-permute-start | bytes 491528 | tf_op jit(solution)/shard_map/ppermute | solution.py:838
  307.5 21.7 %collective-permute-start.32 = (bf16[128,640]{1,0:T(8,128)(2,1)S(1)}, bf16[128,640]{1,0:T(8,128)(2,1)S(1)}, u32[]{:S(2)}, u32[]{:S(2)}) collective-permute-start(bf16[128,640]{1,0:T(8,128)(2,1)S(1)} %get-tuple-element.242), channel_id=1, source_target_pairs={{0,4},{1,5},{2,6},{3,7},{4,0},{5,1},{6,2},{7,3},{8,12},{9,13},{10,... | collective-permute-start | bytes 491528 | tf_op jit(solution)/shard_map/ppermute | solution.py:838
  307.7 21.6 %collective-permute-start.33 = (bf16[128,640]{1,0:T(8,128)(2,1)S(1)}, bf16[128,640]{1,0:T(8,128)(2,1)S(1)}, u32[]{:S(2)}, u32[]{:S(2)}) collective-permute-start(bf16[128,640]{1,0:T(8,128)(2,1)S(1)} %get-tuple-element.241), channel_id=1, source_target_pairs={{0,6},{1,7},{2,0},{3,1},{4,2},{5,3},{6,4},{7,5},{8,14},{9,15},{10,... | collective-permute-start | bytes 491528 | tf_op jit(solution)/shard_map/ppermute | solution.py:838
  329.5 22.8 %copy-start.53 = (bf16[1,256,1024]{2,1,0:T(8,128)(2,1)S(1)}, bf16[1,256,1024]{2,1,0:T(8,128)(2,1)}, u32[]{:S(2)}) copy-start(bf16[1,256,1024]{2,1,0:T(8,128)(2,1)} %param.21) | copy-start | bytes 1572868
  330.8 21.9 %copy-start.56 = (f32[256,1024]{1,0:T(8,128)S(1)}, f32[256,1024]{1,0:T(8,128)}, u32[]{:S(2)}) copy-start(f32[256,1024]{1,0:T(8,128)} %get-tuple-element.225) | copy-start | bytes 3145732
  343.0 21.1 %collective-permute-start.38 = (bf16[384,1024]{1,0:T(8,128)(2,1)}, bf16[384,1024]{1,0:T(8,128)(2,1)S(1)}, u32[]{:S(2)}, u32[]{:S(2)}) collective-permute-start(bf16[384,1024]{1,0:T(8,128)(2,1)} %bitcast.302), channel_id=1, source_target_pairs={{0,16},{8,24},{16,0},{24,8},{1,17},{9,25},{17,1},{25,9},{2,18},{10... | collective-permute-start | bytes 2359304 | tf_op jit(solution)/shard_map/ppermute | solution.py:835
  345.7 10.0 %collective-permute-start.34 = (bf16[128,768]{1,0:T(8,128)(2,1)}, bf16[128,768]{1,0:T(8,128)(2,1)S(1)}, u32[]{:S(2)}, u32[]{:S(2)}) collective-permute-start(bf16[128,768]{1,0:T(8,128)(2,1)} %bitcast.107), channel_id=1, source_target_pairs={{0,2},{1,3},{2,4},{3,5},{4,6},{5,7},{6,0},{7,1},{8,10},{9,11},{10,... | collective-permute-start | bytes 589832 | tf_op jit(solution)/shard_map/ppermute | solution.py:838
  349.0 15.2 %collective-permute-start.35 = (bf16[128,768]{1,0:T(8,128)(2,1)}, bf16[128,768]{1,0:T(8,128)(2,1)S(1)}, u32[]{:S(2)}, u32[]{:S(2)}) collective-permute-start(bf16[128,768]{1,0:T(8,128)(2,1)} %bitcast.108), channel_id=1, source_target_pairs={{0,4},{1,5},{2,6},{3,7},{4,0},{5,1},{6,2},{7,3},{8,12},{9,13},{10,... | collective-permute-start | bytes 589832 | tf_op jit(solution)/shard_map/ppermute | solution.py:838
  349.5 14.7 %collective-permute-start.36 = (bf16[128,768]{1,0:T(8,128)(2,1)}, bf16[128,768]{1,0:T(8,128)(2,1)S(1)}, u32[]{:S(2)}, u32[]{:S(2)}) collective-permute-start(bf16[128,768]{1,0:T(8,128)(2,1)} %bitcast.109), channel_id=1, source_target_pairs={{0,6},{1,7},{2,0},{3,1},{4,2},{5,3},{6,4},{7,5},{8,14},{9,15},{10,... | collective-permute-start | bytes 589832 | tf_op jit(solution)/shard_map/ppermute | solution.py:838
  351.4 2.5 collective-permute-start.37
  353.9 22.7 %copy-start.14 = (bf16[128,2048]{1,0:T(8,128)(2,1)S(1)}, bf16[128,2048]{1,0:T(8,128)(2,1)}, u32[]{:S(2)}) copy-start(bf16[128,2048]{1,0:T(8,128)(2,1)} %w_up.1) | copy-start | bytes 1572868
  353.9 22.7 %copy-start.16 = (bf16[128,2048]{1,0:T(8,128)(2,1)S(1)}, bf16[128,2048]{1,0:T(8,128)(2,1)}, u32[]{:S(2)}) copy-start(bf16[128,2048]{1,0:T(8,128)(2,1)} %w_gate.1) | copy-start | bytes 1572868
  364.5 2.4 collective-permute-start.39
  366.8 21.3 %collective-permute-start.40 = (bf16[128,1920]{1,0:T(8,128)(2,1)S(1)}, bf16[128,1920]{1,0:T(8,128)(2,1)S(1)}, u32[]{:S(2)}, u32[]{:S(2)}) collective-permute-start(bf16[128,1920]{1,0:T(8,128)(2,1)S(1)} %get-tuple-element.202), channel_id=1, source_target_pairs={{0,16},{8,24},{16,0},{24,8},{1,17},{9,25},{17,1},{25,9},{2,18},{10... | collective-permute-start | bytes 1474568 | tf_op jit(solution)/shard_map/ppermute | solution.py:835
  376.6 14.4 %copy-start.21 = (bf16[192,1024]{1,0:T(8,128)(2,1)S(1)}, bf16[192,1024]{1,0:T(8,128)(2,1)}, u32[]{:S(2)}) copy-start(bf16[192,1024]{1,0:T(8,128)(2,1)} %w_out.1) | copy-start | bytes 1179652
  376.7 14.4 %copy-start.23 = (bf16[128,3352]{0,1:T(8,128)(2,1)S(1)}, bf16[128,3352]{0,1:T(8,128)(2,1)}, u32[]{:S(2)}) copy-start(bf16[128,3352]{0,1:T(8,128)(2,1)} %param.26) | copy-start | bytes 2574340
  388.3 2.8 collective-permute-start.41
  (77 other events, 352.3 us)
Sparse Core Ops, SparseCore 0:
  13.5 136.3 all-gather.2
  199.1 143.9 reduce-scatter.1

commit v5 on v4

--- a/solution.py
+++ b/solution.py
@@ -1132,9 +1132,10 @@
     ).reshape((places_x, m) + w_ff.shape)
     if net.direct:
         both_cols = jnp.concatenate([first, second], axis=1)
-        pair = jnp.stack([tokens[0], net.flip_x(tokens[0])])
         near = net.along_z(both_cols)
-        far = net.along_y([tie(near[0], pair)] + near[1:])
+        own_tokens = tie(tokens[0], near[1])
+        pair = jnp.stack([own_tokens, net.flip_x(own_tokens)])
+        far = net.along_y(near)
         all_tokens = put([pair, net.flip_core(pair)], [c, c ^ 2, c ^ 1, c ^ 3])
         w_first, w_second = net.in_order(
             [tie(near[0], all_tokens)[None]] + [p[None] for p in near[1:]],

time: 414 us -> 411 us (level)
  waiting for transfers between devices: 134 us -> 129 us
    ppermute x24, waiting for transfers between devices: 83.9 us -> 74.7 us  [flip(): return lax.ppermute(value, axis, [(i, i ^ bit) for i in range(size)])]
    all_gather x1, waiting for transfers between devices: 0.01 us -> 5.63 us  [per_device(): lax.all_gather(w_ff, ('ctx', 'fsdp'), axis=0, tiled=False, axis_index_gro...]
where the time goes in v5:
time: 411 us; the launch traced here: 404 us
  waiting for transfers between devices  129 us (31%)
  Pallas kernels  70.3 us (17%)
  local copies, waits for them, and re-layouts  63.9 us (16%)
  starting transfers between devices  62 us (15%)
  other arithmetic  30.9 us (8%)
  matrix products  28.7 us (7%)
  between operations  19 us (5%)
    ppermute x24, waiting for transfers between devices, flip(): return lax.ppermute(value, axis, [(i, i ^ bit) for i in range(size)])  74.7 us
    ppermute x12, waiting for transfers between devices, shift_z(): lax.ppermute(value, 'fsdp', [(i, (i + 2 * by) % self.m) for i in range(se...  36.2 us
    ppermute x24, starting transfers between devices, flip(): return lax.ppermute(value, axis, [(i, i ^ bit) for i in range(size)])  29.9 us
    unnamed x200, local copies, waits for them, and re-layouts  25.5 us
    ppermute x12, starting transfers between devices, shift_z(): lax.ppermute(value, 'fsdp', [(i, (i + 2 * by) % self.m) for i in range(se...  24.8 us
    pallas_call x1, Pallas kernels, ssm_backward(): pl.pallas_call(functools.partial(ssm_bwd_kernel, heads), grid=(steps,), i...  19.4 us
    dot_general x7, matrix products, nt(): lax.dot_general(left, right, (((1,), (1,)), ((), ())), preferred_element_...  15.9 us
    pallas_call x1, Pallas kernels, attn_backward(): pl.pallas_call(functools.partial(attn_bwd_kernel, heads, blocks), grid=(b...  9.96 us
  transfers between devices with their start and end apart: 44, of which 26 were waited for; matrix products, arithmetic and copies ran while one was open for 18% of the time, Pallas kernels for 15%

profile of v5, /device:TPU:0, one launch (start us, length us, event | category | flops | bytes accessed | tf_op | source)
XLA Modules:
  0.0 404.3 jit_solution(16351665574593835052)
XLA Ops:
  16.1 3.1 collective-permute-start
  19.2 2.6 collective-permute-start.3
  24.7 6.7 %collective-permute-done = bf16[128,1408]{1,0:T(8,128)(2,1)S(1)} collective-permute-done((bf16[128,1408]{1,0:T(8,128)(2,1)S(1)}, bf16[128,1408]{1,0:T(8,128)(2,1)S(1)}, u32[]{:S(2)}, u32[]{:S(2)}) %collective-permute-start) | collective-permute-done | bytes 360480 | tf_op jit(solution)/shard_map/ppermute | solution.py:838
  31.3 2.0 collective-permute-start.1
  33.6 9.3 %collective-permute-done.1 = bf16[256,1024]{1,0:T(8,128)(2,1)S(1)} collective-permute-done((bf16[256,1024]{1,0:T(8,128)(2,1)S(1)}, bf16[256,1024]{1,0:T(8,128)(2,1)S(1)}, u32[]{:S(2)}, u32[]{:S(2)}) %collective-permute-start.1) | collective-permute-done | bytes 524320 | tf_op jit(solution)/shard_map/ppermute | solution.py:835
  44.9 8.6 %collective-permute-done.3 = bf16[128,1408]{1,0:T(8,128)(2,1)} collective-permute-done((bf16[128,1408]{1,0:T(8,128)(2,1)S(1)}, bf16[128,1408]{1,0:T(8,128)(2,1)}, u32[]{:S(2)}, u32[]{:S(2)}) %collective-permute-start.3) | collective-permute-done | bytes 360480 | tf_op jit(solution)/shard_map/ppermute | solution.py:838
  58.7 5.7 %collective-permute-start.11 = (bf16[256,1024]{1,0:T(8,128)(2,1)}, bf16[256,1024]{1,0:T(8,128)(2,1)}, u32[]{:S(2)}, u32[]{:S(2)}) collective-permute-start(bf16[256,1024]{1,0:T(8,128)(2,1)} %pad_maximum_fusion.10), channel_id=1, source_target_pairs={{0,0},{1,1},{2,8},{3,9},{4,16},{5,17},{6,24},{7,25},{8,2},{9,3},{1... | collective-permute-start | bytes 1572872 | tf_op jit(solution)/shard_map/ppermute | solution.py:847
  66.6 10.5 %collective-permute-done.8 = bf16[128,1408]{1,0:T(8,128)(2,1)} collective-permute-done((bf16[128,1408]{1,0:T(8,128)(2,1)}, bf16[128,1408]{1,0:T(8,128)(2,1)}, u32[]{:S(2)}, u32[]{:S(2)}) %collective-permute-start.8) | collective-permute-done | bytes 360480 | tf_op jit(solution)/shard_map/ppermute | solution.py:835
  77.1 2.8 put.4
  84.1 2.0 fusion.40
  90.4 5.2 %project_conv.1 = (bf16[1024,1024]{1,0:T(8,128)(2,1)S(1)}, bf16[1024,640]{1,0:T(8,128)(2,1)S(1)}, bf16[1024,640]{1,0:T(8,128)(2,1)S(1)}, bf16[1024,640]{1,0:T(8,...) custom-call(bf16[1024,1024]{1,0:T(8,128)(2,1)S(1)} %bitcast.261, f32[1,1024]{1,0:T(1,128)S(1)} %bitcast.270, ...), custom_call_target="tpu_custom_call" | custom-call | flops 1610612736 | bytes 10000000 | tf_op jit(solution)/shard_map/project_conv/pallas_call | solution.py:100
  96.7 7.4 %ssm_forward.1 = (f32[1024,384]{1,0:T(8,128)S(1)}, f32[8,384,128]{2,1,0:T(8,128)S(1)}) custom-call(s32[9]{0:T(128)S(1)} %pad_add_fusion.1.ends, f32[6]{0:T(128)S(1)} %dynamic_slice.150.skip, bf16[1024,640]{1,0:T(8,128)(2,1)S(1)} %get-tuple-element.120.act, f32[1024,256]{1,0:T(8,128)S(1)} %get-tuple-element.121.steps, ...), custom_call_target="tpu_custom_call" | custom-call | flops 1000000000 | bytes 40000000 | tf_op jit(solution)/shard_map/ssm_forward/pallas_call | solution.py:429
  107.4 1.8 collective-permute-start.12
  111.9 1.6 copy-done.11
  113.5 4.0 project_gate.1
  122.4 5.9 %attn_forward.1 = (bf16[1024,128]{1,0:T(8,128)(2,1)S(1)}, f32[1024,2]{1,0:T(8,128)S(1)}) custom-call(bf16[1024,256]{1,0:T(8,128)(2,1)S(1)} %get-tuple-element.148.qkv_ref, s32[1024,1]{1,0:T(8,128)S(1)} %copy-done.7, s32[1,1024]{1,0:T(1,128)S(1)} %copy-done.31), custom_call_target="tpu_custom_call" | custom-call | flops 1000000000 | bytes 20000000 | tf_op jit(solution)/shard_map/attn_forward/pallas_call | solution.py:584
  128.3 4.8 %collective-permute-done.12 = bf16[256,1024]{1,0:T(8,128)(2,1)} collective-permute-done((bf16[256,1024]{1,0:T(8,128)(2,1)}, bf16[256,1024]{1,0:T(8,128)(2,1)}, u32[]{:S(2)}, u32[]{:S(2)}) %collective-permute-start.12) | collective-permute-done | bytes 524320 | tf_op jit(solution)/shard_map/ppermute | solution.py:835
  133.2 1.8 maximum_select_fusion
  137.3 1.9 copy-done.47
  140.4 3.0 collective-permute-done.13
  143.4 2.3 fusion.17
  145.7 5.6 %all-gather.3.cloned.1.call-done = bf16[3072,1024]{1,0:T(8,128)(2,1)} async-done(((bf16[192,1024]{1,0:T(8,128)(2,1)}), bf16[3072,1024]{1,0:T(8,128)(2,1)}) %all-gather.3.cloned.1.call-update) | async-done | bytes 6291472 | tf_op jit(solution)/shard_map/all_gather | solution.py:1130
  152.8 4.1 %slice_bitcast_fusion = (bf16[8,2,64,1024]{3,2,0,1:T(8,128)(2,1)S(1)}, bf16[8,2,64,1024]{3,2,0,1:T(8,128)(2,1)S(1)}, bf16[8,2,64,1024]{3,2,0,1:T(8,128)(2,1)S(1)}) fusion(bf16[2,8,192,1024]{3,2,1,0:T(8,128)(2,1)} %bitcast.281), kind=kLoop, calls=%fused_computation.7 | loop fusion | bytes 12582912 | tf_op jit(solution)/shard_map/transpose | solution.py:1234
  157.6 7.3 %collective-permute-done.14 = bf16[256,1024]{1,0:T(8,128)(2,1)} collective-permute-done((bf16[256,1024]{1,0:T(8,128)(2,1)}, bf16[256,1024]{1,0:T(8,128)(2,1)}, u32[]{:S(2)}, u32[]{:S(2)}) %collective-permute-start.14) | collective-permute-done | bytes 524320 | tf_op jit(solution)/shard_map/ppermute | solution.py:835
  164.9 1.9 multiply_reduce_fusion.2
  167.1 1.9 collective-permute-done.15
  177.2 1.7 collective-permute-done.17
  178.8 1.8 multiply_convert_fusion.1
  180.7 2.6 fusion.46
  183.4 5.7 %ff_gradients.1 = bf16[8,384,1024]{2,1,0:T(8,128)(2,1)S(1)} custom-call(bf16[512,1024]{1,0:T(8,128)(2,1)S(1)} %pad_maximum_fusion.3.both, bf16[512,1024]{1,0:T(8,128)(2,1)S(1)} %get-tuple-element.280.product, bf16[512,1024]{1,0:T(8,128)(2,1)S(1)} %get-tuple-element.143.g_gate, bf16[512,1024]{1,0:T(8,128)(2,1)S(1)} %get-tuple-element.234.g_up, ...), custom_call_target="tpu_custom_call" | custom-call | flops 3221225472 | bytes 10000000 | tf_op jit(solution)/shard_map/ff_gradients/pallas_call | solution.py:640
  189.1 2.6 copy-done.3
  191.7 3.8 convolution_add_fusion.2
  198.0 2.1 collective-permute-done.18
  200.0 2.0 multiply_reduce_fusion.1
  202.0 3.4 fusion.36
  206.9 12.5 %collective-permute-done.19 = bf16[256,1024]{1,0:T(8,128)(2,1)S(1)} collective-permute-done((bf16[256,1024]{1,0:T(8,128)(2,1)S(1)}, bf16[256,1024]{1,0:T(8,128)(2,1)S(1)}, u32[]{:S(2)}, u32[]{:S(2)}) %collective-permute-start.19) | collective-permute-done | bytes 524320 | tf_op jit(solution)/shard_map/ppermute | solution.py:835
  220.5 3.0 collective-permute-done.20.refs_1_
  223.5 3.1 put.5
  226.6 2.5 multiply_reduce_fusion
  235.4 10.0 %attn_backward.1 = bf16[1024,256]{1,0:T(8,128)(2,1)} custom-call(bf16[1024,256]{1,0:T(8,128)(2,1)} %copy-done.28, s32[1024,1]{1,0:T(8,128)} %copy.187.seg_c, s32[1,1024]{1,0:T(1,128)} %seg_r.7, f32[1024,2]{1,0:T(8,128)} %copy-done.29, bf16[1024,128]{1,0:T(8,128)(2,1)} %convolution_convert_fusion.4.go_ref, f32[1024,256]{1,0:T(8,128)} %constant.374.clone.cosine, ...), custom_call_target="tpu_custom_call" | custom-call | flops 10000000 | bytes 1000000 | tf_op jit(solution)/shard_map/attn_backward/pallas_call | solution.py:608
  245.4 2.4 multiply_convert_fusion.3
  247.8 1.9 convolution_convert_fusion.1
  256.0 3.3 collective-permute-start.25
  260.6 2.9 collective-permute-start.27
  264.6 19.4 %ssm_backward.1 = (bf16[1024,768]{1,0:T(8,128)(2,1)}, f32[8,640]{1,0:T(8,128)}, f32[8,384]{1,0:T(8,128)}, f32[8,128]{1,0:T(8,128)}) custom-call(s32[9]{0:T(128)} %copy-done.42, f32[6]{0:T(128)} %copy-done.43, bf16[1024,640]{1,0:T(8,128)(2,1)} %copy-done.26, f32[1024,256]{1,0:T(8,128)} %copy-done.27, f32[16,1024]{1,0:T(8,128)} %copy-done.36, ...), custom_call_target="tpu_custom_call" | custom-call | flops 10000000 | bytes 1000000 | tf_op jit(solution)/shard_map/ssm_backward/pallas_call | solution.py:466
  285.0 3.3 convolution_convert_fusion
  291.1 1.9 copy.220
  295.5 1.8 fusion.47
  297.4 1.9 convolution_add_fusion.1
  299.5 2.6 collective-permute-done.28
  305.5 3.2 collective-permute-start.33
  308.7 7.7 %collective-permute-done.29 = bf16[256,1024]{1,0:T(8,128)(2,1)S(1)} collective-permute-done((bf16[256,1024]{1,0:T(8,128)(2,1)S(1)}, bf16[256,1024]{1,0:T(8,128)(2,1)S(1)}, u32[]{:S(2)}, u32[]{:S(2)}) %collective-permute-start.29) | collective-permute-done | bytes 524320 | tf_op jit(solution)/shard_map/ppermute | solution.py:835
  317.4 10.7 %collective-permute-done.32 = bf16[128,640]{1,0:T(8,128)(2,1)S(1)} collective-permute-done((bf16[128,640]{1,0:T(8,128)(2,1)S(1)}, bf16[128,640]{1,0:T(8,128)(2,1)S(1)}, u32[]{:S(2)}, u32[]{:S(2)}) %collective-permute-start.32) | collective-permute-done | bytes 163872 | tf_op jit(solution)/shard_map/ppermute | solution.py:838
  332.1 1.8 add_convert_fusion.2
  333.9 6.0 %reduce-scatter.2.cloned.1.call-done = bf16[1,384,1024]{2,1,0:T(8,128)(2,1)} async-done(((bf16[8,384,1024]{2,1,0:T(8,128)(2,1)}), bf16[1,384,1024]{2,1,0:T(8,128)(2,1)}) %reduce-scatter.2.cloned.1.call-update) | async-done | bytes 786448 | tf_op jit(solution)/shard_map/reduce_scatter | solution.py:1289
  342.5 4.0 collective-permute-start.34
  346.7 2.2 collective-permute-start.36
  352.5 8.5 %collective-permute-done.35 = bf16[128,768]{1,0:T(8,128)(2,1)S(1)} collective-permute-done((bf16[128,768]{1,0:T(8,128)(2,1)}, bf16[128,768]{1,0:T(8,128)(2,1)S(1)}, u32[]{:S(2)}, u32[]{:S(2)}) %collective-permute-start.35) | collective-permute-done | bytes 196640 | tf_op jit(solution)/shard_map/ppermute | solution.py:838
  361.6 2.0 collective-permute-done.39.mate
  363.6 9.9 %collective-permute-start.40 = (bf16[128,1920]{1,0:T(8,128)(2,1)S(1)}, bf16[128,1920]{1,0:T(8,128)(2,1)S(1)}, u32[]{:S(2)}, u32[]{:S(2)}) collective-permute-start(bf16[128,1920]{1,0:T(8,128)(2,1)S(1)} %get-tuple-element.202), channel_id=1, source_target_pairs={{0,16},{8,24},{16,0},{24,8},{1,17},{9,25},{17,1},{25,9},{2,18},{10... | collective-permute-start | bytes 1474568 | tf_op jit(solution)/shard_map/ppermute | solution.py:835
  373.6 2.1 finish_ff.1
  376.2 8.9 %collective-permute-done.40 = bf16[128,1920]{1,0:T(8,128)(2,1)S(1)} collective-permute-done((bf16[128,1920]{1,0:T(8,128)(2,1)S(1)}, bf16[128,1920]{1,0:T(8,128)(2,1)S(1)}, u32[]{:S(2)}, u32[]{:S(2)}) %collective-permute-start.40) | collective-permute-done | bytes 491552 | tf_op jit(solution)/shard_map/ppermute | solution.py:835
  386.0 1.9 collective-permute-done.41.mates
  387.9 4.0 finish.1
  (427 shorter events, 100.6 us)
Async XLA Ops:
  7.2 144.1 %all-gather.3.cloned.1.call-start = ((), (), s32[]{:S(2)}) async-start(), calls=%async_computation.2 | async-start | bytes 6684672 | tf_op jit(solution)/shard_map/all_gather | solution.py:1130
  12.6 18.8 %copy-start.51 = (bf16[1,256,1024]{2,1,0:T(8,128)(2,1)S(1)}, bf16[1,256,1024]{2,1,0:T(8,128)(2,1)}, u32[]{:S(2)}) copy-start(bf16[1,256,1024]{2,1,0:T(8,128)(2,1)} %param.21) | copy-start | bytes 1572868
  12.6 20.8 %copy-start.31 = (s32[1,1024]{1,0:T(1,128)S(1)}, s32[1,1024]{1,0:T(1,128)}, u32[]{:S(2)}) copy-start(s32[1,1024]{1,0:T(1,128)} %seg_r.7) | copy-start | bytes 12292
  13.4 326.5 %reduce-scatter.2.cloned.1.call-start = ((), (), s32[]{:S(2)}) async-start(), calls=%async_computation.1 | async-start | bytes 7077888 | tf_op jit(solution)/shard_map/reduce_scatter | solution.py:1289
  15.7 40.8 %copy-start.92 = (f32[24]{0:T(128)S(1)}, f32[24]{0:T(128)}, u32[]{:S(2)}) copy-start(f32[24]{0:T(128)} %param.30) | copy-start | bytes 292
  15.9 41.7 %copy-start.93 = (f32[24]{0:T(128)S(1)}, f32[24]{0:T(128)}, u32[]{:S(2)}) copy-start(f32[24]{0:T(128)} %param.31) | copy-start | bytes 292
  15.9 41.8 %copy-start.87 = (f32[24]{0:T(128)S(1)}, f32[24]{0:T(128)}, u32[]{:S(2)}) copy-start(f32[24]{0:T(128)} %param.29) | copy-start | bytes 292
  15.9 41.9 %copy-start.20 = (bf16[192,1024]{1,0:T(8,128)(2,1)S(1)}, bf16[192,1024]{1,0:T(8,128)(2,1)}, u32[]{:S(2)}) copy-start(bf16[192,1024]{1,0:T(8,128)(2,1)} %w_out.1) | copy-start | bytes 1179652
  16.0 41.9 %copy-start.83 = (bf16[64,1024]{1,0:T(8,128)(2,1)S(1)}, bf16[64,1024]{1,0:T(8,128)(2,1)}, u32[]{:S(2)}) copy-start(bf16[64,1024]{1,0:T(8,128)(2,1)} %param.35) | copy-start | bytes 393220
  16.1 15.2 %collective-permute-start = (bf16[128,1408]{1,0:T(8,128)(2,1)S(1)}, bf16[128,1408]{1,0:T(8,128)(2,1)S(1)}, u32[]{:S(2)}, u32[]{:S(2)}) collective-permute-start(bf16[128,1408]{1,0:T(8,128)(2,1)S(1)} %concatenate.111), channel_id=1, source_target_pairs={{0,2},{1,3},{2,4},{3,5},{4,6},{5,7},{6,0},{7,1},{8,10},{9,11},{10,... | collective-permute-start | bytes 1081352 | tf_op jit(solution)/shard_map/ppermute | solution.py:838
  19.2 34.2 %collective-permute-start.3 = (bf16[128,1408]{1,0:T(8,128)(2,1)S(1)}, bf16[128,1408]{1,0:T(8,128)(2,1)}, u32[]{:S(2)}, u32[]{:S(2)}) collective-permute-start(bf16[128,1408]{1,0:T(8,128)(2,1)S(1)} %concatenate.111), channel_id=1, source_target_pairs={{0,4},{1,5},{2,6},{3,7},{4,0},{5,1},{6,2},{7,3},{8,12},{9,13},{10,... | collective-permute-start | bytes 1081352 | tf_op jit(solution)/shard_map/ppermute | solution.py:838
  21.8 33.1 %collective-permute-start.4 = (bf16[128,1408]{1,0:T(8,128)(2,1)S(1)}, bf16[128,1408]{1,0:T(8,128)(2,1)}, u32[]{:S(2)}, u32[]{:S(2)}) collective-permute-start(bf16[128,1408]{1,0:T(8,128)(2,1)S(1)} %concatenate.111), channel_id=1, source_target_pairs={{0,6},{1,7},{2,0},{3,1},{4,2},{5,3},{6,4},{7,5},{8,14},{9,15},{10,... | collective-permute-start | bytes 1081352 | tf_op jit(solution)/shard_map/ppermute | solution.py:838
  23.1 43.4 %collective-permute-start.5 = (bf16[128,1408]{1,0:T(8,128)(2,1)S(1)}, bf16[128,1408]{1,0:T(8,128)(2,1)}, u32[]{:S(2)}, u32[]{:S(2)}) collective-permute-start(bf16[128,1408]{1,0:T(8,128)(2,1)S(1)} %concatenate.111), channel_id=1, source_target_pairs={{0,1},{1,0},{2,3},{3,2},{4,5},{5,4},{6,7},{7,6},{8,9},{9,8},{10,11... | collective-permute-start | bytes 1081352 | tf_op jit(solution)/shard_map/ppermute | solution.py:835
  31.3 27.4 %copy-start.34 = (bf16[128,1408]{1,0:T(8,128)(2,1)}, bf16[128,1408]{1,0:T(8,128)(2,1)S(1)}, u32[]{:S(2)}) copy-start(bf16[128,1408]{1,0:T(8,128)(2,1)S(1)} %collective-permute-done) | copy-start | bytes 1081348
  31.3 11.5 %collective-permute-start.1 = (bf16[256,1024]{1,0:T(8,128)(2,1)S(1)}, bf16[256,1024]{1,0:T(8,128)(2,1)S(1)}, u32[]{:S(2)}, u32[]{:S(2)}) collective-permute-start(bf16[256,1024]{1,0:T(8,128)(2,1)S(1)} %bitcast.280), channel_id=1, source_target_pairs={{0,16},{8,24},{16,0},{24,8},{1,17},{9,25},{17,1},{25,9},{2,18},{10... | collective-permute-start | bytes 1572872 | tf_op jit(solution)/shard_map/ppermute | solution.py:835
  42.9 15.8 %collective-permute-start.2 = (bf16[2,256,1024]{2,1,0:T(8,128)(2,1)S(1)}, bf16[2,256,1024]{2,1,0:T(8,128)(2,1)S(1)}, u32[]{:S(2)}, u32[]{:S(2)}) collective-permute-start(bf16[2,256,1024]{2,1,0:T(8,128)(2,1)S(1)} %pad_maximum_fusion.2.refs_0_), channel_id=1, source_target_pairs={{0,8},{8,0},{16,24},{24,16},{1,9},{9,1},{17,25},{25,17},{2,10},{10... | collective-permute-start | bytes 3145736 | tf_op jit(solution)/shard_map/ppermute | solution.py:835
  43.4 53.3 %copy-start.42 = (s32[9]{0:T(128)}, s32[9]{0:T(128)S(1)}, u32[]{:S(2)}) copy-start(s32[9]{0:T(128)S(1)} %pad_add_fusion.1.ends) | copy-start | bytes 112
  43.5 23.1 %collective-permute-start.6 = (bf16[128,1408]{1,0:T(8,128)(2,1)S(1)}, bf16[128,1408]{1,0:T(8,128)(2,1)}, u32[]{:S(2)}, u32[]{:S(2)}) collective-permute-start(bf16[128,1408]{1,0:T(8,128)(2,1)S(1)} %collective-permute-done), channel_id=1, source_target_pairs={{0,1},{1,0},{2,3},{3,2},{4,5},{5,4},{6,7},{7,6},{8,9},{9,8},{10,11... | collective-permute-start | bytes 1081352 | tf_op jit(solution)/shard_map/ppermute | solution.py:835
  53.4 13.2 %collective-permute-start.7 = (bf16[128,1408]{1,0:T(8,128)(2,1)}, bf16[128,1408]{1,0:T(8,128)(2,1)}, u32[]{:S(2)}, u32[]{:S(2)}) collective-permute-start(bf16[128,1408]{1,0:T(8,128)(2,1)} %collective-permute-done.3), channel_id=1, source_target_pairs={{0,1},{1,0},{2,3},{3,2},{4,5},{5,4},{6,7},{7,6},{8,9},{9,8},{10,11... | collective-permute-start | bytes 1081352 | tf_op jit(solution)/shard_map/ppermute | solution.py:835
  54.9 22.2 %collective-permute-start.8 = (bf16[128,1408]{1,0:T(8,128)(2,1)}, bf16[128,1408]{1,0:T(8,128)(2,1)}, u32[]{:S(2)}, u32[]{:S(2)}) collective-permute-start(bf16[128,1408]{1,0:T(8,128)(2,1)} %collective-permute-done.4), channel_id=1, source_target_pairs={{0,1},{1,0},{2,3},{3,2},{4,5},{5,4},{6,7},{7,6},{8,9},{9,8},{10,11... | collective-permute-start | bytes 1081352 | tf_op jit(solution)/shard_map/ppermute | solution.py:835
  57.7 39.0 %copy-start.43 = (f32[6]{0:T(128)}, f32[6]{0:T(128)S(1)}, u32[]{:S(2)}) copy-start(f32[6]{0:T(128)S(1)} %dynamic_slice.150.skip) | copy-start | bytes 76
  57.9 30.9 %copy-start.41 = (f32[8,128]{1,0:T(8,128)}, f32[8,128]{1,0:T(8,128)S(1)}, u32[]{:S(2)}) copy-start(f32[8,128]{1,0:T(8,128)S(1)} %select_maximum_fusion.params) | copy-start | bytes 12292
  58.7 18.4 %copy-start.35 = (bf16[128,1408]{1,0:T(8,128)(2,1)S(1)}, bf16[128,1408]{1,0:T(8,128)(2,1)}, u32[]{:S(2)}) copy-start(bf16[128,1408]{1,0:T(8,128)(2,1)} %copy-done.34) | copy-start | bytes 1081348
  58.7 48.7 %collective-permute-start.11 = (bf16[256,1024]{1,0:T(8,128)(2,1)}, bf16[256,1024]{1,0:T(8,128)(2,1)}, u32[]{:S(2)}, u32[]{:S(2)}) collective-permute-start(bf16[256,1024]{1,0:T(8,128)(2,1)} %pad_maximum_fusion.10), channel_id=1, source_target_pairs={{0,0},{1,1},{2,8},{3,9},{4,16},{5,17},{6,24},{7,25},{8,2},{9,3},{1... | collective-permute-start | bytes 1572872 | tf_op jit(solution)/shard_map/ppermute | solution.py:847
  96.7 20.8 %copy-start.36 = (f32[16,1024]{1,0:T(8,128)}, f32[16,1024]{1,0:T(8,128)S(1)}, u32[]{:S(2)}) copy-start(f32[16,1024]{1,0:T(8,128)S(1)} %get-tuple-element.122.rows) | copy-start | bytes 196612
  107.4 137.9 %copy-start.2 = (f32[1024,384]{1,0:T(8,128)}, f32[1024,384]{1,0:T(8,128)S(1)}, u32[]{:S(2)}) copy-start(f32[1024,384]{1,0:T(8,128)S(1)} %get-tuple-element.123.y_ref) | copy-start | bytes 4718596
  107.4 25.7 %collective-permute-start.12 = (bf16[256,1024]{1,0:T(8,128)(2,1)}, bf16[256,1024]{1,0:T(8,128)(2,1)}, u32[]{:S(2)}, u32[]{:S(2)}) collective-permute-start(bf16[256,1024]{1,0:T(8,128)(2,1)} %collective-permute-done.11), channel_id=1, source_target_pairs={{0,1},{1,0},{2,3},{3,2},{4,5},{5,4},{6,7},{7,6},{8,9},{9,8},{10,11... | collective-permute-start | bytes 1572872 | tf_op jit(solution)/shard_map/ppermute | solution.py:835
  117.5 17.6 %copy-start.4 = (f32[1024,384]{1,0:T(8,128)}, f32[1024,384]{1,0:T(8,128)S(1)}, u32[]{:S(2)}) copy-start(f32[1024,384]{1,0:T(8,128)S(1)} %get-tuple-element.126.z_ref) | copy-start | bytes 4718596
  119.7 1.2 collective-permute-start.9
  120.9 7.4 %collective-permute-start.10 = (f32[16,128]{1,0:T(8,128)S(1)}, f32[16,128]{1,0:T(8,128)S(1)}, u32[]{:S(2)}, u32[]{:S(2)}) collective-permute-start(f32[16,128]{1,0:T(8,128)S(1)} %add.420), channel_id=1, source_target_pairs={{0,16},{8,24},{16,0},{24,8},{1,17},{9,25},{17,1},{25,9},{2,18},{10... | collective-permute-start | bytes 24584 | tf_op jit(solution)/shard_map/ppermute | solution.py:835
  140.4 3.0 collective-permute-start.13
  151.3 13.6 %collective-permute-start.14 = (bf16[256,1024]{1,0:T(8,128)(2,1)}, bf16[256,1024]{1,0:T(8,128)(2,1)}, u32[]{:S(2)}, u32[]{:S(2)}) collective-permute-start(bf16[256,1024]{1,0:T(8,128)(2,1)} %fusion.17), channel_id=1, source_target_pairs={{0,16},{8,24},{16,0},{24,8},{1,17},{9,25},{17,1},{25,9},{2,18},{10... | collective-permute-start | bytes 1572872 | tf_op jit(solution)/shard_map/ppermute | solution.py:835
  167.0 2.0 collective-permute-start.15
  173.0 2.0 collective-permute-start.16
  176.9 2.0 collective-permute-start.17
  197.8 2.3 collective-permute-start.18
  205.4 14.0 %collective-permute-start.19 = (bf16[256,1024]{1,0:T(8,128)(2,1)S(1)}, bf16[256,1024]{1,0:T(8,128)(2,1)S(1)}, u32[]{:S(2)}, u32[]{:S(2)}) collective-permute-start(bf16[256,1024]{1,0:T(8,128)(2,1)S(1)} %get-tuple-element.224), channel_id=1, source_target_pairs={{0,16},{8,24},{16,0},{24,8},{1,17},{9,25},{17,1},{25,9},{2,18},{10... | collective-permute-start | bytes 1572872 | tf_op jit(solution)/shard_map/ppermute | solution.py:835
  220.5 3.0 collective-permute-start.20
  229.1 3.3 collective-permute-start.21
  232.5 12.9 %collective-permute-start.22 = (f32[8,128]{1,0:T(8,128)S(1)}, f32[8,128]{1,0:T(8,128)S(1)}, u32[]{:S(2)}, u32[]{:S(2)}) collective-permute-start(f32[8,128]{1,0:T(8,128)S(1)} %bitcast_add_fusion), channel_id=1, source_target_pairs={{0,16},{8,24},{16,0},{24,8},{1,17},{9,25},{17,1},{25,9},{2,18},{10... | collective-permute-start | bytes 12296 | tf_op jit(solution)/shard_map/ppermute | solution.py:835
  234.9 16.4 %collective-permute-start.23 = (bf16[256,1024]{1,0:T(8,128)(2,1)}, bf16[256,1024]{1,0:T(8,128)(2,1)}, u32[]{:S(2)}, u32[]{:S(2)}) collective-permute-start(bf16[256,1024]{1,0:T(8,128)(2,1)} %dynamic-slice_bitcast_fusion.2), channel_id=1, source_target_pairs={{0,1},{1,0},{2,3},{3,2},{4,5},{5,4},{6,7},{7,6},{8,9},{9,8},{10,11... | collective-permute-start | bytes 1572872 | tf_op jit(solution)/shard_map/ppermute | solution.py:835
  252.6 31.5 %collective-permute-start.24 = (bf16[4,128,640]{2,1,0:T(8,128)(2,1)}, bf16[4,128,640]{2,1,0:T(8,128)(2,1)S(1)}, u32[]{:S(2)}, u32[]{:S(2)}) collective-permute-start(bf16[4,128,640]{2,1,0:T(8,128)(2,1)} %dynamic-slice_bitcast_fusion.1), channel_id=1, source_target_pairs={{0,1},{1,0},{2,3},{3,2},{4,5},{5,4},{6,7},{7,6},{8,9},{9,8},{10,11... | collective-permute-start | bytes 1966088 | tf_op jit(solution)/shard_map/ppermute | solution.py:835
  256.0 28.0 %collective-permute-start.25 = (bf16[64,1024]{1,0:T(8,128)(2,1)S(1)}, bf16[64,1024]{1,0:T(8,128)(2,1)S(1)}, u32[]{:S(2)}, u32[]{:S(2)}) collective-permute-start(bf16[64,1024]{1,0:T(8,128)(2,1)S(1)} %get-tuple-element.247), channel_id=1, source_target_pairs={{0,2},{1,3},{2,4},{3,5},{4,6},{5,7},{6,0},{7,1},{8,10},{9,11},{10,... | collective-permute-start | bytes 393224 | tf_op jit(solution)/shard_map/ppermute | solution.py:838
  259.3 24.7 %collective-permute-start.26 = (bf16[64,1024]{1,0:T(8,128)(2,1)S(1)}, bf16[64,1024]{1,0:T(8,128)(2,1)S(1)}, u32[]{:S(2)}, u32[]{:S(2)}) collective-permute-start(bf16[64,1024]{1,0:T(8,128)(2,1)S(1)} %get-tuple-element.246), channel_id=1, source_target_pairs={{0,4},{1,5},{2,6},{3,7},{4,0},{5,1},{6,2},{7,3},{8,12},{9,13},{10,... | collective-permute-start | bytes 393224 | tf_op jit(solution)/shard_map/ppermute | solution.py:838
  260.6 23.4 %collective-permute-start.27 = (bf16[64,1024]{1,0:T(8,128)(2,1)S(1)}, bf16[64,1024]{1,0:T(8,128)(2,1)S(1)}, u32[]{:S(2)}, u32[]{:S(2)}) collective-permute-start(bf16[64,1024]{1,0:T(8,128)(2,1)S(1)} %get-tuple-element.245), channel_id=1, source_target_pairs={{0,6},{1,7},{2,0},{3,1},{4,2},{5,3},{6,4},{7,5},{8,14},{9,15},{10,... | collective-permute-start | bytes 393224 | tf_op jit(solution)/shard_map/ppermute | solution.py:838
  264.6 20.4 %copy-start.13 = (bf16[1024,1024]{1,0:T(8,128)(2,1)S(1)}, bf16[1024,1024]{1,0:T(8,128)(2,1)}, u32[]{:S(2)}) copy-start(bf16[1024,1024]{1,0:T(8,128)(2,1)} %copy-done.10) | copy-start | bytes 6291460
  299.4 2.7 collective-permute-start.28
  302.3 14.0 %collective-permute-start.29 = (bf16[256,1024]{1,0:T(8,128)(2,1)S(1)}, bf16[256,1024]{1,0:T(8,128)(2,1)S(1)}, u32[]{:S(2)}, u32[]{:S(2)}) collective-permute-start(bf16[256,1024]{1,0:T(8,128)(2,1)S(1)} %fusion.14), channel_id=1, source_target_pairs={{0,16},{8,24},{16,0},{24,8},{1,17},{9,25},{17,1},{25,9},{2,18},{10... | collective-permute-start | bytes 1572872 | tf_op jit(solution)/shard_map/ppermute | solution.py:835
  303.6 24.4 %collective-permute-start.30 = (bf16[4,128,768]{1,2,0:T(8,128)(2,1)S(1)}, bf16[4,128,768]{1,2,0:T(8,128)(2,1)S(1)}, u32[]{:S(2)}, u32[]{:S(2)}) collective-permute-start(bf16[4,128,768]{1,2,0:T(8,128)(2,1)S(1)} %dynamic-slice_bitcast_fusion), channel_id=1, source_target_pairs={{0,1},{1,0},{2,3},{3,2},{4,5},{5,4},{6,7},{7,6},{8,9},{9,8},{10,11... | collective-permute-start | bytes 2359304 | tf_op jit(solution)/shard_map/ppermute | solution.py:835
  304.8 12.5 %collective-permute-start.31 = (bf16[128,640]{1,0:T(8,128)(2,1)S(1)}, bf16[128,640]{1,0:T(8,128)(2,1)S(1)}, u32[]{:S(2)}, u32[]{:S(2)}) collective-permute-start(bf16[128,640]{1,0:T(8,128)(2,1)S(1)} %get-tuple-element.243), channel_id=1, source_target_pairs={{0,2},{1,3},{2,4},{3,5},{4,6},{5,7},{6,0},{7,1},{8,10},{9,11},{10,... | collective-permute-start | bytes 491528 | tf_op jit(solution)/shard_map/ppermute | solution.py:838
  304.8 23.2 %collective-permute-start.32 = (bf16[128,640]{1,0:T(8,128)(2,1)S(1)}, bf16[128,640]{1,0:T(8,128)(2,1)S(1)}, u32[]{:S(2)}, u32[]{:S(2)}) collective-permute-start(bf16[128,640]{1,0:T(8,128)(2,1)S(1)} %get-tuple-element.242), channel_id=1, source_target_pairs={{0,4},{1,5},{2,6},{3,7},{4,0},{5,1},{6,2},{7,3},{8,12},{9,13},{10,... | collective-permute-start | bytes 491528 | tf_op jit(solution)/shard_map/ppermute | solution.py:838
  305.5 22.6 %collective-permute-start.33 = (bf16[128,640]{1,0:T(8,128)(2,1)S(1)}, bf16[128,640]{1,0:T(8,128)(2,1)S(1)}, u32[]{:S(2)}, u32[]{:S(2)}) collective-permute-start(bf16[128,640]{1,0:T(8,128)(2,1)S(1)} %get-tuple-element.241), channel_id=1, source_target_pairs={{0,6},{1,7},{2,0},{3,1},{4,2},{5,3},{6,4},{7,5},{8,14},{9,15},{10,... | collective-permute-start | bytes 491528 | tf_op jit(solution)/shard_map/ppermute | solution.py:838
  328.3 21.6 %copy-start.53 = (bf16[1,256,1024]{2,1,0:T(8,128)(2,1)S(1)}, bf16[1,256,1024]{2,1,0:T(8,128)(2,1)}, u32[]{:S(2)}) copy-start(bf16[1,256,1024]{2,1,0:T(8,128)(2,1)} %param.21) | copy-start | bytes 1572868
  329.6 20.6 %copy-start.56 = (f32[256,1024]{1,0:T(8,128)S(1)}, f32[256,1024]{1,0:T(8,128)}, u32[]{:S(2)}) copy-start(f32[256,1024]{1,0:T(8,128)} %get-tuple-element.225) | copy-start | bytes 3145732
  339.9 21.1 %collective-permute-start.38 = (bf16[384,1024]{1,0:T(8,128)(2,1)}, bf16[384,1024]{1,0:T(8,128)(2,1)S(1)}, u32[]{:S(2)}, u32[]{:S(2)}) collective-permute-start(bf16[384,1024]{1,0:T(8,128)(2,1)} %bitcast.303), channel_id=1, source_target_pairs={{0,16},{8,24},{16,0},{24,8},{1,17},{9,25},{17,1},{25,9},{2,18},{10... | collective-permute-start | bytes 2359304 | tf_op jit(solution)/shard_map/ppermute | solution.py:835
  342.5 10.0 %collective-permute-start.34 = (bf16[128,768]{1,0:T(8,128)(2,1)}, bf16[128,768]{1,0:T(8,128)(2,1)S(1)}, u32[]{:S(2)}, u32[]{:S(2)}) collective-permute-start(bf16[128,768]{1,0:T(8,128)(2,1)} %bitcast.108), channel_id=1, source_target_pairs={{0,2},{1,3},{2,4},{3,5},{4,6},{5,7},{6,0},{7,1},{8,10},{9,11},{10,... | collective-permute-start | bytes 589832 | tf_op jit(solution)/shard_map/ppermute | solution.py:838
  346.5 14.5 %collective-permute-start.35 = (bf16[128,768]{1,0:T(8,128)(2,1)}, bf16[128,768]{1,0:T(8,128)(2,1)S(1)}, u32[]{:S(2)}, u32[]{:S(2)}) collective-permute-start(bf16[128,768]{1,0:T(8,128)(2,1)} %bitcast.109), channel_id=1, source_target_pairs={{0,4},{1,5},{2,6},{3,7},{4,0},{5,1},{6,2},{7,3},{8,12},{9,13},{10,... | collective-permute-start | bytes 589832 | tf_op jit(solution)/shard_map/ppermute | solution.py:838
  346.7 14.3 %collective-permute-start.36 = (bf16[128,768]{1,0:T(8,128)(2,1)}, bf16[128,768]{1,0:T(8,128)(2,1)S(1)}, u32[]{:S(2)}, u32[]{:S(2)}) collective-permute-start(bf16[128,768]{1,0:T(8,128)(2,1)} %bitcast.110), channel_id=1, source_target_pairs={{0,6},{1,7},{2,0},{3,1},{4,2},{5,3},{6,4},{7,5},{8,14},{9,15},{10,... | collective-permute-start | bytes 589832 | tf_op jit(solution)/shard_map/ppermute | solution.py:838
  348.9 2.5 collective-permute-start.37
  351.4 22.1 %copy-start.14 = (bf16[128,2048]{1,0:T(8,128)(2,1)S(1)}, bf16[128,2048]{1,0:T(8,128)(2,1)}, u32[]{:S(2)}) copy-start(bf16[128,2048]{1,0:T(8,128)(2,1)} %w_up.1) | copy-start | bytes 1572868
  351.4 22.1 %copy-start.16 = (bf16[128,2048]{1,0:T(8,128)(2,1)S(1)}, bf16[128,2048]{1,0:T(8,128)(2,1)}, u32[]{:S(2)}) copy-start(bf16[128,2048]{1,0:T(8,128)(2,1)} %w_gate.1) | copy-start | bytes 1572868
  361.3 2.4 collective-permute-start.39
  363.6 21.4 %collective-permute-start.40 = (bf16[128,1920]{1,0:T(8,128)(2,1)S(1)}, bf16[128,1920]{1,0:T(8,128)(2,1)S(1)}, u32[]{:S(2)}, u32[]{:S(2)}) collective-permute-start(bf16[128,1920]{1,0:T(8,128)(2,1)S(1)} %get-tuple-element.202), channel_id=1, source_target_pairs={{0,16},{8,24},{16,0},{24,8},{1,17},{9,25},{17,1},{25,9},{2,18},{10... | collective-permute-start | bytes 1474568 | tf_op jit(solution)/shard_map/ppermute | solution.py:835
  385.2 2.8 collective-permute-start.41
  (77 other events, 372.0 us)
Sparse Core Ops, SparseCore 0:
  13.5 137.7 all-gather.2
  198.0 141.7 reduce-scatter.1

commit v6 on v5

--- a/solution.py
+++ b/solution.py
@@ -1241,7 +1241,8 @@
 
     if net.direct:
         own, away = net.ctx_halves(outs.reshape(n, rows, dim))
-        (w_g, w_u, w_d), (across,) = stage(ff_weights, (w_ff,), [(net.flip_x, away)])
+        laid_out = ff_weights(w_ff)
+        _, (across,), (w_g, w_u, w_d) = stage(tuple, (), [(net.flip_x, away)], laid_out)
         mixed = tokens[0].astype(F32) + own + across.astype(F32)
     else:
         w_g, w_u, w_d = ff_weights(w_ff)

time: 411 us -> 412 us (level)
    unnamed x200 -> x198, local copies, waits for them, and re-layouts: 25.5 us -> 25.5 us
where the time goes in v6:
time: 412 us; the launch traced here: 406 us
  waiting for transfers between devices  128 us (31%)
  Pallas kernels  70.2 us (17%)
  local copies, waits for them, and re-layouts  65 us (16%)
  starting transfers between devices  63.6 us (15%)
  other arithmetic  30.8 us (7%)
  matrix products  28.7 us (7%)
  between operations  18.9 us (5%)
    ppermute x24, waiting for transfers between devices, flip(): return lax.ppermute(value, axis, [(i, i ^ bit) for i in range(size)])  74.1 us
    ppermute x12, waiting for transfers between devices, shift_z(): lax.ppermute(value, 'fsdp', [(i, (i + 2 * by) % self.m) for i in range(se...  37.2 us
    ppermute x24, starting transfers between devices, flip(): return lax.ppermute(value, axis, [(i, i ^ bit) for i in range(size)])  31.6 us
    unnamed x198, local copies, waits for them, and re-layouts  25.5 us
    ppermute x12, starting transfers between devices, shift_z(): lax.ppermute(value, 'fsdp', [(i, (i + 2 * by) % self.m) for i in range(se...  24.6 us
    pallas_call x1, Pallas kernels, ssm_backward(): pl.pallas_call(functools.partial(ssm_bwd_kernel, heads), grid=(steps,), i...  19.4 us
    dot_general x7, matrix products, nt(): lax.dot_general(left, right, (((1,), (1,)), ((), ())), preferred_element_...  15.9 us
    pallas_call x1, Pallas kernels, attn_backward(): pl.pallas_call(functools.partial(attn_bwd_kernel, heads, blocks), grid=(b...  9.87 us
  transfers between devices with their start and end apart: 44, of which 26 were waited for; matrix products, arithmetic and copies ran while one was open for 18% of the time, Pallas kernels for 15%

profile of v6, /device:TPU:0, one launch (start us, length us, event | category | flops | bytes accessed | tf_op | source)
XLA Modules:
  0.0 405.5 jit_solution(13815345832553149893)
XLA Ops:
  10.2 3.1 dynamic-slice_reduce_fusion
  17.1 3.1 collective-permute-start
  20.2 2.6 collective-permute-start.3
  25.6 6.7 %collective-permute-done = bf16[128,1408]{1,0:T(8,128)(2,1)S(1)} collective-permute-done((bf16[128,1408]{1,0:T(8,128)(2,1)S(1)}, bf16[128,1408]{1,0:T(8,128)(2,1)S(1)}, u32[]{:S(2)}, u32[]{:S(2)}) %collective-permute-start) | collective-permute-done | bytes 360480 | tf_op jit(solution)/shard_map/ppermute | solution.py:838
  32.3 2.0 collective-permute-start.1
  34.6 9.3 %collective-permute-done.1 = bf16[256,1024]{1,0:T(8,128)(2,1)S(1)} collective-permute-done((bf16[256,1024]{1,0:T(8,128)(2,1)S(1)}, bf16[256,1024]{1,0:T(8,128)(2,1)S(1)}, u32[]{:S(2)}, u32[]{:S(2)}) %collective-permute-start.1) | collective-permute-done | bytes 524320 | tf_op jit(solution)/shard_map/ppermute | solution.py:835
  45.8 8.6 %collective-permute-done.3 = bf16[128,1408]{1,0:T(8,128)(2,1)} collective-permute-done((bf16[128,1408]{1,0:T(8,128)(2,1)S(1)}, bf16[128,1408]{1,0:T(8,128)(2,1)}, u32[]{:S(2)}, u32[]{:S(2)}) %collective-permute-start.3) | collective-permute-done | bytes 360480 | tf_op jit(solution)/shard_map/ppermute | solution.py:838
  59.7 5.7 %collective-permute-start.11 = (bf16[256,1024]{1,0:T(8,128)(2,1)}, bf16[256,1024]{1,0:T(8,128)(2,1)}, u32[]{:S(2)}, u32[]{:S(2)}) collective-permute-start(bf16[256,1024]{1,0:T(8,128)(2,1)} %pad_maximum_fusion.10), channel_id=1, source_target_pairs={{0,0},{1,1},{2,8},{3,9},{4,16},{5,17},{6,24},{7,25},{8,2},{9,3},{1... | collective-permute-start | bytes 1572872 | tf_op jit(solution)/shard_map/ppermute | solution.py:847
  67.6 10.5 %collective-permute-done.8 = bf16[128,1408]{1,0:T(8,128)(2,1)} collective-permute-done((bf16[128,1408]{1,0:T(8,128)(2,1)}, bf16[128,1408]{1,0:T(8,128)(2,1)}, u32[]{:S(2)}, u32[]{:S(2)}) %collective-permute-start.8) | collective-permute-done | bytes 360480 | tf_op jit(solution)/shard_map/ppermute | solution.py:835
  78.1 2.8 put.4
  85.1 2.0 fusion.40
  91.4 5.2 %project_conv.1 = (bf16[1024,1024]{1,0:T(8,128)(2,1)S(1)}, bf16[1024,640]{1,0:T(8,128)(2,1)S(1)}, bf16[1024,640]{1,0:T(8,128)(2,1)S(1)}, bf16[1024,640]{1,0:T(8,...) custom-call(bf16[1024,1024]{1,0:T(8,128)(2,1)S(1)} %bitcast.261, f32[1,1024]{1,0:T(1,128)S(1)} %bitcast.270, ...), custom_call_target="tpu_custom_call" | custom-call | flops 1610612736 | bytes 10000000 | tf_op jit(solution)/shard_map/project_conv/pallas_call | solution.py:100
  97.7 7.5 %ssm_forward.1 = (f32[1024,384]{1,0:T(8,128)S(1)}, f32[8,384,128]{2,1,0:T(8,128)S(1)}) custom-call(s32[9]{0:T(128)S(1)} %pad_add_fusion.1.ends, f32[6]{0:T(128)S(1)} %dynamic_slice.150.skip, bf16[1024,640]{1,0:T(8,128)(2,1)S(1)} %get-tuple-element.118.act, f32[1024,256]{1,0:T(8,128)S(1)} %get-tuple-element.119.steps, ...), custom_call_target="tpu_custom_call" | custom-call | flops 1000000000 | bytes 40000000 | tf_op jit(solution)/shard_map/ssm_forward/pallas_call | solution.py:429
  114.5 4.0 project_gate.1
  123.4 5.9 %attn_forward.1 = (bf16[1024,128]{1,0:T(8,128)(2,1)S(1)}, f32[1024,2]{1,0:T(8,128)S(1)}) custom-call(bf16[1024,256]{1,0:T(8,128)(2,1)S(1)} %get-tuple-element.144.qkv_ref, s32[1024,1]{1,0:T(8,128)S(1)} %copy-done.7, s32[1,1024]{1,0:T(1,128)S(1)} %copy-done.30), custom_call_target="tpu_custom_call" | custom-call | flops 1000000000 | bytes 20000000 | tf_op jit(solution)/shard_map/attn_forward/pallas_call | solution.py:584
  129.3 4.8 %collective-permute-done.12 = bf16[256,1024]{1,0:T(8,128)(2,1)} collective-permute-done((bf16[256,1024]{1,0:T(8,128)(2,1)}, bf16[256,1024]{1,0:T(8,128)(2,1)}, u32[]{:S(2)}, u32[]{:S(2)}) %collective-permute-start.12) | collective-permute-done | bytes 524320 | tf_op jit(solution)/shard_map/ppermute | solution.py:835
  134.1 1.8 maximum_select_fusion
  138.2 1.9 copy-done.46
  141.3 3.0 collective-permute-done.13
  144.3 2.3 fusion.17
  148.3 4.0 all-gather.3.cloned.1.call-done
  152.3 4.1 %slice_bitcast_fusion = (bf16[8,2,64,1024]{3,2,0,1:T(8,128)(2,1)S(1)}, bf16[8,2,64,1024]{3,2,0,1:T(8,128)(2,1)S(1)}, bf16[8,2,64,1024]{3,2,0,1:T(8,128)(2,1)S(1)}) fusion(bf16[2,8,192,1024]{3,2,1,0:T(8,128)(2,1)} %bitcast.281), kind=kLoop, calls=%fused_computation.1 | loop fusion | bytes 12582912 | tf_op jit(solution)/shard_map/transpose | solution.py:1234
  157.1 3.8 collective-permute-done.14
  160.9 1.9 multiply_reduce_fusion.2
  163.1 1.9 collective-permute-done.15
  174.8 1.8 multiply_convert_fusion.1
  176.7 2.7 fusion.46
  179.4 5.7 %ff_gradients.1 = bf16[8,384,1024]{2,1,0:T(8,128)(2,1)S(1)} custom-call(bf16[512,1024]{1,0:T(8,128)(2,1)S(1)} %pad_maximum_fusion.3.both, bf16[512,1024]{1,0:T(8,128)(2,1)S(1)} %get-tuple-element.276.product, bf16[512,1024]{1,0:T(8,128)(2,1)S(1)} %get-tuple-element.139.g_gate, bf16[512,1024]{1,0:T(8,128)(2,1)S(1)} %get-tuple-element.230.g_up, ...), custom_call_target="tpu_custom_call" | custom-call | flops 3221225472 | bytes 10000000 | tf_op jit(solution)/shard_map/ff_gradients/pallas_call | solution.py:640
  185.1 2.6 copy-done.3
  187.7 3.8 convolution_add_fusion.2
  194.0 2.0 collective-permute-done.18
  196.0 2.0 multiply_reduce_fusion.1
  198.0 3.4 fusion.36
  203.2 12.3 %collective-permute-done.19 = bf16[256,1024]{1,0:T(8,128)(2,1)S(1)} collective-permute-done((bf16[256,1024]{1,0:T(8,128)(2,1)S(1)}, bf16[256,1024]{1,0:T(8,128)(2,1)S(1)}, u32[]{:S(2)}, u32[]{:S(2)}) %collective-permute-start.19) | collective-permute-done | bytes 524320 | tf_op jit(solution)/shard_map/ppermute | solution.py:835
  216.5 3.0 collective-permute-done.20.refs_1_
  219.5 3.1 put.5
  222.7 2.5 multiply_reduce_fusion
  232.7 9.9 %attn_backward.1 = bf16[1024,256]{1,0:T(8,128)(2,1)} custom-call(bf16[1024,256]{1,0:T(8,128)(2,1)} %copy-done.27, s32[1024,1]{1,0:T(8,128)} %copy.187.seg_c, s32[1,1024]{1,0:T(1,128)} %seg_r.7, f32[1024,2]{1,0:T(8,128)} %copy-done.28, bf16[1024,128]{1,0:T(8,128)(2,1)} %convolution_convert_fusion.4.go_ref, f32[1024,256]{1,0:T(8,128)} %constant.374.clone.cosine, ...), custom_call_target="tpu_custom_call" | custom-call | flops 10000000 | bytes 1000000 | tf_op jit(solution)/shard_map/attn_backward/pallas_call | solution.py:608
  242.6 2.4 multiply_convert_fusion.3
  245.0 1.9 convolution_convert_fusion.1
  247.9 4.1 %collective-permute-done.23 = bf16[256,1024]{1,0:T(8,128)(2,1)} collective-permute-done((bf16[256,1024]{1,0:T(8,128)(2,1)}, bf16[256,1024]{1,0:T(8,128)(2,1)}, u32[]{:S(2)}, u32[]{:S(2)}) %collective-permute-start.23) | collective-permute-done | bytes 524320 | tf_op jit(solution)/shard_map/ppermute | solution.py:835
  256.3 3.3 collective-permute-start.25
  261.1 2.9 collective-permute-start.27
  265.1 19.4 %ssm_backward.1 = (bf16[1024,768]{1,0:T(8,128)(2,1)}, f32[8,640]{1,0:T(8,128)}, f32[8,384]{1,0:T(8,128)}, f32[8,128]{1,0:T(8,128)}) custom-call(s32[9]{0:T(128)} %copy-done.41, f32[6]{0:T(128)} %copy-done.42, bf16[1024,640]{1,0:T(8,128)(2,1)} %copy-done.25, f32[1024,256]{1,0:T(8,128)} %copy-done.26, f32[16,1024]{1,0:T(8,128)} %copy-done.35, ...), custom_call_target="tpu_custom_call" | custom-call | flops 10000000 | bytes 1000000 | tf_op jit(solution)/shard_map/ssm_backward/pallas_call | solution.py:466
  285.4 3.3 convolution_convert_fusion
  291.5 1.9 copy.220
  296.0 1.8 fusion.47
  297.8 1.9 convolution_add_fusion.1
  299.9 2.6 collective-permute-done.28
  302.7 2.0 collective-permute-start.29
  306.5 3.2 collective-permute-start.33
  309.7 7.3 %collective-permute-done.29 = bf16[256,1024]{1,0:T(8,128)(2,1)S(1)} collective-permute-done((bf16[256,1024]{1,0:T(8,128)(2,1)S(1)}, bf16[256,1024]{1,0:T(8,128)(2,1)S(1)}, u32[]{:S(2)}, u32[]{:S(2)}) %collective-permute-start.29) | collective-permute-done | bytes 524320 | tf_op jit(solution)/shard_map/ppermute | solution.py:835
  318.4 10.9 %collective-permute-done.32 = bf16[128,640]{1,0:T(8,128)(2,1)S(1)} collective-permute-done((bf16[128,640]{1,0:T(8,128)(2,1)S(1)}, bf16[128,640]{1,0:T(8,128)(2,1)S(1)}, u32[]{:S(2)}, u32[]{:S(2)}) %collective-permute-start.32) | collective-permute-done | bytes 163872 | tf_op jit(solution)/shard_map/ppermute | solution.py:838
  333.3 1.8 add_convert_fusion.2
  335.1 6.1 %reduce-scatter.2.cloned.1.call-done = bf16[1,384,1024]{2,1,0:T(8,128)(2,1)} async-done(((bf16[8,384,1024]{2,1,0:T(8,128)(2,1)}), bf16[1,384,1024]{2,1,0:T(8,128)(2,1)}) %reduce-scatter.2.cloned.1.call-update) | async-done | bytes 786448 | tf_op jit(solution)/shard_map/reduce_scatter | solution.py:1290
  343.9 3.7 collective-permute-start.34
  347.9 2.1 collective-permute-start.36
  353.9 8.5 %collective-permute-done.35 = bf16[128,768]{1,0:T(8,128)(2,1)S(1)} collective-permute-done((bf16[128,768]{1,0:T(8,128)(2,1)}, bf16[128,768]{1,0:T(8,128)(2,1)S(1)}, u32[]{:S(2)}, u32[]{:S(2)}) %collective-permute-start.35) | collective-permute-done | bytes 196640 | tf_op jit(solution)/shard_map/ppermute | solution.py:838
  363.0 2.0 collective-permute-done.39.mate
  365.0 9.8 %collective-permute-start.40 = (bf16[128,1920]{1,0:T(8,128)(2,1)S(1)}, bf16[128,1920]{1,0:T(8,128)(2,1)S(1)}, u32[]{:S(2)}, u32[]{:S(2)}) collective-permute-start(bf16[128,1920]{1,0:T(8,128)(2,1)S(1)} %get-tuple-element.198), channel_id=1, source_target_pairs={{0,16},{8,24},{16,0},{24,8},{1,17},{9,25},{17,1},{25,9},{2,18},{10... | collective-permute-start | bytes 1474568 | tf_op jit(solution)/shard_map/ppermute | solution.py:835
  374.9 2.1 finish_ff.1
  377.5 8.9 %collective-permute-done.40 = bf16[128,1920]{1,0:T(8,128)(2,1)S(1)} collective-permute-done((bf16[128,1920]{1,0:T(8,128)(2,1)S(1)}, bf16[128,1920]{1,0:T(8,128)(2,1)S(1)}, u32[]{:S(2)}, u32[]{:S(2)}) %collective-permute-start.40) | collective-permute-done | bytes 491552 | tf_op jit(solution)/shard_map/ppermute | solution.py:835
  387.3 1.9 collective-permute-done.41.mates
  389.2 4.0 finish.1
  (425 shorter events, 103.9 us)
Async XLA Ops:
  7.2 145.1 %all-gather.3.cloned.1.call-start = ((), (), s32[]{:S(2)}) async-start(), calls=%async_computation.2 | async-start | bytes 6684672 | tf_op jit(solution)/shard_map/all_gather | solution.py:1130
  13.5 18.8 %copy-start.50 = (bf16[1,256,1024]{2,1,0:T(8,128)(2,1)S(1)}, bf16[1,256,1024]{2,1,0:T(8,128)(2,1)}, u32[]{:S(2)}) copy-start(bf16[1,256,1024]{2,1,0:T(8,128)(2,1)} %param.21) | copy-start | bytes 1572868
  13.5 20.8 %copy-start.30 = (s32[1,1024]{1,0:T(1,128)S(1)}, s32[1,1024]{1,0:T(1,128)}, u32[]{:S(2)}) copy-start(s32[1,1024]{1,0:T(1,128)} %seg_r.7) | copy-start | bytes 12292
  14.4 326.8 %reduce-scatter.2.cloned.1.call-start = ((), (), s32[]{:S(2)}) async-start(), calls=%async_computation.1 | async-start | bytes 7077888 | tf_op jit(solution)/shard_map/reduce_scatter | solution.py:1290
  16.7 40.8 %copy-start.91 = (f32[24]{0:T(128)S(1)}, f32[24]{0:T(128)}, u32[]{:S(2)}) copy-start(f32[24]{0:T(128)} %param.30) | copy-start | bytes 292
  16.9 41.7 %copy-start.92 = (f32[24]{0:T(128)S(1)}, f32[24]{0:T(128)}, u32[]{:S(2)}) copy-start(f32[24]{0:T(128)} %param.31) | copy-start | bytes 292
  16.9 41.8 %copy-start.86 = (f32[24]{0:T(128)S(1)}, f32[24]{0:T(128)}, u32[]{:S(2)}) copy-start(f32[24]{0:T(128)} %param.29) | copy-start | bytes 292
  16.9 41.9 %copy-start.19 = (bf16[192,1024]{1,0:T(8,128)(2,1)S(1)}, bf16[192,1024]{1,0:T(8,128)(2,1)}, u32[]{:S(2)}) copy-start(bf16[192,1024]{1,0:T(8,128)(2,1)} %w_out.1) | copy-start | bytes 1179652
  16.9 41.9 %copy-start.82 = (bf16[64,1024]{1,0:T(8,128)(2,1)S(1)}, bf16[64,1024]{1,0:T(8,128)(2,1)}, u32[]{:S(2)}) copy-start(bf16[64,1024]{1,0:T(8,128)(2,1)} %param.35) | copy-start | bytes 393220
  17.1 15.2 %collective-permute-start = (bf16[128,1408]{1,0:T(8,128)(2,1)S(1)}, bf16[128,1408]{1,0:T(8,128)(2,1)S(1)}, u32[]{:S(2)}, u32[]{:S(2)}) collective-permute-start(bf16[128,1408]{1,0:T(8,128)(2,1)S(1)} %concatenate.111), channel_id=1, source_target_pairs={{0,2},{1,3},{2,4},{3,5},{4,6},{5,7},{6,0},{7,1},{8,10},{9,11},{10,... | collective-permute-start | bytes 1081352 | tf_op jit(solution)/shard_map/ppermute | solution.py:838
  20.2 34.2 %collective-permute-start.3 = (bf16[128,1408]{1,0:T(8,128)(2,1)S(1)}, bf16[128,1408]{1,0:T(8,128)(2,1)}, u32[]{:S(2)}, u32[]{:S(2)}) collective-permute-start(bf16[128,1408]{1,0:T(8,128)(2,1)S(1)} %concatenate.111), channel_id=1, source_target_pairs={{0,4},{1,5},{2,6},{3,7},{4,0},{5,1},{6,2},{7,3},{8,12},{9,13},{10,... | collective-permute-start | bytes 1081352 | tf_op jit(solution)/shard_map/ppermute | solution.py:838
  22.8 33.1 %collective-permute-start.4 = (bf16[128,1408]{1,0:T(8,128)(2,1)S(1)}, bf16[128,1408]{1,0:T(8,128)(2,1)}, u32[]{:S(2)}, u32[]{:S(2)}) collective-permute-start(bf16[128,1408]{1,0:T(8,128)(2,1)S(1)} %concatenate.111), channel_id=1, source_target_pairs={{0,6},{1,7},{2,0},{3,1},{4,2},{5,3},{6,4},{7,5},{8,14},{9,15},{10,... | collective-permute-start | bytes 1081352 | tf_op jit(solution)/shard_map/ppermute | solution.py:838
  24.1 43.5 %collective-permute-start.5 = (bf16[128,1408]{1,0:T(8,128)(2,1)S(1)}, bf16[128,1408]{1,0:T(8,128)(2,1)}, u32[]{:S(2)}, u32[]{:S(2)}) collective-permute-start(bf16[128,1408]{1,0:T(8,128)(2,1)S(1)} %concatenate.111), channel_id=1, source_target_pairs={{0,1},{1,0},{2,3},{3,2},{4,5},{5,4},{6,7},{7,6},{8,9},{9,8},{10,11... | collective-permute-start | bytes 1081352 | tf_op jit(solution)/shard_map/ppermute | solution.py:835
  32.3 27.4 %copy-start.33 = (bf16[128,1408]{1,0:T(8,128)(2,1)}, bf16[128,1408]{1,0:T(8,128)(2,1)S(1)}, u32[]{:S(2)}) copy-start(bf16[128,1408]{1,0:T(8,128)(2,1)S(1)} %collective-permute-done) | copy-start | bytes 1081348
  32.3 11.5 %collective-permute-start.1 = (bf16[256,1024]{1,0:T(8,128)(2,1)S(1)}, bf16[256,1024]{1,0:T(8,128)(2,1)S(1)}, u32[]{:S(2)}, u32[]{:S(2)}) collective-permute-start(bf16[256,1024]{1,0:T(8,128)(2,1)S(1)} %bitcast.280), channel_id=1, source_target_pairs={{0,16},{8,24},{16,0},{24,8},{1,17},{9,25},{17,1},{25,9},{2,18},{10... | collective-permute-start | bytes 1572872 | tf_op jit(solution)/shard_map/ppermute | solution.py:835
  43.9 15.8 %collective-permute-start.2 = (bf16[2,256,1024]{2,1,0:T(8,128)(2,1)S(1)}, bf16[2,256,1024]{2,1,0:T(8,128)(2,1)S(1)}, u32[]{:S(2)}, u32[]{:S(2)}) collective-permute-start(bf16[2,256,1024]{2,1,0:T(8,128)(2,1)S(1)} %pad_maximum_fusion.2.refs_0_), channel_id=1, source_target_pairs={{0,8},{8,0},{16,24},{24,16},{1,9},{9,1},{17,25},{25,17},{2,10},{10... | collective-permute-start | bytes 3145736 | tf_op jit(solution)/shard_map/ppermute | solution.py:835
  44.4 53.3 %copy-start.41 = (s32[9]{0:T(128)}, s32[9]{0:T(128)S(1)}, u32[]{:S(2)}) copy-start(s32[9]{0:T(128)S(1)} %pad_add_fusion.1.ends) | copy-start | bytes 112
  44.5 23.1 %collective-permute-start.6 = (bf16[128,1408]{1,0:T(8,128)(2,1)S(1)}, bf16[128,1408]{1,0:T(8,128)(2,1)}, u32[]{:S(2)}, u32[]{:S(2)}) collective-permute-start(bf16[128,1408]{1,0:T(8,128)(2,1)S(1)} %collective-permute-done), channel_id=1, source_target_pairs={{0,1},{1,0},{2,3},{3,2},{4,5},{5,4},{6,7},{7,6},{8,9},{9,8},{10,11... | collective-permute-start | bytes 1081352 | tf_op jit(solution)/shard_map/ppermute | solution.py:835
  54.4 13.2 %collective-permute-start.7 = (bf16[128,1408]{1,0:T(8,128)(2,1)}, bf16[128,1408]{1,0:T(8,128)(2,1)}, u32[]{:S(2)}, u32[]{:S(2)}) collective-permute-start(bf16[128,1408]{1,0:T(8,128)(2,1)} %collective-permute-done.3), channel_id=1, source_target_pairs={{0,1},{1,0},{2,3},{3,2},{4,5},{5,4},{6,7},{7,6},{8,9},{9,8},{10,11... | collective-permute-start | bytes 1081352 | tf_op jit(solution)/shard_map/ppermute | solution.py:835
  55.9 22.2 %collective-permute-start.8 = (bf16[128,1408]{1,0:T(8,128)(2,1)}, bf16[128,1408]{1,0:T(8,128)(2,1)}, u32[]{:S(2)}, u32[]{:S(2)}) collective-permute-start(bf16[128,1408]{1,0:T(8,128)(2,1)} %collective-permute-done.4), channel_id=1, source_target_pairs={{0,1},{1,0},{2,3},{3,2},{4,5},{5,4},{6,7},{7,6},{8,9},{9,8},{10,11... | collective-permute-start | bytes 1081352 | tf_op jit(solution)/shard_map/ppermute | solution.py:835
  58.7 39.0 %copy-start.42 = (f32[6]{0:T(128)}, f32[6]{0:T(128)S(1)}, u32[]{:S(2)}) copy-start(f32[6]{0:T(128)S(1)} %dynamic_slice.150.skip) | copy-start | bytes 76
  58.9 30.9 %copy-start.40 = (f32[8,128]{1,0:T(8,128)}, f32[8,128]{1,0:T(8,128)S(1)}, u32[]{:S(2)}) copy-start(f32[8,128]{1,0:T(8,128)S(1)} %select_maximum_fusion.params) | copy-start | bytes 12292
  59.7 18.4 %copy-start.34 = (bf16[128,1408]{1,0:T(8,128)(2,1)S(1)}, bf16[128,1408]{1,0:T(8,128)(2,1)}, u32[]{:S(2)}) copy-start(bf16[128,1408]{1,0:T(8,128)(2,1)} %copy-done.33) | copy-start | bytes 1081348
  59.7 48.7 %collective-permute-start.11 = (bf16[256,1024]{1,0:T(8,128)(2,1)}, bf16[256,1024]{1,0:T(8,128)(2,1)}, u32[]{:S(2)}, u32[]{:S(2)}) collective-permute-start(bf16[256,1024]{1,0:T(8,128)(2,1)} %pad_maximum_fusion.10), channel_id=1, source_target_pairs={{0,0},{1,1},{2,8},{3,9},{4,16},{5,17},{6,24},{7,25},{8,2},{9,3},{1... | collective-permute-start | bytes 1572872 | tf_op jit(solution)/shard_map/ppermute | solution.py:847
  97.7 20.8 %copy-start.35 = (f32[16,1024]{1,0:T(8,128)}, f32[16,1024]{1,0:T(8,128)S(1)}, u32[]{:S(2)}) copy-start(f32[16,1024]{1,0:T(8,128)S(1)} %get-tuple-element.120.rows) | copy-start | bytes 196612
  108.4 134.2 %copy-start.2 = (f32[1024,384]{1,0:T(8,128)}, f32[1024,384]{1,0:T(8,128)S(1)}, u32[]{:S(2)}) copy-start(f32[1024,384]{1,0:T(8,128)S(1)} %get-tuple-element.121.y_ref) | copy-start | bytes 4718596
  108.4 25.7 %collective-permute-start.12 = (bf16[256,1024]{1,0:T(8,128)(2,1)}, bf16[256,1024]{1,0:T(8,128)(2,1)}, u32[]{:S(2)}, u32[]{:S(2)}) collective-permute-start(bf16[256,1024]{1,0:T(8,128)(2,1)} %collective-permute-done.11), channel_id=1, source_target_pairs={{0,1},{1,0},{2,3},{3,2},{4,5},{5,4},{6,7},{7,6},{8,9},{9,8},{10,11... | collective-permute-start | bytes 1572872 | tf_op jit(solution)/shard_map/ppermute | solution.py:835
  118.5 17.5 %copy-start.4 = (f32[1024,384]{1,0:T(8,128)}, f32[1024,384]{1,0:T(8,128)S(1)}, u32[]{:S(2)}) copy-start(f32[1024,384]{1,0:T(8,128)S(1)} %get-tuple-element.124.z_ref) | copy-start | bytes 4718596
  120.6 1.2 collective-permute-start.9
  121.9 7.4 %collective-permute-start.10 = (f32[16,128]{1,0:T(8,128)S(1)}, f32[16,128]{1,0:T(8,128)S(1)}, u32[]{:S(2)}, u32[]{:S(2)}) collective-permute-start(f32[16,128]{1,0:T(8,128)S(1)} %add.420), channel_id=1, source_target_pairs={{0,16},{8,24},{16,0},{24,8},{1,17},{9,25},{17,1},{25,9},{2,18},{10... | collective-permute-start | bytes 24584 | tf_op jit(solution)/shard_map/ppermute | solution.py:835
  141.3 3.0 collective-permute-start.13
  146.6 14.3 %collective-permute-start.14 = (bf16[256,1024]{1,0:T(8,128)(2,1)}, bf16[256,1024]{1,0:T(8,128)(2,1)}, u32[]{:S(2)}, u32[]{:S(2)}) collective-permute-start(bf16[256,1024]{1,0:T(8,128)(2,1)} %fusion.17), channel_id=1, source_target_pairs={{0,16},{8,24},{16,0},{24,8},{1,17},{9,25},{17,1},{25,9},{2,18},{10... | collective-permute-start | bytes 1572872 | tf_op jit(solution)/shard_map/ppermute | solution.py:835
  163.0 2.0 collective-permute-start.15
  169.0 2.0 collective-permute-start.16
  172.9 2.0 collective-permute-start.17
  193.8 2.3 collective-permute-start.18
  201.5 14.0 %collective-permute-start.19 = (bf16[256,1024]{1,0:T(8,128)(2,1)S(1)}, bf16[256,1024]{1,0:T(8,128)(2,1)S(1)}, u32[]{:S(2)}, u32[]{:S(2)}) collective-permute-start(bf16[256,1024]{1,0:T(8,128)(2,1)S(1)} %get-tuple-element.220), channel_id=1, source_target_pairs={{0,16},{8,24},{16,0},{24,8},{1,17},{9,25},{17,1},{25,9},{2,18},{10... | collective-permute-start | bytes 1572872 | tf_op jit(solution)/shard_map/ppermute | solution.py:835
  216.5 3.0 collective-permute-start.20
  225.2 3.3 collective-permute-start.21
  228.5 14.0 %collective-permute-start.22 = (f32[8,128]{1,0:T(8,128)S(1)}, f32[8,128]{1,0:T(8,128)S(1)}, u32[]{:S(2)}, u32[]{:S(2)}) collective-permute-start(f32[8,128]{1,0:T(8,128)S(1)} %bitcast_add_fusion), channel_id=1, source_target_pairs={{0,16},{8,24},{16,0},{24,8},{1,17},{9,25},{17,1},{25,9},{2,18},{10... | collective-permute-start | bytes 12296 | tf_op jit(solution)/shard_map/ppermute | solution.py:835
  231.2 20.8 %collective-permute-start.23 = (bf16[256,1024]{1,0:T(8,128)(2,1)}, bf16[256,1024]{1,0:T(8,128)(2,1)}, u32[]{:S(2)}, u32[]{:S(2)}) collective-permute-start(bf16[256,1024]{1,0:T(8,128)(2,1)} %dynamic-slice_bitcast_fusion.2), channel_id=1, source_target_pairs={{0,1},{1,0},{2,3},{3,2},{4,5},{5,4},{6,7},{7,6},{8,9},{9,8},{10,11... | collective-permute-start | bytes 1572872 | tf_op jit(solution)/shard_map/ppermute | solution.py:835
  253.2 31.3 %collective-permute-start.24 = (bf16[4,128,640]{2,1,0:T(8,128)(2,1)}, bf16[4,128,640]{2,1,0:T(8,128)(2,1)S(1)}, u32[]{:S(2)}, u32[]{:S(2)}) collective-permute-start(bf16[4,128,640]{2,1,0:T(8,128)(2,1)} %dynamic-slice_bitcast_fusion.1), channel_id=1, source_target_pairs={{0,1},{1,0},{2,3},{3,2},{4,5},{5,4},{6,7},{7,6},{8,9},{9,8},{10,11... | collective-permute-start | bytes 1966088 | tf_op jit(solution)/shard_map/ppermute | solution.py:835
  256.3 28.2 %collective-permute-start.25 = (bf16[64,1024]{1,0:T(8,128)(2,1)S(1)}, bf16[64,1024]{1,0:T(8,128)(2,1)S(1)}, u32[]{:S(2)}, u32[]{:S(2)}) collective-permute-start(bf16[64,1024]{1,0:T(8,128)(2,1)S(1)} %get-tuple-element.243), channel_id=1, source_target_pairs={{0,2},{1,3},{2,4},{3,5},{4,6},{5,7},{6,0},{7,1},{8,10},{9,11},{10,... | collective-permute-start | bytes 393224 | tf_op jit(solution)/shard_map/ppermute | solution.py:838
  259.6 24.9 %collective-permute-start.26 = (bf16[64,1024]{1,0:T(8,128)(2,1)S(1)}, bf16[64,1024]{1,0:T(8,128)(2,1)S(1)}, u32[]{:S(2)}, u32[]{:S(2)}) collective-permute-start(bf16[64,1024]{1,0:T(8,128)(2,1)S(1)} %get-tuple-element.242), channel_id=1, source_target_pairs={{0,4},{1,5},{2,6},{3,7},{4,0},{5,1},{6,2},{7,3},{8,12},{9,13},{10,... | collective-permute-start | bytes 393224 | tf_op jit(solution)/shard_map/ppermute | solution.py:838
  261.1 23.4 %collective-permute-start.27 = (bf16[64,1024]{1,0:T(8,128)(2,1)S(1)}, bf16[64,1024]{1,0:T(8,128)(2,1)S(1)}, u32[]{:S(2)}, u32[]{:S(2)}) collective-permute-start(bf16[64,1024]{1,0:T(8,128)(2,1)S(1)} %get-tuple-element.241), channel_id=1, source_target_pairs={{0,6},{1,7},{2,0},{3,1},{4,2},{5,3},{6,4},{7,5},{8,14},{9,15},{10,... | collective-permute-start | bytes 393224 | tf_op jit(solution)/shard_map/ppermute | solution.py:838
  265.1 20.4 %copy-start.13 = (bf16[1024,1024]{1,0:T(8,128)(2,1)S(1)}, bf16[1024,1024]{1,0:T(8,128)(2,1)}, u32[]{:S(2)}) copy-start(bf16[1024,1024]{1,0:T(8,128)(2,1)} %copy-done.10) | copy-start | bytes 6291460
  299.9 2.7 collective-permute-start.28
  302.7 14.2 %collective-permute-start.29 = (bf16[256,1024]{1,0:T(8,128)(2,1)S(1)}, bf16[256,1024]{1,0:T(8,128)(2,1)S(1)}, u32[]{:S(2)}, u32[]{:S(2)}) collective-permute-start(bf16[256,1024]{1,0:T(8,128)(2,1)S(1)} %fusion.14), channel_id=1, source_target_pairs={{0,16},{8,24},{16,0},{24,8},{1,17},{9,25},{17,1},{25,9},{2,18},{10... | collective-permute-start | bytes 1572872 | tf_op jit(solution)/shard_map/ppermute | solution.py:835
  304.7 24.6 %collective-permute-start.30 = (bf16[4,128,768]{1,2,0:T(8,128)(2,1)S(1)}, bf16[4,128,768]{1,2,0:T(8,128)(2,1)S(1)}, u32[]{:S(2)}, u32[]{:S(2)}) collective-permute-start(bf16[4,128,768]{1,2,0:T(8,128)(2,1)S(1)} %dynamic-slice_bitcast_fusion), channel_id=1, source_target_pairs={{0,1},{1,0},{2,3},{3,2},{4,5},{5,4},{6,7},{7,6},{8,9},{9,8},{10,11... | collective-permute-start | bytes 2359304 | tf_op jit(solution)/shard_map/ppermute | solution.py:835
  305.8 12.5 %collective-permute-start.31 = (bf16[128,640]{1,0:T(8,128)(2,1)S(1)}, bf16[128,640]{1,0:T(8,128)(2,1)S(1)}, u32[]{:S(2)}, u32[]{:S(2)}) collective-permute-start(bf16[128,640]{1,0:T(8,128)(2,1)S(1)} %get-tuple-element.239), channel_id=1, source_target_pairs={{0,2},{1,3},{2,4},{3,5},{4,6},{5,7},{6,0},{7,1},{8,10},{9,11},{10,... | collective-permute-start | bytes 491528 | tf_op jit(solution)/shard_map/ppermute | solution.py:838
  305.8 23.4 %collective-permute-start.32 = (bf16[128,640]{1,0:T(8,128)(2,1)S(1)}, bf16[128,640]{1,0:T(8,128)(2,1)S(1)}, u32[]{:S(2)}, u32[]{:S(2)}) collective-permute-start(bf16[128,640]{1,0:T(8,128)(2,1)S(1)} %get-tuple-element.238), channel_id=1, source_target_pairs={{0,4},{1,5},{2,6},{3,7},{4,0},{5,1},{6,2},{7,3},{8,12},{9,13},{10,... | collective-permute-start | bytes 491528 | tf_op jit(solution)/shard_map/ppermute | solution.py:838
  306.5 22.8 %collective-permute-start.33 = (bf16[128,640]{1,0:T(8,128)(2,1)S(1)}, bf16[128,640]{1,0:T(8,128)(2,1)S(1)}, u32[]{:S(2)}, u32[]{:S(2)}) collective-permute-start(bf16[128,640]{1,0:T(8,128)(2,1)S(1)} %get-tuple-element.237), channel_id=1, source_target_pairs={{0,6},{1,7},{2,0},{3,1},{4,2},{5,3},{6,4},{7,5},{8,14},{9,15},{10,... | collective-permute-start | bytes 491528 | tf_op jit(solution)/shard_map/ppermute | solution.py:838
  329.5 21.4 %copy-start.52 = (bf16[1,256,1024]{2,1,0:T(8,128)(2,1)S(1)}, bf16[1,256,1024]{2,1,0:T(8,128)(2,1)}, u32[]{:S(2)}) copy-start(bf16[1,256,1024]{2,1,0:T(8,128)(2,1)} %param.21) | copy-start | bytes 1572868
  330.8 20.4 %copy-start.55 = (f32[256,1024]{1,0:T(8,128)S(1)}, f32[256,1024]{1,0:T(8,128)}, u32[]{:S(2)}) copy-start(f32[256,1024]{1,0:T(8,128)} %get-tuple-element.221) | copy-start | bytes 3145732
  341.2 21.1 %collective-permute-start.38 = (bf16[384,1024]{1,0:T(8,128)(2,1)}, bf16[384,1024]{1,0:T(8,128)(2,1)S(1)}, u32[]{:S(2)}, u32[]{:S(2)}) collective-permute-start(bf16[384,1024]{1,0:T(8,128)(2,1)} %bitcast.303), channel_id=1, source_target_pairs={{0,16},{8,24},{16,0},{24,8},{1,17},{9,25},{17,1},{25,9},{2,18},{10... | collective-permute-start | bytes 2359304 | tf_op jit(solution)/shard_map/ppermute | solution.py:835
  343.9 10.0 %collective-permute-start.34 = (bf16[128,768]{1,0:T(8,128)(2,1)}, bf16[128,768]{1,0:T(8,128)(2,1)S(1)}, u32[]{:S(2)}, u32[]{:S(2)}) collective-permute-start(bf16[128,768]{1,0:T(8,128)(2,1)} %bitcast.108), channel_id=1, source_target_pairs={{0,2},{1,3},{2,4},{3,5},{4,6},{5,7},{6,0},{7,1},{8,10},{9,11},{10,... | collective-permute-start | bytes 589832 | tf_op jit(solution)/shard_map/ppermute | solution.py:838
  347.5 14.8 %collective-permute-start.35 = (bf16[128,768]{1,0:T(8,128)(2,1)}, bf16[128,768]{1,0:T(8,128)(2,1)S(1)}, u32[]{:S(2)}, u32[]{:S(2)}) collective-permute-start(bf16[128,768]{1,0:T(8,128)(2,1)} %bitcast.109), channel_id=1, source_target_pairs={{0,4},{1,5},{2,6},{3,7},{4,0},{5,1},{6,2},{7,3},{8,12},{9,13},{10,... | collective-permute-start | bytes 589832 | tf_op jit(solution)/shard_map/ppermute | solution.py:838
  347.9 14.4 %collective-permute-start.36 = (bf16[128,768]{1,0:T(8,128)(2,1)}, bf16[128,768]{1,0:T(8,128)(2,1)S(1)}, u32[]{:S(2)}, u32[]{:S(2)}) collective-permute-start(bf16[128,768]{1,0:T(8,128)(2,1)} %bitcast.110), channel_id=1, source_target_pairs={{0,6},{1,7},{2,0},{3,1},{4,2},{5,3},{6,4},{7,5},{8,14},{9,15},{10,... | collective-permute-start | bytes 589832 | tf_op jit(solution)/shard_map/ppermute | solution.py:838
  350.0 2.5 collective-permute-start.37
  352.5 22.3 %copy-start.14 = (bf16[128,2048]{1,0:T(8,128)(2,1)S(1)}, bf16[128,2048]{1,0:T(8,128)(2,1)}, u32[]{:S(2)}) copy-start(bf16[128,2048]{1,0:T(8,128)(2,1)} %w_up.1) | copy-start | bytes 1572868
  352.5 22.3 %copy-start.15 = (bf16[128,2048]{1,0:T(8,128)(2,1)S(1)}, bf16[128,2048]{1,0:T(8,128)(2,1)}, u32[]{:S(2)}) copy-start(bf16[128,2048]{1,0:T(8,128)(2,1)} %w_gate.1) | copy-start | bytes 1572868
  362.6 2.4 collective-permute-start.39
  365.0 21.3 %collective-permute-start.40 = (bf16[128,1920]{1,0:T(8,128)(2,1)S(1)}, bf16[128,1920]{1,0:T(8,128)(2,1)S(1)}, u32[]{:S(2)}, u32[]{:S(2)}) collective-permute-start(bf16[128,1920]{1,0:T(8,128)(2,1)S(1)} %get-tuple-element.198), channel_id=1, source_target_pairs={{0,16},{8,24},{16,0},{24,8},{1,17},{9,25},{17,1},{25,9},{2,18},{10... | collective-permute-start | bytes 1474568 | tf_op jit(solution)/shard_map/ppermute | solution.py:835
  386.4 2.8 collective-permute-start.41
  (76 other events, 356.9 us)
Sparse Core Ops, SparseCore 0:
  14.5 137.7 all-gather.2
  194.1 147.1 reduce-scatter.1
